TPU v7x, 512 devices: a whole 4x8x8 slice. The times are simulated.
512 devices in a mesh: remap: 32 (over z, x), depth: 16 (over y, core).
Axes of the slice: x: 4, y: 8, z: 8, core: 2. Of those that a mesh axis runs over, the one named last changes fastest.
Arguments:
- wavefunction: bfloat16 [512, 256, 256], P('remap'), may hold values from -6 to 6
- right_home: int32 [512], P('remap'), may hold values from 0 to 511, as said below
- term_links: int32 [32, 512], P('depth', 'remap'), may hold values from 0 to 511, as said below
- sector_rows: int32 [128], P('remap'), may hold values from 64 to 256, as said below
- sector_cols: int32 [128], P('remap'), may hold values from 64 to 256, as said below
- left_env: bfloat16 [32, 128, 256, 256], P('depth', 'remap'), may hold values from -0.0625 to 0.0625
- right_env: bfloat16 [32, 128, 256, 256], P('depth', 'remap'), may hold values from -0.375 to 0.375
Outputs:
- applied: bfloat16 [512, 256, 256], P('remap', 'depth')
Inputs may be any that keep to these rules, and one draw needn't show every extreme that they name: `right_home`: A permutation of the 512 blocks. Remap device i holds positions i * 16 to (i + 1) * 16 - 1 in both groupings; from one remap device to another go at most 1 block, and some pair of devices carries exactly 1 in every draw. `term_links`: for each term a permutation of the 512 blocks; from one remap device to another go at most 1 block of one term, and some pair carries exactly 1 for every term. `sector_rows`: some sector has all 256 rows. `sector_cols`: some sector has all 256 columns.
All inputs are finite; a program needn't handle non-finite values.
Results may differ from a plain program's by a relative error of at most 0.022.
Values may be sent and summed in bfloat16 or wider, within the bound.
No kernel may reach another device: no remote copies, remote signals or barrier semaphores. Data moves between devices by JAX's collectives and lax.ppermute only.
A program may use at most 64 MiB of HBM per device.

v0:
```python
import jax
import jax.numpy as jnp
from jax import lax
from jax.sharding import PartitionSpec as P


def bucket(blocks, targets, block_count, peers, capacity):
    owners = targets // block_count
    target_slot = targets % block_count
    order_index = jnp.arange(block_count)
    earlier = (owners[:, None] == owners[None, :]) & (order_index[None, :] < order_index[:, None])
    rank_in = jnp.sum(earlier.astype(jnp.int32), axis=1)
    position = owners * capacity + rank_in
    buffer = (
        jnp.zeros((peers * capacity,) + blocks.shape[1:], blocks.dtype).at[position].set(blocks)
    )
    labels = jnp.full((peers * capacity,), block_count, jnp.int32).at[position].set(target_slot)
    return (buffer, labels)


def unpack(buffer, labels, block_count):
    empty = jnp.zeros((block_count,) + buffer.shape[1:], buffer.dtype)
    return empty.at[labels].set(buffer, mode="drop")


def local(wavefunction, right_home, term_links, sector_rows, sector_cols, left_env, right_env):
    block_count = wavefunction.shape[0]
    extent = wavefunction.shape[1]
    sectors = sector_rows.shape[0]
    per_sector = block_count // sectors
    peers = lax.axis_size("remap")
    capacity = max(1, (2 * block_count + peers - 1) // peers)
    term_count = left_env.shape[0]
    positions = jnp.arange(extent, dtype=jnp.int32)
    block_rows = jnp.repeat(sector_rows, per_sector)
    row_keep = (positions[None, :] < block_rows[:, None]).astype(jnp.bfloat16)
    masked = wavefunction * row_keep[:, :, None]
    buffer, labels = bucket(masked, right_home, block_count, peers, capacity)
    arrived, arrived_labels = (
        lax.all_to_all(buffer, "remap", split_axis=0, concat_axis=0, tiled=True),
        lax.all_to_all(labels, "remap", split_axis=0, concat_axis=0, tiled=True),
    )
    right_side = unpack(arrived, arrived_labels, block_count)
    col_keep = (positions[None, :] < jnp.repeat(sector_cols, per_sector)[:, None]).astype(
        jnp.bfloat16
    )
    right_side = right_side * col_keep[:, None, :]
    grouped = right_side.reshape(sectors, per_sector, extent, extent)
    accumulated = jnp.zeros((block_count, extent, extent), jnp.float32)
    for term_index in range(term_count):
        right_result = jnp.einsum(
            "sgij,sjk->sgik", grouped, right_env[term_index], preferred_element_type=jnp.float32
        )
        term_buffer, term_labels = bucket(
            right_result.reshape(block_count, extent, extent).astype(jnp.bfloat16),
            term_links[term_index],
            block_count,
            peers,
            capacity,
        )
        arrived, arrived_labels = (
            lax.all_to_all(term_buffer, "remap", split_axis=0, concat_axis=0, tiled=True),
            lax.all_to_all(term_labels, "remap", split_axis=0, concat_axis=0, tiled=True),
        )
        placed = unpack(arrived, arrived_labels, block_count)
        result = jnp.einsum(
            "sij,sgjk->sgik",
            left_env[term_index],
            placed.reshape(sectors, per_sector, extent, extent),
            preferred_element_type=jnp.float32,
        )
        accumulated = accumulated + result.reshape(block_count, extent, extent)
    rounded = lax.optimization_barrier(accumulated.astype(jnp.bfloat16)).astype(jnp.float32)
    summed = lax.psum_scatter(
        rounded.astype(jnp.bfloat16), "depth", scatter_dimension=1, tiled=True
    ).astype(jnp.float32)
    out_share = summed.shape[1]
    out_rows = lax.axis_index("depth") * out_share + jnp.arange(out_share, dtype=jnp.int32)
    out_keep = (out_rows[None, :] < block_rows[:, None]).astype(jnp.float32)
    return (summed * out_keep[:, :, None]).astype(jnp.bfloat16)


def solution(mesh):
    return jax.shard_map(
        local,
        mesh=mesh,
        in_specs=(
            P("remap", None, None),
            P("remap"),
            P("depth", "remap"),
            P("remap"),
            P("remap"),
            P("depth", "remap", None, None),
            P("depth", "remap", None, None),
        ),
        out_specs=P("remap", "depth", None),
        check_vma=False,
    )
```

profile of v0, /device:TPU:1, one launch (start us, length us, event | category | flops | bytes accessed | tf_op | source)
XLA Modules:
  0.0 461.6 jit_solution(6983180773218293042)
XLA Ops:
  8.7 13.7 %all-to-all-start.1 = ((s32[32,1,1]{2,1,0:T(1,128)}), s32[32,1,1]{2,1,0:T(1,128)S(1)}, u32[]{:S(2)}, u32[]{:S(2)}) async-start(s32[32,1,1]{2,1,0:T(1,128)} %copy.26), calls=%async_computation.1 | async-start | bytes 32768 | tf_op jit(solution)/shard_map/all_to_all | solution.py:41
  25.3 2.4 broadcast.320.clone.1
  27.7 5.2 %scatter_fusion = bf16[32,256,256]{2,1,0:T(8,128)(2,1)} fusion(bf16[32,256,256]{2,1,0:T(8,128)(2,1)} %broadcast.320.clone.1, s32[16]{0:T(128)S(1)} %compare_select_fusion.3, bf16[16,256,256]{2,1,0:T(8,128)(2,1)S(1)} %broadcast_multiply_fusion.1), kind=kCustom, calls=%fused_computation.2 | custom fusion | bytes 6291520 | tf_op jit(solution)/shard_map/scatter | solution.py:15
  32.9 9.6 %all-to-all-start.2 = ((bf16[32,256,256]{2,1,0:T(8,128)(2,1)}), bf16[32,256,256]{2,1,0:T(8,128)(2,1)}, u32[]{:S(2)}, u32[]{:S(2)}) async-start(bf16[32,256,256]{2,1,0:T(8,128)(2,1)} %scatter_fusion), calls=%async_computation.2 | async-start | bytes 8388608 | tf_op jit(solution)/shard_map/all_to_all | solution.py:40
  46.3 88.2 %all-to-all-done.2 = bf16[32,256,256]{2,1,0:T(8,128)(2,1)} async-done(((bf16[32,256,256]{2,1,0:T(8,128)(2,1)}), bf16[32,256,256]{2,1,0:T(8,128)(2,1)}, u32[]{:S(2)}, u32[]{:S(2)}) %all-to-all-start.2) | async-done | bytes 4194336 | tf_op jit(solution)/shard_map/all_to_all | solution.py:40
  134.5 8.5 %all-to-all-start = ((s32[32,1,1]{2,1,0:T(1,128)}), s32[32,1,1]{2,1,0:T(1,128)S(1)}, u32[]{:S(2)}, u32[]{:S(2)}) async-start(s32[32,1,1]{2,1,0:T(1,128)} %copy.25), calls=%async_computation | async-start | bytes 32768 | tf_op jit(solution)/shard_map/all_to_all | solution.py:63
  144.5 10.6 %scatter_fusion.1 = bf16[16,256,256]{2,1,0:T(8,128)(2,1)} fusion(bf16[16,256,256]{2,1,0:T(8,128)(2,1)} %broadcast.312.clone.1, s32[32]{0:T(128)S(1)} %fusion.16, bf16[32,256,256]{2,1,0:T(8,128)(2,1)} %all-to-all-done.2), kind=kCustom, calls=%fused_computation.3 | custom fusion | bytes 12583040 | tf_op jit(solution)/shard_map/scatter | solution.py:23
  157.0 9.2 %all-to-all-start.4 = ((s32[32,1,1]{2,1,0:T(1,128)}), s32[32,1,1]{2,1,0:T(1,128)S(1)}, u32[]{:S(2)}, u32[]{:S(2)}) async-start(s32[32,1,1]{2,1,0:T(1,128)} %copy.28), calls=%async_computation.4 | async-start | bytes 32768 | tf_op jit(solution)/shard_map/all_to_all | solution.py:63
  166.2 2.1 convolution_convert_fusion.1
  168.3 2.4 broadcast.320.clone
  170.7 5.9 %scatter_fusion.2 = bf16[32,256,256]{2,1,0:T(8,128)(2,1)} fusion(bf16[32,256,256]{2,1,0:T(8,128)(2,1)} %broadcast.320.clone, s32[16]{0:T(128)S(1)} %get-tuple-element.10, bf16[16,256,256]{2,1,0:T(8,128)(2,1)} %bitcast.116), kind=kCustom, calls=%fused_computation.4 | custom fusion | bytes 6291520 | tf_op jit(solution)/shard_map/scatter | solution.py:15
  176.7 9.4 %all-to-all-start.3 = ((bf16[32,256,256]{2,1,0:T(8,128)(2,1)}), bf16[32,256,256]{2,1,0:T(8,128)(2,1)}, u32[]{:S(2)}, u32[]{:S(2)}) async-start(bf16[32,256,256]{2,1,0:T(8,128)(2,1)} %scatter_fusion.2), calls=%async_computation.3 | async-start | bytes 8388608 | tf_op jit(solution)/shard_map/all_to_all | solution.py:62
  186.0 2.1 convolution_convert_fusion
  188.1 2.4 broadcast.320.clone.2
  190.6 5.2 %scatter_fusion.4 = bf16[32,256,256]{2,1,0:T(8,128)(2,1)} fusion(bf16[32,256,256]{2,1,0:T(8,128)(2,1)} %broadcast.320.clone.2, s32[16]{0:T(128)S(1)} %get-tuple-element.9, bf16[16,256,256]{2,1,0:T(8,128)(2,1)S(1)} %bitcast.115), kind=kCustom, calls=%fused_computation.7 | custom fusion | bytes 6291520 | tf_op jit(solution)/shard_map/scatter | solution.py:15
  195.8 83.0 %all-to-all-done.3 = bf16[32,256,256]{2,1,0:T(8,128)(2,1)} async-done(((bf16[32,256,256]{2,1,0:T(8,128)(2,1)}), bf16[32,256,256]{2,1,0:T(8,128)(2,1)}, u32[]{:S(2)}, u32[]{:S(2)}) %all-to-all-start.3) | async-done | bytes 4194336 | tf_op jit(solution)/shard_map/all_to_all | solution.py:62
  278.7 6.6 %all-to-all-start.5 = ((bf16[32,256,256]{2,1,0:T(8,128)(2,1)}), bf16[32,256,256]{2,1,0:T(8,128)(2,1)}, u32[]{:S(2)}, u32[]{:S(2)}) async-start(bf16[32,256,256]{2,1,0:T(8,128)(2,1)} %scatter_fusion.4), calls=%async_computation.5 | async-start | bytes 8388608 | tf_op jit(solution)/shard_map/all_to_all | solution.py:62
  287.0 6.3 %scatter_fusion.3 = bf16[16,256,256]{2,1,0:T(8,128)(2,1)S(1)} fusion(bf16[16,256,256]{2,1,0:T(8,128)(2,1)S(1)} %broadcast.312.clone, s32[32]{0:T(128)S(1)} %fusion.15, bf16[32,256,256]{2,1,0:T(8,128)(2,1)} %all-to-all-done.3), kind=kCustom, calls=%fused_computation.5 | custom fusion | bytes 12583040 | tf_op jit(solution)/shard_map/scatter | solution.py:23
  293.3 2.9 fusion.2
  296.2 81.3 %all-to-all-done.5 = bf16[32,256,256]{2,1,0:T(8,128)(2,1)} async-done(((bf16[32,256,256]{2,1,0:T(8,128)(2,1)}), bf16[32,256,256]{2,1,0:T(8,128)(2,1)}, u32[]{:S(2)}, u32[]{:S(2)}) %all-to-all-start.5) | async-done | bytes 4194336 | tf_op jit(solution)/shard_map/all_to_all | solution.py:62
  377.7 6.3 %scatter_fusion.5 = bf16[16,256,256]{2,1,0:T(8,128)(2,1)S(1)} fusion(bf16[16,256,256]{2,1,0:T(8,128)(2,1)S(1)} %broadcast.312.clone.2, s32[32]{0:T(128)S(1)} %fusion.18, bf16[32,256,256]{2,1,0:T(8,128)(2,1)} %all-to-all-done.5), kind=kCustom, calls=%fused_computation.8 | custom fusion | bytes 12583040 | tf_op jit(solution)/shard_map/scatter | solution.py:23
  384.0 4.5 add_convert_fusion
  388.5 3.9 copy.30
  392.5 60.6 %reduce-scatter.2.cloned.1.call-done = bf16[16,16,256]{2,1,0:T(8,128)(2,1)} async-done(((bf16[16,256,256]{2,1,0:T(8,128)(2,1)}), bf16[16,16,256]{2,1,0:T(8,128)(2,1)}) %reduce-scatter.2.cloned.1.call-update) | async-done | bytes 131088 | tf_op jit(solution)/shard_map/reduce_scatter | solution.py:74
  (50 shorter events, 15.6 us)
Async XLA Ops:
  8.7 24.2 %all-to-all-start.1 = ((s32[32,1,1]{2,1,0:T(1,128)}), s32[32,1,1]{2,1,0:T(1,128)S(1)}, u32[]{:S(2)}, u32[]{:S(2)}) async-start(s32[32,1,1]{2,1,0:T(1,128)} %copy.26), calls=%async_computation.1 | async-start | bytes 32768 | tf_op jit(solution)/shard_map/all_to_all | solution.py:41
  32.9 9.6 %copy-start.4 = (s32[4]{0:T(128)S(1)}, s32[4]{0:T(128)}, u32[]{:S(2)}) copy-start(s32[4]{0:T(128)} %param.11) | copy-start | bytes 52
  32.9 9.7 %copy-start.3 = (s32[2,16]{1,0:T(2,128)S(1)}, s32[2,16]{1,0:T(2,128)}, u32[]{:S(2)}) copy-start(s32[2,16]{1,0:T(2,128)} %param.9) | copy-start | bytes 388
  32.9 101.6 %all-to-all-start.2 = ((bf16[32,256,256]{2,1,0:T(8,128)(2,1)}), bf16[32,256,256]{2,1,0:T(8,128)(2,1)}, u32[]{:S(2)}, u32[]{:S(2)}) async-start(bf16[32,256,256]{2,1,0:T(8,128)(2,1)} %scatter_fusion), calls=%async_computation.2 | async-start | bytes 8388608 | tf_op jit(solution)/shard_map/all_to_all | solution.py:40
  134.5 22.5 %all-to-all-start = ((s32[32,1,1]{2,1,0:T(1,128)}), s32[32,1,1]{2,1,0:T(1,128)S(1)}, u32[]{:S(2)}, u32[]{:S(2)}) async-start(s32[32,1,1]{2,1,0:T(1,128)} %copy.25), calls=%async_computation | async-start | bytes 32768 | tf_op jit(solution)/shard_map/all_to_all | solution.py:63
  155.2 11.1 %copy-start.1 = (bf16[2,4,256,256]{3,2,1,0:T(8,128)(2,1)S(1)}, bf16[2,4,256,256]{3,2,1,0:T(8,128)(2,1)}, u32[]{:S(2)}) copy-start(bf16[2,4,256,256]{3,2,1,0:T(8,128)(2,1)} %param.13) | copy-start | bytes 3145732
  157.0 19.7 %all-to-all-start.4 = ((s32[32,1,1]{2,1,0:T(1,128)}), s32[32,1,1]{2,1,0:T(1,128)S(1)}, u32[]{:S(2)}, u32[]{:S(2)}) async-start(s32[32,1,1]{2,1,0:T(1,128)} %copy.28), calls=%async_computation.4 | async-start | bytes 32768 | tf_op jit(solution)/shard_map/all_to_all | solution.py:63
  176.7 102.1 %all-to-all-start.3 = ((bf16[32,256,256]{2,1,0:T(8,128)(2,1)}), bf16[32,256,256]{2,1,0:T(8,128)(2,1)}, u32[]{:S(2)}, u32[]{:S(2)}) async-start(bf16[32,256,256]{2,1,0:T(8,128)(2,1)} %scatter_fusion.2), calls=%async_computation.3 | async-start | bytes 8388608 | tf_op jit(solution)/shard_map/all_to_all | solution.py:62
  188.1 2.5 copy-start
  278.7 98.8 %all-to-all-start.5 = ((bf16[32,256,256]{2,1,0:T(8,128)(2,1)}), bf16[32,256,256]{2,1,0:T(8,128)(2,1)}, u32[]{:S(2)}, u32[]{:S(2)}) async-start(bf16[32,256,256]{2,1,0:T(8,128)(2,1)} %scatter_fusion.4), calls=%async_computation.5 | async-start | bytes 8388608 | tf_op jit(solution)/shard_map/all_to_all | solution.py:62
  285.4 167.7 %reduce-scatter.2.cloned.1.call-start = ((), (), s32[]{:S(2)}) async-start(), calls=%async_computation.7 | async-start | bytes 2228224 | tf_op jit(solution)/shard_map/reduce_scatter | solution.py:74
  287.0 6.3 %copy-start.2 = (bf16[2,4,256,256]{3,2,1,0:T(8,128)(2,1)S(1)}, bf16[2,4,256,256]{3,2,1,0:T(8,128)(2,1)}, u32[]{:S(2)}) copy-start(bf16[2,4,256,256]{3,2,1,0:T(8,128)(2,1)} %param.12) | copy-start | bytes 3145732
Sparse Core Ops, SparseCore 0:
  392.5 60.4 reduce-scatter.1
where the time goes:
time: 464 us; the launch traced here: 462 us
  waiting for transfers between devices  313 us (67%)
  local copies, waits for them, and re-layouts  57.6 us (12%)
  starting transfers between devices  57 us (12%)
  between operations  13.6 us (3%)
  matrix products  11.5 us (2%)
  other arithmetic  8.73 us (2%)
    all_to_all x2, waiting for transfers between devices, local(): lax.all_to_all(term_buffer, 'remap', split_axis=0, concat_axis=0, tiled=T...  164 us
    all_to_all x1, waiting for transfers between devices, local(): lax.all_to_all(buffer, 'remap', split_axis=0, concat_axis=0, tiled=True)  88.2 us
    reduce_scatter x1, waiting for transfers between devices, local(): lax.psum_scatter(rounded.astype(jnp.bfloat16), 'depth', scatter_dimension...  60.6 us
    scatter x3, local copies, waits for them, and re-layouts, unpack(): return empty.at[labels].set(buffer, mode='drop')  23.2 us
    all_to_all x2, starting transfers between devices, local(): lax.all_to_all(term_labels, 'remap', split_axis=0, concat_axis=0, tiled=T...  17.7 us
    scatter x3, local copies, waits for them, and re-layouts, bucket(): jnp.zeros((peers * capacity,) + blocks.shape[1:], blocks.dtype).at[position]  16.3 us
    all_to_all x2, starting transfers between devices, local(): lax.all_to_all(term_buffer, 'remap', split_axis=0, concat_axis=0, tiled=T...  16 us
    all_to_all x1, starting transfers between devices, local(): lax.all_to_all(labels, 'remap', split_axis=0, concat_axis=0, tiled=True)  13.7 us
  transfers between devices with their start and end apart: 7, of which 4 were waited for; matrix products, arithmetic and copies ran while one was open for 13% of the time, Pallas kernels for 0%

commit v1 on v0

v1 whole, which is shorter than its diff:
```python
import functools

import jax
import jax.numpy as jnp
from jax import lax
from jax.experimental import pallas as pl
from jax.experimental.pallas import tpu as pltpu
from jax.sharding import Mesh, PartitionSpec as P

LABEL_ROWS = 16
CHUNK = 128
VMEM_LIMIT = 48 * 1024 * 1024


def spread_kernel(count, core_ref, home_ref, links_ref, rows_ref, wave_ref, out_ref, label_ref):
    slots, half = out_ref.shape[0], wave_ref.shape[1]
    terms = links_ref.shape[0]
    per_sector = count // rows_ref.shape[0]
    core = core_ref[0]

    def clear(peer, carry):
        for kind in range(1 + terms):
            label_ref[kind, peer] = count
        return carry

    lax.fori_loop(0, slots, clear, 0)

    def fill(block, carry):
        home = home_ref[block]
        label_ref[0, lax.div(home, count)] = lax.rem(home, count)
        for term in range(terms):
            link = links_ref[term, block]
            label_ref[1 + term, lax.div(link, count)] = lax.rem(link, count)
        return carry

    lax.fori_loop(0, count, fill, 0)

    lane = lax.broadcasted_iota(jnp.int32, (LABEL_ROWS, out_ref.shape[2]), 1)

    def mark(peer, carry):
        tile = jnp.full(lane.shape, label_ref[0, peer], jnp.int32)
        for term in range(terms):
            tile = jnp.where(lane == 1 + term, label_ref[1 + term, peer], tile)
        out_ref[peer, half:, :] = tile.astype(jnp.float32).astype(jnp.bfloat16)
        return carry

    lax.fori_loop(0, slots, mark, 0)

    row = lax.broadcasted_iota(jnp.int32, wave_ref.shape[1:], 0) + core * half

    def put(block, carry):
        owner = lax.div(home_ref[block], count)
        keep = row < rows_ref[lax.div(block, per_sector)]
        value = wave_ref[block]
        out_ref[owner, 0:half, :] = jnp.where(keep, value, jnp.zeros_like(value))
        return carry

    lax.fori_loop(0, count, put, 0)


def spread(core, right_home, term_links, sector_rows, wavefunction, slots):
    count, extent, width = wavefunction.shape
    half = extent // 2
    smem = pl.BlockSpec(memory_space=pltpu.SMEM)
    return pl.pallas_call(
        functools.partial(spread_kernel, count),
        grid_spec=pltpu.PrefetchScalarGridSpec(
            num_scalar_prefetch=1,
            grid=(1,),
            in_specs=[
                smem,
                smem,
                smem,
                pl.BlockSpec((count, half, width), lambda i, core: (0, core[0], 0)),
            ],
            out_specs=pl.BlockSpec((slots, half + LABEL_ROWS, width), lambda i, core: (0, 0, 0)),
            scratch_shapes=[pltpu.SMEM((1 + term_links.shape[0], slots), jnp.int32)],
        ),
        out_shape=jax.ShapeDtypeStruct((slots, half + LABEL_ROWS, width), jnp.bfloat16),
        compiler_params=pltpu.CompilerParams(vmem_limit_bytes=VMEM_LIMIT),
        name="spread_blocks",
    )(core, right_home, term_links, sector_rows, wavefunction)


def right_kernel(core_ref, from_ref, links_ref, cols_ref, own_ref, other_ref, env_ref, out_ref):
    count = from_ref.shape[0]
    sectors = cols_ref.shape[0]
    per_sector = count // sectors
    terms = links_ref.shape[0]
    half = out_ref.shape[2] // 2
    core = core_ref[0]
    sector = pl.program_id(0)
    own_row = pl.multiple_of(core * half, half)
    other_row = pl.multiple_of((1 - core) * half, half)
    column = lax.broadcasted_iota(jnp.int32, (2 * half, own_ref.shape[2]), 1)
    keep = column < cols_ref[sector]
    for place in range(per_sector):
        block = sector * per_sector + place
        slot = from_ref[block]
        moved = jnp.concatenate([own_ref[slot, 0:half, :], other_ref[slot, 0:half, :]], axis=0)
        moved = jnp.where(keep, moved, jnp.zeros_like(moved))
        for term in range(terms):
            product = jnp.dot(
                moved, env_ref[term, 0], preferred_element_type=jnp.float32
            ).astype(jnp.bfloat16)
            owner = lax.div(links_ref[term, block], count)
            out_ref[owner, term, pl.ds(own_row, half), :] = product[0:half]
            out_ref[owner, term, pl.ds(other_row, half), :] = product[half:]


def right_products(core, source, term_links, sector_cols, own, other, right_env, chunk):
    slots, tall, width = own.shape
    terms, sectors, extent, _ = right_env.shape
    smem = pl.BlockSpec(memory_space=pltpu.SMEM)
    whole = pl.BlockSpec((slots, tall, width), lambda i: (0, 0, 0))
    return pl.pallas_call(
        right_kernel,
        grid=(sectors,),
        in_specs=[
            smem,
            smem,
            smem,
            smem,
            whole,
            whole,
            pl.BlockSpec((terms, 1, extent, CHUNK), lambda i: (0, i, 0, chunk)),
        ],
        out_specs=pl.BlockSpec((slots, terms, extent, CHUNK), lambda i: (0, 0, 0, 0)),
        out_shape=jax.ShapeDtypeStruct((slots, terms, extent, CHUNK), jnp.bfloat16),
        compiler_params=pltpu.CompilerParams(vmem_limit_bytes=VMEM_LIMIT),
        name="right_products",
    )(core, source, term_links, sector_cols, own, other, right_env)


def left_kernel(core_ref, from_ref, placed_ref, env_ref, keep_ref, send_ref):
    terms, count = from_ref.shape
    per_sector = count // pl.num_programs(0)
    chips, _, share, _ = keep_ref.shape
    core = core_ref[0]
    sector = pl.program_id(0)
    left = jnp.concatenate([env_ref[term, 0] for term in range(terms)], axis=1)
    for place in range(per_sector):
        block = sector * per_sector + place
        placed = jnp.concatenate(
            [placed_ref[from_ref[term, block], term] for term in range(terms)], axis=0
        )
        partial = jnp.dot(left, placed, preferred_element_type=jnp.float32).astype(jnp.bfloat16)
        halves = [
            jnp.stack([partial[(2 * c + k) * share : (2 * c + k + 1) * share] for c in range(chips)])
            for k in range(2)
        ]
        keep_ref[:, place] = jnp.where(core == 0, halves[0], halves[1])
        send_ref[:, place] = jnp.where(core == 0, halves[1], halves[0])


def left_products(core, source, arrived, left_env, chips):
    slots, terms, extent, width = arrived.shape
    _, sectors, _, _ = left_env.shape
    count = source.shape[1]
    share = extent // (2 * chips)
    smem = pl.BlockSpec(memory_space=pltpu.SMEM)
    out_spec = pl.BlockSpec((chips, count // sectors, share, width), lambda i: (0, i, 0, 0))
    shape = jax.ShapeDtypeStruct((chips, count, share, width), jnp.bfloat16)
    return pl.pallas_call(
        left_kernel,
        grid=(sectors,),
        in_specs=[
            smem,
            smem,
            pl.BlockSpec((slots, terms, extent, width), lambda i: (0, 0, 0, 0)),
            pl.BlockSpec((terms, 1, extent, extent), lambda i: (0, i, 0, 0)),
        ],
        out_specs=[out_spec, out_spec],
        out_shape=[shape, shape],
        compiler_params=pltpu.CompilerParams(vmem_limit_bytes=VMEM_LIMIT),
        name="left_products",
    )(core, source, arrived, left_env)


def local(wavefunction, right_home, term_links, sector_rows, sector_cols, left_env, right_env):
    count, extent, width = wavefunction.shape
    per_sector = count // sector_rows.shape[0]
    slots = lax.axis_size("remap")
    chips = lax.axis_size("y")
    core_index = lax.axis_index("core")
    core = core_index.reshape(1)

    buffer = spread(core, right_home, term_links, sector_rows, wavefunction, slots)
    own = lax.all_to_all(buffer, "remap", 0, 0, tiled=True)
    other = lax.ppermute(own, "core", [(0, 1), (1, 0)])
    labels = own[:, extent // 2, : 1 + term_links.shape[0]].astype(jnp.int32)
    match = labels.T[:, None, :] == jnp.arange(count, dtype=jnp.int32)[None, :, None]
    source = jnp.sum(jnp.where(match, jnp.arange(slots, dtype=jnp.int32), 0), axis=2)

    pieces = []
    for chunk in range(width // CHUNK):
        products = right_products(
            core, source[0], term_links, sector_cols, own, other, right_env, chunk
        )
        arrived = lax.all_to_all(products, "remap", 0, 0, tiled=True)
        keep, send = left_products(core, source[1:], arrived, left_env, chips)
        received = lax.ppermute(send, "core", [(0, 1), (1, 0)])
        pair = (keep.astype(jnp.float32) + received.astype(jnp.float32)).astype(jnp.bfloat16)
        if chunk + 1 < width // CHUNK:
            summed = lax.psum_scatter(pair, "y", scatter_dimension=0, tiled=False)
        else:
            gathered = lax.all_to_all(pair, "y", 0, 0, tiled=True)
            summed = jnp.sum(gathered.astype(jnp.float32), axis=0)
        pieces.append(summed.astype(jnp.float32))
    total = jnp.concatenate(pieces, axis=2)
    share = total.shape[1]
    first = (lax.axis_index("y") * 2 + core_index) * share
    row = first + jnp.arange(share, dtype=jnp.int32)
    keep_rows = row[None, :] < jnp.repeat(sector_rows, per_sector)[:, None]
    return jnp.where(keep_rows[:, :, None], total, 0.0).astype(jnp.bfloat16)


def solution(mesh):
    slots, depth = mesh.devices.shape
    split = Mesh(mesh.devices.reshape(slots, depth // 2, 2), ("remap", "y", "core"))
    deep = ("y", "core")
    return jax.shard_map(
        local,
        mesh=split,
        in_specs=(
            P("remap", None, None),
            P("remap"),
            P(deep, "remap"),
            P("remap"),
            P("remap"),
            P(deep, "remap", None, None),
            P(deep, "remap", None, None),
        ),
        out_specs=P("remap", deep, None),
        check_vma=False,
    )
```

time: 464 us -> 363 us (0.78)
  waiting for transfers between devices: 313 us -> 214 us
  blocking collectives: 0 us -> 69.9 us
  local copies, waits for them, and re-layouts: 57.6 us -> 3.85 us
  starting transfers between devices: 57 us -> 31.6 us
  Pallas kernels: 0 us -> 21 us
  matrix products: 11.5 us -> 0 us
    all_to_all x0 -> x1, blocking collectives: none -> 69.9 us  [local(): own = lax.all_to_all(buffer, 'remap', 0, 0, tiled=True)]
    all_to_all x6 -> x3, waiting for transfers between devices: 253 us -> 191 us  [the longest x2 174 us: local(): arrived = lax.all_to_all(products, 'remap', 0, 0, tiled=True)]
    reduce_scatter x1, waiting for transfers between devices: 60.6 us -> 18.5 us  [local(): summed = lax.psum_scatter(pair, 'y', scatter_dimension=0, tiled=False)]
    scatter x9 -> x0, local copies, waits for them, and re-layouts: 41.4 us -> none  [the longest x3 23.2 us: unpack(): return empty.at[labels].set(buffer, mode='drop')]
    all_to_all x6 -> x3, starting transfers between devices: 57 us -> 20.9 us  [the longest x2 14.2 us: local(): arrived = lax.all_to_all(products, 'remap', 0, 0, tiled=True)]
    pallas_call x0 -> x5, Pallas kernels: none -> 21 us  [the longest x2 11.1 us: right_products(): pl.pallas_call(right_kernel, grid=(sectors,), in_specs=[smem, smem, smem,...]
    dot_general x4 -> x0, matrix products: 11.5 us -> none  [the longest x2 7.32 us: local(): jnp.einsum('sij,sgjk->sgik', left_env[term_index], placed.reshape(sectors...]
    ppermute x0 -> x3, starting transfers between devices: none -> 10.6 us  [the longest x2 6.35 us: local(): received = lax.ppermute(send, 'core', [(0, 1), (1, 0)])]
  transfers between devices with their start and end apart: 7 -> 7, of which waited for: 4 -> 5; matrix products, arithmetic and copies ran while one was open for 13% -> 1% of each run, Pallas kernels for 0% -> 4%
where the time goes in v1:
time: 363 us; the launch traced here: 358 us
  waiting for transfers between devices  214 us (59%)
  blocking collectives  69.9 us (19%)
  starting transfers between devices  31.6 us (9%)
  Pallas kernels  21 us (6%)
  between operations  13.6 us (4%)
  other arithmetic  4.84 us (1%)
  local copies, waits for them, and re-layouts  3.85 us (1%)
    all_to_all x2, waiting for transfers between devices, local(): arrived = lax.all_to_all(products, 'remap', 0, 0, tiled=True)  174 us
    all_to_all x1, blocking collectives, local(): own = lax.all_to_all(buffer, 'remap', 0, 0, tiled=True)  69.9 us
    reduce_scatter x1, waiting for transfers between devices, local(): summed = lax.psum_scatter(pair, 'y', scatter_dimension=0, tiled=False)  18.5 us
    all_to_all x1, waiting for transfers between devices, local(): gathered = lax.all_to_all(pair, 'y', 0, 0, tiled=True)  16.7 us
    all_to_all x2, starting transfers between devices, local(): arrived = lax.all_to_all(products, 'remap', 0, 0, tiled=True)  14.2 us
    pallas_call x2, Pallas kernels, right_products(): pl.pallas_call(right_kernel, grid=(sectors,), in_specs=[smem, smem, smem,...  11.1 us
    pallas_call x2, Pallas kernels, left_products(): pl.pallas_call(left_kernel, grid=(sectors,), in_specs=[smem, smem, pl.Blo...  8.3 us
  transfers between devices with their start and end apart: 7, of which 5 were waited for; matrix products, arithmetic and copies ran while one was open for 1% of the time, Pallas kernels for 4%

profile of v1, /device:TPU:1, one launch (start us, length us, event | category | flops | bytes accessed | tf_op | source)
XLA Modules:
  0.0 358.4 jit_solution(670151459023828303)
XLA Ops:
  6.5 1.6 copy-done.2
  8.1 0.7 copy-done.3
  8.8 0.7 copy-done.6
  9.5 0.7 copy-done.8
  10.1 1.6 spread_blocks.1
  11.8 69.9 %all_to_all.20.own_ref = bf16[32,144,256]{2,1,0:T(8,128)(2,1)S(1)} all-to-all(bf16[32,144,256]{2,1,0:T(8,128)(2,1)S(1)} %spread_blocks.1), channel_id=1, replica_groups=mesh['remap'=32,'y'=8,'core'=2] {'remap'}, dimensions={0} | all-to-all | bytes 4718592 | tf_op jit(solution)/shard_map/all_to_all | solution.py:189
  81.7 4.3 %collective-permute-start = (bf16[32,144,256]{2,1,0:T(8,128)(2,1)S(1)}, bf16[32,144,256]{2,1,0:T(8,128)(2,1)}, u32[]{:S(2)}, u32[]{:S(2)}) collective-permute-start(bf16[32,144,256]{2,1,0:T(8,128)(2,1)S(1)} %all_to_all.20.own_ref), channel_id=1, source_target_pairs={{0,1},{1,0},{2,3},{3,2},{4,5},{5,4},{6,7},{7,6},{8,9},{9,8},{10,11... | collective-permute-start | bytes 7077896 | tf_op jit(solution)/shard_map/ppermute | solution.py:190
  86.3 4.0 %collective-permute-done.other_ref = bf16[32,144,256]{2,1,0:T(8,128)(2,1)} collective-permute-done((bf16[32,144,256]{2,1,0:T(8,128)(2,1)S(1)}, bf16[32,144,256]{2,1,0:T(8,128)(2,1)}, u32[]{:S(2)}, u32[]{:S(2)}) %collective-permute-start) | collective-permute-done | bytes 2359328 | tf_op jit(solution)/shard_map/ppermute | solution.py:190
  90.3 5.5 %right_products.3 = bf16[32,2,256,128]{3,2,1,0:T(8,128)(2,1)} custom-call(s32[1]{0:T(128)} %bitcast.core_ref, s32[16]{0:T(128)S(1)} %slice_bitcast_fusion.from_ref, s32[2,16]{1,0:T(2,128)S(1)} %copy-done.4, s32[4]{0:T(128)S(1)} %copy-done.5, bf16[32,144,256]{2,1,0:T(8,128)(2,1)S(1)} %all_to_all.20.own_ref, ...), custom_call_target="tpu_custom_call" | custom-call | tf_op jit(solution)/shard_map/right_products/pallas_call | solution.py:116
  95.8 4.9 %all-to-all-start.2 = ((bf16[32,2,256,128]{3,2,1,0:T(8,128)(2,1)}), bf16[32,2,256,128]{3,2,1,0:T(8,128)(2,1)}, u32[]{:S(2)}, u32[]{:S(2)}) async-start(bf16[32,2,256,128]{3,2,1,0:T(8,128)(2,1)} %right_products.3), calls=%async_computation.3 | async-start | bytes 8388608 | tf_op jit(solution)/shard_map/all_to_all | solution.py:200
  100.7 5.5 %right_products.2 = bf16[32,2,256,128]{3,2,1,0:T(8,128)(2,1)} custom-call(s32[1]{0:T(128)} %bitcast.core_ref, s32[16]{0:T(128)S(1)} %slice_bitcast_fusion.from_ref, s32[2,16]{1,0:T(2,128)S(1)} %copy-done.4, s32[4]{0:T(128)S(1)} %copy-done.5, bf16[32,144,256]{2,1,0:T(8,128)(2,1)S(1)} %all_to_all.20.own_ref, ...), custom_call_target="tpu_custom_call" | custom-call | tf_op jit(solution)/shard_map/right_products/pallas_call | solution.py:116
  106.2 87.9 %all-to-all-done.2.placed_ref = bf16[32,2,256,128]{3,2,1,0:T(8,128)(2,1)} async-done(((bf16[32,2,256,128]{3,2,1,0:T(8,128)(2,1)}), bf16[32,2,256,128]{3,2,1,0:T(8,128)(2,1)}, u32[]{:S(2)}, u32[]{:S(2)}) %all-to-all-start.2) | async-done | bytes 4194336 | tf_op jit(solution)/shard_map/all_to_all | solution.py:200
  194.1 9.3 %all-to-all-start.1 = ((bf16[32,2,256,128]{3,2,1,0:T(8,128)(2,1)}), bf16[32,2,256,128]{3,2,1,0:T(8,128)(2,1)}, u32[]{:S(2)}, u32[]{:S(2)}) async-start(bf16[32,2,256,128]{3,2,1,0:T(8,128)(2,1)} %right_products.2), calls=%async_computation.1 | async-start | bytes 8388608 | tf_op jit(solution)/shard_map/all_to_all | solution.py:200
  203.4 4.2 %left_products.3 = (bf16[8,16,16,128]{3,2,1,0:T(8,128)(2,1)S(1)}, bf16[8,16,16,128]{3,2,1,0:T(8,128)(2,1)S(1)}) custom-call(s32[1]{0:T(128)} %bitcast.core_ref, s32[2,16]{1,0:T(2,128)S(1)} %slice.12.from_ref, bf16[32,2,256,128]{3,2,1,0:T(8,128)(2,1)} %all-to-all-done.2.placed_ref, bf16[2,4,256,256]{3,2,1,0:T(8,128)(2,1)S(1)} %copy-done), custom_call_target="tpu_custom_call" | custom-call | tf_op jit(solution)/shard_map/left_products/pallas_call | solution.py:164
  207.6 2.7 collective-permute-start.2
  210.3 86.4 %all-to-all-done.1.placed_ref = bf16[32,2,256,128]{3,2,1,0:T(8,128)(2,1)} async-done(((bf16[32,2,256,128]{3,2,1,0:T(8,128)(2,1)}), bf16[32,2,256,128]{3,2,1,0:T(8,128)(2,1)}, u32[]{:S(2)}, u32[]{:S(2)}) %all-to-all-start.1) | async-done | bytes 4194336 | tf_op jit(solution)/shard_map/all_to_all | solution.py:200
  296.7 4.1 %left_products.2 = (bf16[8,16,16,128]{3,2,1,0:T(8,128)(2,1)S(1)}, bf16[8,16,16,128]{3,2,1,0:T(8,128)(2,1)S(1)}) custom-call(s32[1]{0:T(128)} %bitcast.core_ref, s32[2,16]{1,0:T(2,128)S(1)} %slice.12.from_ref, bf16[32,2,256,128]{3,2,1,0:T(8,128)(2,1)} %all-to-all-done.1.placed_ref, bf16[2,4,256,256]{3,2,1,0:T(8,128)(2,1)S(1)} %copy-done), custom_call_target="tpu_custom_call" | custom-call | tf_op jit(solution)/shard_map/left_products/pallas_call | solution.py:164
  300.8 3.7 %collective-permute-start.1 = (bf16[8,16,16,128]{3,2,1,0:T(8,128)(2,1)S(1)}, bf16[8,16,16,128]{3,2,1,0:T(8,128)(2,1)S(1)}, u32[]{:S(2)}, u32[]{:S(2)}) collective-permute-start(bf16[8,16,16,128]{3,2,1,0:T(8,128)(2,1)S(1)} %get-tuple-element.10), channel_id=1, source_target_pairs={{0,1},{1,0},{2,3},{3,2},{4,5},{5,4},{6,7},{7,6},{8,9},{9,8},{10,11... | collective-permute-start | bytes 1572872 | tf_op jit(solution)/shard_map/ppermute | solution.py:202
  304.6 2.0 add_convert_fusion
  306.5 6.8 %all-to-all-start.3 = ((bf16[8,16,16,128]{3,2,1,0:T(8,128)(2,1)}), bf16[8,16,16,128]{3,2,1,0:T(8,128)(2,1)S(1)}, u32[]{:S(2)}, u32[]{:S(2)}) async-start(bf16[8,16,16,128]{3,2,1,0:T(8,128)(2,1)} %add_convert_fusion), calls=%async_computation.4 | async-start | bytes 1048576 | tf_op jit(solution)/shard_map/all_to_all | solution.py:207
  313.4 1.0 add_convert_fusion.1
  314.6 16.7 %all-to-all-done.3 = bf16[8,16,16,128]{3,2,1,0:T(8,128)(2,1)S(1)} async-done(((bf16[8,16,16,128]{3,2,1,0:T(8,128)(2,1)}), bf16[8,16,16,128]{3,2,1,0:T(8,128)(2,1)S(1)}, u32[]{:S(2)}, u32[]{:S(2)}) %all-to-all-start.3) | async-done | bytes 524320 | tf_op jit(solution)/shard_map/all_to_all | solution.py:207
  331.4 18.5 %reduce-scatter.2.cloned.1.call-done = bf16[1,16,16,128]{3,2,1,0:T(8,128)(2,1)} async-done(((bf16[8,16,16,128]{3,2,1,0:T(8,128)(2,1)}), bf16[1,16,16,128]{3,2,1,0:T(8,128)(2,1)}) %reduce-scatter.2.cloned.1.call-update) | async-done | bytes 65552 | tf_op jit(solution)/shard_map/reduce_scatter | solution.py:205
  349.9 1.6 fusion
  (28 shorter events, 0.7 us)
Async XLA Ops:
  6.5 1.6 copy-start.2
  8.1 0.7 copy-start.3
  8.8 0.7 copy-start.6
  9.5 0.7 copy-start.8
  11.8 78.5 %copy-start.1 = (bf16[2,4,256,256]{3,2,1,0:T(8,128)(2,1)S(1)}, bf16[2,4,256,256]{3,2,1,0:T(8,128)(2,1)}, u32[]{:S(2)}) copy-start(bf16[2,4,256,256]{3,2,1,0:T(8,128)(2,1)} %env_ref.6) | copy-start | bytes 3145732
  11.8 78.5 %copy-start.4 = (s32[2,16]{1,0:T(2,128)S(1)}, s32[2,16]{1,0:T(2,128)}, u32[]{:S(2)}) copy-start(s32[2,16]{1,0:T(2,128)} %links_ref.5) | copy-start | bytes 388
  11.8 78.5 %copy-start.5 = (s32[4]{0:T(128)S(1)}, s32[4]{0:T(128)}, u32[]{:S(2)}) copy-start(s32[4]{0:T(128)} %cols_ref.3) | copy-start | bytes 52
  81.7 8.6 %collective-permute-start = (bf16[32,144,256]{2,1,0:T(8,128)(2,1)S(1)}, bf16[32,144,256]{2,1,0:T(8,128)(2,1)}, u32[]{:S(2)}, u32[]{:S(2)}) collective-permute-start(bf16[32,144,256]{2,1,0:T(8,128)(2,1)S(1)} %all_to_all.20.own_ref), channel_id=1, source_target_pairs={{0,1},{1,0},{2,3},{3,2},{4,5},{5,4},{6,7},{7,6},{8,9},{9,8},{10,11... | collective-permute-start | bytes 7077896 | tf_op jit(solution)/shard_map/ppermute | solution.py:190
  95.8 98.3 %all-to-all-start.2 = ((bf16[32,2,256,128]{3,2,1,0:T(8,128)(2,1)}), bf16[32,2,256,128]{3,2,1,0:T(8,128)(2,1)}, u32[]{:S(2)}, u32[]{:S(2)}) async-start(bf16[32,2,256,128]{3,2,1,0:T(8,128)(2,1)} %right_products.3), calls=%async_computation.3 | async-start | bytes 8388608 | tf_op jit(solution)/shard_map/all_to_all | solution.py:200
  106.2 97.2 %copy-start = (bf16[2,4,256,256]{3,2,1,0:T(8,128)(2,1)S(1)}, bf16[2,4,256,256]{3,2,1,0:T(8,128)(2,1)}, u32[]{:S(2)}) copy-start(bf16[2,4,256,256]{3,2,1,0:T(8,128)(2,1)} %env_ref.7) | copy-start | bytes 3145732
  194.1 102.6 %all-to-all-start.1 = ((bf16[32,2,256,128]{3,2,1,0:T(8,128)(2,1)}), bf16[32,2,256,128]{3,2,1,0:T(8,128)(2,1)}, u32[]{:S(2)}, u32[]{:S(2)}) async-start(bf16[32,2,256,128]{3,2,1,0:T(8,128)(2,1)} %right_products.2), calls=%async_computation.1 | async-start | bytes 8388608 | tf_op jit(solution)/shard_map/all_to_all | solution.py:200
  207.6 96.9 %collective-permute-start.2 = (bf16[8,16,16,128]{3,2,1,0:T(8,128)(2,1)S(1)}, bf16[8,16,16,128]{3,2,1,0:T(8,128)(2,1)}, u32[]{:S(2)}, u32[]{:S(2)}) collective-permute-start(bf16[8,16,16,128]{3,2,1,0:T(8,128)(2,1)S(1)} %get-tuple-element.12), channel_id=1, source_target_pairs={{0,1},{1,0},{2,3},{3,2},{4,5},{5,4},{6,7},{7,6},{8,9},{9,8},{10,11... | collective-permute-start | bytes 1572872 | tf_op jit(solution)/shard_map/ppermute | solution.py:202
  300.8 12.5 %collective-permute-start.1 = (bf16[8,16,16,128]{3,2,1,0:T(8,128)(2,1)S(1)}, bf16[8,16,16,128]{3,2,1,0:T(8,128)(2,1)S(1)}, u32[]{:S(2)}, u32[]{:S(2)}) collective-permute-start(bf16[8,16,16,128]{3,2,1,0:T(8,128)(2,1)S(1)} %get-tuple-element.10), channel_id=1, source_target_pairs={{0,1},{1,0},{2,3},{3,2},{4,5},{5,4},{6,7},{7,6},{8,9},{9,8},{10,11... | collective-permute-start | bytes 1572872 | tf_op jit(solution)/shard_map/ppermute | solution.py:202
  304.5 9.8 %copy-start.7 = (s32[4]{0:T(128)S(1)}, s32[4]{0:T(128)}, u32[]{:S(2)}) copy-start(s32[4]{0:T(128)} %rows_ref.1) | copy-start | bytes 52
  306.5 24.8 %all-to-all-start.3 = ((bf16[8,16,16,128]{3,2,1,0:T(8,128)(2,1)}), bf16[8,16,16,128]{3,2,1,0:T(8,128)(2,1)S(1)}, u32[]{:S(2)}, u32[]{:S(2)}) async-start(bf16[8,16,16,128]{3,2,1,0:T(8,128)(2,1)} %add_convert_fusion), calls=%async_computation.4 | async-start | bytes 1048576 | tf_op jit(solution)/shard_map/all_to_all | solution.py:207
  313.3 36.6 %reduce-scatter.2.cloned.1.call-start = ((), (), s32[]{:S(2)}) async-start(), calls=%async_computation.5 | async-start | bytes 589824 | tf_op jit(solution)/shard_map/reduce_scatter | solution.py:205
Sparse Core Ops, SparseCore 0:
  316.9 32.9 reduce-scatter.1

commit v2 on v1

v2 whole, which is shorter than its diff:
```python
import functools

import jax
import jax.numpy as jnp
from jax import lax
from jax.experimental import pallas as pl
from jax.experimental.pallas import tpu as pltpu
from jax.sharding import Mesh, PartitionSpec as P

SHARE = 16
LANES = 128
VMEM_LIMIT = 48 * 1024 * 1024
REMAP = ("zh", "zl", "x")
GROUP = ("zl", "x")
SMEM = pl.BlockSpec(memory_space=pltpu.SMEM)


def spread_kernel(count, depth_ref, home_ref, links_ref, rows_ref, wave_ref, out_ref, label_ref):
    slots = out_ref.shape[0]
    terms = links_ref.shape[0]
    per_sector = count // rows_ref.shape[0]

    def clear(peer, carry):
        for kind in range(1 + terms):
            label_ref[kind, peer] = count
        return carry

    lax.fori_loop(0, slots, clear, 0)

    def fill(block, carry):
        home = home_ref[block]
        label_ref[0, lax.div(home, count)] = lax.rem(home, count)
        for term in range(terms):
            link = links_ref[term, block]
            label_ref[1 + term, lax.div(link, count)] = lax.rem(link, count)
        return carry

    lax.fori_loop(0, count, fill, 0)
    lane = lax.broadcasted_iota(jnp.int32, (SHARE, LANES), 1)

    def mark(peer, carry):
        tile = jnp.full(lane.shape, label_ref[0, peer], jnp.int32)
        for term in range(terms):
            tile = jnp.where(lane == 1 + term, label_ref[1 + term, peer], tile)
        out_ref[peer, 2 * SHARE :, :] = tile.astype(jnp.float32).astype(jnp.bfloat16)
        return carry

    lax.fori_loop(0, slots, mark, 0)
    row = lax.broadcasted_iota(jnp.int32, wave_ref.shape[1:], 0) + depth_ref[0] * SHARE

    def put(block, carry):
        owner = lax.div(home_ref[block], count)
        keep = row < rows_ref[lax.div(block, per_sector)]
        value = wave_ref[block]
        value = jnp.where(keep, value, jnp.zeros_like(value))
        out_ref[owner, 0:SHARE, :] = value[:, :LANES]
        out_ref[owner, SHARE : 2 * SHARE, :] = value[:, LANES:]
        return carry

    lax.fori_loop(0, count, put, 0)


def spread(depth, right_home, term_links, sector_rows, wavefunction, slots):
    count, _, width = wavefunction.shape
    return pl.pallas_call(
        functools.partial(spread_kernel, count),
        grid_spec=pltpu.PrefetchScalarGridSpec(
            num_scalar_prefetch=1,
            grid=(1,),
            in_specs=[
                SMEM,
                SMEM,
                SMEM,
                pl.BlockSpec((count, SHARE, width), lambda i, depth: (0, depth[0], 0)),
            ],
            out_specs=pl.BlockSpec((slots, 3 * SHARE, LANES), lambda i, depth: (0, 0, 0)),
            scratch_shapes=[pltpu.SMEM((1 + term_links.shape[0], slots), jnp.int32)],
        ),
        out_shape=jax.ShapeDtypeStruct((slots, 3 * SHARE, LANES), jnp.bfloat16),
        name="spread_blocks",
    )(depth, right_home, term_links, sector_rows, wavefunction)


def order_kernel(from_ref, links_ref, cols_ref, in_ref, out_ref):
    terms, count = links_ref.shape
    per_sector = count // cols_ref.shape[0]
    lane = lax.broadcasted_iota(jnp.int32, (SHARE, LANES), 1)
    targets = jnp.zeros(lane.shape, jnp.int32)
    for block in range(count):
        slot = from_ref[block]
        cols = cols_ref[block // per_sector]
        for part in range(2):
            value = in_ref[slot, part * SHARE : (part + 1) * SHARE, :]
            out_ref[block, part * SHARE : (part + 1) * SHARE, :] = jnp.where(
                lane + part * LANES < cols, value, jnp.zeros_like(value)
            )
        for term in range(terms):
            owner = lax.div(links_ref[term, block], count)
            targets = jnp.where(lane == term * count + block, owner, targets)
    targets = targets.astype(jnp.float32).astype(jnp.bfloat16)
    out_ref[count, 0:SHARE, :] = targets
    out_ref[count, SHARE:, :] = targets


def order(source, term_links, sector_cols, arrived):
    count = source.shape[0]
    return pl.pallas_call(
        order_kernel,
        in_specs=[SMEM, SMEM, SMEM, pl.BlockSpec(memory_space=pltpu.VMEM)],
        out_specs=pl.BlockSpec(memory_space=pltpu.VMEM),
        out_shape=jax.ShapeDtypeStruct((count + 1, 2 * SHARE, LANES), jnp.bfloat16),
        name="order_blocks",
    )(source, term_links, sector_cols, arrived)


def right_kernel(steps, place_ref, targets_ref, *refs):
    slices, (env_ref, out_ref, moved_ref) = refs[: 2 * len(steps)], refs[2 * len(steps) :]
    group, layers, terms, extent, width = out_ref.shape
    sectors = env_ref.shape[2]
    count = slices[0].shape[1] - 1
    per_sector = count // sectors
    chips = len(steps)
    layer, chip, core = place_ref[0], place_ref[1], place_ref[2]
    turn = pl.program_id(0)
    from_layer = lax.rem(layer + turn, layers)
    for sector in range(sectors):
        for index, step in enumerate(steps):
            from_chip = lax.rem(chip + step + chips, chips)
            for other in range(2):
                from_core = core if other == 0 else 1 - core
                row = (from_chip * 2 + from_core) * SHARE
                source = slices[2 * index + other]
                for place in range(per_sector):
                    at = pl.ds(pl.multiple_of(place * extent + row, SHARE), SHARE)
                    block = sector * per_sector + place
                    moved_ref[sector % 2, at, 0:LANES] = source[0, block, 0:SHARE, :]
                    moved_ref[sector % 2, at, LANES:] = source[0, block, SHARE:, :]
        env = jnp.concatenate([env_ref[0, term, sector] for term in range(terms)], axis=1)
        product = jnp.dot(moved_ref[sector % 2], env, preferred_element_type=jnp.float32)
        product = product.astype(jnp.bfloat16)
        for place in range(per_sector):
            for term in range(terms):
                owner = targets_ref[turn, term * count + sector * per_sector + place]

                @pl.when(lax.div(owner, group) == layer)
                def _(place=place, term=term, owner=owner):
                    out_ref[lax.rem(owner, group), from_layer, term] = product[
                        place * extent : (place + 1) * extent, term * width : (term + 1) * width
                    ]


def right_products(place, targets, steps, slices, env, group):
    layers, terms, sectors, extent, width = env.shape
    _, blocks, tall, lanes = slices[0].shape
    per_sector = (blocks - 1) // sectors
    slice_spec = pl.BlockSpec((1, blocks, tall, lanes), lambda i, place, targets: (i, 0, 0, 0))
    return pl.pallas_call(
        functools.partial(right_kernel, steps),
        grid_spec=pltpu.PrefetchScalarGridSpec(
            num_scalar_prefetch=2,
            grid=(layers,),
            in_specs=[slice_spec] * len(slices)
            + [
                pl.BlockSpec(
                    (1, terms, sectors, extent, width),
                    lambda i, place, targets: (lax.rem(place[0] + i, layers), 0, 0, 0, 0),
                ),
            ],
            out_specs=pl.BlockSpec(
                (group, layers, terms, extent, width), lambda i, place, targets: (0, 0, 0, 0, 0)
            ),
            scratch_shapes=[pltpu.VMEM((2, per_sector * extent, extent), jnp.bfloat16)],
        ),
        out_shape=jax.ShapeDtypeStruct((group, layers, terms, extent, width), jnp.bfloat16),
        compiler_params=pltpu.CompilerParams(vmem_limit_bytes=VMEM_LIMIT),
        name="right_products",
    )(place, targets, *slices, env)


def left_partials(from_ref, placed_ref, env_ref):
    terms, count = from_ref.shape
    group = placed_ref.shape[0]
    per_sector = count // pl.num_programs(0)
    sector = pl.program_id(0)
    left = jnp.concatenate([env_ref[term, 0] for term in range(terms)], axis=1)
    for place in range(per_sector):
        parts = []
        for term in range(terms):
            device = from_ref[term, sector * per_sector + place]
            parts.append(placed_ref[lax.rem(device, group), lax.div(device, group), term])
        placed = jnp.concatenate(parts, axis=0)
        partial = jnp.dot(left, placed, preferred_element_type=jnp.float32)
        yield place, partial.astype(jnp.bfloat16)


def left_kernel(from_ref, placed_ref, env_ref, out_ref):
    for place, partial in left_partials(from_ref, placed_ref, env_ref):
        out_ref[:, place] = partial.reshape(out_ref.shape[0], SHARE, partial.shape[1])


def left_split_kernel(core_ref, from_ref, placed_ref, env_ref, keep_ref, send_ref):
    chips = keep_ref.shape[0]
    core = core_ref[0]
    for place, partial in left_partials(from_ref, placed_ref, env_ref):
        halves = [
            jnp.stack(
                [partial[(2 * c + k) * SHARE : (2 * c + k + 1) * SHARE] for c in range(chips)]
            )
            for k in range(2)
        ]
        keep_ref[:, place] = jnp.where(core == 0, halves[0], halves[1])
        send_ref[:, place] = jnp.where(core == 0, halves[1], halves[0])


def left_products(core, source, arrived, left_env, split):
    _, sectors, extent, _ = left_env.shape
    terms, count = source.shape
    width = arrived.shape[-1]
    pieces = extent // SHARE // (2 if split else 1)
    out_spec = pl.BlockSpec((pieces, count // sectors, SHARE, width), lambda i: (0, i, 0, 0))
    shape = jax.ShapeDtypeStruct((pieces, count, SHARE, width), jnp.bfloat16)
    specs = [
        SMEM,
        pl.BlockSpec(arrived.shape, lambda i: (0,) * arrived.ndim),
        pl.BlockSpec((terms, 1, extent, extent), lambda i: (0, i, 0, 0)),
    ]
    operands = [source, arrived, left_env]
    return pl.pallas_call(
        left_split_kernel if split else left_kernel,
        grid=(sectors,),
        in_specs=[SMEM] + specs if split else specs,
        out_specs=[out_spec, out_spec] if split else out_spec,
        out_shape=[shape, shape] if split else shape,
        compiler_params=pltpu.CompilerParams(vmem_limit_bytes=VMEM_LIMIT),
        name="left_products",
    )(*([core] + operands if split else operands))


def shift(array, axis, step):
    size = lax.axis_size(axis)
    return lax.ppermute(array, axis, [(i, (i + step) % size) for i in range(size)])


def gather_ring(own, axis):
    size = lax.axis_size(axis)
    found = [(0, own)]
    up = down = own
    for step in range(1, size // 2):
        up, down = shift(up, axis, 1), shift(down, axis, -1)
        found += [(-step, up), (step, down)]
    middle = own.shape[0] // 2
    last = jnp.concatenate([shift(up[:middle], axis, 1), shift(down[middle:], axis, -1)])
    return found + [(size // 2, last)]


def local(wavefunction, right_home, term_links, sector_rows, sector_cols, left_env, right_env):
    count, _, width = wavefunction.shape
    per_sector = count // sector_rows.shape[0]
    slots = lax.axis_size(REMAP)
    layers = lax.axis_size("zh")
    terms = term_links.shape[0]
    core_index = lax.axis_index("core")
    depth_index = lax.axis_index("y") * 2 + core_index
    core = core_index.reshape(1)
    place = jnp.stack([lax.axis_index("zh"), lax.axis_index("y"), core_index])
    chunks = [slice(at, at + LANES) for at in range(0, width, LANES)]

    envs = [lax.all_gather(right_env[..., chunk], "zh") for chunk in chunks]
    buffer = spread(depth_index.reshape(1), right_home, term_links, sector_rows, wavefunction, slots)
    arrived = lax.all_to_all(buffer, REMAP, 0, 0, tiled=True)
    labels = arrived[:, 2 * SHARE, : 1 + terms].astype(jnp.int32)
    match = labels.T[:, None, :] == jnp.arange(count, dtype=jnp.int32)[None, :, None]
    source = jnp.sum(jnp.where(match, jnp.arange(slots, dtype=jnp.int32), 0), axis=2)

    ordered = order(source[0], term_links, sector_cols, arrived)
    mine = jnp.stack([ordered] + [shift(ordered, "zh", -step) for step in range(1, layers)])
    targets = mine[:, count, 0, : terms * count].astype(jnp.int32)
    steps, slices = [], []
    for step, shard in gather_ring(mine, "y"):
        steps.append(step)
        slices += [shard, shift(shard, "core", 1)]

    pieces = []
    for env in envs:
        products = right_products(place, targets, steps, slices, env, slots // layers)
        arrived = lax.all_to_all(products, GROUP, 0, 0, tiled=True)
        if len(pieces) + 1 < len(envs):
            partial = left_products(core, source[1:], arrived, left_env, False)
            summed = lax.psum_scatter(partial, ("y", "core"), scatter_dimension=0, tiled=False)
            pieces.append(summed.astype(jnp.float32))
        else:
            keep, send = left_products(core, source[1:], arrived, left_env, True)
            pair = keep.astype(jnp.float32) + shift(send, "core", 1).astype(jnp.float32)
            gathered = lax.all_to_all(pair.astype(jnp.bfloat16), "y", 0, 0, tiled=True)
            pieces.append(jnp.sum(gathered.astype(jnp.float32), axis=0))
    total = jnp.concatenate(pieces, axis=2)
    row = depth_index * SHARE + jnp.arange(SHARE, dtype=jnp.int32)
    keep_rows = row[None, :] < jnp.repeat(sector_rows, per_sector)[:, None]
    return jnp.where(keep_rows[:, :, None], total, 0.0).astype(jnp.bfloat16)


def solution(mesh):
    slots, depth = mesh.devices.shape
    split = Mesh(
        mesh.devices.reshape(4, 2, slots // 8, depth // 2, 2), ("zh", "zl", "x", "y", "core")
    )
    deep = ("y", "core")
    return jax.shard_map(
        local,
        mesh=split,
        in_specs=(
            P(REMAP, None, None),
            P(REMAP),
            P(deep, REMAP),
            P(REMAP),
            P(REMAP),
            P(deep, REMAP, None, None),
            P(deep, REMAP, None, None),
        ),
        out_specs=P(REMAP, deep, None),
        check_vma=False,
    )
```

time: 363 us -> 364 us (level)
  blocking collectives: 69.9 us -> 0 us
  starting transfers between devices: 31.6 us -> 96.1 us
  waiting for transfers between devices: 214 us -> 193 us
  Pallas kernels: 21 us -> 40.7 us
  local copies, waits for them, and re-layouts: 3.85 us -> 14.4 us
    all_to_all x3 -> x4, waiting for transfers between devices: 191 us -> 72.7 us  [the longest x2 43.5 us: local(): arrived = lax.all_to_all(products, GROUP, 0, 0, tiled=True)]
    all_gather x0 -> x2, waiting for transfers between devices: none -> 75 us  [local(): envs = [lax.all_gather(right_env[..., chunk], 'zh') for chunk in chunks]]
    all_to_all x1 -> x0, blocking collectives: 69.9 us -> none  [local(): own = lax.all_to_all(buffer, 'remap', 0, 0, tiled=True)]
    ppermute x3 -> x20, starting transfers between devices: 10.6 us -> 65.5 us  [shift(): lax.ppermute(array, axis, [(i, (i + step) % size) for i in range(size)])]
    ppermute x3 -> x20, waiting for transfers between devices: 4.01 us -> 45.1 us  [shift(): lax.ppermute(array, axis, [(i, (i + step) % size) for i in range(size)])]
    pallas_call x4 -> x5, Pallas kernels: 19.4 us -> 38.1 us  [the longest x2 27.1 us: right_products(): pl.pallas_call(functools.partial(right_kernel, steps), grid_spec=pltpu.Pr...]
    reduce_scatter x1, waiting for transfers between devices: 18.5 us -> 0.02 us  [local(): lax.psum_scatter(partial, ('y', 'core'), scatter_dimension=0, tiled=False)]
    all_to_all x3 -> x4, starting transfers between devices: 20.9 us -> 30.4 us  [the longest x1 13.7 us: local(): arrived = lax.all_to_all(buffer, REMAP, 0, 0, tiled=True)]
  transfers between devices with their start and end apart: 7 -> 27, of which waited for: 5 -> 12; matrix products, arithmetic and copies ran while one was open for 1% -> 2% of each run, Pallas kernels for 4% -> 7%
where the time goes in v2:
time: 364 us; the launch traced here: 362 us
  waiting for transfers between devices  193 us (53%)
  starting transfers between devices  96.1 us (26%)
  Pallas kernels  40.7 us (11%)
  local copies, waits for them, and re-layouts  14.4 us (4%)
  between operations  13.5 us (4%)
  other arithmetic  3.89 us (1%)
    all_gather x2, waiting for transfers between devices, local(): envs = [lax.all_gather(right_env[..., chunk], 'zh') for chunk in chunks]  75 us
    ppermute x20, starting transfers between devices, shift(): lax.ppermute(array, axis, [(i, (i + step) % size) for i in range(size)])  65.5 us
    ppermute x20, waiting for transfers between devices, shift(): lax.ppermute(array, axis, [(i, (i + step) % size) for i in range(size)])  45.1 us
    all_to_all x2, waiting for transfers between devices, local(): arrived = lax.all_to_all(products, GROUP, 0, 0, tiled=True)  43.5 us
    pallas_call x2, Pallas kernels, right_products(): pl.pallas_call(functools.partial(right_kernel, steps), grid_spec=pltpu.Pr...  27.1 us
    all_to_all x1, waiting for transfers between devices, local(): gathered = lax.all_to_all(pair.astype(jnp.bfloat16), 'y', 0, 0, tiled=True)  17.7 us
    all_to_all x1, starting transfers between devices, local(): arrived = lax.all_to_all(buffer, REMAP, 0, 0, tiled=True)  13.7 us
    all_to_all x1, waiting for transfers between devices, local(): arrived = lax.all_to_all(buffer, REMAP, 0, 0, tiled=True)  11.4 us
  transfers between devices with their start and end apart: 27, of which 12 were waited for; matrix products, arithmetic and copies ran while one was open for 2% of the time, Pallas kernels for 7%

profile of v2, /device:TPU:1, one launch (start us, length us, event | category | flops | bytes accessed | tf_op | source)
XLA Modules:
  0.0 362.0 jit_solution(13753914353918366517)
XLA Ops:
  9.2 13.7 %all-to-all-start = ((bf16[32,48,128]{2,1,0:T(8,128)(2,1)}), bf16[32,48,128]{2,1,0:T(8,128)(2,1)S(1)}, u32[]{:S(2)}, u32[]{:S(2)}) async-start(bf16[32,48,128]{2,1,0:T(8,128)(2,1)} %spread_blocks.1), calls=%async_computation | async-start | bytes 786432 | tf_op jit(solution)/shard_map/all_to_all | solution.py:270
  25.3 11.4 %all-to-all-done.in_ref = bf16[32,48,128]{2,1,0:T(8,128)(2,1)S(1)} async-done(((bf16[32,48,128]{2,1,0:T(8,128)(2,1)}), bf16[32,48,128]{2,1,0:T(8,128)(2,1)S(1)}, u32[]{:S(2)}, u32[]{:S(2)}) %all-to-all-start) | async-done | bytes 393248 | tf_op jit(solution)/shard_map/all_to_all | solution.py:270
  39.3 3.6 %collective-permute-start.2 = (bf16[17,32,128]{2,1,0:T(8,128)(2,1)}, bf16[17,32,128]{2,1,0:T(8,128)(2,1)S(1)}, u32[]{:S(2)}, u32[]{:S(2)}) collective-permute-start(bf16[17,32,128]{2,1,0:T(8,128)(2,1)} %order_blocks.1), channel_id=1, source_target_pairs={{0,128},{128,256},{256,384},{384,0},{1,129},{129,257},{257,385},{3... | collective-permute-start | bytes 417800 | tf_op jit(solution)/shard_map/ppermute | solution.py:241
  43.0 4.1 %collective-permute-start.1 = (bf16[17,32,128]{2,1,0:T(8,128)(2,1)}, bf16[17,32,128]{2,1,0:T(8,128)(2,1)S(1)}, u32[]{:S(2)}, u32[]{:S(2)}) collective-permute-start(bf16[17,32,128]{2,1,0:T(8,128)(2,1)} %order_blocks.1), channel_id=1, source_target_pairs={{0,256},{128,384},{256,0},{384,128},{1,257},{129,385},{257,1},{385... | collective-permute-start | bytes 417800 | tf_op jit(solution)/shard_map/ppermute | solution.py:241
  50.3 3.6 collective-permute-done.2
  53.9 14.7 %collective-permute-done.1 = bf16[17,32,128]{2,1,0:T(8,128)(2,1)S(1)} collective-permute-done((bf16[17,32,128]{2,1,0:T(8,128)(2,1)}, bf16[17,32,128]{2,1,0:T(8,128)(2,1)S(1)}, u32[]{:S(2)}, u32[]{:S(2)}) %collective-permute-start.1) | collective-permute-done | bytes 139296 | tf_op jit(solution)/shard_map/ppermute | solution.py:241
  76.3 6.2 %collective-permute-start.6 = (bf16[4,17,32,128]{3,2,1,0:T(8,128)(2,1)S(1)}, bf16[4,17,32,128]{3,2,1,0:T(8,128)(2,1)S(1)}, u32[]{:S(2)}, u32[]{:S(2)}) collective-permute-start(bf16[4,17,32,128]{3,2,1,0:T(8,128)(2,1)S(1)} %pad_maximum_fusion.refs_0_), channel_id=1, source_target_pairs={{0,14},{2,0},{4,2},{6,4},{8,6},{10,8},{12,10},{14,12},{1,15},{3,1}... | collective-permute-start | bytes 1671176 | tf_op jit(solution)/shard_map/ppermute | solution.py:241
  82.5 9.4 %collective-permute-done.4.refs_2_ = bf16[4,17,32,128]{3,2,1,0:T(8,128)(2,1)S(1)} collective-permute-done((bf16[4,17,32,128]{3,2,1,0:T(8,128)(2,1)S(1)}, bf16[4,17,32,128]{3,2,1,0:T(8,128)(2,1)S(1)}, u32[]{:S(2)}, u32[]{:S(2)}) %collective-permute-start.4) | collective-permute-done | bytes 557088 | tf_op jit(solution)/shard_map/ppermute | solution.py:241
  93.8 4.6 %collective-permute-start.10 = (bf16[4,17,32,128]{3,2,1,0:T(8,128)(2,1)S(1)}, bf16[4,17,32,128]{3,2,1,0:T(8,128)(2,1)S(1)}, u32[]{:S(2)}, u32[]{:S(2)}) collective-permute-start(bf16[4,17,32,128]{3,2,1,0:T(8,128)(2,1)S(1)} %collective-permute-done.6.refs_4_), channel_id=1, source_target_pairs={{0,14},{2,0},{4,2},{6,4},{8,6},{10,8},{12,10},{14,12},{1,15},{3,1}... | collective-permute-start | bytes 1671176 | tf_op jit(solution)/shard_map/ppermute | solution.py:241
  98.4 8.5 %collective-permute-done.8.refs_6_ = bf16[4,17,32,128]{3,2,1,0:T(8,128)(2,1)S(1)} collective-permute-done((bf16[4,17,32,128]{3,2,1,0:T(8,128)(2,1)S(1)}, bf16[4,17,32,128]{3,2,1,0:T(8,128)(2,1)S(1)}, u32[]{:S(2)}, u32[]{:S(2)}) %collective-permute-start.8) | collective-permute-done | bytes 557088 | tf_op jit(solution)/shard_map/ppermute | solution.py:241
  108.8 4.6 %collective-permute-start.14 = (bf16[4,17,32,128]{3,2,1,0:T(8,128)(2,1)S(1)}, bf16[4,17,32,128]{3,2,1,0:T(8,128)(2,1)}, u32[]{:S(2)}, u32[]{:S(2)}) collective-permute-start(bf16[4,17,32,128]{3,2,1,0:T(8,128)(2,1)S(1)} %collective-permute-done.10.refs_8_), channel_id=1, source_target_pairs={{0,14},{2,0},{4,2},{6,4},{8,6},{10,8},{12,10},{14,12},{1,15},{3,1}... | collective-permute-start | bytes 1671176 | tf_op jit(solution)/shard_map/ppermute | solution.py:241
  113.4 5.6 %collective-permute-start.3 = (bf16[4,17,32,128]{3,2,1,0:T(8,128)(2,1)S(1)}, bf16[4,17,32,128]{3,2,1,0:T(8,128)(2,1)S(1)}, u32[]{:S(2)}, u32[]{:S(2)}) collective-permute-start(bf16[4,17,32,128]{3,2,1,0:T(8,128)(2,1)S(1)} %pad_maximum_fusion.refs_0_), channel_id=1, source_target_pairs={{0,1},{1,0},{2,3},{3,2},{4,5},{5,4},{6,7},{7,6},{8,9},{9,8},{10,11... | collective-permute-start | bytes 1671176 | tf_op jit(solution)/shard_map/ppermute | solution.py:241
  126.3 4.6 %collective-permute-start.17 = (bf16[2,17,32,128]{3,2,1,0:T(8,128)(2,1)S(1)}, bf16[2,17,32,128]{3,2,1,0:T(8,128)(2,1)S(1)}, u32[]{:S(2)}, u32[]{:S(2)}) collective-permute-start(bf16[2,17,32,128]{3,2,1,0:T(8,128)(2,1)S(1)} %slice.36), channel_id=1, source_target_pairs={{0,14},{2,0},{4,2},{6,4},{8,6},{10,8},{12,10},{14,12},{1,15},{3,1}... | collective-permute-start | bytes 835592 | tf_op jit(solution)/shard_map/ppermute | solution.py:241
  133.0 4.5 %collective-permute-start.9 = (bf16[4,17,32,128]{3,2,1,0:T(8,128)(2,1)S(1)}, bf16[4,17,32,128]{3,2,1,0:T(8,128)(2,1)}, u32[]{:S(2)}, u32[]{:S(2)}) collective-permute-start(bf16[4,17,32,128]{3,2,1,0:T(8,128)(2,1)S(1)} %collective-permute-done.8.refs_6_), channel_id=1, source_target_pairs={{0,1},{1,0},{2,3},{3,2},{4,5},{5,4},{6,7},{7,6},{8,9},{9,8},{10,11... | collective-permute-start | bytes 1671176 | tf_op jit(solution)/shard_map/ppermute | solution.py:241
  155.2 13.5 %right_products.2 = bf16[8,4,2,256,128]{4,3,2,1,0:T(8,128)(2,1)} custom-call(s32[3]{0:T(128)S(1)} %pad_add_fusion.place_ref, s32[4,32]{1,0:T(4,128)S(1)} %bitcast.20, bf16[4,17,32,128]{3,2,1,0:T(8,128)(2,1)S(1)} %pad_maximum_fusion.refs_0_, bf16[4,17,32,128]{3,2,1,0:T(8,128)(2,1)S(1)} %copy-done.2, ...), custom_call_target="tpu_custom_call" | custom-call | tf_op jit(solution)/shard_map/right_products/pallas_call | solution.py:157
  168.7 5.6 %all-to-all-start.1 = ((bf16[8,4,2,256,128]{4,3,2,1,0:T(8,128)(2,1)}), bf16[8,4,2,256,128]{4,3,2,1,0:T(8,128)(2,1)}, u32[]{:S(2)}, u32[]{:S(2)}) async-start(bf16[8,4,2,256,128]{4,3,2,1,0:T(8,128)(2,1)} %right_products.2), calls=%async_computation.1 | async-start | bytes 8388608 | tf_op jit(solution)/shard_map/all_to_all | solution.py:286
  175.0 74.9 %all-gather.7.cloned.1.call-done = bf16[8,4,256,128]{3,2,1,0:T(8,128)(2,1)} async-done(((bf16[2,4,256,128]{3,2,1,0:T(8,128)(2,1)}), bf16[8,4,256,128]{3,2,1,0:T(8,128)(2,1)}) %all-gather.7.cloned.1.call-update) | async-done | bytes 2097168 | tf_op jit(solution)/shard_map/all_gather | solution.py:268
  253.1 13.5 %right_products.3 = bf16[8,4,2,256,128]{4,3,2,1,0:T(8,128)(2,1)} custom-call(s32[3]{0:T(128)S(1)} %pad_add_fusion.place_ref, s32[4,32]{1,0:T(4,128)S(1)} %bitcast.21, bf16[4,17,32,128]{3,2,1,0:T(8,128)(2,1)S(1)} %pad_maximum_fusion.refs_0_, bf16[4,17,32,128]{3,2,1,0:T(8,128)(2,1)S(1)} %copy-done.3, ...), custom_call_target="tpu_custom_call" | custom-call | tf_op jit(solution)/shard_map/right_products/pallas_call | solution.py:157
  266.7 4.7 %all-to-all-start.2 = ((bf16[8,4,2,256,128]{4,3,2,1,0:T(8,128)(2,1)}), bf16[8,4,2,256,128]{4,3,2,1,0:T(8,128)(2,1)}, u32[]{:S(2)}, u32[]{:S(2)}) async-start(bf16[8,4,2,256,128]{4,3,2,1,0:T(8,128)(2,1)} %right_products.3), calls=%async_computation.3 | async-start | bytes 8388608 | tf_op jit(solution)/shard_map/all_to_all | solution.py:286
  271.4 5.1 %left_products.2 = bf16[16,16,16,128]{3,2,1,0:T(8,128)(2,1)} custom-call(s32[2,16]{1,0:T(2,128)S(1)} %slice.26.from_ref, bf16[8,4,2,256,128]{4,3,2,1,0:T(8,128)(2,1)} %all-to-all-done.1.placed_ref, bf16[2,4,256,256]{3,2,1,0:T(8,128)(2,1)S(1)} %copy-done), custom_call_target="tpu_custom_call" | custom-call | tf_op jit(solution)/shard_map/left_products/pallas_call | solution.py:228
  276.5 43.5 %all-to-all-done.2.placed_ref = bf16[8,4,2,256,128]{4,3,2,1,0:T(8,128)(2,1)} async-done(((bf16[8,4,2,256,128]{4,3,2,1,0:T(8,128)(2,1)}), bf16[8,4,2,256,128]{4,3,2,1,0:T(8,128)(2,1)}, u32[]{:S(2)}, u32[]{:S(2)}) %all-to-all-start.2) | async-done | bytes 4194336 | tf_op jit(solution)/shard_map/all_to_all | solution.py:286
  320.0 4.2 %left_products.3 = (bf16[8,16,16,128]{3,2,1,0:T(8,128)(2,1)S(1)}, bf16[8,16,16,128]{3,2,1,0:T(8,128)(2,1)S(1)}) custom-call(s32[1]{0:T(128)} %bitcast.5.core_ref, s32[2,16]{1,0:T(2,128)S(1)} %slice.26.from_ref, bf16[8,4,2,256,128]{4,3,2,1,0:T(8,128)(2,1)} %all-to-all-done.2.placed_ref, bf16[2,4,256,256]{3,2,1,0:T(8,128)(2,1)S(1)} %copy-done), custom_call_target="tpu_custom_call" | custom-call | tf_op jit(solution)/shard_map/left_products/pallas_call | solution.py:228
  329.4 6.5 %all-to-all-start.3 = ((bf16[8,16,16,128]{3,2,1,0:T(8,128)(2,1)}), bf16[8,16,16,128]{3,2,1,0:T(8,128)(2,1)S(1)}, u32[]{:S(2)}, u32[]{:S(2)}) async-start(bf16[8,16,16,128]{3,2,1,0:T(8,128)(2,1)} %add_convert_fusion), calls=%async_computation.4 | async-start | bytes 1048576 | tf_op jit(solution)/shard_map/all_to_all | solution.py:294
  336.1 17.7 %all-to-all-done.3 = bf16[8,16,16,128]{3,2,1,0:T(8,128)(2,1)S(1)} async-done(((bf16[8,16,16,128]{3,2,1,0:T(8,128)(2,1)}), bf16[8,16,16,128]{3,2,1,0:T(8,128)(2,1)S(1)}, u32[]{:S(2)}, u32[]{:S(2)}) %all-to-all-start.3) | async-done | bytes 524320 | tf_op jit(solution)/shard_map/all_to_all | solution.py:294
  (83 shorter events, 60.3 us)
Async XLA Ops:
  9.2 27.5 %all-to-all-start = ((bf16[32,48,128]{2,1,0:T(8,128)(2,1)}), bf16[32,48,128]{2,1,0:T(8,128)(2,1)S(1)}, u32[]{:S(2)}, u32[]{:S(2)}) async-start(bf16[32,48,128]{2,1,0:T(8,128)(2,1)} %spread_blocks.1), calls=%async_computation | async-start | bytes 786432 | tf_op jit(solution)/shard_map/all_to_all | solution.py:270
  22.9 127.3 %all-gather.5.cloned.1.call-start = ((), (), s32[]{:S(2)}) async-start(), calls=%async_computation.6 | async-start | bytes 2621440 | tf_op jit(solution)/shard_map/all_gather | solution.py:268
  39.3 14.6 %collective-permute-start.2 = (bf16[17,32,128]{2,1,0:T(8,128)(2,1)}, bf16[17,32,128]{2,1,0:T(8,128)(2,1)S(1)}, u32[]{:S(2)}, u32[]{:S(2)}) collective-permute-start(bf16[17,32,128]{2,1,0:T(8,128)(2,1)} %order_blocks.1), channel_id=1, source_target_pairs={{0,128},{128,256},{256,384},{384,0},{1,129},{129,257},{257,385},{3... | collective-permute-start | bytes 417800 | tf_op jit(solution)/shard_map/ppermute | solution.py:241
  43.0 25.6 %collective-permute-start.1 = (bf16[17,32,128]{2,1,0:T(8,128)(2,1)}, bf16[17,32,128]{2,1,0:T(8,128)(2,1)S(1)}, u32[]{:S(2)}, u32[]{:S(2)}) collective-permute-start(bf16[17,32,128]{2,1,0:T(8,128)(2,1)} %order_blocks.1), channel_id=1, source_target_pairs={{0,256},{128,384},{256,0},{384,128},{1,257},{129,385},{257,1},{385... | collective-permute-start | bytes 417800 | tf_op jit(solution)/shard_map/ppermute | solution.py:241
  47.1 25.0 %collective-permute-start = (bf16[17,32,128]{2,1,0:T(8,128)(2,1)}, bf16[17,32,128]{2,1,0:T(8,128)(2,1)S(1)}, u32[]{:S(2)}, u32[]{:S(2)}) collective-permute-start(bf16[17,32,128]{2,1,0:T(8,128)(2,1)} %order_blocks.1), channel_id=1, source_target_pairs={{0,384},{128,0},{256,128},{384,256},{1,385},{129,1},{257,129},{385... | collective-permute-start | bytes 417800 | tf_op jit(solution)/shard_map/ppermute | solution.py:241
  73.1 18.8 %collective-permute-start.4 = (bf16[4,17,32,128]{3,2,1,0:T(8,128)(2,1)S(1)}, bf16[4,17,32,128]{3,2,1,0:T(8,128)(2,1)S(1)}, u32[]{:S(2)}, u32[]{:S(2)}) collective-permute-start(bf16[4,17,32,128]{3,2,1,0:T(8,128)(2,1)S(1)} %pad_maximum_fusion.refs_0_), channel_id=1, source_target_pairs={{0,2},{2,4},{4,6},{6,8},{8,10},{10,12},{12,14},{14,0},{1,3},{3,5},... | collective-permute-start | bytes 1671176 | tf_op jit(solution)/shard_map/ppermute | solution.py:241
  76.3 17.5 %collective-permute-start.6 = (bf16[4,17,32,128]{3,2,1,0:T(8,128)(2,1)S(1)}, bf16[4,17,32,128]{3,2,1,0:T(8,128)(2,1)S(1)}, u32[]{:S(2)}, u32[]{:S(2)}) collective-permute-start(bf16[4,17,32,128]{3,2,1,0:T(8,128)(2,1)S(1)} %pad_maximum_fusion.refs_0_), channel_id=1, source_target_pairs={{0,14},{2,0},{4,2},{6,4},{8,6},{10,8},{12,10},{14,12},{1,15},{3,1}... | collective-permute-start | bytes 1671176 | tf_op jit(solution)/shard_map/ppermute | solution.py:241
  91.9 15.0 %collective-permute-start.8 = (bf16[4,17,32,128]{3,2,1,0:T(8,128)(2,1)S(1)}, bf16[4,17,32,128]{3,2,1,0:T(8,128)(2,1)S(1)}, u32[]{:S(2)}, u32[]{:S(2)}) collective-permute-start(bf16[4,17,32,128]{3,2,1,0:T(8,128)(2,1)S(1)} %collective-permute-done.4.refs_2_), channel_id=1, source_target_pairs={{0,2},{2,4},{4,6},{6,8},{8,10},{10,12},{12,14},{14,0},{1,3},{3,5},... | collective-permute-start | bytes 1671176 | tf_op jit(solution)/shard_map/ppermute | solution.py:241
  93.8 15.0 %collective-permute-start.10 = (bf16[4,17,32,128]{3,2,1,0:T(8,128)(2,1)S(1)}, bf16[4,17,32,128]{3,2,1,0:T(8,128)(2,1)S(1)}, u32[]{:S(2)}, u32[]{:S(2)}) collective-permute-start(bf16[4,17,32,128]{3,2,1,0:T(8,128)(2,1)S(1)} %collective-permute-done.6.refs_4_), channel_id=1, source_target_pairs={{0,14},{2,0},{4,2},{6,4},{8,6},{10,8},{12,10},{14,12},{1,15},{3,1}... | collective-permute-start | bytes 1671176 | tf_op jit(solution)/shard_map/ppermute | solution.py:241
  106.9 16.5 %collective-permute-start.12 = (bf16[4,17,32,128]{3,2,1,0:T(8,128)(2,1)S(1)}, bf16[4,17,32,128]{3,2,1,0:T(8,128)(2,1)S(1)}, u32[]{:S(2)}, u32[]{:S(2)}) collective-permute-start(bf16[4,17,32,128]{3,2,1,0:T(8,128)(2,1)S(1)} %collective-permute-done.8.refs_6_), channel_id=1, source_target_pairs={{0,2},{2,4},{4,6},{6,8},{8,10},{10,12},{12,14},{14,0},{1,3},{3,5},... | collective-permute-start | bytes 1671176 | tf_op jit(solution)/shard_map/ppermute | solution.py:241
  108.8 16.5 %collective-permute-start.14 = (bf16[4,17,32,128]{3,2,1,0:T(8,128)(2,1)S(1)}, bf16[4,17,32,128]{3,2,1,0:T(8,128)(2,1)}, u32[]{:S(2)}, u32[]{:S(2)}) collective-permute-start(bf16[4,17,32,128]{3,2,1,0:T(8,128)(2,1)S(1)} %collective-permute-done.10.refs_8_), channel_id=1, source_target_pairs={{0,14},{2,0},{4,2},{6,4},{8,6},{10,8},{12,10},{14,12},{1,15},{3,1}... | collective-permute-start | bytes 1671176 | tf_op jit(solution)/shard_map/ppermute | solution.py:241
  113.4 27.5 %collective-permute-start.3 = (bf16[4,17,32,128]{3,2,1,0:T(8,128)(2,1)S(1)}, bf16[4,17,32,128]{3,2,1,0:T(8,128)(2,1)S(1)}, u32[]{:S(2)}, u32[]{:S(2)}) collective-permute-start(bf16[4,17,32,128]{3,2,1,0:T(8,128)(2,1)S(1)} %pad_maximum_fusion.refs_0_), channel_id=1, source_target_pairs={{0,1},{1,0},{2,3},{3,2},{4,5},{5,4},{6,7},{7,6},{8,9},{9,8},{10,11... | collective-permute-start | bytes 1671176 | tf_op jit(solution)/shard_map/ppermute | solution.py:241
  119.0 25.1 %collective-permute-start.5 = (bf16[4,17,32,128]{3,2,1,0:T(8,128)(2,1)S(1)}, bf16[4,17,32,128]{3,2,1,0:T(8,128)(2,1)S(1)}, u32[]{:S(2)}, u32[]{:S(2)}) collective-permute-start(bf16[4,17,32,128]{3,2,1,0:T(8,128)(2,1)S(1)} %collective-permute-done.4.refs_2_), channel_id=1, source_target_pairs={{0,1},{1,0},{2,3},{3,2},{4,5},{5,4},{6,7},{7,6},{8,9},{9,8},{10,11... | collective-permute-start | bytes 1671176 | tf_op jit(solution)/shard_map/ppermute | solution.py:241
  121.0 25.9 %collective-permute-start.7 = (bf16[4,17,32,128]{3,2,1,0:T(8,128)(2,1)S(1)}, bf16[4,17,32,128]{3,2,1,0:T(8,128)(2,1)S(1)}, u32[]{:S(2)}, u32[]{:S(2)}) collective-permute-start(bf16[4,17,32,128]{3,2,1,0:T(8,128)(2,1)S(1)} %collective-permute-done.6.refs_4_), channel_id=1, source_target_pairs={{0,1},{1,0},{2,3},{3,2},{4,5},{5,4},{6,7},{7,6},{8,9},{9,8},{10,11... | collective-permute-start | bytes 1671176 | tf_op jit(solution)/shard_map/ppermute | solution.py:241
  123.4 9.6 %collective-permute-start.16 = (bf16[2,17,32,128]{3,2,1,0:T(8,128)(2,1)S(1)}, bf16[2,17,32,128]{3,2,1,0:T(8,128)(2,1)S(1)}, u32[]{:S(2)}, u32[]{:S(2)}) collective-permute-start(bf16[2,17,32,128]{3,2,1,0:T(8,128)(2,1)S(1)} %slice.35), channel_id=1, source_target_pairs={{0,2},{2,4},{4,6},{6,8},{8,10},{10,12},{12,14},{14,0},{1,3},{3,5},... | collective-permute-start | bytes 835592 | tf_op jit(solution)/shard_map/ppermute | solution.py:241
  126.3 11.9 %collective-permute-start.17 = (bf16[2,17,32,128]{3,2,1,0:T(8,128)(2,1)S(1)}, bf16[2,17,32,128]{3,2,1,0:T(8,128)(2,1)S(1)}, u32[]{:S(2)}, u32[]{:S(2)}) collective-permute-start(bf16[2,17,32,128]{3,2,1,0:T(8,128)(2,1)S(1)} %slice.36), channel_id=1, source_target_pairs={{0,14},{2,0},{4,2},{6,4},{8,6},{10,8},{12,10},{14,12},{1,15},{3,1}... | collective-permute-start | bytes 835592 | tf_op jit(solution)/shard_map/ppermute | solution.py:241
  133.0 17.2 %collective-permute-start.9 = (bf16[4,17,32,128]{3,2,1,0:T(8,128)(2,1)S(1)}, bf16[4,17,32,128]{3,2,1,0:T(8,128)(2,1)}, u32[]{:S(2)}, u32[]{:S(2)}) collective-permute-start(bf16[4,17,32,128]{3,2,1,0:T(8,128)(2,1)S(1)} %collective-permute-done.8.refs_6_), channel_id=1, source_target_pairs={{0,1},{1,0},{2,3},{3,2},{4,5},{5,4},{6,7},{7,6},{8,9},{9,8},{10,11... | collective-permute-start | bytes 1671176 | tf_op jit(solution)/shard_map/ppermute | solution.py:241
  138.2 12.0 %collective-permute-start.11 = (bf16[4,17,32,128]{3,2,1,0:T(8,128)(2,1)S(1)}, bf16[4,17,32,128]{3,2,1,0:T(8,128)(2,1)}, u32[]{:S(2)}, u32[]{:S(2)}) collective-permute-start(bf16[4,17,32,128]{3,2,1,0:T(8,128)(2,1)S(1)} %collective-permute-done.10.refs_8_), channel_id=1, source_target_pairs={{0,1},{1,0},{2,3},{3,2},{4,5},{5,4},{6,7},{7,6},{8,9},{9,8},{10,11... | collective-permute-start | bytes 1671176 | tf_op jit(solution)/shard_map/ppermute | solution.py:241
  141.7 8.5 %collective-permute-start.13 = (bf16[4,17,32,128]{3,2,1,0:T(8,128)(2,1)S(1)}, bf16[4,17,32,128]{3,2,1,0:T(8,128)(2,1)}, u32[]{:S(2)}, u32[]{:S(2)}) collective-permute-start(bf16[4,17,32,128]{3,2,1,0:T(8,128)(2,1)S(1)} %collective-permute-done.12.refs_10_), channel_id=1, source_target_pairs={{0,1},{1,0},{2,3},{3,2},{4,5},{5,4},{6,7},{7,6},{8,9},{9,8},{10,11... | collective-permute-start | bytes 1671176 | tf_op jit(solution)/shard_map/ppermute | solution.py:241
  168.7 98.0 %all-to-all-start.1 = ((bf16[8,4,2,256,128]{4,3,2,1,0:T(8,128)(2,1)}), bf16[8,4,2,256,128]{4,3,2,1,0:T(8,128)(2,1)}, u32[]{:S(2)}, u32[]{:S(2)}) async-start(bf16[8,4,2,256,128]{4,3,2,1,0:T(8,128)(2,1)} %right_products.2), calls=%async_computation.1 | async-start | bytes 8388608 | tf_op jit(solution)/shard_map/all_to_all | solution.py:286
  174.3 75.7 %all-gather.7.cloned.1.call-start = ((), (), s32[]{:S(2)}) async-start(), calls=%async_computation.7 | async-start | bytes 2621440 | tf_op jit(solution)/shard_map/all_gather | solution.py:268
  266.7 53.4 %all-to-all-start.2 = ((bf16[8,4,2,256,128]{4,3,2,1,0:T(8,128)(2,1)}), bf16[8,4,2,256,128]{4,3,2,1,0:T(8,128)(2,1)}, u32[]{:S(2)}, u32[]{:S(2)}) async-start(bf16[8,4,2,256,128]{4,3,2,1,0:T(8,128)(2,1)} %right_products.3), calls=%async_computation.3 | async-start | bytes 8388608 | tf_op jit(solution)/shard_map/all_to_all | solution.py:286
  271.4 82.5 %reduce-scatter.2.cloned.1.call-start = ((), (), s32[]{:S(2)}) async-start(), calls=%async_computation.5 | async-start | bytes 1114112 | tf_op jit(solution)/shard_map/reduce_scatter | solution.py:289
  329.4 24.4 %all-to-all-start.3 = ((bf16[8,16,16,128]{3,2,1,0:T(8,128)(2,1)}), bf16[8,16,16,128]{3,2,1,0:T(8,128)(2,1)S(1)}, u32[]{:S(2)}, u32[]{:S(2)}) async-start(bf16[8,16,16,128]{3,2,1,0:T(8,128)(2,1)} %add_convert_fusion), calls=%async_computation.4 | async-start | bytes 1048576 | tf_op jit(solution)/shard_map/all_to_all | solution.py:294
  (15 other events, 87.5 us)
Sparse Core Ops, SparseCore 0:
  25.9 67.1 all-gather.4
  177.2 72.7 all-gather.6
  276.6 58.0 reduce-scatter.1

commit v3 on v2

v3 whole, which is shorter than its diff:
```python
import functools

import jax
import jax.numpy as jnp
from jax import lax
from jax.experimental import pallas as pl
from jax.experimental.pallas import tpu as pltpu
from jax.sharding import Mesh, PartitionSpec as P

SHARE = 16
LANES = 128
VMEM_LIMIT = 48 * 1024 * 1024
REMAP = ("zh", "zl", "x")
GROUP = ("zl", "x")
DEPTH = ("y", "core")
SMEM = pl.BlockSpec(memory_space=pltpu.SMEM)


def spread_kernel(count, depth_ref, home_ref, links_ref, rows_ref, wave_ref, out_ref, label_ref):
    slots = out_ref.shape[0]
    terms = links_ref.shape[0]
    per_sector = count // rows_ref.shape[0]

    def clear(peer, carry):
        for kind in range(1 + terms):
            label_ref[kind, peer] = count
        return carry

    lax.fori_loop(0, slots, clear, 0)

    def fill(block, carry):
        home = home_ref[block]
        label_ref[0, lax.div(home, count)] = lax.rem(home, count)
        for term in range(terms):
            link = links_ref[term, block]
            label_ref[1 + term, lax.div(link, count)] = lax.rem(link, count)
        return carry

    lax.fori_loop(0, count, fill, 0)
    lane = lax.broadcasted_iota(jnp.int32, (SHARE, LANES), 1)

    def mark(peer, carry):
        tile = jnp.full(lane.shape, label_ref[0, peer], jnp.int32)
        for term in range(terms):
            tile = jnp.where(lane == 1 + term, label_ref[1 + term, peer], tile)
        out_ref[peer, 2 * SHARE :, :] = tile.astype(jnp.float32).astype(jnp.bfloat16)
        return carry

    lax.fori_loop(0, slots, mark, 0)
    row = lax.broadcasted_iota(jnp.int32, wave_ref.shape[1:], 0) + depth_ref[0] * SHARE

    def put(block, carry):
        owner = lax.div(home_ref[block], count)
        keep = row < rows_ref[lax.div(block, per_sector)]
        value = wave_ref[block]
        value = jnp.where(keep, value, jnp.zeros_like(value))
        out_ref[owner, 0:SHARE, :] = value[:, :LANES]
        out_ref[owner, SHARE : 2 * SHARE, :] = value[:, LANES:]
        return carry

    lax.fori_loop(0, count, put, 0)


def spread(depth, right_home, term_links, sector_rows, wavefunction, slots):
    count, _, width = wavefunction.shape
    return pl.pallas_call(
        functools.partial(spread_kernel, count),
        grid_spec=pltpu.PrefetchScalarGridSpec(
            num_scalar_prefetch=1,
            grid=(1,),
            in_specs=[
                SMEM,
                SMEM,
                SMEM,
                pl.BlockSpec((count, SHARE, width), lambda i, depth: (0, depth[0], 0)),
            ],
            out_specs=pl.BlockSpec((slots, 3 * SHARE, LANES), lambda i, depth: (0, 0, 0)),
            scratch_shapes=[pltpu.SMEM((1 + term_links.shape[0], slots), jnp.int32)],
        ),
        out_shape=jax.ShapeDtypeStruct((slots, 3 * SHARE, LANES), jnp.bfloat16),
        name="spread_blocks",
    )(depth, right_home, term_links, sector_rows, wavefunction)


def order_kernel(from_ref, links_ref, cols_ref, in_ref, out_ref):
    terms, count = links_ref.shape
    per_sector = count // cols_ref.shape[0]
    lane = lax.broadcasted_iota(jnp.int32, (SHARE, LANES), 1)
    targets = jnp.zeros(lane.shape, jnp.int32)
    for block in range(count):
        slot = from_ref[block]
        cols = cols_ref[block // per_sector]
        for part in range(2):
            value = in_ref[slot, part * SHARE : (part + 1) * SHARE, :]
            out_ref[block, part * SHARE : (part + 1) * SHARE, :] = jnp.where(
                lane + part * LANES < cols, value, jnp.zeros_like(value)
            )
        for term in range(terms):
            owner = lax.div(links_ref[term, block], count)
            targets = jnp.where(lane == term * count + block, owner, targets)
    targets = targets.astype(jnp.float32).astype(jnp.bfloat16)
    out_ref[count, 0:SHARE, :] = targets
    out_ref[count, SHARE:, :] = targets


def order(source, term_links, sector_cols, arrived):
    count = source.shape[0]
    return pl.pallas_call(
        order_kernel,
        in_specs=[SMEM, SMEM, SMEM, pl.BlockSpec(memory_space=pltpu.VMEM)],
        out_specs=pl.BlockSpec(memory_space=pltpu.VMEM),
        out_shape=jax.ShapeDtypeStruct((count + 1, 2 * SHARE, LANES), jnp.bfloat16),
        name="order_blocks",
    )(source, term_links, sector_cols, arrived)


def right_kernel(place_ref, targets_ref, slices_ref, *refs):
    envs, (out_ref, moved_ref, env_ref) = refs[:-3], refs[-3:]
    group, _, terms, extent, width = out_ref.shape
    sectors = env_ref.shape[0]
    depth, count = slices_ref.shape[0], slices_ref.shape[2] - 1
    per_sector = count // sectors
    turn = pl.program_id(0)
    for index in range(len(envs) // terms):

        @pl.when(turn == index)
        def _(index=index):
            for term in range(terms):
                env = envs[index * terms + term][0]
                env_ref[:, :, term * width : (term + 1) * width] = env

    for sector in range(sectors):
        half = sector % 2
        for share in range(depth):
            for place in range(per_sector):
                at = slice(place * extent + share * SHARE, place * extent + (share + 1) * SHARE)
                block = sector * per_sector + place
                moved_ref[half, at, 0:LANES] = slices_ref[share, 0, block, 0:SHARE, :]
                moved_ref[half, at, LANES:] = slices_ref[share, 0, block, SHARE:, :]
        product = jnp.dot(moved_ref[half], env_ref[sector], preferred_element_type=jnp.float32)
        product = product.astype(jnp.bfloat16)
        for place in range(per_sector):
            for term in range(terms):
                owner = targets_ref[turn, term * count + sector * per_sector + place]

                @pl.when(lax.div(owner, group) == place_ref[0])
                def _(place=place, term=term, owner=owner):
                    out_ref[lax.rem(owner, group), 0, term] = product[
                        place * extent : (place + 1) * extent, term * width : (term + 1) * width
                    ]


def right_products(place, targets, slices, envs, group, chunk, width):
    depth, layers, blocks, tall, lanes = slices.shape
    terms = len(envs[0])
    sectors, extent = envs[0][0][0].shape[1:3]
    per_sector = (blocks - 1) // sectors
    flat = [pair for layer in envs for pair in layer]
    shape = (group, layers, terms, extent, width)
    return pl.pallas_call(
        right_kernel,
        grid_spec=pltpu.PrefetchScalarGridSpec(
            num_scalar_prefetch=2,
            grid=(layers,),
            in_specs=[pl.BlockSpec((depth, 1, blocks, tall, lanes), lambda i, p, t: (0, i, 0, 0, 0))]
            + [
                pl.BlockSpec(
                    (1, sectors, extent, width), lambda i, p, t, term=term: (term, 0, 0, chunk)
                )
                for _, term in flat
            ],
            out_specs=pl.BlockSpec((group, 1, terms, extent, width), lambda i, p, t: (0, i, 0, 0, 0)),
            scratch_shapes=[
                pltpu.VMEM((2, per_sector * extent, extent), jnp.bfloat16),
                pltpu.VMEM((sectors, extent, terms * width), jnp.bfloat16),
            ],
        ),
        out_shape=jax.ShapeDtypeStruct(shape, jnp.bfloat16),
        compiler_params=pltpu.CompilerParams(vmem_limit_bytes=VMEM_LIMIT),
        name="right_products",
    )(place, targets, slices, *[array for array, _ in flat])


def left_partials(place_ref, from_ref, own_ref, far_ref, env_ref, placed_ref):
    terms, count = from_ref.shape
    group, _, _, extent, _ = own_ref.shape
    layers = far_ref.shape[1] + 1
    per_sector = count // pl.num_programs(0)
    sector = pl.program_id(0)
    left = jnp.concatenate([env_ref[term, 0] for term in range(terms)], axis=1)
    for place in range(per_sector):
        for term in range(terms):
            device = from_ref[term, sector * per_sector + place]
            peer = lax.rem(device, group)
            step = lax.rem(lax.div(device, group) + layers - place_ref[0], layers)
            at = slice(term * extent, (term + 1) * extent)

            @pl.when(step == 0)
            def _(place=place, term=term, peer=peer, at=at):
                placed_ref[place, at, :] = own_ref[peer, 0, term]

            @pl.when(step > 0)
            def _(place=place, term=term, peer=peer, at=at, step=step):
                placed_ref[place, at, :] = far_ref[peer, jnp.maximum(step - 1, 0), term]

        partial = jnp.dot(left, placed_ref[place], preferred_element_type=jnp.float32)
        yield place, partial.astype(jnp.bfloat16)


def left_kernel(place_ref, from_ref, own_ref, far_ref, env_ref, out_ref, placed_ref):
    for place, partial in left_partials(place_ref, from_ref, own_ref, far_ref, env_ref, placed_ref):
        out_ref[:, place] = partial.reshape(out_ref.shape[0], SHARE, partial.shape[1])


def left_split_kernel(place_ref, from_ref, own_ref, far_ref, env_ref, keep_ref, send_ref, placed_ref):
    chips = keep_ref.shape[0]
    core = place_ref[2]
    for place, partial in left_partials(place_ref, from_ref, own_ref, far_ref, env_ref, placed_ref):
        halves = [
            jnp.stack(
                [partial[(2 * c + k) * SHARE : (2 * c + k + 1) * SHARE] for c in range(chips)]
            )
            for k in range(2)
        ]
        keep_ref[:, place] = jnp.where(core == 0, halves[0], halves[1])
        send_ref[:, place] = jnp.where(core == 0, halves[1], halves[0])


def left_products(place, source, own, far, left_env, chunk, split):
    _, sectors, extent, _ = left_env.shape
    terms, count = source.shape
    width = far.shape[-1]
    per_sector = count // sectors
    pieces = extent // SHARE // (2 if split else 1)
    out_spec = pl.BlockSpec((pieces, per_sector, SHARE, width), lambda i: (0, i, 0, 0))
    shape = jax.ShapeDtypeStruct((pieces, count, SHARE, width), jnp.bfloat16)
    return pl.pallas_call(
        left_split_kernel if split else left_kernel,
        grid=(sectors,),
        in_specs=[
            SMEM,
            SMEM,
            pl.BlockSpec(own.shape[:-1] + (width,), lambda i: (0, 0, 0, 0, chunk)),
            pl.BlockSpec(far.shape, lambda i: (0, 0, 0, 0, 0)),
            pl.BlockSpec((terms, 1, extent, extent), lambda i: (0, i, 0, 0)),
        ],
        out_specs=[out_spec, out_spec] if split else out_spec,
        out_shape=[shape, shape] if split else shape,
        scratch_shapes=[pltpu.VMEM((per_sector, terms * extent, width), jnp.bfloat16)],
        compiler_params=pltpu.CompilerParams(vmem_limit_bytes=VMEM_LIMIT),
        name="left_products",
    )(place, source, own, far, left_env)


def shift(array, axis, step):
    size = lax.axis_size(axis)
    return lax.ppermute(array, axis, [(i, (i + step) % size) for i in range(size)])


def local(wavefunction, right_home, term_links, sector_rows, sector_cols, left_env, right_env):
    count, _, width = wavefunction.shape
    per_sector = count // sector_rows.shape[0]
    slots = lax.axis_size(REMAP)
    layers = lax.axis_size("zh")
    group = slots // layers
    terms = term_links.shape[0]
    layer = lax.axis_index("zh")
    core_index = lax.axis_index("core")
    depth_index = lax.axis_index("y") * 2 + core_index
    place = jnp.stack([layer, lax.axis_index("y"), core_index])

    buffer = spread(depth_index.reshape(1), right_home, term_links, sector_rows, wavefunction, slots)
    arrived = lax.all_to_all(buffer, REMAP, 0, 0, tiled=True)
    labels = arrived[:, 2 * SHARE, : 1 + terms].astype(jnp.int32)
    match = labels.T[:, None, :] == jnp.arange(count, dtype=jnp.int32)[None, :, None]
    source = jnp.sum(jnp.where(match, jnp.arange(slots, dtype=jnp.int32), 0), axis=2)
    ordered = order(source[0], term_links, sector_cols, arrived)

    parts = [right_env[..., at : at + LANES] for at in range(0, width, LANES)]
    above = [shift(part, "zh", -1) for part in parts]
    below = [shift(part, "zh", 1) for part in parts]

    slices = lax.all_gather(ordered[None], DEPTH)
    targets = (term_links // count).reshape(1, terms * count)
    envs = [[(right_env, term) for term in range(terms)]]
    products = right_products(place, targets, slices, envs, group, 0, width)
    products, above[0], below[0] = lax.optimization_barrier((products, above[0], below[0]))
    own = lax.all_to_all(products, GROUP, 0, 0, tiled=True)

    around = lax.all_gather(ordered, "zh")
    others = lax.dynamic_slice_in_dim(jnp.concatenate([around, around]), layer + 1, layers - 1)
    targets = others[:, count, 0, : terms * count].astype(jnp.int32)
    slices = lax.all_gather(others, DEPTH)
    pieces = []
    for chunk in range(width // LANES):
        up, down = above[chunk], below[chunk]
        across = [shift(up[:1], "zh", -1), shift(down[1:], "zh", 1)]
        envs = [[(up, 0), (up, 1)], [(across[0], 0), (across[1], 0)], [(down, 0), (down, 1)]]
        products = right_products(place, targets, slices, envs, group, 0, LANES)
        slices, products = lax.optimization_barrier((slices, products))
        far = lax.all_to_all(products, GROUP, 0, 0, tiled=True)
        last = (chunk + 1) * LANES == width
        partial = left_products(place, source[1:], own, far, left_env, chunk, last)
        if last:
            keep, send = partial
            pair = keep.astype(jnp.float32) + shift(send, "core", 1).astype(jnp.float32)
            gathered = lax.all_to_all(pair.astype(jnp.bfloat16), "y", 0, 0, tiled=True)
            pieces.append(jnp.sum(gathered.astype(jnp.float32), axis=0))
        else:
            summed = lax.psum_scatter(partial, DEPTH, scatter_dimension=0, tiled=False)
            pieces.append(summed.astype(jnp.float32))
    total = jnp.concatenate(pieces, axis=2)
    row = depth_index * SHARE + jnp.arange(SHARE, dtype=jnp.int32)
    keep_rows = row[None, :] < jnp.repeat(sector_rows, per_sector)[:, None]
    return jnp.where(keep_rows[:, :, None], total, 0.0).astype(jnp.bfloat16)


def solution(mesh):
    slots, depth = mesh.devices.shape
    split = Mesh(
        mesh.devices.reshape(4, 2, slots // 8, depth // 2, 2), ("zh", "zl", "x", "y", "core")
    )
    return jax.shard_map(
        local,
        mesh=split,
        in_specs=(
            P(REMAP, None, None),
            P(REMAP),
            P(DEPTH, REMAP),
            P(REMAP),
            P(REMAP),
            P(DEPTH, REMAP, None, None),
            P(DEPTH, REMAP, None, None),
        ),
        out_specs=P(REMAP, DEPTH, None),
        check_vma=False,
    )
```

time: 364 us -> 323 us (0.89)
  blocking collectives: 0 us -> 42.8 us
  waiting for transfers between devices: 193 us -> 154 us
  starting transfers between devices: 96.1 us -> 57.7 us
  local copies, waits for them, and re-layouts: 14.4 us -> 9.95 us
    all_gather x2, waiting for transfers between devices: 75 us -> 18.5 us  [the longest x1 16.8 us: local(): slices = lax.all_gather(ordered[None], DEPTH)]
    ppermute x20 -> x9, waiting for transfers between devices: 45.1 us -> 88.3 us  [shift(): lax.ppermute(array, axis, [(i, (i + step) % size) for i in range(size)])]
    ppermute x20 -> x9, starting transfers between devices: 65.5 us -> 32 us  [shift(): lax.ppermute(array, axis, [(i, (i + step) % size) for i in range(size)])]
    all_to_all x0 -> x1, blocking collectives: none -> 27.6 us  [local(): arrived = lax.all_to_all(buffer, REMAP, 0, 0, tiled=True)]
    all_to_all x3, waiting for transfers between devices: 54.9 us -> 30.3 us  [the longest x2 30.3 us: local(): far = lax.all_to_all(products, GROUP, 0, 0, tiled=True)]
    all_gather x0 -> x1, blocking collectives: none -> 15.1 us  [local(): around = lax.all_gather(ordered, 'zh')]
    pallas_call x2 -> x3, Pallas kernels: 27.1 us -> 20.4 us  [right_products(): pl.pallas_call(right_kernel, grid_spec=pltpu.PrefetchScalarGridSpec(num_s...]
    pallas_call x2, Pallas kernels: 9.24 us -> 13.5 us  [left_products(): pl.pallas_call(left_split_kernel if split else left_kernel, grid=(sectors...]
  transfers between devices with their start and end apart: 27 -> 16, of which waited for: 12 -> 11; matrix products, arithmetic and copies ran while one was open for 2% -> 1% of each run, Pallas kernels for 7% -> 11%
where the time goes in v3:
time: 323 us; the launch traced here: 321 us
  waiting for transfers between devices  154 us (48%)
  starting transfers between devices  57.7 us (18%)
  blocking collectives  42.8 us (13%)
  Pallas kernels  38.4 us (12%)
  between operations  13.4 us (4%)
  local copies, waits for them, and re-layouts  9.95 us (3%)
  other arithmetic  4.57 us (1%)
    ppermute x9, waiting for transfers between devices, shift(): lax.ppermute(array, axis, [(i, (i + step) % size) for i in range(size)])  88.3 us
    ppermute x9, starting transfers between devices, shift(): lax.ppermute(array, axis, [(i, (i + step) % size) for i in range(size)])  32 us
    all_to_all x2, waiting for transfers between devices, local(): far = lax.all_to_all(products, GROUP, 0, 0, tiled=True)  30.3 us
    all_to_all x1, blocking collectives, local(): arrived = lax.all_to_all(buffer, REMAP, 0, 0, tiled=True)  27.6 us
    pallas_call x3, Pallas kernels, right_products(): pl.pallas_call(right_kernel, grid_spec=pltpu.PrefetchScalarGridSpec(num_s...  20.4 us
    all_to_all x1, waiting for transfers between devices, local(): gathered = lax.all_to_all(pair.astype(jnp.bfloat16), 'y', 0, 0, tiled=True)  17.3 us
    all_to_all x2, starting transfers between devices, local(): far = lax.all_to_all(products, GROUP, 0, 0, tiled=True)  16.9 us
    all_gather x1, waiting for transfers between devices, local(): slices = lax.all_gather(ordered[None], DEPTH)  16.8 us
  transfers between devices with their start and end apart: 16, of which 11 were waited for; matrix products, arithmetic and copies ran while one was open for 1% of the time, Pallas kernels for 11%

profile of v3, /device:TPU:1, one launch (start us, length us, event | category | flops | bytes accessed | tf_op | source)
XLA Modules:
  0.0 321.2 jit_solution(2674530661336189153)
XLA Ops:
  9.2 27.6 %all_to_all.25.in_ref = bf16[32,48,128]{2,1,0:T(8,128)(2,1)S(1)} all-to-all(bf16[32,48,128]{2,1,0:T(8,128)(2,1)} %spread_blocks.1), channel_id=1, replica_groups=mesh['zh'=4,'zl'=2,'x'=4,'y'=8,'core'=2] {'zh','zl','x'}, dimensions={0} | all-to-all | bytes 786432 | tf_op jit(solution)/shard_map/all_to_all | solution.py:273
  39.5 15.1 %all-gather.1 = bf16[68,32,128]{2,1,0:T(8,128)(2,1)S(1)} all-gather(bf16[17,32,128]{2,1,0:T(8,128)(2,1)} %order_blocks.1), channel_id=3, replica_groups=mesh['zh'=4,'zl'=2,'x'=4,'y'=8,'core'=2] {'zh'}, dimensions={0}, use_global_device_ids=true | all-gather | bytes 696320 | tf_op jit(solution)/shard_map/all_gather | solution.py:290
  56.5 3.5 %collective-permute-start = (bf16[2,4,256,128]{3,2,1,0:T(8,128)(2,1)S(1)}, bf16[2,4,256,128]{3,2,1,0:T(8,128)(2,1)S(1)}, u32[]{:S(2)}, u32[]{:S(2)}) collective-permute-start(bf16[2,4,256,128]{3,2,1,0:T(8,128)(2,1)S(1)} %get-tuple-element.22), channel_id=1, source_target_pairs={{0,384},{128,0},{256,128},{384,256},{1,385},{129,1},{257,129},{385... | collective-permute-start | bytes 1572872 | tf_op jit(solution)/shard_map/ppermute | solution.py:257
  60.0 2.7 collective-permute-start.1
  62.9 16.8 %all-gather.6.cloned.1.call-done = bf16[272,32,128]{2,1,0:T(8,128)(2,1)} async-done(((bf16[17,32,128]{2,1,0:T(8,128)(2,1)}), bf16[272,32,128]{2,1,0:T(8,128)(2,1)}) %all-gather.6.cloned.1.call-update) | async-done | bytes 2228240 | tf_op jit(solution)/shard_map/all_gather | solution.py:283
  81.3 2.7 right_products.3
  85.9 4.5 %all-to-all-start.1 = ((bf16[8,1,2,256,256]{4,3,2,1,0:T(8,128)(2,1)}), bf16[8,1,2,256,256]{4,3,2,1,0:T(8,128)(2,1)S(1)}, u32[]{:S(2)}, u32[]{:S(2)}) async-start(bf16[8,1,2,256,256]{4,3,2,1,0:T(8,128)(2,1)} %copy-done.3), calls=%async_computation.1 | async-start | bytes 4194304 | tf_op jit(solution)/shard_map/all_to_all | solution.py:288
  90.5 5.4 %collective-permute-start.2 = (bf16[1,4,256,128]{3,2,1,0:T(8,128)(2,1)S(1)}, bf16[1,4,256,128]{3,2,1,0:T(8,128)(2,1)S(1)}, u32[]{:S(2)}, u32[]{:S(2)}) collective-permute-start(bf16[1,4,256,128]{3,2,1,0:T(8,128)(2,1)S(1)} %slice.36), channel_id=1, source_target_pairs={{0,384},{128,0},{256,128},{384,256},{1,385},{129,1},{257,129},{385... | collective-permute-start | bytes 786440 | tf_op jit(solution)/shard_map/ppermute | solution.py:257
  101.0 27.5 %collective-permute-done.3.refs_3_ = bf16[1,4,256,128]{3,2,1,0:T(8,128)(2,1)S(1)} collective-permute-done((bf16[1,4,256,128]{3,2,1,0:T(8,128)(2,1)S(1)}, bf16[1,4,256,128]{3,2,1,0:T(8,128)(2,1)S(1)}, u32[]{:S(2)}, u32[]{:S(2)}) %collective-permute-start.3) | collective-permute-done | bytes 262176 | tf_op jit(solution)/shard_map/ppermute | solution.py:257
  131.9 8.8 %right_products.4 = bf16[8,3,2,256,128]{4,3,2,1,0:T(8,128)(2,1)S(1)} custom-call(s32[3]{0:T(128)S(1)} %pad_add_fusion.place_ref, s32[3,32]{1,0:T(4,128)S(1)} %bitcast.20, bf16[16,3,17,32,128]{4,3,2,1,0:T(8,128)(2,1)} %bitcast.22, bf16[2,4,256,128]{3,2,1,0:T(8,128)(2,1)S(1)} %collective-permute-done.refs_0_.refs_1_, ...), custom_call_target="tpu_custom_call" | custom-call | tf_op jit(solution)/shard_map/right_products/pallas_call | solution.py:160
  142.5 5.0 %all-to-all-start.2 = ((bf16[8,3,2,256,128]{4,3,2,1,0:T(8,128)(2,1)}), bf16[8,3,2,256,128]{4,3,2,1,0:T(8,128)(2,1)}, u32[]{:S(2)}, u32[]{:S(2)}) async-start(bf16[8,3,2,256,128]{4,3,2,1,0:T(8,128)(2,1)} %copy-done), calls=%async_computation.2 | async-start | bytes 6291456 | tf_op jit(solution)/shard_map/all_to_all | solution.py:301
  147.6 5.7 %collective-permute-start.4 = (bf16[2,4,256,128]{3,2,1,0:T(8,128)(2,1)}, bf16[2,4,256,128]{3,2,1,0:T(8,128)(2,1)S(1)}, u32[]{:S(2)}, u32[]{:S(2)}) collective-permute-start(bf16[2,4,256,128]{3,2,1,0:T(8,128)(2,1)} %get-tuple-element.21), channel_id=1, source_target_pairs={{0,384},{128,0},{256,128},{384,256},{1,385},{129,1},{257,129},{385... | collective-permute-start | bytes 1572872 | tf_op jit(solution)/shard_map/ppermute | solution.py:257
  155.2 9.5 %collective-permute-done.4.refs_0_.refs_1_ = bf16[2,4,256,128]{3,2,1,0:T(8,128)(2,1)S(1)} collective-permute-done((bf16[2,4,256,128]{3,2,1,0:T(8,128)(2,1)}, bf16[2,4,256,128]{3,2,1,0:T(8,128)(2,1)S(1)}, u32[]{:S(2)}, u32[]{:S(2)}) %collective-permute-start.4) | collective-permute-done | bytes 524320 | tf_op jit(solution)/shard_map/ppermute | solution.py:257
  164.7 6.1 %collective-permute-start.5 = (bf16[1,4,256,128]{3,2,1,0:T(8,128)(2,1)S(1)}, bf16[1,4,256,128]{3,2,1,0:T(8,128)(2,1)S(1)}, u32[]{:S(2)}, u32[]{:S(2)}) collective-permute-start(bf16[1,4,256,128]{3,2,1,0:T(8,128)(2,1)S(1)} %slice.43), channel_id=1, source_target_pairs={{0,384},{128,0},{256,128},{384,256},{1,385},{129,1},{257,129},{385... | collective-permute-start | bytes 786440 | tf_op jit(solution)/shard_map/ppermute | solution.py:257
  170.8 37.7 %collective-permute-done.6.refs_4_.refs_5_ = bf16[2,4,256,128]{3,2,1,0:T(8,128)(2,1)S(1)} collective-permute-done((bf16[2,4,256,128]{3,2,1,0:T(8,128)(2,1)}, bf16[2,4,256,128]{3,2,1,0:T(8,128)(2,1)S(1)}, u32[]{:S(2)}, u32[]{:S(2)}) %collective-permute-start.6) | collective-permute-done | bytes 524320 | tf_op jit(solution)/shard_map/ppermute | solution.py:257
  210.5 9.1 %collective-permute-done.7.refs_3_ = bf16[1,4,256,128]{3,2,1,0:T(8,128)(2,1)S(1)} collective-permute-done((bf16[1,4,256,128]{3,2,1,0:T(8,128)(2,1)S(1)}, bf16[1,4,256,128]{3,2,1,0:T(8,128)(2,1)S(1)}, u32[]{:S(2)}, u32[]{:S(2)}) %collective-permute-start.7) | collective-permute-done | bytes 262176 | tf_op jit(solution)/shard_map/ppermute | solution.py:257
  219.6 8.8 %right_products.5 = bf16[8,3,2,256,128]{4,3,2,1,0:T(8,128)(2,1)S(1)} custom-call(s32[3]{0:T(128)S(1)} %pad_add_fusion.place_ref, s32[3,32]{1,0:T(4,128)S(1)} %bitcast.21, bf16[16,3,17,32,128]{4,3,2,1,0:T(8,128)(2,1)} %bitcast.23, bf16[2,4,256,128]{3,2,1,0:T(8,128)(2,1)S(1)} %collective-permute-done.4.refs_0_.refs_1_, ...), custom_call_target="tpu_custom_call" | custom-call | tf_op jit(solution)/shard_map/right_products/pallas_call | solution.py:160
  230.1 11.9 %all-to-all-start.3 = ((bf16[8,3,2,256,128]{4,3,2,1,0:T(8,128)(2,1)}), bf16[8,3,2,256,128]{4,3,2,1,0:T(8,128)(2,1)}, u32[]{:S(2)}, u32[]{:S(2)}) async-start(bf16[8,3,2,256,128]{4,3,2,1,0:T(8,128)(2,1)} %copy-done.1), calls=%async_computation.4 | async-start | bytes 6291456 | tf_op jit(solution)/shard_map/all_to_all | solution.py:301
  242.1 7.1 %left_products.2 = bf16[16,16,16,128]{3,2,1,0:T(8,128)(2,1)} custom-call(s32[3]{0:T(128)S(1)} %pad_add_fusion.place_ref, s32[2,16]{1,0:T(2,128)S(1)} %slice.32.from_ref, bf16[8,1,2,256,256]{4,3,2,1,0:T(8,128)(2,1)S(1)} %all-to-all-done.1.own_ref, bf16[8,3,2,256,128]{4,3,2,1,0:T(8,128)(2,1)} %all-to-all-done.2.far_ref, bf16[2,4,256,256]{3,2,1,0:T(8,128)(2,1)S(1)} %copy-done.4), custom_call_target="tpu_custom_call" | custom-call | tf_op jit(solution)/shard_map/left_products/pallas_call | solution.py:237
  249.2 30.3 %all-to-all-done.3.far_ref = bf16[8,3,2,256,128]{4,3,2,1,0:T(8,128)(2,1)} async-done(((bf16[8,3,2,256,128]{4,3,2,1,0:T(8,128)(2,1)}), bf16[8,3,2,256,128]{4,3,2,1,0:T(8,128)(2,1)}, u32[]{:S(2)}, u32[]{:S(2)}) %all-to-all-start.3) | async-done | bytes 3145760 | tf_op jit(solution)/shard_map/all_to_all | solution.py:301
  279.5 6.5 %left_products.3 = (bf16[8,16,16,128]{3,2,1,0:T(8,128)(2,1)S(1)}, bf16[8,16,16,128]{3,2,1,0:T(8,128)(2,1)S(1)}) custom-call(s32[3]{0:T(128)S(1)} %pad_add_fusion.place_ref, s32[2,16]{1,0:T(2,128)S(1)} %slice.32.from_ref, bf16[8,1,2,256,256]{4,3,2,1,0:T(8,128)(2,1)S(1)} %all-to-all-done.1.own_ref, bf16[8,3,2,256,128]{4,3,2,1,0:T(8,128)(2,1)} %all-to-all-done.3.far_ref, ...), custom_call_target="tpu_custom_call" | custom-call | tf_op jit(solution)/shard_map/left_products/pallas_call | solution.py:237
  286.0 2.8 collective-permute-start.8
  291.2 4.2 %all-to-all-start.4 = ((bf16[8,16,16,128]{3,2,1,0:T(8,128)(2,1)}), bf16[8,16,16,128]{3,2,1,0:T(8,128)(2,1)S(1)}, u32[]{:S(2)}, u32[]{:S(2)}) async-start(bf16[8,16,16,128]{3,2,1,0:T(8,128)(2,1)} %add_convert_fusion), calls=%async_computation.5 | async-start | bytes 1048576 | tf_op jit(solution)/shard_map/all_to_all | solution.py:307
  295.6 17.3 %all-to-all-done.4 = bf16[8,16,16,128]{3,2,1,0:T(8,128)(2,1)S(1)} async-done(((bf16[8,16,16,128]{3,2,1,0:T(8,128)(2,1)}), bf16[8,16,16,128]{3,2,1,0:T(8,128)(2,1)S(1)}, u32[]{:S(2)}, u32[]{:S(2)}) %all-to-all-start.4) | async-done | bytes 524320 | tf_op jit(solution)/shard_map/all_to_all | solution.py:307
  (65 shorter events, 31.1 us)
Async XLA Ops:
  6.5 73.2 %all-gather.6.cloned.1.call-start = ((), (), s32[]{:S(2)}) async-start(), calls=%async_computation.7 | async-start | bytes 2367488 | tf_op jit(solution)/shard_map/all_gather | solution.py:283
  9.2 46.4 %copy-start.2 = (bf16[2,4,256,256]{3,2,1,0:T(8,128)(2,1)S(1)}, bf16[2,4,256,256]{3,2,1,0:T(8,128)(2,1)}, u32[]{:S(2)}) copy-start(bf16[2,4,256,256]{3,2,1,0:T(8,128)(2,1)} %refs_1_.1) | copy-start | bytes 3145732
  39.4 23.3 %copy-start.9 = (s32[2,16]{1,0:T(2,128)S(1)}, s32[2,16]{1,0:T(2,128)}, u32[]{:S(2)}) copy-start(s32[2,16]{1,0:T(2,128)} %links_ref.3) | copy-start | bytes 388
  39.4 91.5 %all-gather.8.cloned.1.call-start = ((), (), s32[]{:S(2)}) async-start(), calls=%async_computation.8 | async-start | bytes 7102464 | tf_op jit(solution)/shard_map/all_gather | solution.py:293
  56.5 28.9 %collective-permute-start = (bf16[2,4,256,128]{3,2,1,0:T(8,128)(2,1)S(1)}, bf16[2,4,256,128]{3,2,1,0:T(8,128)(2,1)S(1)}, u32[]{:S(2)}, u32[]{:S(2)}) collective-permute-start(bf16[2,4,256,128]{3,2,1,0:T(8,128)(2,1)S(1)} %get-tuple-element.22), channel_id=1, source_target_pairs={{0,384},{128,0},{256,128},{384,256},{1,385},{129,1},{257,129},{385... | collective-permute-start | bytes 1572872 | tf_op jit(solution)/shard_map/ppermute | solution.py:257
  60.0 25.9 %collective-permute-start.1 = (bf16[2,4,256,128]{3,2,1,0:T(8,128)(2,1)S(1)}, bf16[2,4,256,128]{3,2,1,0:T(8,128)(2,1)S(1)}, u32[]{:S(2)}, u32[]{:S(2)}) collective-permute-start(bf16[2,4,256,128]{3,2,1,0:T(8,128)(2,1)S(1)} %get-tuple-element.22), channel_id=1, source_target_pairs={{0,128},{128,256},{256,384},{384,0},{1,129},{129,257},{257,385},{3... | collective-permute-start | bytes 1572872 | tf_op jit(solution)/shard_map/ppermute | solution.py:257
  79.7 1.6 copy-start.5
  84.0 1.4 copy-start.3
  85.9 56.6 %all-to-all-start.1 = ((bf16[8,1,2,256,256]{4,3,2,1,0:T(8,128)(2,1)}), bf16[8,1,2,256,256]{4,3,2,1,0:T(8,128)(2,1)S(1)}, u32[]{:S(2)}, u32[]{:S(2)}) async-start(bf16[8,1,2,256,256]{4,3,2,1,0:T(8,128)(2,1)} %copy-done.3), calls=%async_computation.1 | async-start | bytes 4194304 | tf_op jit(solution)/shard_map/all_to_all | solution.py:288
  90.5 10.6 %collective-permute-start.2 = (bf16[1,4,256,128]{3,2,1,0:T(8,128)(2,1)S(1)}, bf16[1,4,256,128]{3,2,1,0:T(8,128)(2,1)S(1)}, u32[]{:S(2)}, u32[]{:S(2)}) collective-permute-start(bf16[1,4,256,128]{3,2,1,0:T(8,128)(2,1)S(1)} %slice.36), channel_id=1, source_target_pairs={{0,384},{128,0},{256,128},{384,256},{1,385},{129,1},{257,129},{385... | collective-permute-start | bytes 786440 | tf_op jit(solution)/shard_map/ppermute | solution.py:257
  95.9 32.7 %collective-permute-start.3 = (bf16[1,4,256,128]{3,2,1,0:T(8,128)(2,1)S(1)}, bf16[1,4,256,128]{3,2,1,0:T(8,128)(2,1)S(1)}, u32[]{:S(2)}, u32[]{:S(2)}) collective-permute-start(bf16[1,4,256,128]{3,2,1,0:T(8,128)(2,1)S(1)} %slice.37), channel_id=1, source_target_pairs={{0,128},{128,256},{256,384},{384,0},{1,129},{129,257},{257,385},{3... | collective-permute-start | bytes 786440 | tf_op jit(solution)/shard_map/ppermute | solution.py:257
  140.8 1.7 copy-start
  142.5 87.6 %all-to-all-start.2 = ((bf16[8,3,2,256,128]{4,3,2,1,0:T(8,128)(2,1)}), bf16[8,3,2,256,128]{4,3,2,1,0:T(8,128)(2,1)}, u32[]{:S(2)}, u32[]{:S(2)}) async-start(bf16[8,3,2,256,128]{4,3,2,1,0:T(8,128)(2,1)} %copy-done), calls=%async_computation.2 | async-start | bytes 6291456 | tf_op jit(solution)/shard_map/all_to_all | solution.py:301
  147.6 17.1 %collective-permute-start.4 = (bf16[2,4,256,128]{3,2,1,0:T(8,128)(2,1)}, bf16[2,4,256,128]{3,2,1,0:T(8,128)(2,1)S(1)}, u32[]{:S(2)}, u32[]{:S(2)}) collective-permute-start(bf16[2,4,256,128]{3,2,1,0:T(8,128)(2,1)} %get-tuple-element.21), channel_id=1, source_target_pairs={{0,384},{128,0},{256,128},{384,256},{1,385},{129,1},{257,129},{385... | collective-permute-start | bytes 1572872 | tf_op jit(solution)/shard_map/ppermute | solution.py:257
  153.3 55.3 %collective-permute-start.6 = (bf16[2,4,256,128]{3,2,1,0:T(8,128)(2,1)}, bf16[2,4,256,128]{3,2,1,0:T(8,128)(2,1)S(1)}, u32[]{:S(2)}, u32[]{:S(2)}) collective-permute-start(bf16[2,4,256,128]{3,2,1,0:T(8,128)(2,1)} %get-tuple-element.21), channel_id=1, source_target_pairs={{0,128},{128,256},{256,384},{384,0},{1,129},{129,257},{257,385},{3... | collective-permute-start | bytes 1572872 | tf_op jit(solution)/shard_map/ppermute | solution.py:257
  164.7 45.8 %collective-permute-start.5 = (bf16[1,4,256,128]{3,2,1,0:T(8,128)(2,1)S(1)}, bf16[1,4,256,128]{3,2,1,0:T(8,128)(2,1)S(1)}, u32[]{:S(2)}, u32[]{:S(2)}) collective-permute-start(bf16[1,4,256,128]{3,2,1,0:T(8,128)(2,1)S(1)} %slice.43), channel_id=1, source_target_pairs={{0,384},{128,0},{256,128},{384,256},{1,385},{129,1},{257,129},{385... | collective-permute-start | bytes 786440 | tf_op jit(solution)/shard_map/ppermute | solution.py:257
  208.6 11.0 %collective-permute-start.7 = (bf16[1,4,256,128]{3,2,1,0:T(8,128)(2,1)S(1)}, bf16[1,4,256,128]{3,2,1,0:T(8,128)(2,1)S(1)}, u32[]{:S(2)}, u32[]{:S(2)}) collective-permute-start(bf16[1,4,256,128]{3,2,1,0:T(8,128)(2,1)S(1)} %slice.44), channel_id=1, source_target_pairs={{0,128},{128,256},{256,384},{384,0},{1,129},{129,257},{257,385},{3... | collective-permute-start | bytes 786440 | tf_op jit(solution)/shard_map/ppermute | solution.py:257
  228.5 1.6 copy-start.1
  230.1 11.9 %copy-start.4 = (bf16[2,4,256,256]{3,2,1,0:T(8,128)(2,1)S(1)}, bf16[2,4,256,256]{3,2,1,0:T(8,128)(2,1)}, u32[]{:S(2)}) copy-start(bf16[2,4,256,256]{3,2,1,0:T(8,128)(2,1)} %env_ref.3) | copy-start | bytes 3145732
  230.1 49.3 %all-to-all-start.3 = ((bf16[8,3,2,256,128]{4,3,2,1,0:T(8,128)(2,1)}), bf16[8,3,2,256,128]{4,3,2,1,0:T(8,128)(2,1)}, u32[]{:S(2)}, u32[]{:S(2)}) async-start(bf16[8,3,2,256,128]{4,3,2,1,0:T(8,128)(2,1)} %copy-done.1), calls=%async_computation.4 | async-start | bytes 6291456 | tf_op jit(solution)/shard_map/all_to_all | solution.py:301
  242.0 71.0 %reduce-scatter.2.cloned.1.call-start = ((), (), s32[]{:S(2)}) async-start(), calls=%async_computation.6 | async-start | bytes 1114112 | tf_op jit(solution)/shard_map/reduce_scatter | solution.py:310
  285.9 9.5 %copy-start.10 = (s32[4]{0:T(128)S(1)}, s32[4]{0:T(128)}, u32[]{:S(2)}) copy-start(s32[4]{0:T(128)} %rows_ref.1) | copy-start | bytes 52
  286.0 4.3 %collective-permute-start.8 = (bf16[8,16,16,128]{3,2,1,0:T(8,128)(2,1)S(1)}, bf16[8,16,16,128]{3,2,1,0:T(8,128)(2,1)S(1)}, u32[]{:S(2)}, u32[]{:S(2)}) collective-permute-start(bf16[8,16,16,128]{3,2,1,0:T(8,128)(2,1)S(1)} %get-tuple-element.20), channel_id=1, source_target_pairs={{0,1},{1,0},{2,3},{3,2},{4,5},{5,4},{6,7},{7,6},{8,9},{9,8},{10,11... | collective-permute-start | bytes 1572872 | tf_op jit(solution)/shard_map/ppermute | solution.py:257
  291.2 21.7 %all-to-all-start.4 = ((bf16[8,16,16,128]{3,2,1,0:T(8,128)(2,1)}), bf16[8,16,16,128]{3,2,1,0:T(8,128)(2,1)S(1)}, u32[]{:S(2)}, u32[]{:S(2)}) async-start(bf16[8,16,16,128]{3,2,1,0:T(8,128)(2,1)} %add_convert_fusion), calls=%async_computation.5 | async-start | bytes 1048576 | tf_op jit(solution)/shard_map/all_to_all | solution.py:307
  (3 other events, 2.4 us)
Sparse Core Ops, SparseCore 0:
  39.5 40.1 all-gather.5
  81.8 49.1 all-gather.7
  249.3 62.4 reduce-scatter.1

commit v4 on v3

--- a/solution.py
+++ b/solution.py
@@ -9,11 +9,15 @@
 
 SHARE = 16
 LANES = 128
-VMEM_LIMIT = 48 * 1024 * 1024
+VMEM_LIMIT = 40 * 1024 * 1024
 REMAP = ("zh", "zl", "x")
 GROUP = ("zl", "x")
 DEPTH = ("y", "core")
 SMEM = pl.BlockSpec(memory_space=pltpu.SMEM)
+
+
+def in_hbm(array):
+    return pltpu.with_memory_space_constraint(array, pltpu.HBM)
 
 
 def spread_kernel(count, depth_ref, home_ref, links_ref, rows_ref, wave_ref, out_ref, label_ref):
@@ -77,9 +81,9 @@
             out_specs=pl.BlockSpec((slots, 3 * SHARE, LANES), lambda i, depth: (0, 0, 0)),
             scratch_shapes=[pltpu.SMEM((1 + term_links.shape[0], slots), jnp.int32)],
         ),
-        out_shape=jax.ShapeDtypeStruct((slots, 3 * SHARE, LANES), jnp.bfloat16),
+        out_shape=pltpu.HBM((slots, 3 * SHARE, LANES), jnp.bfloat16),
         name="spread_blocks",
-    )(depth, right_home, term_links, sector_rows, wavefunction)
+    )(depth, right_home, term_links, sector_rows, in_hbm(wavefunction))
 
 
 def order_kernel(from_ref, links_ref, cols_ref, in_ref, out_ref):
@@ -175,10 +179,10 @@
                 pltpu.VMEM((sectors, extent, terms * width), jnp.bfloat16),
             ],
         ),
-        out_shape=jax.ShapeDtypeStruct(shape, jnp.bfloat16),
+        out_shape=pltpu.HBM(shape, jnp.bfloat16),
         compiler_params=pltpu.CompilerParams(vmem_limit_bytes=VMEM_LIMIT),
         name="right_products",
-    )(place, targets, slices, *[array for array, _ in flat])
+    )(place, targets, in_hbm(slices), *[array for array, _ in flat])
 
 
 def left_partials(place_ref, from_ref, own_ref, far_ref, env_ref, placed_ref):
@@ -297,7 +301,9 @@
         across = [shift(up[:1], "zh", -1), shift(down[1:], "zh", 1)]
         envs = [[(up, 0), (up, 1)], [(across[0], 0), (across[1], 0)], [(down, 0), (down, 1)]]
         products = right_products(place, targets, slices, envs, group, 0, LANES)
-        slices, products = lax.optimization_barrier((slices, products))
+        if chunk + 1 < len(parts):
+            after = slices, products, above[chunk + 1], below[chunk + 1]
+            slices, products, above[chunk + 1], below[chunk + 1] = lax.optimization_barrier(after)
         far = lax.all_to_all(products, GROUP, 0, 0, tiled=True)
         last = (chunk + 1) * LANES == width
         partial = left_products(place, source[1:], own, far, left_env, chunk, last)

time: 323 us -> 311 us (0.963)
  starting transfers between devices: 57.7 us -> 50.5 us
  waiting for transfers between devices: 154 us -> 147 us
  Pallas kernels: 38.4 us -> 42.9 us
    all_to_all x2, starting transfers between devices: 16.9 us -> 9.45 us  [local(): far = lax.all_to_all(products, GROUP, 0, 0, tiled=True)]
    pallas_call x3, Pallas kernels: 20.4 us -> 24.9 us  [right_products(): pl.pallas_call(right_kernel, grid_spec=pltpu.PrefetchScalarGridSpec(num_s...]
    ppermute x9, waiting for transfers between devices: 88.3 us -> 84.6 us  [shift(): lax.ppermute(array, axis, [(i, (i + step) % size) for i in range(size)])]
    unnamed x23, local copies, waits for them, and re-layouts: 8.05 us -> 4.6 us
  transfers between devices with their start and end apart: 16 -> 16, of which waited for: 11 -> 7; matrix products, arithmetic and copies ran while one was open for 1% -> 2% of each run, Pallas kernels for 11% -> 12%
where the time goes in v4:
time: 311 us; the launch traced here: 310 us
  waiting for transfers between devices  147 us (47%)
  starting transfers between devices  50.5 us (16%)
  Pallas kernels  42.9 us (14%)
  blocking collectives  42.8 us (14%)
  between operations  13.3 us (4%)
  local copies, waits for them, and re-layouts  8.45 us (3%)
  other arithmetic  4.58 us (1%)
    ppermute x9, waiting for transfers between devices, shift(): lax.ppermute(array, axis, [(i, (i + step) % size) for i in range(size)])  84.6 us
    ppermute x9, starting transfers between devices, shift(): lax.ppermute(array, axis, [(i, (i + step) % size) for i in range(size)])  32.3 us
    all_to_all x2, waiting for transfers between devices, local(): far = lax.all_to_all(products, GROUP, 0, 0, tiled=True)  30.3 us
    all_to_all x1, blocking collectives, local(): arrived = lax.all_to_all(buffer, REMAP, 0, 0, tiled=True)  27.6 us
    pallas_call x3, Pallas kernels, right_products(): pl.pallas_call(right_kernel, grid_spec=pltpu.PrefetchScalarGridSpec(num_s...  24.9 us
    all_to_all x1, waiting for transfers between devices, local(): gathered = lax.all_to_all(pair.astype(jnp.bfloat16), 'y', 0, 0, tiled=True)  16.8 us
    all_gather x1, waiting for transfers between devices, local(): slices = lax.all_gather(ordered[None], DEPTH)  15.6 us
    all_gather x1, blocking collectives, local(): around = lax.all_gather(ordered, 'zh')  15.1 us
  transfers between devices with their start and end apart: 16, of which 7 were waited for; matrix products, arithmetic and copies ran while one was open for 2% of the time, Pallas kernels for 12%

profile of v4, /device:TPU:1, one launch (start us, length us, event | category | flops | bytes accessed | tf_op | source)
XLA Modules:
  0.0 309.9 jit_solution(5371557488344921164)
XLA Ops:
  9.2 27.6 %all_to_all.25.in_ref = bf16[32,48,128]{2,1,0:T(8,128)(2,1)S(1)} all-to-all(bf16[32,48,128]{2,1,0:T(8,128)(2,1)} %spread_blocks.1), channel_id=1, replica_groups=mesh['zh'=4,'zl'=2,'x'=4,'y'=8,'core'=2] {'zh','zl','x'}, dimensions={0} | all-to-all | bytes 786432 | tf_op jit(solution)/shard_map/all_to_all | solution.py:277
  39.5 15.1 %all-gather.1 = bf16[68,32,128]{2,1,0:T(8,128)(2,1)S(1)} all-gather(bf16[17,32,128]{2,1,0:T(8,128)(2,1)} %order_blocks.1), channel_id=3, replica_groups=mesh['zh'=4,'zl'=2,'x'=4,'y'=8,'core'=2] {'zh'}, dimensions={0}, use_global_device_ids=true | all-gather | bytes 696320 | tf_op jit(solution)/shard_map/all_gather | solution.py:294
  56.6 3.0 collective-permute-start.1
  59.6 4.4 %collective-permute-start = (bf16[2,4,256,128]{3,2,1,0:T(8,128)(2,1)S(1)}, bf16[2,4,256,128]{3,2,1,0:T(8,128)(2,1)S(1)}, u32[]{:S(2)}, u32[]{:S(2)}) collective-permute-start(bf16[2,4,256,128]{3,2,1,0:T(8,128)(2,1)S(1)} %get-tuple-element.24), channel_id=1, source_target_pairs={{0,384},{128,0},{256,128},{384,256},{1,385},{129,1},{257,129},{385... | collective-permute-start | bytes 1572872 | tf_op jit(solution)/shard_map/ppermute | solution.py:261
  64.2 15.6 %all-gather.6.cloned.1.call-done = bf16[272,32,128]{2,1,0:T(8,128)(2,1)} async-done(((bf16[17,32,128]{2,1,0:T(8,128)(2,1)}), bf16[272,32,128]{2,1,0:T(8,128)(2,1)}) %all-gather.6.cloned.1.call-update) | async-done | bytes 2228240 | tf_op jit(solution)/shard_map/all_gather | solution.py:287
  79.7 5.7 %right_products.3 = bf16[8,1,2,256,256]{4,3,2,1,0:T(8,128)(2,1)} custom-call(s32[3]{0:T(128)S(1)} %pad_add_fusion.place_ref, s32[1,32]{1,0:T(1,128)S(1)} %reshape.49.targets_ref, bf16[16,1,17,32,128]{4,3,2,1,0:T(8,128)(2,1)} %bitcast.24, bf16[2,4,256,256]{3,2,1,0:T(8,128)(2,1)S(1)} %copy-done, bf16[2,4,256,256]{3,2,1,0:T(8,128)(2,1)S(1)} %copy-done), custom_call_target="tpu_custom_call" | custom-call | tf_op jit(solution)/shard_map/right_products/pallas_call | solution.py:164
  86.9 4.4 %all-to-all-start.1 = ((bf16[8,1,2,256,256]{4,3,2,1,0:T(8,128)(2,1)}), bf16[8,1,2,256,256]{4,3,2,1,0:T(8,128)(2,1)S(1)}, u32[]{:S(2)}, u32[]{:S(2)}) async-start(bf16[8,1,2,256,256]{4,3,2,1,0:T(8,128)(2,1)} %right_products.3), calls=%async_computation.1 | async-start | bytes 4194304 | tf_op jit(solution)/shard_map/all_to_all | solution.py:292
  91.3 4.4 %collective-permute-start.5 = (bf16[2,4,256,128]{3,2,1,0:T(8,128)(2,1)}, bf16[2,4,256,128]{3,2,1,0:T(8,128)(2,1)S(1)}, u32[]{:S(2)}, u32[]{:S(2)}) collective-permute-start(bf16[2,4,256,128]{3,2,1,0:T(8,128)(2,1)} %get-tuple-element.23), channel_id=1, source_target_pairs={{0,128},{128,256},{256,384},{384,0},{1,129},{129,257},{257,385},{3... | collective-permute-start | bytes 1572872 | tf_op jit(solution)/shard_map/ppermute | solution.py:261
  95.7 3.0 collective-permute-start.4
  100.7 3.6 %collective-permute-start.3 = (bf16[1,4,256,128]{3,2,1,0:T(8,128)(2,1)S(1)}, bf16[1,4,256,128]{3,2,1,0:T(8,128)(2,1)S(1)}, u32[]{:S(2)}, u32[]{:S(2)}) collective-permute-start(bf16[1,4,256,128]{3,2,1,0:T(8,128)(2,1)S(1)} %slice.37), channel_id=1, source_target_pairs={{0,128},{128,256},{256,384},{384,0},{1,129},{129,257},{257,385},{3... | collective-permute-start | bytes 786440 | tf_op jit(solution)/shard_map/ppermute | solution.py:261
  104.2 3.8 %collective-permute-start.2 = (bf16[1,4,256,128]{3,2,1,0:T(8,128)(2,1)S(1)}, bf16[1,4,256,128]{3,2,1,0:T(8,128)(2,1)S(1)}, u32[]{:S(2)}, u32[]{:S(2)}) collective-permute-start(bf16[1,4,256,128]{3,2,1,0:T(8,128)(2,1)S(1)} %slice.36), channel_id=1, source_target_pairs={{0,384},{128,0},{256,128},{384,256},{1,385},{129,1},{257,129},{385... | collective-permute-start | bytes 786440 | tf_op jit(solution)/shard_map/ppermute | solution.py:261
  108.8 43.1 %collective-permute-done.3.refs_3_ = bf16[1,4,256,128]{3,2,1,0:T(8,128)(2,1)S(1)} collective-permute-done((bf16[1,4,256,128]{3,2,1,0:T(8,128)(2,1)S(1)}, bf16[1,4,256,128]{3,2,1,0:T(8,128)(2,1)S(1)}, u32[]{:S(2)}, u32[]{:S(2)}) %collective-permute-start.3) | collective-permute-done | bytes 262176 | tf_op jit(solution)/shard_map/ppermute | solution.py:261
  155.7 9.6 %right_products.4 = bf16[8,3,2,256,128]{4,3,2,1,0:T(8,128)(2,1)} custom-call(s32[3]{0:T(128)S(1)} %pad_add_fusion.place_ref, s32[3,32]{1,0:T(4,128)S(1)} %bitcast.19, bf16[16,3,17,32,128]{4,3,2,1,0:T(8,128)(2,1)} %bitcast.21, bf16[2,4,256,128]{3,2,1,0:T(8,128)(2,1)S(1)} %copy-done.5, bf16[2,4,256,128]{3,2,1,0:T(8,128)(2,1)S(1)} %copy-done.5, ...), custom_call_target="tpu_custom_call" | custom-call | tf_op jit(solution)/shard_map/right_products/pallas_call | solution.py:164
  165.3 4.5 %all-to-all-start.2 = ((bf16[8,3,2,256,128]{4,3,2,1,0:T(8,128)(2,1)}), bf16[8,3,2,256,128]{4,3,2,1,0:T(8,128)(2,1)}, u32[]{:S(2)}, u32[]{:S(2)}) async-start(bf16[8,3,2,256,128]{4,3,2,1,0:T(8,128)(2,1)} %right_products.4), calls=%async_computation.2 | async-start | bytes 6291456 | tf_op jit(solution)/shard_map/all_to_all | solution.py:307
  169.8 4.0 %collective-permute-start.7 = (bf16[1,4,256,128]{3,2,1,0:T(8,128)(2,1)S(1)}, bf16[1,4,256,128]{3,2,1,0:T(8,128)(2,1)S(1)}, u32[]{:S(2)}, u32[]{:S(2)}) collective-permute-start(bf16[1,4,256,128]{3,2,1,0:T(8,128)(2,1)S(1)} %slice.40), channel_id=1, source_target_pairs={{0,128},{128,256},{256,384},{384,0},{1,129},{129,257},{257,385},{3... | collective-permute-start | bytes 786440 | tf_op jit(solution)/shard_map/ppermute | solution.py:261
  173.8 3.4 %collective-permute-start.6 = (bf16[1,4,256,128]{3,2,1,0:T(8,128)(2,1)S(1)}, bf16[1,4,256,128]{3,2,1,0:T(8,128)(2,1)S(1)}, u32[]{:S(2)}, u32[]{:S(2)}) collective-permute-start(bf16[1,4,256,128]{3,2,1,0:T(8,128)(2,1)S(1)} %slice.39), channel_id=1, source_target_pairs={{0,384},{128,0},{256,128},{384,256},{1,385},{129,1},{257,129},{385... | collective-permute-start | bytes 786440 | tf_op jit(solution)/shard_map/ppermute | solution.py:261
  177.2 39.3 %collective-permute-done.7.refs_3_ = bf16[1,4,256,128]{3,2,1,0:T(8,128)(2,1)S(1)} collective-permute-done((bf16[1,4,256,128]{3,2,1,0:T(8,128)(2,1)S(1)}, bf16[1,4,256,128]{3,2,1,0:T(8,128)(2,1)S(1)}, u32[]{:S(2)}, u32[]{:S(2)}) %collective-permute-start.7) | collective-permute-done | bytes 262176 | tf_op jit(solution)/shard_map/ppermute | solution.py:261
  216.5 9.6 %right_products.5 = bf16[8,3,2,256,128]{4,3,2,1,0:T(8,128)(2,1)} custom-call(s32[3]{0:T(128)S(1)} %pad_add_fusion.place_ref, s32[3,32]{1,0:T(4,128)S(1)} %bitcast.20, bf16[16,3,17,32,128]{4,3,2,1,0:T(8,128)(2,1)} %bitcast.22, bf16[2,4,256,128]{3,2,1,0:T(8,128)(2,1)S(1)} %collective-permute-done.4.refs_0_.refs_1_, ...), custom_call_target="tpu_custom_call" | custom-call | tf_op jit(solution)/shard_map/right_products/pallas_call | solution.py:164
  226.1 5.0 %all-to-all-start.3 = ((bf16[8,3,2,256,128]{4,3,2,1,0:T(8,128)(2,1)}), bf16[8,3,2,256,128]{4,3,2,1,0:T(8,128)(2,1)}, u32[]{:S(2)}, u32[]{:S(2)}) async-start(bf16[8,3,2,256,128]{4,3,2,1,0:T(8,128)(2,1)} %right_products.5), calls=%async_computation.4 | async-start | bytes 6291456 | tf_op jit(solution)/shard_map/all_to_all | solution.py:307
  231.2 7.1 %left_products.2 = bf16[16,16,16,128]{3,2,1,0:T(8,128)(2,1)} custom-call(s32[3]{0:T(128)S(1)} %pad_add_fusion.place_ref, s32[2,16]{1,0:T(2,128)S(1)} %slice.32.from_ref, bf16[8,1,2,256,256]{4,3,2,1,0:T(8,128)(2,1)S(1)} %all-to-all-done.1.own_ref, bf16[8,3,2,256,128]{4,3,2,1,0:T(8,128)(2,1)} %all-to-all-done.2.far_ref, bf16[2,4,256,256]{3,2,1,0:T(8,128)(2,1)S(1)} %copy-done.1), custom_call_target="tpu_custom_call" | custom-call | tf_op jit(solution)/shard_map/left_products/pallas_call | solution.py:241
  238.3 30.3 %all-to-all-done.3.far_ref = bf16[8,3,2,256,128]{4,3,2,1,0:T(8,128)(2,1)} async-done(((bf16[8,3,2,256,128]{4,3,2,1,0:T(8,128)(2,1)}), bf16[8,3,2,256,128]{4,3,2,1,0:T(8,128)(2,1)}, u32[]{:S(2)}, u32[]{:S(2)}) %all-to-all-start.3) | async-done | bytes 3145760 | tf_op jit(solution)/shard_map/all_to_all | solution.py:307
  268.6 6.5 %left_products.3 = (bf16[8,16,16,128]{3,2,1,0:T(8,128)(2,1)S(1)}, bf16[8,16,16,128]{3,2,1,0:T(8,128)(2,1)S(1)}) custom-call(s32[3]{0:T(128)S(1)} %pad_add_fusion.place_ref, s32[2,16]{1,0:T(2,128)S(1)} %slice.32.from_ref, bf16[8,1,2,256,256]{4,3,2,1,0:T(8,128)(2,1)S(1)} %all-to-all-done.1.own_ref, bf16[8,3,2,256,128]{4,3,2,1,0:T(8,128)(2,1)} %all-to-all-done.3.far_ref, ...), custom_call_target="tpu_custom_call" | custom-call | tf_op jit(solution)/shard_map/left_products/pallas_call | solution.py:241
  280.3 4.3 %all-to-all-start.4 = ((bf16[8,16,16,128]{3,2,1,0:T(8,128)(2,1)}), bf16[8,16,16,128]{3,2,1,0:T(8,128)(2,1)S(1)}, u32[]{:S(2)}, u32[]{:S(2)}) async-start(bf16[8,16,16,128]{3,2,1,0:T(8,128)(2,1)} %add_convert_fusion), calls=%async_computation.5 | async-start | bytes 1048576 | tf_op jit(solution)/shard_map/all_to_all | solution.py:313
  284.8 16.8 %all-to-all-done.4 = bf16[8,16,16,128]{3,2,1,0:T(8,128)(2,1)S(1)} async-done(((bf16[8,16,16,128]{3,2,1,0:T(8,128)(2,1)}), bf16[8,16,16,128]{3,2,1,0:T(8,128)(2,1)S(1)}, u32[]{:S(2)}, u32[]{:S(2)}) %all-to-all-start.4) | async-done | bytes 524320 | tf_op jit(solution)/shard_map/all_to_all | solution.py:313
  (65 shorter events, 22.6 us)
Async XLA Ops:
  6.5 73.2 %all-gather.6.cloned.1.call-start = ((), (), s32[]{:S(2)}) async-start(), calls=%async_computation.7 | async-start | bytes 2367488 | tf_op jit(solution)/shard_map/all_gather | solution.py:287
  9.2 46.4 %copy-start = (bf16[2,4,256,256]{3,2,1,0:T(8,128)(2,1)S(1)}, bf16[2,4,256,256]{3,2,1,0:T(8,128)(2,1)}, u32[]{:S(2)}) copy-start(bf16[2,4,256,256]{3,2,1,0:T(8,128)(2,1)} %refs_1_.1) | copy-start | bytes 3145732
  36.8 0.8 copy-start.8
  39.4 24.5 %copy-start.9 = (s32[2,16]{1,0:T(2,128)S(1)}, s32[2,16]{1,0:T(2,128)}, u32[]{:S(2)}) copy-start(s32[2,16]{1,0:T(2,128)} %links_ref.3) | copy-start | bytes 388
  39.5 113.2 %all-gather.8.cloned.1.call-start = ((), (), s32[]{:S(2)}) async-start(), calls=%async_computation.8 | async-start | bytes 7102464 | tf_op jit(solution)/shard_map/all_gather | solution.py:297
  56.6 28.8 %collective-permute-start.1 = (bf16[2,4,256,128]{3,2,1,0:T(8,128)(2,1)S(1)}, bf16[2,4,256,128]{3,2,1,0:T(8,128)(2,1)S(1)}, u32[]{:S(2)}, u32[]{:S(2)}) collective-permute-start(bf16[2,4,256,128]{3,2,1,0:T(8,128)(2,1)S(1)} %get-tuple-element.24), channel_id=1, source_target_pairs={{0,128},{128,256},{256,384},{384,0},{1,129},{129,257},{257,385},{3... | collective-permute-start | bytes 1572872 | tf_op jit(solution)/shard_map/ppermute | solution.py:261
  59.6 26.6 %collective-permute-start = (bf16[2,4,256,128]{3,2,1,0:T(8,128)(2,1)S(1)}, bf16[2,4,256,128]{3,2,1,0:T(8,128)(2,1)S(1)}, u32[]{:S(2)}, u32[]{:S(2)}) collective-permute-start(bf16[2,4,256,128]{3,2,1,0:T(8,128)(2,1)S(1)} %get-tuple-element.24), channel_id=1, source_target_pairs={{0,384},{128,0},{256,128},{384,256},{1,385},{129,1},{257,129},{385... | collective-permute-start | bytes 1572872 | tf_op jit(solution)/shard_map/ppermute | solution.py:261
  86.9 78.3 %all-to-all-start.1 = ((bf16[8,1,2,256,256]{4,3,2,1,0:T(8,128)(2,1)}), bf16[8,1,2,256,256]{4,3,2,1,0:T(8,128)(2,1)S(1)}, u32[]{:S(2)}, u32[]{:S(2)}) async-start(bf16[8,1,2,256,256]{4,3,2,1,0:T(8,128)(2,1)} %right_products.3), calls=%async_computation.1 | async-start | bytes 4194304 | tf_op jit(solution)/shard_map/all_to_all | solution.py:292
  91.3 73.9 %collective-permute-start.5 = (bf16[2,4,256,128]{3,2,1,0:T(8,128)(2,1)}, bf16[2,4,256,128]{3,2,1,0:T(8,128)(2,1)S(1)}, u32[]{:S(2)}, u32[]{:S(2)}) collective-permute-start(bf16[2,4,256,128]{3,2,1,0:T(8,128)(2,1)} %get-tuple-element.23), channel_id=1, source_target_pairs={{0,128},{128,256},{256,384},{384,0},{1,129},{129,257},{257,385},{3... | collective-permute-start | bytes 1572872 | tf_op jit(solution)/shard_map/ppermute | solution.py:261
  95.7 69.5 %collective-permute-start.4 = (bf16[2,4,256,128]{3,2,1,0:T(8,128)(2,1)}, bf16[2,4,256,128]{3,2,1,0:T(8,128)(2,1)S(1)}, u32[]{:S(2)}, u32[]{:S(2)}) collective-permute-start(bf16[2,4,256,128]{3,2,1,0:T(8,128)(2,1)} %get-tuple-element.23), channel_id=1, source_target_pairs={{0,384},{128,0},{256,128},{384,256},{1,385},{129,1},{257,129},{385... | collective-permute-start | bytes 1572872 | tf_op jit(solution)/shard_map/ppermute | solution.py:261
  100.7 51.2 %collective-permute-start.3 = (bf16[1,4,256,128]{3,2,1,0:T(8,128)(2,1)S(1)}, bf16[1,4,256,128]{3,2,1,0:T(8,128)(2,1)S(1)}, u32[]{:S(2)}, u32[]{:S(2)}) collective-permute-start(bf16[1,4,256,128]{3,2,1,0:T(8,128)(2,1)S(1)} %slice.37), channel_id=1, source_target_pairs={{0,128},{128,256},{256,384},{384,0},{1,129},{129,257},{257,385},{3... | collective-permute-start | bytes 786440 | tf_op jit(solution)/shard_map/ppermute | solution.py:261
  104.2 47.6 %collective-permute-start.2 = (bf16[1,4,256,128]{3,2,1,0:T(8,128)(2,1)S(1)}, bf16[1,4,256,128]{3,2,1,0:T(8,128)(2,1)S(1)}, u32[]{:S(2)}, u32[]{:S(2)}) collective-permute-start(bf16[1,4,256,128]{3,2,1,0:T(8,128)(2,1)S(1)} %slice.36), channel_id=1, source_target_pairs={{0,384},{128,0},{256,128},{384,256},{1,385},{129,1},{257,129},{385... | collective-permute-start | bytes 786440 | tf_op jit(solution)/shard_map/ppermute | solution.py:261
  152.6 1.0 copy-start.3
  153.7 1.0 copy-start.5
  154.7 0.9 copy-start.7
  165.3 60.9 %all-to-all-start.2 = ((bf16[8,3,2,256,128]{4,3,2,1,0:T(8,128)(2,1)}), bf16[8,3,2,256,128]{4,3,2,1,0:T(8,128)(2,1)}, u32[]{:S(2)}, u32[]{:S(2)}) async-start(bf16[8,3,2,256,128]{4,3,2,1,0:T(8,128)(2,1)} %right_products.4), calls=%async_computation.2 | async-start | bytes 6291456 | tf_op jit(solution)/shard_map/all_to_all | solution.py:307
  169.8 46.7 %collective-permute-start.7 = (bf16[1,4,256,128]{3,2,1,0:T(8,128)(2,1)S(1)}, bf16[1,4,256,128]{3,2,1,0:T(8,128)(2,1)S(1)}, u32[]{:S(2)}, u32[]{:S(2)}) collective-permute-start(bf16[1,4,256,128]{3,2,1,0:T(8,128)(2,1)S(1)} %slice.40), channel_id=1, source_target_pairs={{0,128},{128,256},{256,384},{384,0},{1,129},{129,257},{257,385},{3... | collective-permute-start | bytes 786440 | tf_op jit(solution)/shard_map/ppermute | solution.py:261
  173.8 42.7 %collective-permute-start.6 = (bf16[1,4,256,128]{3,2,1,0:T(8,128)(2,1)S(1)}, bf16[1,4,256,128]{3,2,1,0:T(8,128)(2,1)S(1)}, u32[]{:S(2)}, u32[]{:S(2)}) collective-permute-start(bf16[1,4,256,128]{3,2,1,0:T(8,128)(2,1)S(1)} %slice.39), channel_id=1, source_target_pairs={{0,384},{128,0},{256,128},{384,256},{1,385},{129,1},{257,129},{385... | collective-permute-start | bytes 786440 | tf_op jit(solution)/shard_map/ppermute | solution.py:261
  226.1 5.0 %copy-start.1 = (bf16[2,4,256,256]{3,2,1,0:T(8,128)(2,1)S(1)}, bf16[2,4,256,256]{3,2,1,0:T(8,128)(2,1)}, u32[]{:S(2)}) copy-start(bf16[2,4,256,256]{3,2,1,0:T(8,128)(2,1)} %env_ref.3) | copy-start | bytes 3145732
  226.1 42.5 %all-to-all-start.3 = ((bf16[8,3,2,256,128]{4,3,2,1,0:T(8,128)(2,1)}), bf16[8,3,2,256,128]{4,3,2,1,0:T(8,128)(2,1)}, u32[]{:S(2)}, u32[]{:S(2)}) async-start(bf16[8,3,2,256,128]{4,3,2,1,0:T(8,128)(2,1)} %right_products.5), calls=%async_computation.4 | async-start | bytes 6291456 | tf_op jit(solution)/shard_map/all_to_all | solution.py:307
  231.1 70.6 %reduce-scatter.2.cloned.1.call-start = ((), (), s32[]{:S(2)}) async-start(), calls=%async_computation.6 | async-start | bytes 1114112 | tf_op jit(solution)/shard_map/reduce_scatter | solution.py:316
  275.1 9.5 %copy-start.10 = (s32[4]{0:T(128)S(1)}, s32[4]{0:T(128)}, u32[]{:S(2)}) copy-start(s32[4]{0:T(128)} %rows_ref.1) | copy-start | bytes 52
  275.1 4.3 %collective-permute-start.8 = (bf16[8,16,16,128]{3,2,1,0:T(8,128)(2,1)S(1)}, bf16[8,16,16,128]{3,2,1,0:T(8,128)(2,1)S(1)}, u32[]{:S(2)}, u32[]{:S(2)}) collective-permute-start(bf16[8,16,16,128]{3,2,1,0:T(8,128)(2,1)S(1)} %get-tuple-element.22), channel_id=1, source_target_pairs={{0,1},{1,0},{2,3},{3,2},{4,5},{5,4},{6,7},{7,6},{8,9},{9,8},{10,11... | collective-permute-start | bytes 1572872 | tf_op jit(solution)/shard_map/ppermute | solution.py:261
  280.3 21.3 %all-to-all-start.4 = ((bf16[8,16,16,128]{3,2,1,0:T(8,128)(2,1)}), bf16[8,16,16,128]{3,2,1,0:T(8,128)(2,1)S(1)}, u32[]{:S(2)}, u32[]{:S(2)}) async-start(bf16[8,16,16,128]{3,2,1,0:T(8,128)(2,1)} %add_convert_fusion), calls=%async_computation.5 | async-start | bytes 1048576 | tf_op jit(solution)/shard_map/all_to_all | solution.py:313
  (3 other events, 2.3 us)
Sparse Core Ops, SparseCore 0:
  39.6 40.1 all-gather.5
  81.9 49.1 all-gather.7
  238.4 60.5 reduce-scatter.1

commit v5 on v4

--- a/solution.py
+++ b/solution.py
@@ -9,6 +9,7 @@
 
 SHARE = 16
 LANES = 128
+NEAR = 2
 VMEM_LIMIT = 40 * 1024 * 1024
 REMAP = ("zh", "zl", "x")
 GROUP = ("zl", "x")
@@ -154,7 +155,7 @@
                     ]
 
 
-def right_products(place, targets, slices, envs, group, chunk, width):
+def right_products(place, targets, slices, envs, group, width):
     depth, layers, blocks, tall, lanes = slices.shape
     terms = len(envs[0])
     sectors, extent = envs[0][0][0].shape[1:3]
@@ -168,10 +169,8 @@
             grid=(layers,),
             in_specs=[pl.BlockSpec((depth, 1, blocks, tall, lanes), lambda i, p, t: (0, i, 0, 0, 0))]
             + [
-                pl.BlockSpec(
-                    (1, sectors, extent, width), lambda i, p, t, term=term: (term, 0, 0, chunk)
-                )
-                for _, term in flat
+                pl.BlockSpec((1, sectors, extent, width), lambda i, p, t, at=at: (at(p), 0, 0, 0))
+                for _, at in flat
             ],
             out_specs=pl.BlockSpec((group, 1, terms, extent, width), lambda i, p, t: (0, i, 0, 0, 0)),
             scratch_shapes=[
@@ -185,10 +184,10 @@
     )(place, targets, in_hbm(slices), *[array for array, _ in flat])
 
 
-def left_partials(place_ref, from_ref, own_ref, far_ref, env_ref, placed_ref):
+def left_partials(place_ref, from_ref, near_ref, far_ref, env_ref, placed_ref):
     terms, count = from_ref.shape
-    group, _, _, extent, _ = own_ref.shape
-    layers = far_ref.shape[1] + 1
+    group, near, _, extent, width = near_ref.shape
+    layers = near + far_ref.shape[1]
     per_sector = count // pl.num_programs(0)
     sector = pl.program_id(0)
     left = jnp.concatenate([env_ref[term, 0] for term in range(terms)], axis=1)
@@ -197,29 +196,32 @@
             device = from_ref[term, sector * per_sector + place]
             peer = lax.rem(device, group)
             step = lax.rem(lax.div(device, group) + layers - place_ref[0], layers)
-            at = slice(term * extent, (term + 1) * extent)
-
-            @pl.when(step == 0)
-            def _(place=place, term=term, peer=peer, at=at):
-                placed_ref[place, at, :] = own_ref[peer, 0, term]
-
-            @pl.when(step > 0)
-            def _(place=place, term=term, peer=peer, at=at, step=step):
-                placed_ref[place, at, :] = far_ref[peer, jnp.maximum(step - 1, 0), term]
-
-        partial = jnp.dot(left, placed_ref[place], preferred_element_type=jnp.float32)
-        yield place, partial.astype(jnp.bfloat16)
-
-
-def left_kernel(place_ref, from_ref, own_ref, far_ref, env_ref, out_ref, placed_ref):
-    for place, partial in left_partials(place_ref, from_ref, own_ref, far_ref, env_ref, placed_ref):
+            rows = slice(term * extent, (term + 1) * extent)
+            columns = slice(place * width, (place + 1) * width)
+
+            @pl.when(step < near)
+            def _(term=term, peer=peer, step=step, rows=rows, columns=columns):
+                placed_ref[rows, columns] = near_ref[peer, jnp.minimum(step, near - 1), term]
+
+            @pl.when(step >= near)
+            def _(term=term, peer=peer, step=step, rows=rows, columns=columns):
+                placed_ref[rows, columns] = far_ref[peer, jnp.maximum(step - near, 0), term]
+
+    partial = jnp.dot(left, placed_ref[...], preferred_element_type=jnp.float32)
+    partial = partial.astype(jnp.bfloat16)
+    for place in range(per_sector):
+        yield place, partial[:, place * width : (place + 1) * width]
+
+
+def left_kernel(place_ref, from_ref, near_ref, far_ref, env_ref, out_ref, placed_ref):
+    for place, partial in left_partials(place_ref, from_ref, near_ref, far_ref, env_ref, placed_ref):
         out_ref[:, place] = partial.reshape(out_ref.shape[0], SHARE, partial.shape[1])
 
 
-def left_split_kernel(place_ref, from_ref, own_ref, far_ref, env_ref, keep_ref, send_ref, placed_ref):
+def left_split_kernel(place_ref, from_ref, near_ref, far_ref, env_ref, keep_ref, send_ref, placed_ref):
     chips = keep_ref.shape[0]
     core = place_ref[2]
-    for place, partial in left_partials(place_ref, from_ref, own_ref, far_ref, env_ref, placed_ref):
+    for place, partial in left_partials(place_ref, from_ref, near_ref, far_ref, env_ref, placed_ref):
         halves = [
             jnp.stack(
                 [partial[(2 * c + k) * SHARE : (2 * c + k + 1) * SHARE] for c in range(chips)]
@@ -230,7 +232,7 @@
         send_ref[:, place] = jnp.where(core == 0, halves[1], halves[0])
 
 
-def left_products(place, source, own, far, left_env, chunk, split):
+def left_products(place, source, near, far, left_env, split):
     _, sectors, extent, _ = left_env.shape
     terms, count = source.shape
     width = far.shape[-1]
@@ -244,16 +246,16 @@
         in_specs=[
             SMEM,
             SMEM,
-            pl.BlockSpec(own.shape[:-1] + (width,), lambda i: (0, 0, 0, 0, chunk)),
+            pl.BlockSpec(near.shape, lambda i: (0, 0, 0, 0, 0)),
             pl.BlockSpec(far.shape, lambda i: (0, 0, 0, 0, 0)),
             pl.BlockSpec((terms, 1, extent, extent), lambda i: (0, i, 0, 0)),
         ],
         out_specs=[out_spec, out_spec] if split else out_spec,
         out_shape=[shape, shape] if split else shape,
-        scratch_shapes=[pltpu.VMEM((per_sector, terms * extent, width), jnp.bfloat16)],
+        scratch_shapes=[pltpu.VMEM((terms * extent, per_sector * width), jnp.bfloat16)],
         compiler_params=pltpu.CompilerParams(vmem_limit_bytes=VMEM_LIMIT),
         name="left_products",
-    )(place, source, own, far, left_env)
+    )(place, source, near, far, left_env)
 
 
 def shift(array, axis, step):
@@ -273,6 +275,8 @@
     depth_index = lax.axis_index("y") * 2 + core_index
     place = jnp.stack([layer, lax.axis_index("y"), core_index])
 
+    second = right_env[..., LANES:]
+    gathered_env = lax.all_gather(right_env[..., :LANES], "zh")
     buffer = spread(depth_index.reshape(1), right_home, term_links, sector_rows, wavefunction, slots)
     arrived = lax.all_to_all(buffer, REMAP, 0, 0, tiled=True)
     labels = arrived[:, 2 * SHARE, : 1 + terms].astype(jnp.int32)
@@ -280,41 +284,51 @@
     source = jnp.sum(jnp.where(match, jnp.arange(slots, dtype=jnp.int32), 0), axis=2)
     ordered = order(source[0], term_links, sector_cols, arrived)
 
-    parts = [right_env[..., at : at + LANES] for at in range(0, width, LANES)]
-    above = [shift(part, "zh", -1) for part in parts]
-    below = [shift(part, "zh", 1) for part in parts]
-
-    slices = lax.all_gather(ordered[None], DEPTH)
-    targets = (term_links // count).reshape(1, terms * count)
-    envs = [[(right_env, term) for term in range(terms)]]
-    products = right_products(place, targets, slices, envs, group, 0, width)
-    products, above[0], below[0] = lax.optimization_barrier((products, above[0], below[0]))
-    own = lax.all_to_all(products, GROUP, 0, 0, tiled=True)
-
     around = lax.all_gather(ordered, "zh")
-    others = lax.dynamic_slice_in_dim(jnp.concatenate([around, around]), layer + 1, layers - 1)
-    targets = others[:, count, 0, : terms * count].astype(jnp.int32)
-    slices = lax.all_gather(others, DEPTH)
-    pieces = []
-    for chunk in range(width // LANES):
-        up, down = above[chunk], below[chunk]
-        across = [shift(up[:1], "zh", -1), shift(down[1:], "zh", 1)]
-        envs = [[(up, 0), (up, 1)], [(across[0], 0), (across[1], 0)], [(down, 0), (down, 1)]]
-        products = right_products(place, targets, slices, envs, group, 0, LANES)
-        if chunk + 1 < len(parts):
-            after = slices, products, above[chunk + 1], below[chunk + 1]
-            slices, products, above[chunk + 1], below[chunk + 1] = lax.optimization_barrier(after)
-        far = lax.all_to_all(products, GROUP, 0, 0, tiled=True)
-        last = (chunk + 1) * LANES == width
-        partial = left_products(place, source[1:], own, far, left_env, chunk, last)
-        if last:
-            keep, send = partial
-            pair = keep.astype(jnp.float32) + shift(send, "core", 1).astype(jnp.float32)
-            gathered = lax.all_to_all(pair.astype(jnp.bfloat16), "y", 0, 0, tiled=True)
-            pieces.append(jnp.sum(gathered.astype(jnp.float32), axis=0))
-        else:
-            summed = lax.psum_scatter(partial, DEPTH, scatter_dimension=0, tiled=False)
-            pieces.append(summed.astype(jnp.float32))
+    around = lax.dynamic_slice_in_dim(jnp.concatenate([around, around]), layer, layers)
+    targets = around[:, count, 0, : terms * count].astype(jnp.int32)
+    far = around[NEAR:]
+    near, gathered_env = lax.optimization_barrier((around[:NEAR], gathered_env))
+    near = lax.all_gather(near, DEPTH)
+    far = lax.all_gather(far, DEPTH)
+
+    above, below = shift(second, "zh", -1), shift(second, "zh", 1)
+    across = [shift(above[:1], "zh", -1), shift(below[1:], "zh", 1)]
+    held = gathered_env.reshape((layers * terms,) + gathered_env.shape[2:])
+    first_envs = [
+        [
+            (held, lambda p, step=step, term=term: lax.rem(p[0] + step, layers) * terms + term)
+            for term in range(terms)
+        ]
+        for step in range(layers)
+    ]
+    begun = right_products(place, targets[:NEAR], near, first_envs[:NEAR], group, LANES)
+    begun, above, below, across = lax.optimization_barrier((begun, above, below, across))
+    second_envs = [
+        [(second, lambda p: 0), (second, lambda p: 1)],
+        [(above, lambda p: 0), (above, lambda p: 1)],
+        [(across[0], lambda p: 0), (across[1], lambda p: 0)],
+        [(below, lambda p: 0), (below, lambda p: 1)],
+    ]
+    sent = {("near", 0): lax.all_to_all(begun, GROUP, 0, 0, tiled=True)}
+    for key, chunk, slices, envs in (
+        ("near", 1, near, second_envs[:NEAR]),
+        ("far", 0, far, first_envs[NEAR:]),
+        ("far", 1, far, second_envs[NEAR:]),
+    ):
+        steps = targets[:NEAR] if key == "near" else targets[NEAR:]
+        products = right_products(place, steps, slices, envs, group, LANES)
+        before = list(sent)[-1]
+        products, sent[before] = lax.optimization_barrier((products, sent[before]))
+        sent[key, chunk] = lax.all_to_all(products, GROUP, 0, 0, tiled=True)
+
+    partial = left_products(place, source[1:], sent["near", 0], sent["far", 0], left_env, False)
+    summed = lax.psum_scatter(partial, DEPTH, scatter_dimension=0, tiled=False)
+    pieces = [summed.astype(jnp.float32)]
+    keep, send = left_products(place, source[1:], sent["near", 1], sent["far", 1], left_env, True)
+    pair = keep.astype(jnp.float32) + shift(send, "core", 1).astype(jnp.float32)
+    shares = lax.all_to_all(pair.astype(jnp.bfloat16), "y", 0, 0, tiled=True)
+    pieces.append(jnp.sum(shares.astype(jnp.float32), axis=0))
     total = jnp.concatenate(pieces, axis=2)
     row = depth_index * SHARE + jnp.arange(SHARE, dtype=jnp.int32)
     keep_rows = row[None, :] < jnp.repeat(sector_rows, per_sector)[:, None]

time: 311 us -> 311 us (level)
  blocking collectives: 42.8 us -> 22.1 us
  waiting for transfers between devices: 147 us -> 159 us
  starting transfers between devices: 50.5 us -> 58 us
    ppermute x9 -> x5, waiting for transfers between devices: 84.6 us -> 21.6 us  [shift(): lax.ppermute(array, axis, [(i, (i + step) % size) for i in range(size)])]
    all_to_all x4 -> x6, waiting for transfers between devices: 47.1 us -> 105 us  [the longest x3 55.4 us: local(): sent[key, chunk] = lax.all_to_all(products, GROUP, 0, 0, tiled=True)]
    all_to_all x1 -> x0, blocking collectives: 27.6 us -> none  [local(): arrived = lax.all_to_all(buffer, REMAP, 0, 0, tiled=True)]
    all_to_all x4 -> x6, starting transfers between devices: 18.1 us -> 34.8 us  [the longest x1 13.7 us: local(): arrived = lax.all_to_all(buffer, REMAP, 0, 0, tiled=True)]
    ppermute x9 -> x5, starting transfers between devices: 32.3 us -> 23.1 us  [shift(): lax.ppermute(array, axis, [(i, (i + step) % size) for i in range(size)])]
    reduce_scatter x1, waiting for transfers between devices: 0.02 us -> 8.9 us  [local(): summed = lax.psum_scatter(partial, DEPTH, scatter_dimension=0, tiled=False)]
    all_gather x1, blocking collectives: 15.1 us -> 22.1 us  [local(): around = lax.all_gather(ordered, 'zh')]
    all_gather x2 -> x3, waiting for transfers between devices: 15.6 us -> 22.4 us  [the longest x1 10.5 us: local(): near = lax.all_gather(near, DEPTH)]
  transfers between devices with their start and end apart: 16 -> 15, of which waited for: 7 -> 12; matrix products, arithmetic and copies ran while one was open for 2% -> 1% of each run, Pallas kernels for 12% -> 14%
where the time goes in v5:
time: 311 us; the launch traced here: 307 us
  waiting for transfers between devices  159 us (51%)
  starting transfers between devices  58 us (19%)
  Pallas kernels  43.2 us (14%)
  blocking collectives  22.1 us (7%)
  between operations  13.3 us (4%)
  local copies, waits for them, and re-layouts  8.29 us (3%)
  other arithmetic  3.15 us (1%)
    all_to_all x3, waiting for transfers between devices, local(): sent[key, chunk] = lax.all_to_all(products, GROUP, 0, 0, tiled=True)  55.4 us
    pallas_call x4, Pallas kernels, right_products(): pl.pallas_call(right_kernel, grid_spec=pltpu.PrefetchScalarGridSpec(num_s...  29.8 us
    ppermute x5, starting transfers between devices, shift(): lax.ppermute(array, axis, [(i, (i + step) % size) for i in range(size)])  23.1 us
    all_gather x1, blocking collectives, local(): around = lax.all_gather(ordered, 'zh')  22.1 us
    ppermute x5, waiting for transfers between devices, shift(): lax.ppermute(array, axis, [(i, (i + step) % size) for i in range(size)])  21.6 us
    all_to_all x1, waiting for transfers between devices, local(): sent = {('near', 0): lax.all_to_all(begun, GROUP, 0, 0, tiled=True)}  18.8 us
    all_to_all x1, waiting for transfers between devices, local(): shares = lax.all_to_all(pair.astype(jnp.bfloat16), 'y', 0, 0, tiled=True)  17.3 us
    all_to_all x1, waiting for transfers between devices, local(): arrived = lax.all_to_all(buffer, REMAP, 0, 0, tiled=True)  13.8 us
  transfers between devices with their start and end apart: 15, of which 12 were waited for; matrix products, arithmetic and copies ran while one was open for 1% of the time, Pallas kernels for 14%

profile of v5, /device:TPU:1, one launch (start us, length us, event | category | flops | bytes accessed | tf_op | source)
XLA Modules:
  0.0 307.0 jit_solution(11471199327623508702)
XLA Ops:
  11.3 13.7 %all-to-all-start = ((bf16[32,48,128]{2,1,0:T(8,128)(2,1)}), bf16[32,48,128]{2,1,0:T(8,128)(2,1)S(1)}, u32[]{:S(2)}, u32[]{:S(2)}) async-start(bf16[32,48,128]{2,1,0:T(8,128)(2,1)} %spread_blocks.1), calls=%async_computation | async-start | bytes 786432 | tf_op jit(solution)/shard_map/all_to_all | solution.py:281
  25.1 13.8 %all-to-all-done.in_ref = bf16[32,48,128]{2,1,0:T(8,128)(2,1)S(1)} async-done(((bf16[32,48,128]{2,1,0:T(8,128)(2,1)}), bf16[32,48,128]{2,1,0:T(8,128)(2,1)S(1)}, u32[]{:S(2)}, u32[]{:S(2)}) %all-to-all-start) | async-done | bytes 393248 | tf_op jit(solution)/shard_map/all_to_all | solution.py:281
  41.4 22.1 %all-gather = bf16[68,32,128]{2,1,0:T(8,128)(2,1)S(1)} all-gather(bf16[17,32,128]{2,1,0:T(8,128)(2,1)} %order_blocks.1), channel_id=2, replica_groups=mesh['zh'=4,'zl'=2,'x'=4,'y'=8,'core'=2] {'zh'}, dimensions={0}, use_global_device_ids=true | all-gather | bytes 696320 | tf_op jit(solution)/shard_map/all_gather | solution.py:287
  64.6 10.2 %all-gather.8.cloned.1.call-done = bf16[8,4,256,128]{3,2,1,0:T(8,128)(2,1)} async-done(((bf16[2,4,256,128]{3,2,1,0:T(8,128)(2,1)}), bf16[8,4,256,128]{3,2,1,0:T(8,128)(2,1)}) %all-gather.8.cloned.1.call-update) | async-done | bytes 2097168 | tf_op jit(solution)/shard_map/all_gather | solution.py:279
  75.6 10.3 %collective-permute-start = (bf16[2,4,256,128]{3,2,1,0:T(8,128)(2,1)S(1)}, bf16[2,4,256,128]{3,2,1,0:T(8,128)(2,1)S(1)}, u32[]{:S(2)}, u32[]{:S(2)}) collective-permute-start(bf16[2,4,256,128]{3,2,1,0:T(8,128)(2,1)S(1)} %get-tuple-element.35.refs_0_.refs_1_), channel_id=1, source_target_pairs={{0,384},{128,0},{256,128},{384,256},{1,385},{129,1},{257,129},{385... | collective-permute-start | bytes 1572872 | tf_op jit(solution)/shard_map/ppermute | solution.py:263
  87.9 20.1 %collective-permute-done.refs_2_.refs_3_ = bf16[2,4,256,128]{3,2,1,0:T(8,128)(2,1)S(1)} collective-permute-done((bf16[2,4,256,128]{3,2,1,0:T(8,128)(2,1)S(1)}, bf16[2,4,256,128]{3,2,1,0:T(8,128)(2,1)S(1)}, u32[]{:S(2)}, u32[]{:S(2)}) %collective-permute-start) | collective-permute-done | bytes 524320 | tf_op jit(solution)/shard_map/ppermute | solution.py:263
  108.0 6.2 %collective-permute-start.2 = (bf16[1,4,256,128]{3,2,1,0:T(8,128)(2,1)S(1)}, bf16[1,4,256,128]{3,2,1,0:T(8,128)(2,1)S(1)}, u32[]{:S(2)}, u32[]{:S(2)}) collective-permute-start(bf16[1,4,256,128]{3,2,1,0:T(8,128)(2,1)S(1)} %slice.63), channel_id=1, source_target_pairs={{0,384},{128,0},{256,128},{384,256},{1,385},{129,1},{257,129},{385... | collective-permute-start | bytes 786440 | tf_op jit(solution)/shard_map/ppermute | solution.py:263
  116.3 10.5 %all-gather.10.cloned.1.call-done = bf16[32,17,32,128]{3,2,1,0:T(8,128)(2,1)} async-done(((bf16[2,17,32,128]{3,2,1,0:T(8,128)(2,1)}), bf16[32,17,32,128]{3,2,1,0:T(8,128)(2,1)}) %all-gather.10.cloned.1.call-update) | async-done | bytes 4456464 | tf_op jit(solution)/shard_map/all_gather | solution.py:292
  128.3 7.5 %right_products.4 = bf16[8,2,2,256,128]{4,3,2,1,0:T(8,128)(2,1)} custom-call(s32[3]{0:T(128)S(1)} %pad_add_fusion.place_ref, s32[2,32]{1,0:T(2,128)S(1)} %bitcast.22, bf16[16,2,17,32,128]{4,3,2,1,0:T(8,128)(2,1)} %bitcast.26, bf16[8,4,256,128]{3,2,1,0:T(8,128)(2,1)S(1)} %copy-done, bf16[8,4,256,128]{3,2,1,0:T(8,128)(2,1)S(1)} %copy-done, ...), custom_call_target="tpu_custom_call" | custom-call | tf_op jit(solution)/shard_map/right_products/pallas_call | solution.py:165
  135.8 4.9 %all-to-all-start.1 = ((bf16[8,2,2,256,128]{4,3,2,1,0:T(8,128)(2,1)}), bf16[8,2,2,256,128]{4,3,2,1,0:T(8,128)(2,1)}, u32[]{:S(2)}, u32[]{:S(2)}) async-start(bf16[8,2,2,256,128]{4,3,2,1,0:T(8,128)(2,1)} %right_products.4), calls=%async_computation.1 | async-start | bytes 4194304 | tf_op jit(solution)/shard_map/all_to_all | solution.py:313
  140.7 7.5 %right_products.5 = bf16[8,2,2,256,128]{4,3,2,1,0:T(8,128)(2,1)} custom-call(s32[3]{0:T(128)S(1)} %pad_add_fusion.place_ref, s32[2,32]{1,0:T(2,128)S(1)} %bitcast.23, bf16[16,2,17,32,128]{4,3,2,1,0:T(8,128)(2,1)} %bitcast.27, bf16[2,4,256,128]{3,2,1,0:T(8,128)(2,1)S(1)} %get-tuple-element.35.refs_0_.refs_1_, ...), custom_call_target="tpu_custom_call" | custom-call | tf_op jit(solution)/shard_map/right_products/pallas_call | solution.py:165
  148.2 18.8 %all-to-all-done.1.near_ref = bf16[8,2,2,256,128]{4,3,2,1,0:T(8,128)(2,1)} async-done(((bf16[8,2,2,256,128]{4,3,2,1,0:T(8,128)(2,1)}), bf16[8,2,2,256,128]{4,3,2,1,0:T(8,128)(2,1)}, u32[]{:S(2)}, u32[]{:S(2)}) %all-to-all-start.1) | async-done | bytes 2097184 | tf_op jit(solution)/shard_map/all_to_all | solution.py:313
  167.0 4.4 %all-to-all-start.2 = ((bf16[8,2,2,256,128]{4,3,2,1,0:T(8,128)(2,1)}), bf16[8,2,2,256,128]{4,3,2,1,0:T(8,128)(2,1)}, u32[]{:S(2)}, u32[]{:S(2)}) async-start(bf16[8,2,2,256,128]{4,3,2,1,0:T(8,128)(2,1)} %right_products.5), calls=%async_computation.2 | async-start | bytes 4194304 | tf_op jit(solution)/shard_map/all_to_all | solution.py:323
  173.1 7.4 %right_products.7 = bf16[8,2,2,256,128]{4,3,2,1,0:T(8,128)(2,1)} custom-call(s32[3]{0:T(128)S(1)} %pad_add_fusion.place_ref, s32[2,32]{1,0:T(2,128)S(1)} %bitcast.20, bf16[16,2,17,32,128]{4,3,2,1,0:T(8,128)(2,1)} %bitcast.24, bf16[8,4,256,128]{3,2,1,0:T(8,128)(2,1)S(1)} %copy-done.1, bf16[8,4,256,128]{3,2,1,0:T(8,128)(2,1)S(1)} %copy-done.1, ...), custom_call_target="tpu_custom_call" | custom-call | tf_op jit(solution)/shard_map/right_products/pallas_call | solution.py:165
  180.5 17.1 %all-to-all-done.2.near_ref = bf16[8,2,2,256,128]{4,3,2,1,0:T(8,128)(2,1)} async-done(((bf16[8,2,2,256,128]{4,3,2,1,0:T(8,128)(2,1)}), bf16[8,2,2,256,128]{4,3,2,1,0:T(8,128)(2,1)}, u32[]{:S(2)}, u32[]{:S(2)}) %all-to-all-start.2) | async-done | bytes 2097184 | tf_op jit(solution)/shard_map/all_to_all | solution.py:323
  201.2 7.4 %right_products.6 = bf16[8,2,2,256,128]{4,3,2,1,0:T(8,128)(2,1)} custom-call(s32[3]{0:T(128)S(1)} %pad_add_fusion.place_ref, s32[2,32]{1,0:T(2,128)S(1)} %bitcast.21, bf16[16,2,17,32,128]{4,3,2,1,0:T(8,128)(2,1)} %bitcast.25, bf16[1,4,256,128]{3,2,1,0:T(8,128)(2,1)S(1)} %collective-permute-done.2.refs_0_, ...), custom_call_target="tpu_custom_call" | custom-call | tf_op jit(solution)/shard_map/right_products/pallas_call | solution.py:165
  208.7 18.7 %all-to-all-done.3.far_ref = bf16[8,2,2,256,128]{4,3,2,1,0:T(8,128)(2,1)S(1)} async-done(((bf16[8,2,2,256,128]{4,3,2,1,0:T(8,128)(2,1)}), bf16[8,2,2,256,128]{4,3,2,1,0:T(8,128)(2,1)S(1)}, u32[]{:S(2)}, u32[]{:S(2)}) %all-to-all-start.3) | async-done | bytes 2097184 | tf_op jit(solution)/shard_map/all_to_all | solution.py:323
  228.7 3.7 %all-to-all-start.4 = ((bf16[8,2,2,256,128]{4,3,2,1,0:T(8,128)(2,1)}), bf16[8,2,2,256,128]{4,3,2,1,0:T(8,128)(2,1)S(1)}, u32[]{:S(2)}, u32[]{:S(2)}) async-start(bf16[8,2,2,256,128]{4,3,2,1,0:T(8,128)(2,1)} %right_products.6), calls=%async_computation.5 | async-start | bytes 4194304 | tf_op jit(solution)/shard_map/all_to_all | solution.py:323
  234.0 4.8 %left_products.2 = bf16[16,16,16,128]{3,2,1,0:T(8,128)(2,1)} custom-call(s32[3]{0:T(128)S(1)} %pad_add_fusion.place_ref, s32[2,16]{1,0:T(2,128)S(1)} %slice.46.from_ref, bf16[8,2,2,256,128]{4,3,2,1,0:T(8,128)(2,1)} %all-to-all-done.1.near_ref, bf16[8,2,2,256,128]{4,3,2,1,0:T(8,128)(2,1)S(1)} %copy-done.3, bf16[2,4,256,256]{3,2,1,0:T(8,128)(2,1)S(1)} %copy-done.4), custom_call_target="tpu_custom_call" | custom-call | tf_op jit(solution)/shard_map/left_products/pallas_call | solution.py:243
  238.9 19.6 %all-to-all-done.4.far_ref = bf16[8,2,2,256,128]{4,3,2,1,0:T(8,128)(2,1)S(1)} async-done(((bf16[8,2,2,256,128]{4,3,2,1,0:T(8,128)(2,1)}), bf16[8,2,2,256,128]{4,3,2,1,0:T(8,128)(2,1)S(1)}, u32[]{:S(2)}, u32[]{:S(2)}) %all-to-all-start.4) | async-done | bytes 2097184 | tf_op jit(solution)/shard_map/all_to_all | solution.py:323
  258.5 4.1 %left_products.3 = (bf16[8,16,16,128]{3,2,1,0:T(8,128)(2,1)S(1)}, bf16[8,16,16,128]{3,2,1,0:T(8,128)(2,1)S(1)}) custom-call(s32[3]{0:T(128)S(1)} %pad_add_fusion.place_ref, s32[2,16]{1,0:T(2,128)S(1)} %slice.46.from_ref, bf16[8,2,2,256,128]{4,3,2,1,0:T(8,128)(2,1)} %all-to-all-done.2.near_ref, bf16[8,2,2,256,128]{4,3,2,1,0:T(8,128)(2,1)S(1)} %all-to-all-done.4.far_ref, ...), custom_call_target="tpu_custom_call" | custom-call | tf_op jit(solution)/shard_map/left_products/pallas_call | solution.py:243
  267.9 4.4 %all-to-all-start.5 = ((bf16[8,16,16,128]{3,2,1,0:T(8,128)(2,1)}), bf16[8,16,16,128]{3,2,1,0:T(8,128)(2,1)S(1)}, u32[]{:S(2)}, u32[]{:S(2)}) async-start(bf16[8,16,16,128]{3,2,1,0:T(8,128)(2,1)} %add_convert_fusion), calls=%async_computation.6 | async-start | bytes 1048576 | tf_op jit(solution)/shard_map/all_to_all | solution.py:330
  272.6 17.3 %all-to-all-done.5 = bf16[8,16,16,128]{3,2,1,0:T(8,128)(2,1)S(1)} async-done(((bf16[8,16,16,128]{3,2,1,0:T(8,128)(2,1)}), bf16[8,16,16,128]{3,2,1,0:T(8,128)(2,1)S(1)}, u32[]{:S(2)}, u32[]{:S(2)}) %all-to-all-start.5) | async-done | bytes 524320 | tf_op jit(solution)/shard_map/all_to_all | solution.py:330
  290.0 8.9 %reduce-scatter.2.cloned.1.call-done = bf16[1,16,16,128]{3,2,1,0:T(8,128)(2,1)} async-done(((bf16[16,16,16,128]{3,2,1,0:T(8,128)(2,1)}), bf16[1,16,16,128]{3,2,1,0:T(8,128)(2,1)}) %reduce-scatter.2.cloned.1.call-update) | async-done | bytes 65552 | tf_op jit(solution)/shard_map/reduce_scatter | solution.py:326
  (53 shorter events, 30.2 us)
Async XLA Ops:
  6.5 68.3 %all-gather.8.cloned.1.call-start = ((), (), s32[]{:S(2)}) async-start(), calls=%async_computation.8 | async-start | bytes 2621440 | tf_op jit(solution)/shard_map/all_gather | solution.py:279
  11.3 27.5 %all-to-all-start = ((bf16[32,48,128]{2,1,0:T(8,128)(2,1)}), bf16[32,48,128]{2,1,0:T(8,128)(2,1)S(1)}, u32[]{:S(2)}, u32[]{:S(2)}) async-start(bf16[32,48,128]{2,1,0:T(8,128)(2,1)} %spread_blocks.1), calls=%async_computation | async-start | bytes 786432 | tf_op jit(solution)/shard_map/all_to_all | solution.py:281
  25.0 101.7 %all-gather.10.cloned.1.call-start = ((), (), s32[]{:S(2)}) async-start(), calls=%async_computation.9 | async-start | bytes 4734976 | tf_op jit(solution)/shard_map/all_gather | solution.py:292
  38.8 0.8 copy-start.5
  74.9 98.2 %all-gather.12.cloned.1.call-start = ((), (), s32[]{:S(2)}) async-start(), calls=%async_computation.10 | async-start | bytes 4734976 | tf_op jit(solution)/shard_map/all_gather | solution.py:293
  75.6 32.4 %collective-permute-start = (bf16[2,4,256,128]{3,2,1,0:T(8,128)(2,1)S(1)}, bf16[2,4,256,128]{3,2,1,0:T(8,128)(2,1)S(1)}, u32[]{:S(2)}, u32[]{:S(2)}) collective-permute-start(bf16[2,4,256,128]{3,2,1,0:T(8,128)(2,1)S(1)} %get-tuple-element.35.refs_0_.refs_1_), channel_id=1, source_target_pairs={{0,384},{128,0},{256,128},{384,256},{1,385},{129,1},{257,129},{385... | collective-permute-start | bytes 1572872 | tf_op jit(solution)/shard_map/ppermute | solution.py:263
  85.9 28.4 %collective-permute-start.1 = (bf16[2,4,256,128]{3,2,1,0:T(8,128)(2,1)S(1)}, bf16[2,4,256,128]{3,2,1,0:T(8,128)(2,1)S(1)}, u32[]{:S(2)}, u32[]{:S(2)}) collective-permute-start(bf16[2,4,256,128]{3,2,1,0:T(8,128)(2,1)S(1)} %get-tuple-element.35.refs_0_.refs_1_), channel_id=1, source_target_pairs={{0,128},{128,256},{256,384},{384,0},{1,129},{129,257},{257,385},{3... | collective-permute-start | bytes 1572872 | tf_op jit(solution)/shard_map/ppermute | solution.py:263
  108.0 27.7 %collective-permute-start.2 = (bf16[1,4,256,128]{3,2,1,0:T(8,128)(2,1)S(1)}, bf16[1,4,256,128]{3,2,1,0:T(8,128)(2,1)S(1)}, u32[]{:S(2)}, u32[]{:S(2)}) collective-permute-start(bf16[1,4,256,128]{3,2,1,0:T(8,128)(2,1)S(1)} %slice.63), channel_id=1, source_target_pairs={{0,384},{128,0},{256,128},{384,256},{1,385},{129,1},{257,129},{385... | collective-permute-start | bytes 786440 | tf_op jit(solution)/shard_map/ppermute | solution.py:263
  114.3 21.5 %collective-permute-start.3 = (bf16[1,4,256,128]{3,2,1,0:T(8,128)(2,1)S(1)}, bf16[1,4,256,128]{3,2,1,0:T(8,128)(2,1)S(1)}, u32[]{:S(2)}, u32[]{:S(2)}) collective-permute-start(bf16[1,4,256,128]{3,2,1,0:T(8,128)(2,1)S(1)} %slice.64), channel_id=1, source_target_pairs={{0,128},{128,256},{256,384},{384,0},{1,129},{129,257},{257,385},{3... | collective-permute-start | bytes 786440 | tf_op jit(solution)/shard_map/ppermute | solution.py:263
  126.7 1.6 copy-start
  135.8 31.2 %all-to-all-start.1 = ((bf16[8,2,2,256,128]{4,3,2,1,0:T(8,128)(2,1)}), bf16[8,2,2,256,128]{4,3,2,1,0:T(8,128)(2,1)}, u32[]{:S(2)}, u32[]{:S(2)}) async-start(bf16[8,2,2,256,128]{4,3,2,1,0:T(8,128)(2,1)} %right_products.4), calls=%async_computation.1 | async-start | bytes 4194304 | tf_op jit(solution)/shard_map/all_to_all | solution.py:313
  148.2 24.9 %copy-start.1 = (bf16[8,4,256,128]{3,2,1,0:T(8,128)(2,1)S(1)}, bf16[8,4,256,128]{3,2,1,0:T(8,128)(2,1)}, u32[]{:S(2)}) copy-start(bf16[8,4,256,128]{3,2,1,0:T(8,128)(2,1)} %all-gather.8.cloned.1.call-done) | copy-start | bytes 6291460
  167.0 30.5 %all-to-all-start.2 = ((bf16[8,2,2,256,128]{4,3,2,1,0:T(8,128)(2,1)}), bf16[8,2,2,256,128]{4,3,2,1,0:T(8,128)(2,1)}, u32[]{:S(2)}, u32[]{:S(2)}) async-start(bf16[8,2,2,256,128]{4,3,2,1,0:T(8,128)(2,1)} %right_products.5), calls=%async_computation.2 | async-start | bytes 4194304 | tf_op jit(solution)/shard_map/all_to_all | solution.py:323
  197.5 29.8 %all-to-all-start.3 = ((bf16[8,2,2,256,128]{4,3,2,1,0:T(8,128)(2,1)}), bf16[8,2,2,256,128]{4,3,2,1,0:T(8,128)(2,1)S(1)}, u32[]{:S(2)}, u32[]{:S(2)}) async-start(bf16[8,2,2,256,128]{4,3,2,1,0:T(8,128)(2,1)} %right_products.7), calls=%async_computation.3 | async-start | bytes 4194304 | tf_op jit(solution)/shard_map/all_to_all | solution.py:323
  208.7 23.8 %copy-start.4 = (bf16[2,4,256,256]{3,2,1,0:T(8,128)(2,1)S(1)}, bf16[2,4,256,256]{3,2,1,0:T(8,128)(2,1)}, u32[]{:S(2)}) copy-start(bf16[2,4,256,256]{3,2,1,0:T(8,128)(2,1)} %env_ref.3) | copy-start | bytes 3145732
  227.4 1.3 copy-start.2
  228.7 29.9 %all-to-all-start.4 = ((bf16[8,2,2,256,128]{4,3,2,1,0:T(8,128)(2,1)}), bf16[8,2,2,256,128]{4,3,2,1,0:T(8,128)(2,1)S(1)}, u32[]{:S(2)}, u32[]{:S(2)}) async-start(bf16[8,2,2,256,128]{4,3,2,1,0:T(8,128)(2,1)} %right_products.6), calls=%async_computation.5 | async-start | bytes 4194304 | tf_op jit(solution)/shard_map/all_to_all | solution.py:323
  232.4 66.5 %reduce-scatter.2.cloned.1.call-start = ((), (), s32[]{:S(2)}) async-start(), calls=%async_computation.7 | async-start | bytes 1114112 | tf_op jit(solution)/shard_map/reduce_scatter | solution.py:326
  232.4 1.6 copy-start.3
  262.7 9.7 %copy-start.6 = (s32[4]{0:T(128)S(1)}, s32[4]{0:T(128)}, u32[]{:S(2)}) copy-start(s32[4]{0:T(128)} %rows_ref.1) | copy-start | bytes 52
  262.7 4.3 %collective-permute-start.4 = (bf16[8,16,16,128]{3,2,1,0:T(8,128)(2,1)S(1)}, bf16[8,16,16,128]{3,2,1,0:T(8,128)(2,1)S(1)}, u32[]{:S(2)}, u32[]{:S(2)}) collective-permute-start(bf16[8,16,16,128]{3,2,1,0:T(8,128)(2,1)S(1)} %get-tuple-element.34), channel_id=1, source_target_pairs={{0,1},{1,0},{2,3},{3,2},{4,5},{5,4},{6,7},{7,6},{8,9},{9,8},{10,11... | collective-permute-start | bytes 1572872 | tf_op jit(solution)/shard_map/ppermute | solution.py:263
  267.9 22.0 %all-to-all-start.5 = ((bf16[8,16,16,128]{3,2,1,0:T(8,128)(2,1)}), bf16[8,16,16,128]{3,2,1,0:T(8,128)(2,1)S(1)}, u32[]{:S(2)}, u32[]{:S(2)}) async-start(bf16[8,16,16,128]{3,2,1,0:T(8,128)(2,1)} %add_convert_fusion), calls=%async_computation.6 | async-start | bytes 1048576 | tf_op jit(solution)/shard_map/all_to_all | solution.py:330
Sparse Core Ops, SparseCore 0:
  9.5 65.3 all-gather.7
  77.0 49.7 all-gather.9
  128.8 44.1 all-gather.11
  239.0 59.8 reduce-scatter.1

commit v6 on v4

--- a/solution.py
+++ b/solution.py
@@ -185,10 +185,10 @@
     )(place, targets, in_hbm(slices), *[array for array, _ in flat])
 
 
-def left_partials(place_ref, from_ref, own_ref, far_ref, env_ref, placed_ref):
+def left_partials(place_ref, from_ref, near_ref, far_ref, env_ref, placed_ref):
     terms, count = from_ref.shape
-    group, _, _, extent, _ = own_ref.shape
-    layers = far_ref.shape[1] + 1
+    group, near, _, extent, width = near_ref.shape
+    layers = near + far_ref.shape[1]
     per_sector = count // pl.num_programs(0)
     sector = pl.program_id(0)
     left = jnp.concatenate([env_ref[term, 0] for term in range(terms)], axis=1)
@@ -197,29 +197,32 @@
             device = from_ref[term, sector * per_sector + place]
             peer = lax.rem(device, group)
             step = lax.rem(lax.div(device, group) + layers - place_ref[0], layers)
-            at = slice(term * extent, (term + 1) * extent)
-
-            @pl.when(step == 0)
-            def _(place=place, term=term, peer=peer, at=at):
-                placed_ref[place, at, :] = own_ref[peer, 0, term]
-
-            @pl.when(step > 0)
-            def _(place=place, term=term, peer=peer, at=at, step=step):
-                placed_ref[place, at, :] = far_ref[peer, jnp.maximum(step - 1, 0), term]
-
-        partial = jnp.dot(left, placed_ref[place], preferred_element_type=jnp.float32)
-        yield place, partial.astype(jnp.bfloat16)
-
-
-def left_kernel(place_ref, from_ref, own_ref, far_ref, env_ref, out_ref, placed_ref):
-    for place, partial in left_partials(place_ref, from_ref, own_ref, far_ref, env_ref, placed_ref):
+            rows = slice(term * extent, (term + 1) * extent)
+            columns = slice(place * width, (place + 1) * width)
+
+            @pl.when(step < near)
+            def _(term=term, peer=peer, step=step, rows=rows, columns=columns):
+                placed_ref[rows, columns] = near_ref[peer, jnp.minimum(step, near - 1), term]
+
+            @pl.when(step >= near)
+            def _(term=term, peer=peer, step=step, rows=rows, columns=columns):
+                placed_ref[rows, columns] = far_ref[peer, jnp.maximum(step - near, 0), term]
+
+    partial = jnp.dot(left, placed_ref[...], preferred_element_type=jnp.float32)
+    partial = partial.astype(jnp.bfloat16)
+    for place in range(per_sector):
+        yield place, partial[:, place * width : (place + 1) * width]
+
+
+def left_kernel(place_ref, from_ref, near_ref, far_ref, env_ref, out_ref, placed_ref):
+    for place, partial in left_partials(place_ref, from_ref, near_ref, far_ref, env_ref, placed_ref):
         out_ref[:, place] = partial.reshape(out_ref.shape[0], SHARE, partial.shape[1])
 
 
-def left_split_kernel(place_ref, from_ref, own_ref, far_ref, env_ref, keep_ref, send_ref, placed_ref):
+def left_split_kernel(place_ref, from_ref, near_ref, far_ref, env_ref, keep_ref, send_ref, placed_ref):
     chips = keep_ref.shape[0]
     core = place_ref[2]
-    for place, partial in left_partials(place_ref, from_ref, own_ref, far_ref, env_ref, placed_ref):
+    for place, partial in left_partials(place_ref, from_ref, near_ref, far_ref, env_ref, placed_ref):
         halves = [
             jnp.stack(
                 [partial[(2 * c + k) * SHARE : (2 * c + k + 1) * SHARE] for c in range(chips)]
@@ -230,7 +233,7 @@
         send_ref[:, place] = jnp.where(core == 0, halves[1], halves[0])
 
 
-def left_products(place, source, own, far, left_env, chunk, split):
+def left_products(place, source, near, far, left_env, chunk, split):
     _, sectors, extent, _ = left_env.shape
     terms, count = source.shape
     width = far.shape[-1]
@@ -244,16 +247,16 @@
         in_specs=[
             SMEM,
             SMEM,
-            pl.BlockSpec(own.shape[:-1] + (width,), lambda i: (0, 0, 0, 0, chunk)),
+            pl.BlockSpec(near.shape[:-1] + (width,), lambda i: (0, 0, 0, 0, chunk)),
             pl.BlockSpec(far.shape, lambda i: (0, 0, 0, 0, 0)),
             pl.BlockSpec((terms, 1, extent, extent), lambda i: (0, i, 0, 0)),
         ],
         out_specs=[out_spec, out_spec] if split else out_spec,
         out_shape=[shape, shape] if split else shape,
-        scratch_shapes=[pltpu.VMEM((per_sector, terms * extent, width), jnp.bfloat16)],
+        scratch_shapes=[pltpu.VMEM((terms * extent, per_sector * width), jnp.bfloat16)],
         compiler_params=pltpu.CompilerParams(vmem_limit_bytes=VMEM_LIMIT),
         name="left_products",
-    )(place, source, own, far, left_env)
+    )(place, source, near, far, left_env)
 
 
 def shift(array, axis, step):
@@ -285,27 +288,30 @@
     below = [shift(part, "zh", 1) for part in parts]
 
     slices = lax.all_gather(ordered[None], DEPTH)
+    around = lax.all_gather(ordered, "zh")
+    around, above[0], below[0] = lax.optimization_barrier((around, above[0], below[0]))
+    others = lax.dynamic_slice_in_dim(jnp.concatenate([around, around]), layer + 1, layers - 1)
+    far_targets = others[:, count, 0, : terms * count].astype(jnp.int32)
+    far_slices = lax.all_gather(others, DEPTH)
+
     targets = (term_links // count).reshape(1, terms * count)
     envs = [[(right_env, term) for term in range(terms)]]
     products = right_products(place, targets, slices, envs, group, 0, width)
-    products, above[0], below[0] = lax.optimization_barrier((products, above[0], below[0]))
+    across = [
+        (shift(up[:1], "zh", -1), shift(down[1:], "zh", 1)) for up, down in zip(above, below)
+    ]
+    products, above, below, across = lax.optimization_barrier((products, above, below, across))
     own = lax.all_to_all(products, GROUP, 0, 0, tiled=True)
 
-    around = lax.all_gather(ordered, "zh")
-    others = lax.dynamic_slice_in_dim(jnp.concatenate([around, around]), layer + 1, layers - 1)
-    targets = others[:, count, 0, : terms * count].astype(jnp.int32)
-    slices = lax.all_gather(others, DEPTH)
     pieces = []
-    for chunk in range(width // LANES):
+    for chunk in range(len(parts)):
         up, down = above[chunk], below[chunk]
-        across = [shift(up[:1], "zh", -1), shift(down[1:], "zh", 1)]
-        envs = [[(up, 0), (up, 1)], [(across[0], 0), (across[1], 0)], [(down, 0), (down, 1)]]
-        products = right_products(place, targets, slices, envs, group, 0, LANES)
-        if chunk + 1 < len(parts):
-            after = slices, products, above[chunk + 1], below[chunk + 1]
-            slices, products, above[chunk + 1], below[chunk + 1] = lax.optimization_barrier(after)
+        first, second = across[chunk]
+        envs = [[(up, 0), (up, 1)], [(first, 0), (second, 0)], [(down, 0), (down, 1)]]
+        products = right_products(place, far_targets, far_slices, envs, group, 0, LANES)
+        far_slices, products = lax.optimization_barrier((far_slices, products))
         far = lax.all_to_all(products, GROUP, 0, 0, tiled=True)
-        last = (chunk + 1) * LANES == width
+        last = chunk + 1 == len(parts)
         partial = left_products(place, source[1:], own, far, left_env, chunk, last)
         if last:
             keep, send = partial

time: 311 us -> 308 us (level)
  waiting for transfers between devices: 147 us -> 98.7 us
  starting transfers between devices: 50.5 us -> 78.4 us
  blocking collectives: 42.8 us -> 64.6 us
  Pallas kernels: 42.9 us -> 39.5 us
  local copies, waits for them, and re-layouts: 8.45 us -> 5.16 us
    ppermute x9, waiting for transfers between devices: 84.6 us -> 20.2 us  [shift(): lax.ppermute(array, axis, [(i, (i + step) % size) for i in range(size)])]
    ppermute x9, starting transfers between devices: 32.3 us -> 54.6 us  [shift(): lax.ppermute(array, axis, [(i, (i + step) % size) for i in range(size)])]
    all_gather x1, blocking collectives: 15.1 us -> 37.1 us  [local(): around = lax.all_gather(ordered, 'zh')]
    all_gather x1, waiting for transfers between devices: 15.6 us -> 0.01 us  [local(): slices = lax.all_gather(ordered[None], DEPTH)]
    all_to_all x2, waiting for transfers between devices: 30.3 us -> 45.1 us  [local(): far = lax.all_to_all(products, GROUP, 0, 0, tiled=True)]
    reduce_scatter x1, waiting for transfers between devices: 0.02 us -> 9.99 us  [local(): summed = lax.psum_scatter(partial, DEPTH, scatter_dimension=0, tiled=False)]
    all_gather x1, waiting for transfers between devices: 0.01 us -> 5.93 us  [local(): far_slices = lax.all_gather(others, DEPTH)]
    unnamed x23 -> x25, local copies, waits for them, and re-layouts: 4.6 us -> 0.05 us
  transfers between devices with their start and end apart: 16 -> 16, of which waited for: 7 -> 9; matrix products, arithmetic and copies ran while one was open for 2% -> 2% of each run, Pallas kernels for 12% -> 12%
where the time goes in v6:
time: 308 us; the launch traced here: 304 us
  waiting for transfers between devices  98.7 us (32%)
  starting transfers between devices  78.4 us (25%)
  blocking collectives  64.6 us (21%)
  Pallas kernels  39.5 us (13%)
  between operations  13.4 us (4%)
  local copies, waits for them, and re-layouts  5.16 us (2%)
  other arithmetic  4.57 us (1%)
    ppermute x9, starting transfers between devices, shift(): lax.ppermute(array, axis, [(i, (i + step) % size) for i in range(size)])  54.6 us
    all_to_all x2, waiting for transfers between devices, local(): far = lax.all_to_all(products, GROUP, 0, 0, tiled=True)  45.1 us
    all_gather x1, blocking collectives, local(): around = lax.all_gather(ordered, 'zh')  37.1 us
    all_to_all x1, blocking collectives, local(): arrived = lax.all_to_all(buffer, REMAP, 0, 0, tiled=True)  27.5 us
    pallas_call x3, Pallas kernels, right_products(): pl.pallas_call(right_kernel, grid_spec=pltpu.PrefetchScalarGridSpec(num_s...  25 us
    ppermute x9, waiting for transfers between devices, shift(): lax.ppermute(array, axis, [(i, (i + step) % size) for i in range(size)])  20.2 us
    all_to_all x1, waiting for transfers between devices, local(): gathered = lax.all_to_all(pair.astype(jnp.bfloat16), 'y', 0, 0, tiled=True)  17.4 us
    pallas_call x2, Pallas kernels, left_products(): pl.pallas_call(left_split_kernel if split else left_kernel, grid=(sectors...  10 us
  transfers between devices with their start and end apart: 16, of which 9 were waited for; matrix products, arithmetic and copies ran while one was open for 2% of the time, Pallas kernels for 12%

profile of v6, /device:TPU:1, one launch (start us, length us, event | category | flops | bytes accessed | tf_op | source)
XLA Modules:
  0.0 304.2 jit_solution(8734682664616003105)
XLA Ops:
  6.5 2.7 spread_blocks.1
  9.3 27.5 %all_to_all.25.in_ref = bf16[32,48,128]{2,1,0:T(8,128)(2,1)S(1)} all-to-all(bf16[32,48,128]{2,1,0:T(8,128)(2,1)} %spread_blocks.1), channel_id=1, replica_groups=mesh['zh'=4,'zl'=2,'x'=4,'y'=8,'core'=2] {'zh','zl','x'}, dimensions={0} | all-to-all | bytes 786432 | tf_op jit(solution)/shard_map/all_to_all | solution.py:280
  40.7 3.9 %collective-permute-start = (bf16[2,4,256,128]{3,2,1,0:T(8,128)(2,1)}, bf16[2,4,256,128]{3,2,1,0:T(8,128)(2,1)S(1)}, u32[]{:S(2)}, u32[]{:S(2)}) collective-permute-start(bf16[2,4,256,128]{3,2,1,0:T(8,128)(2,1)} %get-tuple-element.40), channel_id=1, source_target_pairs={{0,384},{128,0},{256,128},{384,256},{1,385},{129,1},{257,129},{385... | collective-permute-start | bytes 1572872 | tf_op jit(solution)/shard_map/ppermute | solution.py:264
  47.1 37.1 %all-gather.1 = bf16[68,32,128]{2,1,0:T(8,128)(2,1)S(1)} all-gather(bf16[17,32,128]{2,1,0:T(8,128)(2,1)S(1)} %copy-done.7), channel_id=3, replica_groups=mesh['zh'=4,'zl'=2,'x'=4,'y'=8,'core'=2] {'zh'}, dimensions={0}, use_global_device_ids=true | all-gather | bytes 696320 | tf_op jit(solution)/shard_map/all_gather | solution.py:291
  87.4 3.9 %collective-permute-start.3 = (bf16[2,4,256,128]{3,2,1,0:T(8,128)(2,1)}, bf16[2,4,256,128]{3,2,1,0:T(8,128)(2,1)S(1)}, u32[]{:S(2)}, u32[]{:S(2)}) collective-permute-start(bf16[2,4,256,128]{3,2,1,0:T(8,128)(2,1)} %get-tuple-element.39), channel_id=1, source_target_pairs={{0,128},{128,256},{256,384},{384,0},{1,129},{129,257},{257,385},{3... | collective-permute-start | bytes 1572872 | tf_op jit(solution)/shard_map/ppermute | solution.py:264
  91.3 15.3 %collective-permute-done.2.refs_0_.refs_1_ = bf16[2,4,256,128]{3,2,1,0:T(8,128)(2,1)S(1)} collective-permute-done((bf16[2,4,256,128]{3,2,1,0:T(8,128)(2,1)}, bf16[2,4,256,128]{3,2,1,0:T(8,128)(2,1)S(1)}, u32[]{:S(2)}, u32[]{:S(2)}) %collective-permute-start.2) | collective-permute-done | bytes 524320 | tf_op jit(solution)/shard_map/ppermute | solution.py:264
  110.5 4.7 %collective-permute-start.7 = (bf16[1,4,256,128]{3,2,1,0:T(8,128)(2,1)}, bf16[1,4,256,128]{3,2,1,0:T(8,128)(2,1)}, u32[]{:S(2)}, u32[]{:S(2)}) collective-permute-start(bf16[1,4,256,128]{3,2,1,0:T(8,128)(2,1)} %slice.43), channel_id=1, source_target_pairs={{0,128},{128,256},{256,384},{384,0},{1,129},{129,257},{257,385},{3... | collective-permute-start | bytes 786440 | tf_op jit(solution)/shard_map/ppermute | solution.py:264
  115.9 2.7 collective-permute-start.4
  119.3 4.7 %collective-permute-start.5 = (bf16[1,4,256,128]{3,2,1,0:T(8,128)(2,1)}, bf16[1,4,256,128]{3,2,1,0:T(8,128)(2,1)}, u32[]{:S(2)}, u32[]{:S(2)}) collective-permute-start(bf16[1,4,256,128]{3,2,1,0:T(8,128)(2,1)} %slice.37), channel_id=1, source_target_pairs={{0,128},{128,256},{256,384},{384,0},{1,129},{129,257},{257,385},{3... | collective-permute-start | bytes 786440 | tf_op jit(solution)/shard_map/ppermute | solution.py:264
  124.2 5.7 %right_products.3 = bf16[8,1,2,256,256]{4,3,2,1,0:T(8,128)(2,1)} custom-call(s32[3]{0:T(128)S(1)} %pad_add_fusion.place_ref, s32[1,32]{1,0:T(1,128)S(1)} %reshape.49.targets_ref, bf16[16,1,17,32,128]{4,3,2,1,0:T(8,128)(2,1)} %bitcast.24, bf16[2,4,256,256]{3,2,1,0:T(8,128)(2,1)S(1)} %copy-done, bf16[2,4,256,256]{3,2,1,0:T(8,128)(2,1)S(1)} %copy-done), custom_call_target="tpu_custom_call" | custom-call | tf_op jit(solution)/shard_map/right_products/pallas_call | solution.py:164
  133.3 7.5 %all-to-all-start.1 = ((bf16[8,1,2,256,256]{4,3,2,1,0:T(8,128)(2,1)}), bf16[8,1,2,256,256]{4,3,2,1,0:T(8,128)(2,1)S(1)}, u32[]{:S(2)}, u32[]{:S(2)}) async-start(bf16[8,1,2,256,256]{4,3,2,1,0:T(8,128)(2,1)} %right_products.3), calls=%async_computation.1 | async-start | bytes 4194304 | tf_op jit(solution)/shard_map/all_to_all | solution.py:304
  141.5 5.9 %all-gather.8.cloned.1.call-done = bf16[48,17,32,128]{3,2,1,0:T(8,128)(2,1)} async-done(((bf16[3,17,32,128]{3,2,1,0:T(8,128)(2,1)}), bf16[48,17,32,128]{3,2,1,0:T(8,128)(2,1)}) %all-gather.8.cloned.1.call-update) | async-done | bytes 6684688 | tf_op jit(solution)/shard_map/all_gather | solution.py:295
  147.4 9.7 %right_products.4 = bf16[8,3,2,256,128]{4,3,2,1,0:T(8,128)(2,1)} custom-call(s32[3]{0:T(128)S(1)} %pad_add_fusion.place_ref, s32[3,32]{1,0:T(4,128)S(1)} %bitcast.19, bf16[16,3,17,32,128]{4,3,2,1,0:T(8,128)(2,1)} %bitcast.21, bf16[2,4,256,128]{3,2,1,0:T(8,128)(2,1)S(1)} %collective-permute-done.refs_0_.refs_1_, ...), custom_call_target="tpu_custom_call" | custom-call | tf_op jit(solution)/shard_map/right_products/pallas_call | solution.py:164
  157.1 5.2 %all-to-all-start.2 = ((bf16[8,3,2,256,128]{4,3,2,1,0:T(8,128)(2,1)}), bf16[8,3,2,256,128]{4,3,2,1,0:T(8,128)(2,1)}, u32[]{:S(2)}, u32[]{:S(2)}) async-start(bf16[8,3,2,256,128]{4,3,2,1,0:T(8,128)(2,1)} %right_products.4), calls=%async_computation.2 | async-start | bytes 6291456 | tf_op jit(solution)/shard_map/all_to_all | solution.py:313
  162.3 9.6 %right_products.5 = bf16[8,3,2,256,128]{4,3,2,1,0:T(8,128)(2,1)} custom-call(s32[3]{0:T(128)S(1)} %pad_add_fusion.place_ref, s32[3,32]{1,0:T(4,128)S(1)} %bitcast.20, bf16[16,3,17,32,128]{4,3,2,1,0:T(8,128)(2,1)} %bitcast.22, bf16[2,4,256,128]{3,2,1,0:T(8,128)(2,1)S(1)} %copy-done.3, bf16[2,4,256,128]{3,2,1,0:T(8,128)(2,1)S(1)} %copy-done.3, ...), custom_call_target="tpu_custom_call" | custom-call | tf_op jit(solution)/shard_map/right_products/pallas_call | solution.py:164
  171.9 14.9 %all-to-all-done.2.far_ref = bf16[8,3,2,256,128]{4,3,2,1,0:T(8,128)(2,1)} async-done(((bf16[8,3,2,256,128]{4,3,2,1,0:T(8,128)(2,1)}), bf16[8,3,2,256,128]{4,3,2,1,0:T(8,128)(2,1)}, u32[]{:S(2)}, u32[]{:S(2)}) %all-to-all-start.2) | async-done | bytes 3145760 | tf_op jit(solution)/shard_map/all_to_all | solution.py:313
  186.8 4.5 %all-to-all-start.3 = ((bf16[8,3,2,256,128]{4,3,2,1,0:T(8,128)(2,1)}), bf16[8,3,2,256,128]{4,3,2,1,0:T(8,128)(2,1)}, u32[]{:S(2)}, u32[]{:S(2)}) async-start(bf16[8,3,2,256,128]{4,3,2,1,0:T(8,128)(2,1)} %right_products.5), calls=%async_computation.4 | async-start | bytes 6291456 | tf_op jit(solution)/shard_map/all_to_all | solution.py:313
  191.4 5.4 %left_products.2 = bf16[16,16,16,128]{3,2,1,0:T(8,128)(2,1)} custom-call(s32[3]{0:T(128)S(1)} %pad_add_fusion.place_ref, s32[2,16]{1,0:T(2,128)S(1)} %slice.32.from_ref, bf16[8,1,2,256,256]{4,3,2,1,0:T(8,128)(2,1)S(1)} %all-to-all-done.1.near_ref, bf16[8,3,2,256,128]{4,3,2,1,0:T(8,128)(2,1)} %all-to-all-done.2.far_ref, bf16[2,4,256,256]{3,2,1,0:T(8,128)(2,1)S(1)} %copy-done.1), custom_call_target="tpu_custom_call" | custom-call | tf_op jit(solution)/shard_map/left_products/pallas_call | solution.py:244
  196.8 30.2 %all-to-all-done.3.far_ref = bf16[8,3,2,256,128]{4,3,2,1,0:T(8,128)(2,1)} async-done(((bf16[8,3,2,256,128]{4,3,2,1,0:T(8,128)(2,1)}), bf16[8,3,2,256,128]{4,3,2,1,0:T(8,128)(2,1)}, u32[]{:S(2)}, u32[]{:S(2)}) %all-to-all-start.3) | async-done | bytes 3145760 | tf_op jit(solution)/shard_map/all_to_all | solution.py:313
  227.0 4.6 %left_products.3 = (bf16[8,16,16,128]{3,2,1,0:T(8,128)(2,1)S(1)}, bf16[8,16,16,128]{3,2,1,0:T(8,128)(2,1)S(1)}) custom-call(s32[3]{0:T(128)S(1)} %pad_add_fusion.place_ref, s32[2,16]{1,0:T(2,128)S(1)} %slice.32.from_ref, bf16[8,1,2,256,256]{4,3,2,1,0:T(8,128)(2,1)S(1)} %all-to-all-done.1.near_ref, bf16[8,3,2,256,128]{4,3,2,1,0:T(8,128)(2,1)} %all-to-all-done.3.far_ref, ...), custom_call_target="tpu_custom_call" | custom-call | tf_op jit(solution)/shard_map/left_products/pallas_call | solution.py:244
  231.6 27.8 %collective-permute-start.8 = (bf16[8,16,16,128]{3,2,1,0:T(8,128)(2,1)S(1)}, bf16[8,16,16,128]{3,2,1,0:T(8,128)(2,1)S(1)}, u32[]{:S(2)}, u32[]{:S(2)}) collective-permute-start(bf16[8,16,16,128]{3,2,1,0:T(8,128)(2,1)S(1)} %get-tuple-element.38), channel_id=1, source_target_pairs={{0,1},{1,0},{2,3},{3,2},{4,5},{5,4},{6,7},{7,6},{8,9},{9,8},{10,11... | collective-permute-start | bytes 1572872 | tf_op jit(solution)/shard_map/ppermute | solution.py:264
  261.9 6.5 %all-to-all-start.4 = ((bf16[8,16,16,128]{3,2,1,0:T(8,128)(2,1)}), bf16[8,16,16,128]{3,2,1,0:T(8,128)(2,1)S(1)}, u32[]{:S(2)}, u32[]{:S(2)}) async-start(bf16[8,16,16,128]{3,2,1,0:T(8,128)(2,1)} %add_convert_fusion), calls=%async_computation.5 | async-start | bytes 1048576 | tf_op jit(solution)/shard_map/all_to_all | solution.py:319
  268.7 17.4 %all-to-all-done.4 = bf16[8,16,16,128]{3,2,1,0:T(8,128)(2,1)S(1)} async-done(((bf16[8,16,16,128]{3,2,1,0:T(8,128)(2,1)}), bf16[8,16,16,128]{3,2,1,0:T(8,128)(2,1)S(1)}, u32[]{:S(2)}, u32[]{:S(2)}) %all-to-all-start.4) | async-done | bytes 524320 | tf_op jit(solution)/shard_map/all_to_all | solution.py:319
  286.1 10.0 %reduce-scatter.2.cloned.1.call-done = bf16[1,16,16,128]{3,2,1,0:T(8,128)(2,1)} async-done(((bf16[16,16,16,128]{3,2,1,0:T(8,128)(2,1)}), bf16[1,16,16,128]{3,2,1,0:T(8,128)(2,1)}) %reduce-scatter.2.cloned.1.call-update) | async-done | bytes 65552 | tf_op jit(solution)/shard_map/reduce_scatter | solution.py:322
  (67 shorter events, 23.6 us)
Async XLA Ops:
  6.5 32.9 %copy-start = (bf16[2,4,256,256]{3,2,1,0:T(8,128)(2,1)S(1)}, bf16[2,4,256,256]{3,2,1,0:T(8,128)(2,1)}, u32[]{:S(2)}) copy-start(bf16[2,4,256,256]{3,2,1,0:T(8,128)(2,1)} %refs_1_.1) | copy-start | bytes 3145732
  6.5 117.6 %all-gather.6.cloned.1.call-start = ((), (), s32[]{:S(2)}) async-start(), calls=%async_computation.7 | async-start | bytes 2367488 | tf_op jit(solution)/shard_map/all_gather | solution.py:290
  37.0 10.0 %copy-start.9 = (s32[3,16]{1,0:T(4,128)}, s32[3,16]{1,0:T(4,128)S(1)}, u32[]{:S(2)}) copy-start(s32[3,16]{1,0:T(4,128)S(1)} %select_reduce_fusion) | copy-start | bytes 580
  39.4 108.0 %all-gather.8.cloned.1.call-start = ((), (), s32[]{:S(2)}) async-start(), calls=%async_computation.8 | async-start | bytes 7102464 | tf_op jit(solution)/shard_map/all_gather | solution.py:295
  40.7 83.2 %copy-start.8 = (s32[2,16]{1,0:T(2,128)S(1)}, s32[2,16]{1,0:T(2,128)}, u32[]{:S(2)}) copy-start(s32[2,16]{1,0:T(2,128)} %links_ref.3) | copy-start | bytes 388
  40.7 43.4 %collective-permute-start = (bf16[2,4,256,128]{3,2,1,0:T(8,128)(2,1)}, bf16[2,4,256,128]{3,2,1,0:T(8,128)(2,1)S(1)}, u32[]{:S(2)}, u32[]{:S(2)}) collective-permute-start(bf16[2,4,256,128]{3,2,1,0:T(8,128)(2,1)} %get-tuple-element.40), channel_id=1, source_target_pairs={{0,384},{128,0},{256,128},{384,256},{1,385},{129,1},{257,129},{385... | collective-permute-start | bytes 1572872 | tf_op jit(solution)/shard_map/ppermute | solution.py:264
  44.6 39.5 %collective-permute-start.1 = (bf16[2,4,256,128]{3,2,1,0:T(8,128)(2,1)}, bf16[2,4,256,128]{3,2,1,0:T(8,128)(2,1)S(1)}, u32[]{:S(2)}, u32[]{:S(2)}) collective-permute-start(bf16[2,4,256,128]{3,2,1,0:T(8,128)(2,1)} %get-tuple-element.40), channel_id=1, source_target_pairs={{0,128},{128,256},{256,384},{384,0},{1,129},{129,257},{257,385},{3... | collective-permute-start | bytes 1572872 | tf_op jit(solution)/shard_map/ppermute | solution.py:264
  85.1 21.5 %collective-permute-start.2 = (bf16[2,4,256,128]{3,2,1,0:T(8,128)(2,1)}, bf16[2,4,256,128]{3,2,1,0:T(8,128)(2,1)S(1)}, u32[]{:S(2)}, u32[]{:S(2)}) collective-permute-start(bf16[2,4,256,128]{3,2,1,0:T(8,128)(2,1)} %get-tuple-element.39), channel_id=1, source_target_pairs={{0,384},{128,0},{256,128},{384,256},{1,385},{129,1},{257,129},{385... | collective-permute-start | bytes 1572872 | tf_op jit(solution)/shard_map/ppermute | solution.py:264
  87.4 22.3 %collective-permute-start.3 = (bf16[2,4,256,128]{3,2,1,0:T(8,128)(2,1)}, bf16[2,4,256,128]{3,2,1,0:T(8,128)(2,1)S(1)}, u32[]{:S(2)}, u32[]{:S(2)}) collective-permute-start(bf16[2,4,256,128]{3,2,1,0:T(8,128)(2,1)} %get-tuple-element.39), channel_id=1, source_target_pairs={{0,128},{128,256},{256,384},{384,0},{1,129},{129,257},{257,385},{3... | collective-permute-start | bytes 1572872 | tf_op jit(solution)/shard_map/ppermute | solution.py:264
  106.6 23.3 %copy-start.2 = (bf16[2,4,256,128]{3,2,1,0:T(8,128)(2,1)}, bf16[2,4,256,128]{3,2,1,0:T(8,128)(2,1)S(1)}, u32[]{:S(2)}) copy-start(bf16[2,4,256,128]{3,2,1,0:T(8,128)(2,1)S(1)} %collective-permute-done.2.refs_0_.refs_1_) | copy-start | bytes 1572868
  107.3 22.5 %collective-permute-start.6 = (bf16[1,4,256,128]{3,2,1,0:T(8,128)(2,1)}, bf16[1,4,256,128]{3,2,1,0:T(8,128)(2,1)S(1)}, u32[]{:S(2)}, u32[]{:S(2)}) collective-permute-start(bf16[1,4,256,128]{3,2,1,0:T(8,128)(2,1)} %slice.42), channel_id=1, source_target_pairs={{0,384},{128,0},{256,128},{384,256},{1,385},{129,1},{257,129},{385... | collective-permute-start | bytes 786440 | tf_op jit(solution)/shard_map/ppermute | solution.py:264
  109.7 20.2 %copy-start.4 = (bf16[2,4,256,128]{3,2,1,0:T(8,128)(2,1)}, bf16[2,4,256,128]{3,2,1,0:T(8,128)(2,1)S(1)}, u32[]{:S(2)}) copy-start(bf16[2,4,256,128]{3,2,1,0:T(8,128)(2,1)S(1)} %collective-permute-done.3.refs_4_.refs_5_) | copy-start | bytes 1572868
  110.5 19.4 %collective-permute-start.7 = (bf16[1,4,256,128]{3,2,1,0:T(8,128)(2,1)}, bf16[1,4,256,128]{3,2,1,0:T(8,128)(2,1)}, u32[]{:S(2)}, u32[]{:S(2)}) collective-permute-start(bf16[1,4,256,128]{3,2,1,0:T(8,128)(2,1)} %slice.43), channel_id=1, source_target_pairs={{0,128},{128,256},{256,384},{384,0},{1,129},{129,257},{257,385},{3... | collective-permute-start | bytes 786440 | tf_op jit(solution)/shard_map/ppermute | solution.py:264
  115.9 15.3 %collective-permute-start.4 = (bf16[1,4,256,128]{3,2,1,0:T(8,128)(2,1)}, bf16[1,4,256,128]{3,2,1,0:T(8,128)(2,1)}, u32[]{:S(2)}, u32[]{:S(2)}) collective-permute-start(bf16[1,4,256,128]{3,2,1,0:T(8,128)(2,1)} %slice.36), channel_id=1, source_target_pairs={{0,384},{128,0},{256,128},{384,256},{1,385},{129,1},{257,129},{385... | collective-permute-start | bytes 786440 | tf_op jit(solution)/shard_map/ppermute | solution.py:264
  119.3 14.0 %collective-permute-start.5 = (bf16[1,4,256,128]{3,2,1,0:T(8,128)(2,1)}, bf16[1,4,256,128]{3,2,1,0:T(8,128)(2,1)}, u32[]{:S(2)}, u32[]{:S(2)}) collective-permute-start(bf16[1,4,256,128]{3,2,1,0:T(8,128)(2,1)} %slice.37), channel_id=1, source_target_pairs={{0,128},{128,256},{256,384},{384,0},{1,129},{129,257},{257,385},{3... | collective-permute-start | bytes 786440 | tf_op jit(solution)/shard_map/ppermute | solution.py:264
  133.3 23.8 %all-to-all-start.1 = ((bf16[8,1,2,256,256]{4,3,2,1,0:T(8,128)(2,1)}), bf16[8,1,2,256,256]{4,3,2,1,0:T(8,128)(2,1)S(1)}, u32[]{:S(2)}, u32[]{:S(2)}) async-start(bf16[8,1,2,256,256]{4,3,2,1,0:T(8,128)(2,1)} %right_products.3), calls=%async_computation.1 | async-start | bytes 4194304 | tf_op jit(solution)/shard_map/all_to_all | solution.py:304
  157.1 29.8 %all-to-all-start.2 = ((bf16[8,3,2,256,128]{4,3,2,1,0:T(8,128)(2,1)}), bf16[8,3,2,256,128]{4,3,2,1,0:T(8,128)(2,1)}, u32[]{:S(2)}, u32[]{:S(2)}) async-start(bf16[8,3,2,256,128]{4,3,2,1,0:T(8,128)(2,1)} %right_products.4), calls=%async_computation.2 | async-start | bytes 6291456 | tf_op jit(solution)/shard_map/all_to_all | solution.py:313
  171.9 19.5 %copy-start.10 = (s32[3,16]{1,0:T(4,128)S(1)}, s32[3,16]{1,0:T(4,128)}, u32[]{:S(2)}) copy-start(s32[3,16]{1,0:T(4,128)} %copy-done.9) | copy-start | bytes 580
  171.9 19.5 %copy-start.1 = (bf16[2,4,256,256]{3,2,1,0:T(8,128)(2,1)S(1)}, bf16[2,4,256,256]{3,2,1,0:T(8,128)(2,1)}, u32[]{:S(2)}) copy-start(bf16[2,4,256,256]{3,2,1,0:T(8,128)(2,1)} %env_ref.3) | copy-start | bytes 3145732
  186.8 40.1 %all-to-all-start.3 = ((bf16[8,3,2,256,128]{4,3,2,1,0:T(8,128)(2,1)}), bf16[8,3,2,256,128]{4,3,2,1,0:T(8,128)(2,1)}, u32[]{:S(2)}, u32[]{:S(2)}) async-start(bf16[8,3,2,256,128]{4,3,2,1,0:T(8,128)(2,1)} %right_products.5), calls=%async_computation.4 | async-start | bytes 6291456 | tf_op jit(solution)/shard_map/all_to_all | solution.py:313
  191.3 104.8 %reduce-scatter.2.cloned.1.call-start = ((), (), s32[]{:S(2)}) async-start(), calls=%async_computation.6 | async-start | bytes 1114112 | tf_op jit(solution)/shard_map/reduce_scatter | solution.py:322
  231.6 36.8 %copy-start.11 = (s32[4]{0:T(128)S(1)}, s32[4]{0:T(128)}, u32[]{:S(2)}) copy-start(s32[4]{0:T(128)} %rows_ref.1) | copy-start | bytes 52
  231.6 29.3 %collective-permute-start.8 = (bf16[8,16,16,128]{3,2,1,0:T(8,128)(2,1)S(1)}, bf16[8,16,16,128]{3,2,1,0:T(8,128)(2,1)S(1)}, u32[]{:S(2)}, u32[]{:S(2)}) collective-permute-start(bf16[8,16,16,128]{3,2,1,0:T(8,128)(2,1)S(1)} %get-tuple-element.38), channel_id=1, source_target_pairs={{0,1},{1,0},{2,3},{3,2},{4,5},{5,4},{6,7},{7,6},{8,9},{9,8},{10,11... | collective-permute-start | bytes 1572872 | tf_op jit(solution)/shard_map/ppermute | solution.py:264
  261.9 24.1 %all-to-all-start.4 = ((bf16[8,16,16,128]{3,2,1,0:T(8,128)(2,1)}), bf16[8,16,16,128]{3,2,1,0:T(8,128)(2,1)S(1)}, u32[]{:S(2)}, u32[]{:S(2)}) async-start(bf16[8,16,16,128]{3,2,1,0:T(8,128)(2,1)} %add_convert_fusion), calls=%async_computation.5 | async-start | bytes 1048576 | tf_op jit(solution)/shard_map/all_to_all | solution.py:319
  (4 other events, 18.9 us)
Sparse Core Ops, SparseCore 0:
  39.5 39.9 all-gather.5
  85.2 62.1 all-gather.7
  196.9 99.1 reduce-scatter.1

commit v7 on v6

--- a/solution.py
+++ b/solution.py
@@ -185,6 +185,15 @@
     )(place, targets, in_hbm(slices), *[array for array, _ in flat])
 
 
+def far_products(place, targets, slices, above, below, across, group):
+    envs = [
+        [(above, 0), (above, 1)],
+        [(across[0], 0), (across[1], 0)],
+        [(below, 0), (below, 1)],
+    ]
+    return right_products(place, targets, slices, envs, group, 0, LANES)
+
+
 def left_partials(place_ref, from_ref, near_ref, far_ref, env_ref, placed_ref):
     terms, count = from_ref.shape
     group, near, _, extent, width = near_ref.shape
@@ -284,12 +293,11 @@
     ordered = order(source[0], term_links, sector_cols, arrived)
 
     parts = [right_env[..., at : at + LANES] for at in range(0, width, LANES)]
-    above = [shift(part, "zh", -1) for part in parts]
-    below = [shift(part, "zh", 1) for part in parts]
+    above, below = shift(parts[0], "zh", -1), shift(parts[0], "zh", 1)
+    across = shift(above[:1], "zh", -1), shift(below[1:], "zh", 1)
 
     slices = lax.all_gather(ordered[None], DEPTH)
     around = lax.all_gather(ordered, "zh")
-    around, above[0], below[0] = lax.optimization_barrier((around, above[0], below[0]))
     others = lax.dynamic_slice_in_dim(jnp.concatenate([around, around]), layer + 1, layers - 1)
     far_targets = others[:, count, 0, : terms * count].astype(jnp.int32)
     far_slices = lax.all_gather(others, DEPTH)
@@ -297,30 +305,32 @@
     targets = (term_links // count).reshape(1, terms * count)
     envs = [[(right_env, term) for term in range(terms)]]
     products = right_products(place, targets, slices, envs, group, 0, width)
-    across = [
-        (shift(up[:1], "zh", -1), shift(down[1:], "zh", 1)) for up, down in zip(above, below)
-    ]
     products, above, below, across = lax.optimization_barrier((products, above, below, across))
     own = lax.all_to_all(products, GROUP, 0, 0, tiled=True)
 
-    pieces = []
-    for chunk in range(len(parts)):
-        up, down = above[chunk], below[chunk]
-        first, second = across[chunk]
-        envs = [[(up, 0), (up, 1)], [(first, 0), (second, 0)], [(down, 0), (down, 1)]]
-        products = right_products(place, far_targets, far_slices, envs, group, 0, LANES)
-        far_slices, products = lax.optimization_barrier((far_slices, products))
-        far = lax.all_to_all(products, GROUP, 0, 0, tiled=True)
-        last = chunk + 1 == len(parts)
-        partial = left_products(place, source[1:], own, far, left_env, chunk, last)
-        if last:
-            keep, send = partial
-            pair = keep.astype(jnp.float32) + shift(send, "core", 1).astype(jnp.float32)
-            gathered = lax.all_to_all(pair.astype(jnp.bfloat16), "y", 0, 0, tiled=True)
-            pieces.append(jnp.sum(gathered.astype(jnp.float32), axis=0))
-        else:
-            summed = lax.psum_scatter(partial, DEPTH, scatter_dimension=0, tiled=False)
-            pieces.append(summed.astype(jnp.float32))
+    own, second = lax.optimization_barrier((own, parts[1]))
+    next_above, next_below = shift(second, "zh", -1), shift(second, "zh", 1)
+    next_across = shift(next_above[:1], "zh", -1), shift(next_below[1:], "zh", 1)
+
+    products = far_products(place, far_targets, far_slices, above, below, across, group)
+    after = products, far_slices, next_above, next_below, next_across
+    products, far_slices, next_above, next_below, next_across = lax.optimization_barrier(after)
+    far = lax.all_to_all(products, GROUP, 0, 0, tiled=True)
+    partial = left_products(place, source[1:], own, far, left_env, 0, False)
+    partial = partial.reshape((-1, 2) + partial.shape[1:])
+    summed = lax.psum_scatter(partial, "y", scatter_dimension=0, tiled=False)
+    received = shift(lax.dynamic_index_in_dim(summed, 1 - core_index, 0, False), "core", 1)
+    kept = lax.dynamic_index_in_dim(summed, core_index, 0, False)
+    pieces = [kept.astype(jnp.float32) + received.astype(jnp.float32)]
+
+    products = far_products(
+        place, far_targets, far_slices, next_above, next_below, next_across, group
+    )
+    far = lax.all_to_all(products, GROUP, 0, 0, tiled=True)
+    keep, send = left_products(place, source[1:], own, far, left_env, 1, True)
+    pair = keep.astype(jnp.float32) + shift(send, "core", 1).astype(jnp.float32)
+    shares = lax.all_to_all(pair.astype(jnp.bfloat16), "y", 0, 0, tiled=True)
+    pieces.append(jnp.sum(shares.astype(jnp.float32), axis=0))
     total = jnp.concatenate(pieces, axis=2)
     row = depth_index * SHARE + jnp.arange(SHARE, dtype=jnp.int32)
     keep_rows = row[None, :] < jnp.repeat(sector_rows, per_sector)[:, None]

time: 308 us -> 307 us (level)
  starting transfers between devices: 78.4 us -> 46.6 us
  waiting for transfers between devices: 98.7 us -> 123 us
  blocking collectives: 64.6 us -> 71.7 us
    all_to_all x0 -> x1, blocking collectives: none -> 28.9 us  [local(): own = lax.all_to_all(products, GROUP, 0, 0, tiled=True)]
    ppermute x9 -> x10, waiting for transfers between devices: 20.2 us -> 47.8 us  [shift(): lax.ppermute(array, axis, [(i, (i + step) % size) for i in range(size)])]
    ppermute x9 -> x10, starting transfers between devices: 54.6 us -> 30.9 us  [shift(): lax.ppermute(array, axis, [(i, (i + step) % size) for i in range(size)])]
    all_gather x1, blocking collectives: 37.1 us -> 15.1 us  [local(): around = lax.all_gather(ordered, 'zh')]
    all_to_all x2, waiting for transfers between devices: 45.1 us -> 60.4 us  [local(): far = lax.all_to_all(products, GROUP, 0, 0, tiled=True)]
    reduce_scatter x1, waiting for transfers between devices: 9.99 us -> 0.01 us  [local(): summed = lax.psum_scatter(partial, 'y', scatter_dimension=0, tiled=False)]
    all_to_all x2 -> x1, starting transfers between devices: 14 us -> 6.53 us  [local(): shares = lax.all_to_all(pair.astype(jnp.bfloat16), 'y', 0, 0, tiled=True)]
    all_gather x1, waiting for transfers between devices: 5.93 us -> 0.01 us  [local(): far_slices = lax.all_gather(others, DEPTH)]
  transfers between devices with their start and end apart: 16 -> 16, of which waited for: 9 -> 7; matrix products, arithmetic and copies ran while one was open for 2% -> 2% of each run, Pallas kernels for 12% -> 11%
where the time goes in v7:
time: 307 us; the launch traced here: 306 us
  waiting for transfers between devices  123 us (40%)
  blocking collectives  71.7 us (23%)
  starting transfers between devices  46.6 us (15%)
  Pallas kernels  39.4 us (13%)
  between operations  13.3 us (4%)
  local copies, waits for them, and re-layouts  7.58 us (2%)
  other arithmetic  4.6 us (1%)
    all_to_all x2, waiting for transfers between devices, local(): far = lax.all_to_all(products, GROUP, 0, 0, tiled=True)  60.4 us
    ppermute x10, waiting for transfers between devices, shift(): lax.ppermute(array, axis, [(i, (i + step) % size) for i in range(size)])  47.8 us
    ppermute x10, starting transfers between devices, shift(): lax.ppermute(array, axis, [(i, (i + step) % size) for i in range(size)])  30.9 us
    all_to_all x1, blocking collectives, local(): own = lax.all_to_all(products, GROUP, 0, 0, tiled=True)  28.9 us
    all_to_all x1, blocking collectives, local(): arrived = lax.all_to_all(buffer, REMAP, 0, 0, tiled=True)  27.6 us
    pallas_call x3, Pallas kernels, right_products(): pl.pallas_call(right_kernel, grid_spec=pltpu.PrefetchScalarGridSpec(num_s...  25 us
    all_gather x1, blocking collectives, local(): around = lax.all_gather(ordered, 'zh')  15.1 us
    all_to_all x1, waiting for transfers between devices, local(): shares = lax.all_to_all(pair.astype(jnp.bfloat16), 'y', 0, 0, tiled=True)  14.3 us
  transfers between devices with their start and end apart: 16, of which 7 were waited for; matrix products, arithmetic and copies ran while one was open for 2% of the time, Pallas kernels for 11%

profile of v7, /device:TPU:1, one launch (start us, length us, event | category | flops | bytes accessed | tf_op | source)
XLA Modules:
  0.0 305.8 jit_solution(10979798054497397157)
XLA Ops:
  6.5 2.7 spread_blocks.1
  9.2 27.6 %all_to_all.25.in_ref = bf16[32,48,128]{2,1,0:T(8,128)(2,1)S(1)} all-to-all(bf16[32,48,128]{2,1,0:T(8,128)(2,1)} %spread_blocks.1), channel_id=1, replica_groups=mesh['zh'=4,'zl'=2,'x'=4,'y'=8,'core'=2] {'zh','zl','x'}, dimensions={0} | all-to-all | bytes 786432 | tf_op jit(solution)/shard_map/all_to_all | solution.py:289
  39.5 15.1 %all-gather.1 = bf16[68,32,128]{2,1,0:T(8,128)(2,1)S(1)} all-gather(bf16[17,32,128]{2,1,0:T(8,128)(2,1)} %order_blocks.1), channel_id=3, replica_groups=mesh['zh'=4,'zl'=2,'x'=4,'y'=8,'core'=2] {'zh'}, dimensions={0}, use_global_device_ids=true | all-gather | bytes 696320 | tf_op jit(solution)/shard_map/all_gather | solution.py:300
  56.7 3.5 %collective-permute-start = (bf16[2,4,256,128]{3,2,1,0:T(8,128)(2,1)S(1)}, bf16[2,4,256,128]{3,2,1,0:T(8,128)(2,1)S(1)}, u32[]{:S(2)}, u32[]{:S(2)}) collective-permute-start(bf16[2,4,256,128]{3,2,1,0:T(8,128)(2,1)S(1)} %get-tuple-element.36), channel_id=1, source_target_pairs={{0,384},{128,0},{256,128},{384,256},{1,385},{129,1},{257,129},{385... | collective-permute-start | bytes 1572872 | tf_op jit(solution)/shard_map/ppermute | solution.py:273
  60.1 2.7 collective-permute-start.1
  62.9 23.6 %collective-permute-done.refs_0_.refs_1_ = bf16[2,4,256,128]{3,2,1,0:T(8,128)(2,1)S(1)} collective-permute-done((bf16[2,4,256,128]{3,2,1,0:T(8,128)(2,1)S(1)}, bf16[2,4,256,128]{3,2,1,0:T(8,128)(2,1)S(1)}, u32[]{:S(2)}, u32[]{:S(2)}) %collective-permute-start) | collective-permute-done | bytes 524320 | tf_op jit(solution)/shard_map/ppermute | solution.py:273
  86.5 4.5 %collective-permute-start.2 = (bf16[1,4,256,128]{3,2,1,0:T(8,128)(2,1)S(1)}, bf16[1,4,256,128]{3,2,1,0:T(8,128)(2,1)S(1)}, u32[]{:S(2)}, u32[]{:S(2)}) collective-permute-start(bf16[1,4,256,128]{3,2,1,0:T(8,128)(2,1)S(1)} %slice.42), channel_id=1, source_target_pairs={{0,384},{128,0},{256,128},{384,256},{1,385},{129,1},{257,129},{385... | collective-permute-start | bytes 786440 | tf_op jit(solution)/shard_map/ppermute | solution.py:273
  91.0 2.6 collective-permute-start.3
  93.8 5.7 %right_products.3 = bf16[8,1,2,256,256]{4,3,2,1,0:T(8,128)(2,1)} custom-call(s32[3]{0:T(128)S(1)} %pad_add_fusion.place_ref, s32[1,32]{1,0:T(1,128)S(1)} %reshape.56.targets_ref, bf16[16,1,17,32,128]{4,3,2,1,0:T(8,128)(2,1)} %bitcast.26, bf16[2,4,256,256]{3,2,1,0:T(8,128)(2,1)S(1)} %copy-done, bf16[2,4,256,256]{3,2,1,0:T(8,128)(2,1)S(1)} %copy-done), custom_call_target="tpu_custom_call" | custom-call | tf_op jit(solution)/shard_map/right_products/pallas_call | solution.py:164
  102.7 28.9 %all_to_all.26.near_ref = bf16[8,1,2,256,256]{4,3,2,1,0:T(8,128)(2,1)S(1)} all-to-all(bf16[8,1,2,256,256]{4,3,2,1,0:T(8,128)(2,1)} %right_products.3), channel_id=1, replica_groups=mesh['zh'=4,'zl'=2,'x'=4,'y'=8,'core'=2] {'zl','x'}, dimensions={0} | all-to-all | bytes 4194304 | tf_op jit(solution)/shard_map/all_to_all | solution.py:309
  133.8 4.0 %collective-permute-start.5 = (bf16[2,4,256,128]{3,2,1,0:T(8,128)(2,1)S(1)}, bf16[2,4,256,128]{3,2,1,0:T(8,128)(2,1)S(1)}, u32[]{:S(2)}, u32[]{:S(2)}) collective-permute-start(bf16[2,4,256,128]{3,2,1,0:T(8,128)(2,1)S(1)} %copy-done.9), channel_id=1, source_target_pairs={{0,128},{128,256},{256,384},{384,0},{1,129},{129,257},{257,385},{3... | collective-permute-start | bytes 1572872 | tf_op jit(solution)/shard_map/ppermute | solution.py:273
  137.8 20.2 %collective-permute-done.4.refs_0_.refs_1_ = bf16[2,4,256,128]{3,2,1,0:T(8,128)(2,1)S(1)} collective-permute-done((bf16[2,4,256,128]{3,2,1,0:T(8,128)(2,1)S(1)}, bf16[2,4,256,128]{3,2,1,0:T(8,128)(2,1)S(1)}, u32[]{:S(2)}, u32[]{:S(2)}) %collective-permute-start.4) | collective-permute-done | bytes 524320 | tf_op jit(solution)/shard_map/ppermute | solution.py:273
  159.5 4.0 %collective-permute-start.6 = (bf16[1,4,256,128]{3,2,1,0:T(8,128)(2,1)}, bf16[1,4,256,128]{3,2,1,0:T(8,128)(2,1)}, u32[]{:S(2)}, u32[]{:S(2)}) collective-permute-start(bf16[1,4,256,128]{3,2,1,0:T(8,128)(2,1)} %slice.45), channel_id=1, source_target_pairs={{0,384},{128,0},{256,128},{384,256},{1,385},{129,1},{257,129},{385... | collective-permute-start | bytes 786440 | tf_op jit(solution)/shard_map/ppermute | solution.py:273
  168.9 9.7 %right_products.4 = bf16[8,3,2,256,128]{4,3,2,1,0:T(8,128)(2,1)} custom-call(s32[3]{0:T(128)S(1)} %pad_add_fusion.place_ref, s32[3,32]{1,0:T(4,128)S(1)} %bitcast.21, bf16[16,3,17,32,128]{4,3,2,1,0:T(8,128)(2,1)} %bitcast.23, bf16[2,4,256,128]{3,2,1,0:T(8,128)(2,1)S(1)} %collective-permute-done.refs_0_.refs_1_, ...), custom_call_target="tpu_custom_call" | custom-call | tf_op jit(solution)/shard_map/right_products/pallas_call | solution.py:164
  178.6 4.6 %all-to-all-start.2 = ((bf16[8,3,2,256,128]{4,3,2,1,0:T(8,128)(2,1)}), bf16[8,3,2,256,128]{4,3,2,1,0:T(8,128)(2,1)}, u32[]{:S(2)}, u32[]{:S(2)}) async-start(bf16[8,3,2,256,128]{4,3,2,1,0:T(8,128)(2,1)} %right_products.4), calls=%async_computation.2 | async-start | bytes 6291456 | tf_op jit(solution)/shard_map/all_to_all | solution.py:318
  183.2 9.7 %right_products.5 = bf16[8,3,2,256,128]{4,3,2,1,0:T(8,128)(2,1)} custom-call(s32[3]{0:T(128)S(1)} %pad_add_fusion.place_ref, s32[3,32]{1,0:T(4,128)S(1)} %bitcast.22, bf16[16,3,17,32,128]{4,3,2,1,0:T(8,128)(2,1)} %bitcast.24, bf16[2,4,256,128]{3,2,1,0:T(8,128)(2,1)S(1)} %copy-done.3, bf16[2,4,256,128]{3,2,1,0:T(8,128)(2,1)S(1)} %copy-done.3, ...), custom_call_target="tpu_custom_call" | custom-call | tf_op jit(solution)/shard_map/right_products/pallas_call | solution.py:164
  192.9 28.4 %all-to-all-done.2.far_ref = bf16[8,3,2,256,128]{4,3,2,1,0:T(8,128)(2,1)} async-done(((bf16[8,3,2,256,128]{4,3,2,1,0:T(8,128)(2,1)}), bf16[8,3,2,256,128]{4,3,2,1,0:T(8,128)(2,1)}, u32[]{:S(2)}, u32[]{:S(2)}) %all-to-all-start.2) | async-done | bytes 3145760 | tf_op jit(solution)/shard_map/all_to_all | solution.py:318
  221.3 4.5 %all-to-all-start.3 = ((bf16[8,3,2,256,128]{4,3,2,1,0:T(8,128)(2,1)}), bf16[8,3,2,256,128]{4,3,2,1,0:T(8,128)(2,1)}, u32[]{:S(2)}, u32[]{:S(2)}) async-start(bf16[8,3,2,256,128]{4,3,2,1,0:T(8,128)(2,1)} %right_products.5), calls=%async_computation.4 | async-start | bytes 6291456 | tf_op jit(solution)/shard_map/all_to_all | solution.py:329
  225.9 5.3 %left_products.2 = bf16[16,16,16,128]{3,2,1,0:T(8,128)(2,1)} custom-call(s32[3]{0:T(128)S(1)} %pad_add_fusion.place_ref, s32[2,16]{1,0:T(2,128)S(1)} %slice.32.from_ref, bf16[8,1,2,256,256]{4,3,2,1,0:T(8,128)(2,1)S(1)} %all_to_all.26.near_ref, bf16[8,3,2,256,128]{4,3,2,1,0:T(8,128)(2,1)} %all-to-all-done.2.far_ref, bf16[2,4,256,256]{3,2,1,0:T(8,128)(2,1)S(1)} %copy-done.1), custom_call_target="tpu_custom_call" | custom-call | tf_op jit(solution)/shard_map/left_products/pallas_call | solution.py:253
  231.2 32.0 %all-to-all-done.3.far_ref = bf16[8,3,2,256,128]{4,3,2,1,0:T(8,128)(2,1)} async-done(((bf16[8,3,2,256,128]{4,3,2,1,0:T(8,128)(2,1)}), bf16[8,3,2,256,128]{4,3,2,1,0:T(8,128)(2,1)}, u32[]{:S(2)}, u32[]{:S(2)}) %all-to-all-start.3) | async-done | bytes 3145760 | tf_op jit(solution)/shard_map/all_to_all | solution.py:329
  263.2 4.6 %left_products.3 = (bf16[8,16,16,128]{3,2,1,0:T(8,128)(2,1)S(1)}, bf16[8,16,16,128]{3,2,1,0:T(8,128)(2,1)S(1)}) custom-call(s32[3]{0:T(128)S(1)} %pad_add_fusion.place_ref, s32[2,16]{1,0:T(2,128)S(1)} %slice.32.from_ref, bf16[8,1,2,256,256]{4,3,2,1,0:T(8,128)(2,1)S(1)} %all_to_all.26.near_ref, bf16[8,3,2,256,128]{4,3,2,1,0:T(8,128)(2,1)} %all-to-all-done.3.far_ref, ...), custom_call_target="tpu_custom_call" | custom-call | tf_op jit(solution)/shard_map/left_products/pallas_call | solution.py:253
  267.9 2.7 collective-permute-start.9
  273.1 6.5 %all-to-all-start.4 = ((bf16[8,16,16,128]{3,2,1,0:T(8,128)(2,1)}), bf16[8,16,16,128]{3,2,1,0:T(8,128)(2,1)S(1)}, u32[]{:S(2)}, u32[]{:S(2)}) async-start(bf16[8,16,16,128]{3,2,1,0:T(8,128)(2,1)} %add_convert_fusion), calls=%async_computation.5 | async-start | bytes 1048576 | tf_op jit(solution)/shard_map/all_to_all | solution.py:332
  283.2 14.3 %all-to-all-done.4 = bf16[8,16,16,128]{3,2,1,0:T(8,128)(2,1)S(1)} async-done(((bf16[8,16,16,128]{3,2,1,0:T(8,128)(2,1)}), bf16[8,16,16,128]{3,2,1,0:T(8,128)(2,1)S(1)}, u32[]{:S(2)}, u32[]{:S(2)}) %all-to-all-start.4) | async-done | bytes 524320 | tf_op jit(solution)/shard_map/all_to_all | solution.py:332
  (70 shorter events, 25.0 us)
Async XLA Ops:
  6.5 87.3 %all-gather.6.cloned.1.call-start = ((), (), s32[]{:S(2)}) async-start(), calls=%async_computation.7 | async-start | bytes 2367488 | tf_op jit(solution)/shard_map/all_gather | solution.py:299
  9.2 46.4 %copy-start = (bf16[2,4,256,256]{3,2,1,0:T(8,128)(2,1)S(1)}, bf16[2,4,256,256]{3,2,1,0:T(8,128)(2,1)}, u32[]{:S(2)}) copy-start(bf16[2,4,256,256]{3,2,1,0:T(8,128)(2,1)} %refs_1_.1) | copy-start | bytes 3145732
  39.5 128.5 %all-gather.8.cloned.1.call-start = ((), (), s32[]{:S(2)}) async-start(), calls=%async_computation.8 | async-start | bytes 7102464 | tf_op jit(solution)/shard_map/all_gather | solution.py:303
  54.6 39.0 %copy-start.10 = (s32[2,16]{1,0:T(2,128)S(1)}, s32[2,16]{1,0:T(2,128)}, u32[]{:S(2)}) copy-start(s32[2,16]{1,0:T(2,128)} %links_ref.3) | copy-start | bytes 388
  56.7 29.8 %collective-permute-start = (bf16[2,4,256,128]{3,2,1,0:T(8,128)(2,1)S(1)}, bf16[2,4,256,128]{3,2,1,0:T(8,128)(2,1)S(1)}, u32[]{:S(2)}, u32[]{:S(2)}) collective-permute-start(bf16[2,4,256,128]{3,2,1,0:T(8,128)(2,1)S(1)} %get-tuple-element.36), channel_id=1, source_target_pairs={{0,384},{128,0},{256,128},{384,256},{1,385},{129,1},{257,129},{385... | collective-permute-start | bytes 1572872 | tf_op jit(solution)/shard_map/ppermute | solution.py:273
  60.1 30.8 %collective-permute-start.1 = (bf16[2,4,256,128]{3,2,1,0:T(8,128)(2,1)S(1)}, bf16[2,4,256,128]{3,2,1,0:T(8,128)(2,1)S(1)}, u32[]{:S(2)}, u32[]{:S(2)}) collective-permute-start(bf16[2,4,256,128]{3,2,1,0:T(8,128)(2,1)S(1)} %get-tuple-element.36), channel_id=1, source_target_pairs={{0,128},{128,256},{256,384},{384,0},{1,129},{129,257},{257,385},{3... | collective-permute-start | bytes 1572872 | tf_op jit(solution)/shard_map/ppermute | solution.py:273
  86.5 13.0 %collective-permute-start.2 = (bf16[1,4,256,128]{3,2,1,0:T(8,128)(2,1)S(1)}, bf16[1,4,256,128]{3,2,1,0:T(8,128)(2,1)S(1)}, u32[]{:S(2)}, u32[]{:S(2)}) collective-permute-start(bf16[1,4,256,128]{3,2,1,0:T(8,128)(2,1)S(1)} %slice.42), channel_id=1, source_target_pairs={{0,384},{128,0},{256,128},{384,256},{1,385},{129,1},{257,129},{385... | collective-permute-start | bytes 786440 | tf_op jit(solution)/shard_map/ppermute | solution.py:273
  91.0 11.0 %collective-permute-start.3 = (bf16[1,4,256,128]{3,2,1,0:T(8,128)(2,1)S(1)}, bf16[1,4,256,128]{3,2,1,0:T(8,128)(2,1)S(1)}, u32[]{:S(2)}, u32[]{:S(2)}) collective-permute-start(bf16[1,4,256,128]{3,2,1,0:T(8,128)(2,1)S(1)} %slice.43), channel_id=1, source_target_pairs={{0,128},{128,256},{256,384},{384,0},{1,129},{129,257},{257,385},{3... | collective-permute-start | bytes 786440 | tf_op jit(solution)/shard_map/ppermute | solution.py:273
  99.5 32.1 %copy-start.9 = (bf16[2,4,256,128]{3,2,1,0:T(8,128)(2,1)S(1)}, bf16[2,4,256,128]{3,2,1,0:T(8,128)(2,1)}, u32[]{:S(2)}) copy-start(bf16[2,4,256,128]{3,2,1,0:T(8,128)(2,1)} %get-tuple-element.26) | copy-start | bytes 1572868
  131.6 26.4 %collective-permute-start.4 = (bf16[2,4,256,128]{3,2,1,0:T(8,128)(2,1)S(1)}, bf16[2,4,256,128]{3,2,1,0:T(8,128)(2,1)S(1)}, u32[]{:S(2)}, u32[]{:S(2)}) collective-permute-start(bf16[2,4,256,128]{3,2,1,0:T(8,128)(2,1)S(1)} %copy-done.9), channel_id=1, source_target_pairs={{0,384},{128,0},{256,128},{384,256},{1,385},{129,1},{257,129},{385... | collective-permute-start | bytes 1572872 | tf_op jit(solution)/shard_map/ppermute | solution.py:273
  133.8 29.7 %collective-permute-start.5 = (bf16[2,4,256,128]{3,2,1,0:T(8,128)(2,1)S(1)}, bf16[2,4,256,128]{3,2,1,0:T(8,128)(2,1)S(1)}, u32[]{:S(2)}, u32[]{:S(2)}) collective-permute-start(bf16[2,4,256,128]{3,2,1,0:T(8,128)(2,1)S(1)} %copy-done.9), channel_id=1, source_target_pairs={{0,128},{128,256},{256,384},{384,0},{1,129},{129,257},{257,385},{3... | collective-permute-start | bytes 1572872 | tf_op jit(solution)/shard_map/ppermute | solution.py:273
  159.5 19.1 %collective-permute-start.6 = (bf16[1,4,256,128]{3,2,1,0:T(8,128)(2,1)}, bf16[1,4,256,128]{3,2,1,0:T(8,128)(2,1)}, u32[]{:S(2)}, u32[]{:S(2)}) collective-permute-start(bf16[1,4,256,128]{3,2,1,0:T(8,128)(2,1)} %slice.45), channel_id=1, source_target_pairs={{0,384},{128,0},{256,128},{384,256},{1,385},{129,1},{257,129},{385... | collective-permute-start | bytes 786440 | tf_op jit(solution)/shard_map/ppermute | solution.py:273
  165.0 13.5 %collective-permute-start.7 = (bf16[1,4,256,128]{3,2,1,0:T(8,128)(2,1)}, bf16[1,4,256,128]{3,2,1,0:T(8,128)(2,1)}, u32[]{:S(2)}, u32[]{:S(2)}) collective-permute-start(bf16[1,4,256,128]{3,2,1,0:T(8,128)(2,1)} %slice.46), channel_id=1, source_target_pairs={{0,128},{128,256},{256,384},{384,0},{1,129},{129,257},{257,385},{3... | collective-permute-start | bytes 786440 | tf_op jit(solution)/shard_map/ppermute | solution.py:273
  167.9 1.0 copy-start.7
  178.6 4.6 %copy-start.3 = (bf16[2,4,256,128]{3,2,1,0:T(8,128)(2,1)S(1)}, bf16[2,4,256,128]{3,2,1,0:T(8,128)(2,1)}, u32[]{:S(2)}) copy-start(bf16[2,4,256,128]{3,2,1,0:T(8,128)(2,1)} %copy-done.2) | copy-start | bytes 1572868
  178.6 4.6 %copy-start.5 = (bf16[2,4,256,128]{3,2,1,0:T(8,128)(2,1)S(1)}, bf16[2,4,256,128]{3,2,1,0:T(8,128)(2,1)}, u32[]{:S(2)}) copy-start(bf16[2,4,256,128]{3,2,1,0:T(8,128)(2,1)} %copy-done.4) | copy-start | bytes 1572868
  178.6 42.7 %all-to-all-start.2 = ((bf16[8,3,2,256,128]{4,3,2,1,0:T(8,128)(2,1)}), bf16[8,3,2,256,128]{4,3,2,1,0:T(8,128)(2,1)}, u32[]{:S(2)}, u32[]{:S(2)}) async-start(bf16[8,3,2,256,128]{4,3,2,1,0:T(8,128)(2,1)} %right_products.4), calls=%async_computation.2 | async-start | bytes 6291456 | tf_op jit(solution)/shard_map/all_to_all | solution.py:318
  192.9 32.9 %copy-start.1 = (bf16[2,4,256,256]{3,2,1,0:T(8,128)(2,1)S(1)}, bf16[2,4,256,256]{3,2,1,0:T(8,128)(2,1)}, u32[]{:S(2)}) copy-start(bf16[2,4,256,256]{3,2,1,0:T(8,128)(2,1)} %env_ref.3) | copy-start | bytes 3145732
  221.3 41.9 %all-to-all-start.3 = ((bf16[8,3,2,256,128]{4,3,2,1,0:T(8,128)(2,1)}), bf16[8,3,2,256,128]{4,3,2,1,0:T(8,128)(2,1)}, u32[]{:S(2)}, u32[]{:S(2)}) async-start(bf16[8,3,2,256,128]{4,3,2,1,0:T(8,128)(2,1)} %right_products.5), calls=%async_computation.4 | async-start | bytes 6291456 | tf_op jit(solution)/shard_map/all_to_all | solution.py:329
  225.8 54.1 %reduce-scatter.2.cloned.1.call-start = ((), (), s32[]{:S(2)}) async-start(), calls=%async_computation.6 | async-start | bytes 1179648 | tf_op jit(solution)/shard_map/reduce_scatter | solution.py:321
  267.9 11.7 %copy-start.11 = (s32[4]{0:T(128)S(1)}, s32[4]{0:T(128)}, u32[]{:S(2)}) copy-start(s32[4]{0:T(128)} %rows_ref.1) | copy-start | bytes 52
  267.9 4.2 %collective-permute-start.9 = (bf16[8,16,16,128]{3,2,1,0:T(8,128)(2,1)S(1)}, bf16[8,16,16,128]{3,2,1,0:T(8,128)(2,1)S(1)}, u32[]{:S(2)}, u32[]{:S(2)}) collective-permute-start(bf16[8,16,16,128]{3,2,1,0:T(8,128)(2,1)S(1)} %get-tuple-element.34), channel_id=1, source_target_pairs={{0,1},{1,0},{2,3},{3,2},{4,5},{5,4},{6,7},{7,6},{8,9},{9,8},{10,11... | collective-permute-start | bytes 1572872 | tf_op jit(solution)/shard_map/ppermute | solution.py:273
  273.1 24.5 %all-to-all-start.4 = ((bf16[8,16,16,128]{3,2,1,0:T(8,128)(2,1)}), bf16[8,16,16,128]{3,2,1,0:T(8,128)(2,1)S(1)}, u32[]{:S(2)}, u32[]{:S(2)}) async-start(bf16[8,16,16,128]{3,2,1,0:T(8,128)(2,1)} %add_convert_fusion), calls=%async_computation.5 | async-start | bytes 1048576 | tf_op jit(solution)/shard_map/all_to_all | solution.py:332
  280.7 16.9 %collective-permute-start.8 = (bf16[16,16,128]{2,1,0:T(8,128)(2,1)S(1)}, bf16[16,16,128]{2,1,0:T(8,128)(2,1)S(1)}, u32[]{:S(2)}, u32[]{:S(2)}) collective-permute-start(bf16[16,16,128]{2,1,0:T(8,128)(2,1)S(1)} %dynamic-slice_bitcast_fusion), channel_id=1, source_target_pairs={{0,1},{1,0},{2,3},{3,2},{4,5},{5,4},{6,7},{7,6},{8,9},{9,8},{10,11... | collective-permute-start | bytes 196616 | tf_op jit(solution)/shard_map/ppermute | solution.py:273
  (4 other events, 3.1 us)
Sparse Core Ops, SparseCore 0:
  39.6 40.1 all-gather.5
  81.9 49.1 all-gather.7
  231.3 37.1 reduce-scatter.1

commit v8 on v7

--- a/solution.py
+++ b/solution.py
@@ -11,7 +11,6 @@
 LANES = 128
 VMEM_LIMIT = 40 * 1024 * 1024
 REMAP = ("zh", "zl", "x")
-GROUP = ("zl", "x")
 DEPTH = ("y", "core")
 SMEM = pl.BlockSpec(memory_space=pltpu.SMEM)
 
@@ -273,6 +272,22 @@
     return lax.ppermute(array, axis, [(i, (i + step) % size) for i in range(size)])
 
 
+def exchange(products):
+    axes = ("zh", "zl", "x", "core")
+    along_x, cores = lax.axis_size("x"), lax.axis_size("core")
+    along_z = lax.axis_size("zh") * lax.axis_size("zl")
+    groups = [
+        [
+            (((2 * pair + core + step) % along_z) * along_x + x) * cores + core
+            for step in range(2)
+            for x in range(along_x)
+        ]
+        for core in range(cores)
+        for pair in range(along_z // 2)
+    ]
+    return lax.all_to_all(products, axes, 0, 0, axis_index_groups=groups, tiled=True)
+
+
 def local(wavefunction, right_home, term_links, sector_rows, sector_cols, left_env, right_env):
     count, _, width = wavefunction.shape
     per_sector = count // sector_rows.shape[0]
@@ -283,13 +298,16 @@
     layer = lax.axis_index("zh")
     core_index = lax.axis_index("core")
     depth_index = lax.axis_index("y") * 2 + core_index
-    place = jnp.stack([layer, lax.axis_index("y"), core_index])
+    scheme_index = lax.rem(lax.axis_index(REMAP) + slots - core_index * (group // 2), slots)
+    place = jnp.stack([scheme_index // group, lax.axis_index("y"), core_index])
 
     buffer = spread(depth_index.reshape(1), right_home, term_links, sector_rows, wavefunction, slots)
     arrived = lax.all_to_all(buffer, REMAP, 0, 0, tiled=True)
     labels = arrived[:, 2 * SHARE, : 1 + terms].astype(jnp.int32)
     match = labels.T[:, None, :] == jnp.arange(count, dtype=jnp.int32)[None, :, None]
     source = jnp.sum(jnp.where(match, jnp.arange(slots, dtype=jnp.int32), 0), axis=2)
+    moved_by = slots - core_index * (group // 2)
+    peers = lax.rem(source[1:] + moved_by, slots)
     ordered = order(source[0], term_links, sector_cols, arrived)
 
     parts = [right_env[..., at : at + LANES] for at in range(0, width, LANES)]
@@ -300,23 +318,24 @@
     around = lax.all_gather(ordered, "zh")
     others = lax.dynamic_slice_in_dim(jnp.concatenate([around, around]), layer + 1, layers - 1)
     far_targets = others[:, count, 0, : terms * count].astype(jnp.int32)
+    far_targets = lax.rem(far_targets + moved_by, slots)
     far_slices = lax.all_gather(others, DEPTH)
 
-    targets = (term_links // count).reshape(1, terms * count)
+    targets = lax.rem((term_links // count).reshape(1, terms * count) + moved_by, slots)
     envs = [[(right_env, term) for term in range(terms)]]
     products = right_products(place, targets, slices, envs, group, 0, width)
-    products, above, below, across = lax.optimization_barrier((products, above, below, across))
-    own = lax.all_to_all(products, GROUP, 0, 0, tiled=True)
-
-    own, second = lax.optimization_barrier((own, parts[1]))
+    products, above, below = lax.optimization_barrier((products, above, below))
+    own = exchange(products)
+
+    across, second = lax.optimization_barrier((across, parts[1]))
     next_above, next_below = shift(second, "zh", -1), shift(second, "zh", 1)
     next_across = shift(next_above[:1], "zh", -1), shift(next_below[1:], "zh", 1)
 
     products = far_products(place, far_targets, far_slices, above, below, across, group)
-    after = products, far_slices, next_above, next_below, next_across
-    products, far_slices, next_above, next_below, next_across = lax.optimization_barrier(after)
-    far = lax.all_to_all(products, GROUP, 0, 0, tiled=True)
-    partial = left_products(place, source[1:], own, far, left_env, 0, False)
+    after = products, far_slices, next_above, next_below
+    products, far_slices, next_above, next_below = lax.optimization_barrier(after)
+    far = exchange(products)
+    partial = left_products(place, peers, own, far, left_env, 0, False)
     partial = partial.reshape((-1, 2) + partial.shape[1:])
     summed = lax.psum_scatter(partial, "y", scatter_dimension=0, tiled=False)
     received = shift(lax.dynamic_index_in_dim(summed, 1 - core_index, 0, False), "core", 1)
@@ -326,8 +345,8 @@
     products = far_products(
         place, far_targets, far_slices, next_above, next_below, next_across, group
     )
-    far = lax.all_to_all(products, GROUP, 0, 0, tiled=True)
-    keep, send = left_products(place, source[1:], own, far, left_env, 1, True)
+    far = exchange(products)
+    keep, send = left_products(place, peers, own, far, left_env, 1, True)
     pair = keep.astype(jnp.float32) + shift(send, "core", 1).astype(jnp.float32)
     shares = lax.all_to_all(pair.astype(jnp.bfloat16), "y", 0, 0, tiled=True)
     pieces.append(jnp.sum(shares.astype(jnp.float32), axis=0))

time: 307 us -> 287 us (0.935)
  blocking collectives: 71.7 us -> 42.8 us
  starting transfers between devices: 46.6 us -> 54.1 us
    all_to_all x1 -> x0, blocking collectives: 28.9 us -> none  [local(): own = lax.all_to_all(products, GROUP, 0, 0, tiled=True)]
    all_to_all x2 -> x3, waiting for transfers between devices: 60.4 us -> 31.7 us  [exchange(): lax.all_to_all(products, axes, 0, 0, axis_index_groups=groups, tiled=True)]
    all_gather x1, waiting for transfers between devices: 0.01 us -> 16.7 us  [local(): slices = lax.all_gather(ordered[None], DEPTH)]
    ppermute x10, waiting for transfers between devices: 47.8 us -> 57.8 us  [shift(): lax.ppermute(array, axis, [(i, (i + step) % size) for i in range(size)])]
    all_to_all x2 -> x3, starting transfers between devices: 9.07 us -> 16.5 us  [exchange(): lax.all_to_all(products, axes, 0, 0, axis_index_groups=groups, tiled=True)]
    all_gather x1, waiting for transfers between devices: 0.01 us -> 4.51 us  [local(): far_slices = lax.all_gather(others, DEPTH)]
  transfers between devices with their start and end apart: 16 -> 17, of which waited for: 7 -> 10; matrix products, arithmetic and copies ran while one was open for 2% -> 2% of each run, Pallas kernels for 11% -> 12%
where the time goes in v8:
time: 287 us; the launch traced here: 286 us
  waiting for transfers between devices  125 us (44%)
  starting transfers between devices  54.1 us (19%)
  blocking collectives  42.8 us (15%)
  Pallas kernels  39.6 us (14%)
  between operations  13.3 us (5%)
  local copies, waits for them, and re-layouts  6.42 us (2%)
  other arithmetic  4.61 us (2%)
    ppermute x10, waiting for transfers between devices, shift(): lax.ppermute(array, axis, [(i, (i + step) % size) for i in range(size)])  57.8 us
    all_to_all x3, waiting for transfers between devices, exchange(): lax.all_to_all(products, axes, 0, 0, axis_index_groups=groups, tiled=True)  31.7 us
    ppermute x10, starting transfers between devices, shift(): lax.ppermute(array, axis, [(i, (i + step) % size) for i in range(size)])  30.2 us
    all_to_all x1, blocking collectives, local(): arrived = lax.all_to_all(buffer, REMAP, 0, 0, tiled=True)  27.6 us
    pallas_call x3, Pallas kernels, right_products(): pl.pallas_call(right_kernel, grid_spec=pltpu.PrefetchScalarGridSpec(num_s...  25.2 us
    all_gather x1, waiting for transfers between devices, local(): slices = lax.all_gather(ordered[None], DEPTH)  16.7 us
    all_to_all x3, starting transfers between devices, exchange(): lax.all_to_all(products, axes, 0, 0, axis_index_groups=groups, tiled=True)  16.5 us
    all_gather x1, blocking collectives, local(): around = lax.all_gather(ordered, 'zh')  15.1 us
  transfers between devices with their start and end apart: 17, of which 10 were waited for; matrix products, arithmetic and copies ran while one was open for 2% of the time, Pallas kernels for 12%

profile of v8, /device:TPU:1, one launch (start us, length us, event | category | flops | bytes accessed | tf_op | source)
XLA Modules:
  0.0 285.8 jit_solution(5597022664966356994)
XLA Ops:
  9.2 27.6 %all_to_all.25.in_ref = bf16[32,48,128]{2,1,0:T(8,128)(2,1)S(1)} all-to-all(bf16[32,48,128]{2,1,0:T(8,128)(2,1)} %spread_blocks.1), channel_id=1, replica_groups=mesh['zh'=4,'zl'=2,'x'=4,'y'=8,'core'=2] {'zh','zl','x'}, dimensions={0} | all-to-all | bytes 786432 | tf_op jit(solution)/shard_map/all_to_all | solution.py:305
  39.5 15.1 %all-gather.1 = bf16[68,32,128]{2,1,0:T(8,128)(2,1)S(1)} all-gather(bf16[17,32,128]{2,1,0:T(8,128)(2,1)} %order_blocks.1), channel_id=3, replica_groups=mesh['zh'=4,'zl'=2,'x'=4,'y'=8,'core'=2] {'zh'}, dimensions={0}, use_global_device_ids=true | all-gather | bytes 696320 | tf_op jit(solution)/shard_map/all_gather | solution.py:318
  56.6 3.5 %collective-permute-start = (bf16[2,4,256,128]{3,2,1,0:T(8,128)(2,1)S(1)}, bf16[2,4,256,128]{3,2,1,0:T(8,128)(2,1)S(1)}, u32[]{:S(2)}, u32[]{:S(2)}) collective-permute-start(bf16[2,4,256,128]{3,2,1,0:T(8,128)(2,1)S(1)} %get-tuple-element.30), channel_id=1, source_target_pairs={{0,384},{128,0},{256,128},{384,256},{1,385},{129,1},{257,129},{385... | collective-permute-start | bytes 1572872 | tf_op jit(solution)/shard_map/ppermute | solution.py:272
  63.0 16.7 %all-gather.6.cloned.1.call-done = bf16[272,32,128]{2,1,0:T(8,128)(2,1)} async-done(((bf16[17,32,128]{2,1,0:T(8,128)(2,1)}), bf16[272,32,128]{2,1,0:T(8,128)(2,1)}) %all-gather.6.cloned.1.call-update) | async-done | bytes 2228240 | tf_op jit(solution)/shard_map/all_gather | solution.py:317
  79.7 5.7 %right_products.3 = bf16[8,1,2,256,256]{4,3,2,1,0:T(8,128)(2,1)} custom-call(s32[3]{0:T(128)S(1)} %pad_add_fusion.place_ref, s32[1,32]{1,0:T(1,128)S(1)} %compare_select_fusion.targets_ref, bf16[16,1,17,32,128]{4,3,2,1,0:T(8,128)(2,1)} %bitcast.23, bf16[2,4,256,256]{3,2,1,0:T(8,128)(2,1)S(1)} %copy-done, bf16[2,4,256,256]{3,2,1,0:T(8,128)(2,1)S(1)} %copy-done), custom_call_target="tpu_custom_call" | custom-call | tf_op jit(solution)/shard_map/right_products/pallas_call | solution.py:163
  85.9 7.0 %all-to-all-start.1 = ((bf16[8,1,2,256,256]{4,3,2,1,0:T(8,128)(2,1)}), bf16[8,1,2,256,256]{4,3,2,1,0:T(8,128)(2,1)S(1)}, u32[]{:S(2)}, u32[]{:S(2)}) async-start(bf16[8,1,2,256,256]{4,3,2,1,0:T(8,128)(2,1)} %right_products.3), calls=%async_computation.1 | async-start | bytes 4194304 | tf_op jit(solution)/shard_map/all_to_all | solution.py:288
  93.0 3.7 %collective-permute-start.2 = (bf16[1,4,256,128]{3,2,1,0:T(8,128)(2,1)S(1)}, bf16[1,4,256,128]{3,2,1,0:T(8,128)(2,1)S(1)}, u32[]{:S(2)}, u32[]{:S(2)}) collective-permute-start(bf16[1,4,256,128]{3,2,1,0:T(8,128)(2,1)S(1)} %slice.42), channel_id=1, source_target_pairs={{0,384},{128,0},{256,128},{384,256},{1,385},{129,1},{257,129},{385... | collective-permute-start | bytes 786440 | tf_op jit(solution)/shard_map/ppermute | solution.py:272
  99.2 19.5 %collective-permute-done.2.refs_2_ = bf16[1,4,256,128]{3,2,1,0:T(8,128)(2,1)S(1)} collective-permute-done((bf16[1,4,256,128]{3,2,1,0:T(8,128)(2,1)S(1)}, bf16[1,4,256,128]{3,2,1,0:T(8,128)(2,1)S(1)}, u32[]{:S(2)}, u32[]{:S(2)}) %collective-permute-start.2) | collective-permute-done | bytes 262176 | tf_op jit(solution)/shard_map/ppermute | solution.py:272
  119.4 3.7 %collective-permute-start.4 = (bf16[2,4,256,128]{3,2,1,0:T(8,128)(2,1)}, bf16[2,4,256,128]{3,2,1,0:T(8,128)(2,1)}, u32[]{:S(2)}, u32[]{:S(2)}) collective-permute-start(bf16[2,4,256,128]{3,2,1,0:T(8,128)(2,1)} %get-tuple-element.22), channel_id=1, source_target_pairs={{0,384},{128,0},{256,128},{384,256},{1,385},{129,1},{257,129},{385... | collective-permute-start | bytes 1572872 | tf_op jit(solution)/shard_map/ppermute | solution.py:272
  126.4 4.5 %all-gather.8.cloned.1.call-done = bf16[48,17,32,128]{3,2,1,0:T(8,128)(2,1)} async-done(((bf16[3,17,32,128]{3,2,1,0:T(8,128)(2,1)}), bf16[48,17,32,128]{3,2,1,0:T(8,128)(2,1)}) %all-gather.8.cloned.1.call-update) | async-done | bytes 6684688 | tf_op jit(solution)/shard_map/all_gather | solution.py:322
  131.9 9.6 %right_products.4 = bf16[8,3,2,256,128]{4,3,2,1,0:T(8,128)(2,1)} custom-call(s32[3]{0:T(128)S(1)} %pad_add_fusion.place_ref, s32[3,32]{1,0:T(4,128)S(1)} %negate_select_fusion.targets_ref, bf16[16,3,17,32,128]{4,3,2,1,0:T(8,128)(2,1)} %bitcast.20, bf16[2,4,256,128]{3,2,1,0:T(8,128)(2,1)S(1)} %collective-permute-done.refs_0_.refs_1_, ...), custom_call_target="tpu_custom_call" | custom-call | tf_op jit(solution)/shard_map/right_products/pallas_call | solution.py:163
  141.5 3.7 %collective-permute-done.4.refs_0_.refs_1_ = bf16[2,4,256,128]{3,2,1,0:T(8,128)(2,1)} collective-permute-done((bf16[2,4,256,128]{3,2,1,0:T(8,128)(2,1)}, bf16[2,4,256,128]{3,2,1,0:T(8,128)(2,1)}, u32[]{:S(2)}, u32[]{:S(2)}) %collective-permute-start.4) | collective-permute-done | bytes 524320 | tf_op jit(solution)/shard_map/ppermute | solution.py:272
  145.2 6.7 %collective-permute-done.5.refs_4_.refs_5_ = bf16[2,4,256,128]{3,2,1,0:T(8,128)(2,1)} collective-permute-done((bf16[2,4,256,128]{3,2,1,0:T(8,128)(2,1)}, bf16[2,4,256,128]{3,2,1,0:T(8,128)(2,1)}, u32[]{:S(2)}, u32[]{:S(2)}) %collective-permute-start.5) | collective-permute-done | bytes 524320 | tf_op jit(solution)/shard_map/ppermute | solution.py:272
  151.9 4.6 %all-to-all-start.2 = ((bf16[8,3,2,256,128]{4,3,2,1,0:T(8,128)(2,1)}), bf16[8,3,2,256,128]{4,3,2,1,0:T(8,128)(2,1)}, u32[]{:S(2)}, u32[]{:S(2)}) async-start(bf16[8,3,2,256,128]{4,3,2,1,0:T(8,128)(2,1)} %right_products.4), calls=%async_computation.2 | async-start | bytes 6291456 | tf_op jit(solution)/shard_map/all_to_all | solution.py:288
  157.5 4.0 %collective-permute-start.7 = (bf16[1,4,256,128]{3,2,1,0:T(8,128)(2,1)S(1)}, bf16[1,4,256,128]{3,2,1,0:T(8,128)(2,1)S(1)}, u32[]{:S(2)}, u32[]{:S(2)}) collective-permute-start(bf16[1,4,256,128]{3,2,1,0:T(8,128)(2,1)S(1)} %slice.44), channel_id=1, source_target_pairs={{0,384},{128,0},{256,128},{384,256},{1,385},{129,1},{257,129},{385... | collective-permute-start | bytes 786440 | tf_op jit(solution)/shard_map/ppermute | solution.py:272
  164.6 25.9 %collective-permute-done.7.refs_2_ = bf16[1,4,256,128]{3,2,1,0:T(8,128)(2,1)S(1)} collective-permute-done((bf16[1,4,256,128]{3,2,1,0:T(8,128)(2,1)S(1)}, bf16[1,4,256,128]{3,2,1,0:T(8,128)(2,1)S(1)}, u32[]{:S(2)}, u32[]{:S(2)}) %collective-permute-start.7) | collective-permute-done | bytes 262176 | tf_op jit(solution)/shard_map/ppermute | solution.py:272
  190.5 9.9 %right_products.5 = bf16[8,3,2,256,128]{4,3,2,1,0:T(8,128)(2,1)} custom-call(s32[3]{0:T(128)S(1)} %pad_add_fusion.place_ref, s32[3,32]{1,0:T(4,128)S(1)} %negate_select_fusion.targets_ref, bf16[16,3,17,32,128]{4,3,2,1,0:T(8,128)(2,1)} %bitcast.21, bf16[2,4,256,128]{3,2,1,0:T(8,128)(2,1)} %collective-permute-done.4.refs_0_.refs_1_, ...), custom_call_target="tpu_custom_call" | custom-call | tf_op jit(solution)/shard_map/right_products/pallas_call | solution.py:163
  200.4 4.9 %all-to-all-start.3 = ((bf16[8,3,2,256,128]{4,3,2,1,0:T(8,128)(2,1)}), bf16[8,3,2,256,128]{4,3,2,1,0:T(8,128)(2,1)}, u32[]{:S(2)}, u32[]{:S(2)}) async-start(bf16[8,3,2,256,128]{4,3,2,1,0:T(8,128)(2,1)} %right_products.5), calls=%async_computation.4 | async-start | bytes 6291456 | tf_op jit(solution)/shard_map/all_to_all | solution.py:288
  205.3 5.4 %left_products.2 = bf16[16,16,16,128]{3,2,1,0:T(8,128)(2,1)} custom-call(s32[3]{0:T(128)S(1)} %pad_add_fusion.place_ref, s32[2,16]{1,0:T(2,128)S(1)} %compare_select_fusion.2.from_ref, bf16[8,1,2,256,256]{4,3,2,1,0:T(8,128)(2,1)S(1)} %all-to-all-done.1.near_ref, bf16[8,3,2,256,128]{4,3,2,1,0:T(8,128)(2,1)} %all-to-all-done.2.far_ref, ...), custom_call_target="tpu_custom_call" | custom-call | tf_op jit(solution)/shard_map/left_products/pallas_call | solution.py:252
  210.7 31.7 %all-to-all-done.3.far_ref = bf16[8,3,2,256,128]{4,3,2,1,0:T(8,128)(2,1)} async-done(((bf16[8,3,2,256,128]{4,3,2,1,0:T(8,128)(2,1)}), bf16[8,3,2,256,128]{4,3,2,1,0:T(8,128)(2,1)}, u32[]{:S(2)}, u32[]{:S(2)}) %all-to-all-start.3) | async-done | bytes 3145760 | tf_op jit(solution)/shard_map/all_to_all | solution.py:288
  242.4 4.6 %left_products.3 = (bf16[8,16,16,128]{3,2,1,0:T(8,128)(2,1)S(1)}, bf16[8,16,16,128]{3,2,1,0:T(8,128)(2,1)S(1)}) custom-call(s32[3]{0:T(128)S(1)} %pad_add_fusion.place_ref, s32[2,16]{1,0:T(2,128)S(1)} %compare_select_fusion.2.from_ref, bf16[8,1,2,256,256]{4,3,2,1,0:T(8,128)(2,1)S(1)} %all-to-all-done.1.near_ref, ...), custom_call_target="tpu_custom_call" | custom-call | tf_op jit(solution)/shard_map/left_products/pallas_call | solution.py:252
  247.0 2.9 collective-permute-start.9
  252.4 7.3 %all-to-all-start.4 = ((bf16[8,16,16,128]{3,2,1,0:T(8,128)(2,1)}), bf16[8,16,16,128]{3,2,1,0:T(8,128)(2,1)S(1)}, u32[]{:S(2)}, u32[]{:S(2)}) async-start(bf16[8,16,16,128]{3,2,1,0:T(8,128)(2,1)} %add_convert_fusion), calls=%async_computation.5 | async-start | bytes 1048576 | tf_op jit(solution)/shard_map/all_to_all | solution.py:351
  263.3 14.3 %all-to-all-done.4 = bf16[8,16,16,128]{3,2,1,0:T(8,128)(2,1)S(1)} async-done(((bf16[8,16,16,128]{3,2,1,0:T(8,128)(2,1)}), bf16[8,16,16,128]{3,2,1,0:T(8,128)(2,1)S(1)}, u32[]{:S(2)}, u32[]{:S(2)}) %all-to-all-start.4) | async-done | bytes 524320 | tf_op jit(solution)/shard_map/all_to_all | solution.py:351
  (62 shorter events, 30.1 us)
Async XLA Ops:
  6.5 73.1 %all-gather.6.cloned.1.call-start = ((), (), s32[]{:S(2)}) async-start(), calls=%async_computation.7 | async-start | bytes 2367488 | tf_op jit(solution)/shard_map/all_gather | solution.py:317
  9.2 46.3 %copy-start = (bf16[2,4,256,256]{3,2,1,0:T(8,128)(2,1)S(1)}, bf16[2,4,256,256]{3,2,1,0:T(8,128)(2,1)}, u32[]{:S(2)}) copy-start(bf16[2,4,256,256]{3,2,1,0:T(8,128)(2,1)} %refs_1_.1) | copy-start | bytes 3145732
  36.8 0.8 copy-start.4
  39.4 23.4 %copy-start.5 = (s32[2,16]{1,0:T(2,128)S(1)}, s32[2,16]{1,0:T(2,128)}, u32[]{:S(2)}) copy-start(s32[2,16]{1,0:T(2,128)} %links_ref.3) | copy-start | bytes 388
  39.4 91.5 %all-gather.8.cloned.1.call-start = ((), (), s32[]{:S(2)}) async-start(), calls=%async_computation.8 | async-start | bytes 7102464 | tf_op jit(solution)/shard_map/all_gather | solution.py:322
  56.6 28.8 %collective-permute-start = (bf16[2,4,256,128]{3,2,1,0:T(8,128)(2,1)S(1)}, bf16[2,4,256,128]{3,2,1,0:T(8,128)(2,1)S(1)}, u32[]{:S(2)}, u32[]{:S(2)}) collective-permute-start(bf16[2,4,256,128]{3,2,1,0:T(8,128)(2,1)S(1)} %get-tuple-element.30), channel_id=1, source_target_pairs={{0,384},{128,0},{256,128},{384,256},{1,385},{129,1},{257,129},{385... | collective-permute-start | bytes 1572872 | tf_op jit(solution)/shard_map/ppermute | solution.py:272
  60.1 25.9 %collective-permute-start.1 = (bf16[2,4,256,128]{3,2,1,0:T(8,128)(2,1)S(1)}, bf16[2,4,256,128]{3,2,1,0:T(8,128)(2,1)S(1)}, u32[]{:S(2)}, u32[]{:S(2)}) collective-permute-start(bf16[2,4,256,128]{3,2,1,0:T(8,128)(2,1)S(1)} %get-tuple-element.30), channel_id=1, source_target_pairs={{0,128},{128,256},{256,384},{384,0},{1,129},{129,257},{257,385},{3... | collective-permute-start | bytes 1572872 | tf_op jit(solution)/shard_map/ppermute | solution.py:272
  85.9 65.9 %all-to-all-start.1 = ((bf16[8,1,2,256,256]{4,3,2,1,0:T(8,128)(2,1)}), bf16[8,1,2,256,256]{4,3,2,1,0:T(8,128)(2,1)S(1)}, u32[]{:S(2)}, u32[]{:S(2)}) async-start(bf16[8,1,2,256,256]{4,3,2,1,0:T(8,128)(2,1)} %right_products.3), calls=%async_computation.1 | async-start | bytes 4194304 | tf_op jit(solution)/shard_map/all_to_all | solution.py:288
  93.0 25.7 %collective-permute-start.2 = (bf16[1,4,256,128]{3,2,1,0:T(8,128)(2,1)S(1)}, bf16[1,4,256,128]{3,2,1,0:T(8,128)(2,1)S(1)}, u32[]{:S(2)}, u32[]{:S(2)}) collective-permute-start(bf16[1,4,256,128]{3,2,1,0:T(8,128)(2,1)S(1)} %slice.42), channel_id=1, source_target_pairs={{0,384},{128,0},{256,128},{384,256},{1,385},{129,1},{257,129},{385... | collective-permute-start | bytes 786440 | tf_op jit(solution)/shard_map/ppermute | solution.py:272
  96.7 22.0 %collective-permute-start.3 = (bf16[1,4,256,128]{3,2,1,0:T(8,128)(2,1)S(1)}, bf16[1,4,256,128]{3,2,1,0:T(8,128)(2,1)S(1)}, u32[]{:S(2)}, u32[]{:S(2)}) collective-permute-start(bf16[1,4,256,128]{3,2,1,0:T(8,128)(2,1)S(1)} %slice.43), channel_id=1, source_target_pairs={{0,128},{128,256},{256,384},{384,0},{1,129},{129,257},{257,385},{3... | collective-permute-start | bytes 786440 | tf_op jit(solution)/shard_map/ppermute | solution.py:272
  118.7 0.7 copy-start.2
  119.4 25.8 %collective-permute-start.4 = (bf16[2,4,256,128]{3,2,1,0:T(8,128)(2,1)}, bf16[2,4,256,128]{3,2,1,0:T(8,128)(2,1)}, u32[]{:S(2)}, u32[]{:S(2)}) collective-permute-start(bf16[2,4,256,128]{3,2,1,0:T(8,128)(2,1)} %get-tuple-element.22), channel_id=1, source_target_pairs={{0,384},{128,0},{256,128},{384,256},{1,385},{129,1},{257,129},{385... | collective-permute-start | bytes 1572872 | tf_op jit(solution)/shard_map/ppermute | solution.py:272
  123.1 28.7 %collective-permute-start.5 = (bf16[2,4,256,128]{3,2,1,0:T(8,128)(2,1)}, bf16[2,4,256,128]{3,2,1,0:T(8,128)(2,1)}, u32[]{:S(2)}, u32[]{:S(2)}) collective-permute-start(bf16[2,4,256,128]{3,2,1,0:T(8,128)(2,1)} %get-tuple-element.22), channel_id=1, source_target_pairs={{0,128},{128,256},{256,384},{384,0},{1,129},{129,257},{257,385},{3... | collective-permute-start | bytes 1572872 | tf_op jit(solution)/shard_map/ppermute | solution.py:272
  130.9 0.9 copy-start.3
  151.9 48.5 %all-to-all-start.2 = ((bf16[8,3,2,256,128]{4,3,2,1,0:T(8,128)(2,1)}), bf16[8,3,2,256,128]{4,3,2,1,0:T(8,128)(2,1)}, u32[]{:S(2)}, u32[]{:S(2)}) async-start(bf16[8,3,2,256,128]{4,3,2,1,0:T(8,128)(2,1)} %right_products.4), calls=%async_computation.2 | async-start | bytes 6291456 | tf_op jit(solution)/shard_map/all_to_all | solution.py:288
  157.5 33.0 %collective-permute-start.7 = (bf16[1,4,256,128]{3,2,1,0:T(8,128)(2,1)S(1)}, bf16[1,4,256,128]{3,2,1,0:T(8,128)(2,1)S(1)}, u32[]{:S(2)}, u32[]{:S(2)}) collective-permute-start(bf16[1,4,256,128]{3,2,1,0:T(8,128)(2,1)S(1)} %slice.44), channel_id=1, source_target_pairs={{0,384},{128,0},{256,128},{384,256},{1,385},{129,1},{257,129},{385... | collective-permute-start | bytes 786440 | tf_op jit(solution)/shard_map/ppermute | solution.py:272
  162.4 28.0 %collective-permute-start.8 = (bf16[1,4,256,128]{3,2,1,0:T(8,128)(2,1)S(1)}, bf16[1,4,256,128]{3,2,1,0:T(8,128)(2,1)S(1)}, u32[]{:S(2)}, u32[]{:S(2)}) collective-permute-start(bf16[1,4,256,128]{3,2,1,0:T(8,128)(2,1)S(1)} %slice.45), channel_id=1, source_target_pairs={{0,128},{128,256},{256,384},{384,0},{1,129},{129,257},{257,385},{3... | collective-permute-start | bytes 786440 | tf_op jit(solution)/shard_map/ppermute | solution.py:272
  200.4 4.9 %copy-start.1 = (bf16[2,4,256,256]{3,2,1,0:T(8,128)(2,1)S(1)}, bf16[2,4,256,256]{3,2,1,0:T(8,128)(2,1)}, u32[]{:S(2)}) copy-start(bf16[2,4,256,256]{3,2,1,0:T(8,128)(2,1)} %env_ref.3) | copy-start | bytes 3145732
  200.4 42.0 %all-to-all-start.3 = ((bf16[8,3,2,256,128]{4,3,2,1,0:T(8,128)(2,1)}), bf16[8,3,2,256,128]{4,3,2,1,0:T(8,128)(2,1)}, u32[]{:S(2)}, u32[]{:S(2)}) async-start(bf16[8,3,2,256,128]{4,3,2,1,0:T(8,128)(2,1)} %right_products.5), calls=%async_computation.4 | async-start | bytes 6291456 | tf_op jit(solution)/shard_map/all_to_all | solution.py:288
  205.3 54.6 %reduce-scatter.2.cloned.1.call-start = ((), (), s32[]{:S(2)}) async-start(), calls=%async_computation.6 | async-start | bytes 1179648 | tf_op jit(solution)/shard_map/reduce_scatter | solution.py:340
  247.0 12.6 %copy-start.6 = (s32[4]{0:T(128)S(1)}, s32[4]{0:T(128)}, u32[]{:S(2)}) copy-start(s32[4]{0:T(128)} %rows_ref.1) | copy-start | bytes 52
  247.0 4.4 %collective-permute-start.9 = (bf16[8,16,16,128]{3,2,1,0:T(8,128)(2,1)S(1)}, bf16[8,16,16,128]{3,2,1,0:T(8,128)(2,1)S(1)}, u32[]{:S(2)}, u32[]{:S(2)}) collective-permute-start(bf16[8,16,16,128]{3,2,1,0:T(8,128)(2,1)S(1)} %get-tuple-element.28), channel_id=1, source_target_pairs={{0,1},{1,0},{2,3},{3,2},{4,5},{5,4},{6,7},{7,6},{8,9},{9,8},{10,11... | collective-permute-start | bytes 1572872 | tf_op jit(solution)/shard_map/ppermute | solution.py:272
  252.4 25.2 %all-to-all-start.4 = ((bf16[8,16,16,128]{3,2,1,0:T(8,128)(2,1)}), bf16[8,16,16,128]{3,2,1,0:T(8,128)(2,1)S(1)}, u32[]{:S(2)}, u32[]{:S(2)}) async-start(bf16[8,16,16,128]{3,2,1,0:T(8,128)(2,1)} %add_convert_fusion), calls=%async_computation.5 | async-start | bytes 1048576 | tf_op jit(solution)/shard_map/all_to_all | solution.py:351
  260.7 16.9 %collective-permute-start.6 = (bf16[16,16,128]{2,1,0:T(8,128)(2,1)S(1)}, bf16[16,16,128]{2,1,0:T(8,128)(2,1)S(1)}, u32[]{:S(2)}, u32[]{:S(2)}) collective-permute-start(bf16[16,16,128]{2,1,0:T(8,128)(2,1)S(1)} %dynamic-slice_bitcast_fusion), channel_id=1, source_target_pairs={{0,1},{1,0},{2,3},{3,2},{4,5},{5,4},{6,7},{7,6},{8,9},{9,8},{10,11... | collective-permute-start | bytes 196616 | tf_op jit(solution)/shard_map/ppermute | solution.py:272
Sparse Core Ops, SparseCore 0:
  39.5 40.1 all-gather.5
  81.8 49.1 all-gather.7
  210.8 35.5 reduce-scatter.1

commit v9 on v8

--- a/solution.py
+++ b/solution.py
@@ -184,19 +184,10 @@
     )(place, targets, in_hbm(slices), *[array for array, _ in flat])
 
 
-def far_products(place, targets, slices, above, below, across, group):
-    envs = [
-        [(above, 0), (above, 1)],
-        [(across[0], 0), (across[1], 0)],
-        [(below, 0), (below, 1)],
-    ]
-    return right_products(place, targets, slices, envs, group, 0, LANES)
-
-
-def left_partials(place_ref, from_ref, near_ref, far_ref, env_ref, placed_ref):
+def left_partials(place_ref, from_ref, own_ref, side_ref, back_ref, env_ref, placed_ref):
     terms, count = from_ref.shape
-    group, near, _, extent, width = near_ref.shape
-    layers = near + far_ref.shape[1]
+    group, _, _, extent, width = own_ref.shape
+    layers = 2 + side_ref.shape[1]
     per_sector = count // pl.num_programs(0)
     sector = pl.program_id(0)
     left = jnp.concatenate([env_ref[term, 0] for term in range(terms)], axis=1)
@@ -208,13 +199,17 @@
             rows = slice(term * extent, (term + 1) * extent)
             columns = slice(place * width, (place + 1) * width)
 
-            @pl.when(step < near)
+            @pl.when(step == 0)
+            def _(term=term, peer=peer, rows=rows, columns=columns):
+                placed_ref[rows, columns] = own_ref[peer, 0, term]
+
+            @pl.when(step == layers // 2)
+            def _(term=term, peer=peer, rows=rows, columns=columns):
+                placed_ref[rows, columns] = back_ref[peer, 0, term]
+
+            @pl.when(lax.rem(step, 2) == 1)
             def _(term=term, peer=peer, step=step, rows=rows, columns=columns):
-                placed_ref[rows, columns] = near_ref[peer, jnp.minimum(step, near - 1), term]
-
-            @pl.when(step >= near)
-            def _(term=term, peer=peer, step=step, rows=rows, columns=columns):
-                placed_ref[rows, columns] = far_ref[peer, jnp.maximum(step - near, 0), term]
+                placed_ref[rows, columns] = side_ref[peer, lax.div(step, 2), term]
 
     partial = jnp.dot(left, placed_ref[...], preferred_element_type=jnp.float32)
     partial = partial.astype(jnp.bfloat16)
@@ -222,15 +217,15 @@
         yield place, partial[:, place * width : (place + 1) * width]
 
 
-def left_kernel(place_ref, from_ref, near_ref, far_ref, env_ref, out_ref, placed_ref):
-    for place, partial in left_partials(place_ref, from_ref, near_ref, far_ref, env_ref, placed_ref):
+def left_kernel(place_ref, from_ref, own_ref, side_ref, back_ref, env_ref, out_ref, placed_ref):
+    for place, partial in left_partials(place_ref, from_ref, own_ref, side_ref, back_ref, env_ref, placed_ref):
         out_ref[:, place] = partial.reshape(out_ref.shape[0], SHARE, partial.shape[1])
 
 
-def left_split_kernel(place_ref, from_ref, near_ref, far_ref, env_ref, keep_ref, send_ref, placed_ref):
+def left_split_kernel(place_ref, from_ref, own_ref, side_ref, back_ref, env_ref, keep_ref, send_ref, placed_ref):
     chips = keep_ref.shape[0]
     core = place_ref[2]
-    for place, partial in left_partials(place_ref, from_ref, near_ref, far_ref, env_ref, placed_ref):
+    for place, partial in left_partials(place_ref, from_ref, own_ref, side_ref, back_ref, env_ref, placed_ref):
         halves = [
             jnp.stack(
                 [partial[(2 * c + k) * SHARE : (2 * c + k + 1) * SHARE] for c in range(chips)]
@@ -241,10 +236,10 @@
         send_ref[:, place] = jnp.where(core == 0, halves[1], halves[0])
 
 
-def left_products(place, source, near, far, left_env, chunk, split):
+def left_products(place, source, own, side, back, left_env, chunk, split):
     _, sectors, extent, _ = left_env.shape
     terms, count = source.shape
-    width = far.shape[-1]
+    width = side.shape[-1]
     per_sector = count // sectors
     pieces = extent // SHARE // (2 if split else 1)
     out_spec = pl.BlockSpec((pieces, per_sector, SHARE, width), lambda i: (0, i, 0, 0))
@@ -255,8 +250,9 @@
         in_specs=[
             SMEM,
             SMEM,
-            pl.BlockSpec(near.shape[:-1] + (width,), lambda i: (0, 0, 0, 0, chunk)),
-            pl.BlockSpec(far.shape, lambda i: (0, 0, 0, 0, 0)),
+            pl.BlockSpec(own.shape[:-1] + (width,), lambda i: (0, 0, 0, 0, chunk)),
+            pl.BlockSpec(side.shape, lambda i: (0, 0, 0, 0, 0)),
+            pl.BlockSpec(back.shape, lambda i: (0, 0, 0, 0, 0)),
             pl.BlockSpec((terms, 1, extent, extent), lambda i: (0, i, 0, 0)),
         ],
         out_specs=[out_spec, out_spec] if split else out_spec,
@@ -264,7 +260,7 @@
         scratch_shapes=[pltpu.VMEM((terms * extent, per_sector * width), jnp.bfloat16)],
         compiler_params=pltpu.CompilerParams(vmem_limit_bytes=VMEM_LIMIT),
         name="left_products",
-    )(place, source, near, far, left_env)
+    )(place, source, own, side, back, left_env)
 
 
 def shift(array, axis, step):
@@ -310,8 +306,7 @@
     peers = lax.rem(source[1:] + moved_by, slots)
     ordered = order(source[0], term_links, sector_cols, arrived)
 
-    parts = [right_env[..., at : at + LANES] for at in range(0, width, LANES)]
-    above, below = shift(parts[0], "zh", -1), shift(parts[0], "zh", 1)
+    above, below = shift(right_env, "zh", -1), shift(right_env, "zh", 1)
     across = shift(above[:1], "zh", -1), shift(below[1:], "zh", 1)
 
     slices = lax.all_gather(ordered[None], DEPTH)
@@ -319,7 +314,8 @@
     others = lax.dynamic_slice_in_dim(jnp.concatenate([around, around]), layer + 1, layers - 1)
     far_targets = others[:, count, 0, : terms * count].astype(jnp.int32)
     far_targets = lax.rem(far_targets + moved_by, slots)
-    far_slices = lax.all_gather(others, DEPTH)
+    side_slices = lax.all_gather(jnp.stack([others[0], others[2]]), DEPTH)
+    back_slices = lax.all_gather(others[1:2], DEPTH)
 
     targets = lax.rem((term_links // count).reshape(1, terms * count) + moved_by, slots)
     envs = [[(right_env, term) for term in range(terms)]]
@@ -327,26 +323,34 @@
     products, above, below = lax.optimization_barrier((products, above, below))
     own = exchange(products)
 
-    across, second = lax.optimization_barrier((across, parts[1]))
-    next_above, next_below = shift(second, "zh", -1), shift(second, "zh", 1)
-    next_across = shift(next_above[:1], "zh", -1), shift(next_below[1:], "zh", 1)
-
-    products = far_products(place, far_targets, far_slices, above, below, across, group)
-    after = products, far_slices, next_above, next_below
-    products, far_slices, next_above, next_below = lax.optimization_barrier(after)
-    far = exchange(products)
-    partial = left_products(place, peers, own, far, left_env, 0, False)
+    sides, backs = [], []
+    targets = jnp.stack([far_targets[0], far_targets[2]])
+    envs = [[(above, 0), (above, 1)], [(below, 0), (below, 1)]]
+    for chunk in range(width // LANES):
+        products = right_products(place, targets, side_slices, envs, group, chunk, LANES)
+        if sides:
+            after = products, sides[-1], across
+            products, sides[-1], across = lax.optimization_barrier(after)
+        else:
+            products, own = lax.optimization_barrier((products, own))
+        sides.append(exchange(products))
+    envs = [[(across[0], 0), (across[1], 0)]]
+    for chunk in range(width // LANES):
+        products = right_products(place, far_targets[1:2], back_slices, envs, group, chunk, LANES)
+        if backs:
+            products, backs[-1] = lax.optimization_barrier((products, backs[-1]))
+        else:
+            products, sides[-1] = lax.optimization_barrier((products, sides[-1]))
+        backs.append(exchange(products))
+
+    partial = left_products(place, peers, own, sides[0], backs[0], left_env, 0, False)
     partial = partial.reshape((-1, 2) + partial.shape[1:])
     summed = lax.psum_scatter(partial, "y", scatter_dimension=0, tiled=False)
     received = shift(lax.dynamic_index_in_dim(summed, 1 - core_index, 0, False), "core", 1)
     kept = lax.dynamic_index_in_dim(summed, core_index, 0, False)
     pieces = [kept.astype(jnp.float32) + received.astype(jnp.float32)]
 
-    products = far_products(
-        place, far_targets, far_slices, next_above, next_below, next_across, group
-    )
-    far = exchange(products)
-    keep, send = left_products(place, peers, own, far, left_env, 1, True)
+    keep, send = left_products(place, peers, own, sides[1], backs[1], left_env, 1, True)
     pair = keep.astype(jnp.float32) + shift(send, "core", 1).astype(jnp.float32)
     shares = lax.all_to_all(pair.astype(jnp.bfloat16), "y", 0, 0, tiled=True)
     pieces.append(jnp.sum(shares.astype(jnp.float32), axis=0))

time: 287 us -> 303 us (1.056)
  Pallas kernels: 39.6 us -> 44.8 us
  local copies, waits for them, and re-layouts: 6.42 us -> 11.5 us
    reduce_scatter x1, waiting for transfers between devices: 0.01 us -> 15.4 us  [local(): summed = lax.psum_scatter(partial, 'y', scatter_dimension=0, tiled=False)]
    all_gather x1 -> x2, waiting for transfers between devices: 4.51 us -> 19 us  [the longest x1 9.89 us: local(): side_slices = lax.all_gather(jnp.stack([others[0], others[2]]), DEPTH)]
    all_to_all x1, waiting for transfers between devices: 14.3 us -> 0.01 us  [local(): shares = lax.all_to_all(pair.astype(jnp.bfloat16), 'y', 0, 0, tiled=True)]
    ppermute x10 -> x6, waiting for transfers between devices: 57.8 us -> 43.6 us  [shift(): lax.ppermute(array, axis, [(i, (i + step) % size) for i in range(size)])]
    all_to_all x3 -> x5, starting transfers between devices: 16.5 us -> 27.4 us  [exchange(): lax.all_to_all(products, axes, 0, 0, axis_index_groups=groups, tiled=True)]
    ppermute x10 -> x6, starting transfers between devices: 30.2 us -> 21.8 us  [shift(): lax.ppermute(array, axis, [(i, (i + step) % size) for i in range(size)])]
    pallas_call x3 -> x5, Pallas kernels: 25.2 us -> 31.1 us  [right_products(): pl.pallas_call(right_kernel, grid_spec=pltpu.PrefetchScalarGridSpec(num_s...]
    unnamed x14 -> x26, local copies, waits for them, and re-layouts: 1.69 us -> 7.5 us
  transfers between devices with their start and end apart: 17 -> 16, of which waited for: 10 -> 14; matrix products, arithmetic and copies ran while one was open for 2% -> 2% of each run, Pallas kernels for 12% -> 13%
where the time goes in v9:
time: 303 us; the launch traced here: 301 us
  waiting for transfers between devices  128 us (42%)
  starting transfers between devices  56.1 us (19%)
  Pallas kernels  44.8 us (15%)
  blocking collectives  42.6 us (14%)
  between operations  13.3 us (4%)
  local copies, waits for them, and re-layouts  11.5 us (4%)
  other arithmetic  4.57 us (2%)
    ppermute x6, waiting for transfers between devices, shift(): lax.ppermute(array, axis, [(i, (i + step) % size) for i in range(size)])  43.6 us
    all_to_all x5, waiting for transfers between devices, exchange(): lax.all_to_all(products, axes, 0, 0, axis_index_groups=groups, tiled=True)  34 us
    pallas_call x5, Pallas kernels, right_products(): pl.pallas_call(right_kernel, grid_spec=pltpu.PrefetchScalarGridSpec(num_s...  31.1 us
    all_to_all x1, blocking collectives, local(): arrived = lax.all_to_all(buffer, REMAP, 0, 0, tiled=True)  27.5 us
    all_to_all x5, starting transfers between devices, exchange(): lax.all_to_all(products, axes, 0, 0, axis_index_groups=groups, tiled=True)  27.4 us
    ppermute x6, starting transfers between devices, shift(): lax.ppermute(array, axis, [(i, (i + step) % size) for i in range(size)])  21.8 us
    all_gather x1, waiting for transfers between devices, local(): slices = lax.all_gather(ordered[None], DEPTH)  16.3 us
    reduce_scatter x1, waiting for transfers between devices, local(): summed = lax.psum_scatter(partial, 'y', scatter_dimension=0, tiled=False)  15.4 us
  transfers between devices with their start and end apart: 16, of which 14 were waited for; matrix products, arithmetic and copies ran while one was open for 2% of the time, Pallas kernels for 13%

profile of v9, /device:TPU:1, one launch (start us, length us, event | category | flops | bytes accessed | tf_op | source)
XLA Modules:
  0.0 301.2 jit_solution(18421967855777425004)
XLA Ops:
  9.2 27.5 %all_to_all.35.in_ref = bf16[32,48,128]{2,1,0:T(8,128)(2,1)S(1)} all-to-all(bf16[32,48,128]{2,1,0:T(8,128)(2,1)} %spread_blocks.1), channel_id=1, replica_groups=mesh['zh'=4,'zl'=2,'x'=4,'y'=8,'core'=2] {'zh','zl','x'}, dimensions={0} | all-to-all | bytes 786432 | tf_op jit(solution)/shard_map/all_to_all | solution.py:301
  39.3 15.1 %all-gather = bf16[68,32,128]{2,1,0:T(8,128)(2,1)S(1)} all-gather(bf16[17,32,128]{2,1,0:T(8,128)(2,1)} %order_blocks.1), channel_id=2, replica_groups=mesh['zh'=4,'zl'=2,'x'=4,'y'=8,'core'=2] {'zh'}, dimensions={0}, use_global_device_ids=true | all-gather | bytes 696320 | tf_op jit(solution)/shard_map/all_gather | solution.py:313
  63.3 16.3 %all-gather.10.cloned.1.call-done = bf16[272,32,128]{2,1,0:T(8,128)(2,1)} async-done(((bf16[17,32,128]{2,1,0:T(8,128)(2,1)}), bf16[272,32,128]{2,1,0:T(8,128)(2,1)}) %all-gather.10.cloned.1.call-update) | async-done | bytes 2228240 | tf_op jit(solution)/shard_map/all_gather | solution.py:312
  79.5 5.7 %right_products.5 = bf16[8,1,2,256,256]{4,3,2,1,0:T(8,128)(2,1)} custom-call(s32[3]{0:T(128)S(1)} %pad_add_fusion.1.place_ref, s32[1,32]{1,0:T(1,128)S(1)} %compare_select_fusion.targets_ref, bf16[16,1,17,32,128]{4,3,2,1,0:T(8,128)(2,1)} %bitcast.26, bf16[2,4,256,256]{3,2,1,0:T(8,128)(2,1)S(1)} %copy-done.2, bf16[2,4,256,256]{3,2,1,0:T(8,128)(2,1)S(1)} %copy-done.2), custom_call_target="tpu_custom_call" | custom-call | tf_op jit(solution)/shard_map/right_products/pallas_call | solution.py:163
  85.3 20.3 %collective-permute-done.refs_0_.refs_1_ = bf16[2,4,256,256]{3,2,1,0:T(8,128)(2,1)S(1)} collective-permute-done((bf16[2,4,256,256]{3,2,1,0:T(8,128)(2,1)S(1)}, bf16[2,4,256,256]{3,2,1,0:T(8,128)(2,1)S(1)}, u32[]{:S(2)}, u32[]{:S(2)}) %collective-permute-start) | collective-permute-done | bytes 1048608 | tf_op jit(solution)/shard_map/ppermute | solution.py:268
  108.7 5.9 %all-to-all-start.1 = ((bf16[8,1,2,256,256]{4,3,2,1,0:T(8,128)(2,1)}), bf16[8,1,2,256,256]{4,3,2,1,0:T(8,128)(2,1)}, u32[]{:S(2)}, u32[]{:S(2)}) async-start(bf16[8,1,2,256,256]{4,3,2,1,0:T(8,128)(2,1)} %right_products.5), calls=%async_computation.1 | async-start | bytes 4194304 | tf_op jit(solution)/shard_map/all_to_all | solution.py:284
  115.4 9.9 %all-gather.8.cloned.1.call-done = bf16[32,17,32,128]{3,2,1,0:T(8,128)(2,1)} async-done(((bf16[2,17,32,128]{3,2,1,0:T(8,128)(2,1)}), bf16[32,17,32,128]{3,2,1,0:T(8,128)(2,1)}) %all-gather.8.cloned.1.call-update) | async-done | bytes 4456464 | tf_op jit(solution)/shard_map/all_gather | solution.py:317
  125.3 7.5 %right_products.6 = bf16[8,2,2,256,128]{4,3,2,1,0:T(8,128)(2,1)} custom-call(s32[3]{0:T(128)S(1)} %pad_add_fusion.1.place_ref, s32[2,32]{1,0:T(2,128)S(1)} %pad_add_fusion.targets_ref, bf16[16,2,17,32,128]{4,3,2,1,0:T(8,128)(2,1)} %bitcast.21, bf16[2,4,256,256]{3,2,1,0:T(8,128)(2,1)S(1)} %collective-permute-done.refs_0_.refs_1_, ...), custom_call_target="tpu_custom_call" | custom-call | tf_op jit(solution)/shard_map/right_products/pallas_call | solution.py:163
  132.8 8.1 %all-to-all-done.1.own_ref = bf16[8,1,2,256,256]{4,3,2,1,0:T(8,128)(2,1)} async-done(((bf16[8,1,2,256,256]{4,3,2,1,0:T(8,128)(2,1)}), bf16[8,1,2,256,256]{4,3,2,1,0:T(8,128)(2,1)}, u32[]{:S(2)}, u32[]{:S(2)}) %all-to-all-start.1) | async-done | bytes 2097184 | tf_op jit(solution)/shard_map/all_to_all | solution.py:284
  140.9 5.0 %all-to-all-start.2 = ((bf16[8,2,2,256,128]{4,3,2,1,0:T(8,128)(2,1)}), bf16[8,2,2,256,128]{4,3,2,1,0:T(8,128)(2,1)}, u32[]{:S(2)}, u32[]{:S(2)}) async-start(bf16[8,2,2,256,128]{4,3,2,1,0:T(8,128)(2,1)} %right_products.6), calls=%async_computation.2 | async-start | bytes 4194304 | tf_op jit(solution)/shard_map/all_to_all | solution.py:284
  153.8 7.4 %right_products.7 = bf16[8,2,2,256,128]{4,3,2,1,0:T(8,128)(2,1)} custom-call(s32[3]{0:T(128)S(1)} %pad_add_fusion.1.place_ref, s32[2,32]{1,0:T(2,128)S(1)} %pad_add_fusion.targets_ref, bf16[16,2,17,32,128]{4,3,2,1,0:T(8,128)(2,1)} %bitcast.22, bf16[2,4,256,256]{3,2,1,0:T(8,128)(2,1)S(1)} %collective-permute-done.refs_0_.refs_1_, ...), custom_call_target="tpu_custom_call" | custom-call | tf_op jit(solution)/shard_map/right_products/pallas_call | solution.py:163
  161.2 14.4 %collective-permute-done.2.refs_0_ = bf16[1,4,256,256]{3,2,1,0:T(8,128)(2,1)S(1)} collective-permute-done((bf16[1,4,256,256]{3,2,1,0:T(8,128)(2,1)}, bf16[1,4,256,256]{3,2,1,0:T(8,128)(2,1)S(1)}, u32[]{:S(2)}, u32[]{:S(2)}) %collective-permute-start.2) | collective-permute-done | bytes 524320 | tf_op jit(solution)/shard_map/ppermute | solution.py:268
  179.0 6.4 %all-to-all-start.3 = ((bf16[8,2,2,256,128]{4,3,2,1,0:T(8,128)(2,1)}), bf16[8,2,2,256,128]{4,3,2,1,0:T(8,128)(2,1)S(1)}, u32[]{:S(2)}, u32[]{:S(2)}) async-start(bf16[8,2,2,256,128]{4,3,2,1,0:T(8,128)(2,1)} %right_products.7), calls=%async_computation.3 | async-start | bytes 4194304 | tf_op jit(solution)/shard_map/all_to_all | solution.py:284
  185.4 9.1 %all-gather.12.cloned.1.call-done = bf16[16,17,32,128]{3,2,1,0:T(8,128)(2,1)} async-done(((bf16[1,17,32,128]{3,2,1,0:T(8,128)(2,1)}), bf16[16,17,32,128]{3,2,1,0:T(8,128)(2,1)}) %all-gather.12.cloned.1.call-update) | async-done | bytes 2228240 | tf_op jit(solution)/shard_map/all_gather | solution.py:318
  194.4 5.2 %right_products.9 = bf16[8,1,2,256,128]{4,3,2,1,0:T(8,128)(2,1)} custom-call(s32[3]{0:T(128)S(1)} %pad_add_fusion.1.place_ref, s32[1,32]{1,0:T(1,128)S(1)} %get-tuple-element.38.targets_ref, bf16[16,1,17,32,128]{4,3,2,1,0:T(8,128)(2,1)} %bitcast.23, bf16[1,4,256,256]{3,2,1,0:T(8,128)(2,1)S(1)} %collective-permute-done.2.refs_0_, ...), custom_call_target="tpu_custom_call" | custom-call | tf_op jit(solution)/shard_map/right_products/pallas_call | solution.py:163
  199.7 11.5 %all-to-all-done.3.side_ref = bf16[8,2,2,256,128]{4,3,2,1,0:T(8,128)(2,1)S(1)} async-done(((bf16[8,2,2,256,128]{4,3,2,1,0:T(8,128)(2,1)}), bf16[8,2,2,256,128]{4,3,2,1,0:T(8,128)(2,1)S(1)}, u32[]{:S(2)}, u32[]{:S(2)}) %all-to-all-start.3) | async-done | bytes 2097184 | tf_op jit(solution)/shard_map/all_to_all | solution.py:284
  211.2 5.2 %all-to-all-start.4 = ((bf16[8,1,2,256,128]{4,3,2,1,0:T(8,128)(2,1)}), bf16[8,1,2,256,128]{4,3,2,1,0:T(8,128)(2,1)S(1)}, u32[]{:S(2)}, u32[]{:S(2)}) async-start(bf16[8,1,2,256,128]{4,3,2,1,0:T(8,128)(2,1)} %right_products.9), calls=%async_computation.4 | async-start | bytes 2097152 | tf_op jit(solution)/shard_map/all_to_all | solution.py:284
  218.5 5.2 %right_products.8 = bf16[8,1,2,256,128]{4,3,2,1,0:T(8,128)(2,1)} custom-call(s32[3]{0:T(128)S(1)} %pad_add_fusion.1.place_ref, s32[1,32]{1,0:T(1,128)S(1)} %get-tuple-element.38.targets_ref, bf16[16,1,17,32,128]{4,3,2,1,0:T(8,128)(2,1)} %bitcast.24, bf16[1,4,256,256]{3,2,1,0:T(8,128)(2,1)S(1)} %copy-done.6, bf16[1,4,256,256]{3,2,1,0:T(8,128)(2,1)S(1)} %copy-done.8), custom_call_target="tpu_custom_call" | custom-call | tf_op jit(solution)/shard_map/right_products/pallas_call | solution.py:163
  223.7 7.6 %all-to-all-done.4.back_ref = bf16[8,1,2,256,128]{4,3,2,1,0:T(8,128)(2,1)S(1)} async-done(((bf16[8,1,2,256,128]{4,3,2,1,0:T(8,128)(2,1)}), bf16[8,1,2,256,128]{4,3,2,1,0:T(8,128)(2,1)S(1)}, u32[]{:S(2)}, u32[]{:S(2)}) %all-to-all-start.4) | async-done | bytes 1048608 | tf_op jit(solution)/shard_map/all_to_all | solution.py:284
  239.5 5.3 %left_products.2 = bf16[16,16,16,128]{3,2,1,0:T(8,128)(2,1)} custom-call(s32[3]{0:T(128)S(1)} %pad_add_fusion.1.place_ref, s32[2,16]{1,0:T(2,128)S(1)} %compare_select_fusion.2.from_ref, bf16[8,1,2,256,256]{4,3,2,1,0:T(8,128)(2,1)} %all-to-all-done.1.own_ref, bf16[8,2,2,256,128]{4,3,2,1,0:T(8,128)(2,1)} %all-to-all-done.2.side_ref, ...), custom_call_target="tpu_custom_call" | custom-call | tf_op jit(solution)/shard_map/left_products/pallas_call | solution.py:247
  244.9 6.8 %all-to-all-done.5.back_ref = bf16[8,1,2,256,128]{4,3,2,1,0:T(8,128)(2,1)S(1)} async-done(((bf16[8,1,2,256,128]{4,3,2,1,0:T(8,128)(2,1)}), bf16[8,1,2,256,128]{4,3,2,1,0:T(8,128)(2,1)S(1)}, u32[]{:S(2)}, u32[]{:S(2)}) %all-to-all-start.5) | async-done | bytes 1048608 | tf_op jit(solution)/shard_map/all_to_all | solution.py:284
  261.7 6.8 %all-to-all-start.6 = ((bf16[8,16,16,128]{3,2,1,0:T(8,128)(2,1)}), bf16[8,16,16,128]{3,2,1,0:T(8,128)(2,1)S(1)}, u32[]{:S(2)}, u32[]{:S(2)}) async-start(bf16[8,16,16,128]{3,2,1,0:T(8,128)(2,1)} %add_convert_fusion), calls=%async_computation.7 | async-start | bytes 1048576 | tf_op jit(solution)/shard_map/all_to_all | solution.py:355
  268.7 15.4 %reduce-scatter.2.cloned.1.call-done = bf16[1,2,16,16,128]{4,3,2,1,0:T(8,128)(2,1)} async-done(((bf16[8,2,16,16,128]{4,3,2,1,0:T(8,128)(2,1)}), bf16[1,2,16,16,128]{4,3,2,1,0:T(8,128)(2,1)}) %reduce-scatter.2.cloned.1.call-update) | async-done | bytes 131088 | tf_op jit(solution)/shard_map/reduce_scatter | solution.py:348
  284.9 7.2 %collective-permute-start.4 = (bf16[16,16,128]{2,1,0:T(8,128)(2,1)S(1)}, bf16[16,16,128]{2,1,0:T(8,128)(2,1)S(1)}, u32[]{:S(2)}, u32[]{:S(2)}) collective-permute-start(bf16[16,16,128]{2,1,0:T(8,128)(2,1)S(1)} %dynamic-slice_bitcast_fusion), channel_id=1, source_target_pairs={{0,1},{1,0},{2,3},{3,2},{4,5},{5,4},{6,7},{7,6},{8,9},{9,8},{10,11... | collective-permute-start | bytes 196616 | tf_op jit(solution)/shard_map/ppermute | solution.py:268
  (76 shorter events, 52.9 us)
Async XLA Ops:
  6.5 73.0 %all-gather.10.cloned.1.call-start = ((), (), s32[]{:S(2)}) async-start(), calls=%async_computation.10 | async-start | bytes 2367488 | tf_op jit(solution)/shard_map/all_gather | solution.py:312
  36.7 20.1 %copy-start.2 = (bf16[2,4,256,256]{3,2,1,0:T(8,128)(2,1)S(1)}, bf16[2,4,256,256]{3,2,1,0:T(8,128)(2,1)}, u32[]{:S(2)}) copy-start(bf16[2,4,256,256]{3,2,1,0:T(8,128)(2,1)} %refs_1_.1) | copy-start | bytes 3145732
  36.7 26.4 %copy-start.11 = (s32[2,16]{1,0:T(2,128)S(1)}, s32[2,16]{1,0:T(2,128)}, u32[]{:S(2)}) copy-start(s32[2,16]{1,0:T(2,128)} %links_ref.3) | copy-start | bytes 388
  39.3 86.0 %all-gather.8.cloned.1.call-start = ((), (), s32[]{:S(2)}) async-start(), calls=%async_computation.9 | async-start | bytes 4734976 | tf_op jit(solution)/shard_map/all_gather | solution.py:317
  56.8 48.8 %collective-permute-start = (bf16[2,4,256,256]{3,2,1,0:T(8,128)(2,1)S(1)}, bf16[2,4,256,256]{3,2,1,0:T(8,128)(2,1)S(1)}, u32[]{:S(2)}, u32[]{:S(2)}) collective-permute-start(bf16[2,4,256,256]{3,2,1,0:T(8,128)(2,1)S(1)} %copy-done.2), channel_id=1, source_target_pairs={{0,384},{128,0},{256,128},{384,256},{1,385},{129,1},{257,129},{385... | collective-permute-start | bytes 3145736 | tf_op jit(solution)/shard_map/ppermute | solution.py:268
  60.3 48.4 %collective-permute-start.1 = (bf16[2,4,256,256]{3,2,1,0:T(8,128)(2,1)S(1)}, bf16[2,4,256,256]{3,2,1,0:T(8,128)(2,1)S(1)}, u32[]{:S(2)}, u32[]{:S(2)}) collective-permute-start(bf16[2,4,256,256]{3,2,1,0:T(8,128)(2,1)S(1)} %copy-done.2), channel_id=1, source_target_pairs={{0,128},{128,256},{256,384},{384,0},{1,129},{129,257},{257,385},{3... | collective-permute-start | bytes 3145736 | tf_op jit(solution)/shard_map/ppermute | solution.py:268
  108.7 32.1 %all-to-all-start.1 = ((bf16[8,1,2,256,256]{4,3,2,1,0:T(8,128)(2,1)}), bf16[8,1,2,256,256]{4,3,2,1,0:T(8,128)(2,1)}, u32[]{:S(2)}, u32[]{:S(2)}) async-start(bf16[8,1,2,256,256]{4,3,2,1,0:T(8,128)(2,1)} %right_products.5), calls=%async_computation.1 | async-start | bytes 4194304 | tf_op jit(solution)/shard_map/all_to_all | solution.py:284
  140.9 38.1 %all-to-all-start.2 = ((bf16[8,2,2,256,128]{4,3,2,1,0:T(8,128)(2,1)}), bf16[8,2,2,256,128]{4,3,2,1,0:T(8,128)(2,1)}, u32[]{:S(2)}, u32[]{:S(2)}) async-start(bf16[8,2,2,256,128]{4,3,2,1,0:T(8,128)(2,1)} %right_products.6), calls=%async_computation.2 | async-start | bytes 4194304 | tf_op jit(solution)/shard_map/all_to_all | solution.py:284
  145.9 48.5 %all-gather.12.cloned.1.call-start = ((), (), s32[]{:S(2)}) async-start(), calls=%async_computation.11 | async-start | bytes 2367488 | tf_op jit(solution)/shard_map/all_gather | solution.py:318
  146.8 28.8 %collective-permute-start.2 = (bf16[1,4,256,256]{3,2,1,0:T(8,128)(2,1)}, bf16[1,4,256,256]{3,2,1,0:T(8,128)(2,1)S(1)}, u32[]{:S(2)}, u32[]{:S(2)}) collective-permute-start(bf16[1,4,256,256]{3,2,1,0:T(8,128)(2,1)} %slice.53), channel_id=1, source_target_pairs={{0,384},{128,0},{256,128},{384,256},{1,385},{129,1},{257,129},{385... | collective-permute-start | bytes 1572872 | tf_op jit(solution)/shard_map/ppermute | solution.py:268
  149.5 29.4 %collective-permute-start.3 = (bf16[1,4,256,256]{3,2,1,0:T(8,128)(2,1)}, bf16[1,4,256,256]{3,2,1,0:T(8,128)(2,1)S(1)}, u32[]{:S(2)}, u32[]{:S(2)}) collective-permute-start(bf16[1,4,256,256]{3,2,1,0:T(8,128)(2,1)} %slice.54), channel_id=1, source_target_pairs={{0,128},{128,256},{256,384},{384,0},{1,129},{129,257},{257,385},{3... | collective-permute-start | bytes 1572872 | tf_op jit(solution)/shard_map/ppermute | solution.py:268
  175.6 18.8 %copy-start.5 = (bf16[1,4,256,256]{3,2,1,0:T(8,128)(2,1)}, bf16[1,4,256,256]{3,2,1,0:T(8,128)(2,1)S(1)}, u32[]{:S(2)}) copy-start(bf16[1,4,256,256]{3,2,1,0:T(8,128)(2,1)S(1)} %collective-permute-done.2.refs_0_) | copy-start | bytes 1572868
  179.0 15.5 %copy-start.7 = (bf16[1,4,256,256]{3,2,1,0:T(8,128)(2,1)}, bf16[1,4,256,256]{3,2,1,0:T(8,128)(2,1)S(1)}, u32[]{:S(2)}) copy-start(bf16[1,4,256,256]{3,2,1,0:T(8,128)(2,1)S(1)} %collective-permute-done.3.refs_1_) | copy-start | bytes 1572868
  179.0 32.2 %all-to-all-start.3 = ((bf16[8,2,2,256,128]{4,3,2,1,0:T(8,128)(2,1)}), bf16[8,2,2,256,128]{4,3,2,1,0:T(8,128)(2,1)S(1)}, u32[]{:S(2)}, u32[]{:S(2)}) async-start(bf16[8,2,2,256,128]{4,3,2,1,0:T(8,128)(2,1)} %right_products.7), calls=%async_computation.3 | async-start | bytes 4194304 | tf_op jit(solution)/shard_map/all_to_all | solution.py:284
  211.2 20.1 %all-to-all-start.4 = ((bf16[8,1,2,256,128]{4,3,2,1,0:T(8,128)(2,1)}), bf16[8,1,2,256,128]{4,3,2,1,0:T(8,128)(2,1)S(1)}, u32[]{:S(2)}, u32[]{:S(2)}) async-start(bf16[8,1,2,256,128]{4,3,2,1,0:T(8,128)(2,1)} %right_products.9), calls=%async_computation.4 | async-start | bytes 2097152 | tf_op jit(solution)/shard_map/all_to_all | solution.py:284
  232.2 19.5 %all-to-all-start.5 = ((bf16[8,1,2,256,128]{4,3,2,1,0:T(8,128)(2,1)}), bf16[8,1,2,256,128]{4,3,2,1,0:T(8,128)(2,1)S(1)}, u32[]{:S(2)}, u32[]{:S(2)}) async-start(bf16[8,1,2,256,128]{4,3,2,1,0:T(8,128)(2,1)} %right_products.8), calls=%async_computation.6 | async-start | bytes 2097152 | tf_op jit(solution)/shard_map/all_to_all | solution.py:284
  237.1 47.0 %reduce-scatter.2.cloned.1.call-start = ((), (), s32[]{:S(2)}) async-start(), calls=%async_computation.8 | async-start | bytes 1179648 | tf_op jit(solution)/shard_map/reduce_scatter | solution.py:348
  237.1 1.2 copy-start.1
  238.3 1.2 copy-start.3
  251.7 1.2 copy-start.4
  256.9 11.6 %copy-start.12 = (s32[4]{0:T(128)S(1)}, s32[4]{0:T(128)}, u32[]{:S(2)}) copy-start(s32[4]{0:T(128)} %rows_ref.1) | copy-start | bytes 52
  256.9 3.8 %collective-permute-start.5 = (bf16[8,16,16,128]{3,2,1,0:T(8,128)(2,1)S(1)}, bf16[8,16,16,128]{3,2,1,0:T(8,128)(2,1)S(1)}, u32[]{:S(2)}, u32[]{:S(2)}) collective-permute-start(bf16[8,16,16,128]{3,2,1,0:T(8,128)(2,1)S(1)} %get-tuple-element.34), channel_id=1, source_target_pairs={{0,1},{1,0},{2,3},{3,2},{4,5},{5,4},{6,7},{7,6},{8,9},{9,8},{10,11... | collective-permute-start | bytes 1572872 | tf_op jit(solution)/shard_map/ppermute | solution.py:268
  261.7 32.1 %all-to-all-start.6 = ((bf16[8,16,16,128]{3,2,1,0:T(8,128)(2,1)}), bf16[8,16,16,128]{3,2,1,0:T(8,128)(2,1)S(1)}, u32[]{:S(2)}, u32[]{:S(2)}) async-start(bf16[8,16,16,128]{3,2,1,0:T(8,128)(2,1)} %add_convert_fusion), calls=%async_computation.7 | async-start | bytes 1048576 | tf_op jit(solution)/shard_map/all_to_all | solution.py:355
  284.9 8.1 %collective-permute-start.4 = (bf16[16,16,128]{2,1,0:T(8,128)(2,1)S(1)}, bf16[16,16,128]{2,1,0:T(8,128)(2,1)S(1)}, u32[]{:S(2)}, u32[]{:S(2)}) collective-permute-start(bf16[16,16,128]{2,1,0:T(8,128)(2,1)S(1)} %dynamic-slice_bitcast_fusion), channel_id=1, source_target_pairs={{0,1},{1,0},{2,3},{3,2},{4,5},{5,4},{6,7},{7,6},{8,9},{9,8},{10,11... | collective-permute-start | bytes 196616 | tf_op jit(solution)/shard_map/ppermute | solution.py:268
  (5 other events, 4.6 us)
Sparse Core Ops, SparseCore 0:
  39.4 40.1 all-gather.9
  81.7 43.5 all-gather.7
  153.9 40.4 all-gather.11
  245.0 38.9 reduce-scatter.1

commit v10 on v8

--- a/solution.py
+++ b/solution.py
@@ -118,7 +118,7 @@
 
 
 def right_kernel(place_ref, targets_ref, slices_ref, *refs):
-    envs, (out_ref, moved_ref, env_ref) = refs[:-3], refs[-3:]
+    envs, (out_ref, moved_ref, env_ref, slot_ref) = refs[:-4], refs[-4:]
     group, _, terms, extent, width = out_ref.shape
     sectors = env_ref.shape[0]
     depth, count = slices_ref.shape[0], slices_ref.shape[2] - 1
@@ -146,11 +146,11 @@
             for term in range(terms):
                 owner = targets_ref[turn, term * count + sector * per_sector + place]
 
-                @pl.when(lax.div(owner, group) == place_ref[0])
-                def _(place=place, term=term, owner=owner):
-                    out_ref[lax.rem(owner, group), 0, term] = product[
-                        place * extent : (place + 1) * extent, term * width : (term + 1) * width
-                    ]
+                here = lax.div(owner, group) == place_ref[0]
+                slot_ref[jnp.where(here, lax.rem(owner, group), group), term] = product[
+                    place * extent : (place + 1) * extent, term * width : (term + 1) * width
+                ]
+    out_ref[:, 0] = slot_ref[:group]
 
 
 def right_products(place, targets, slices, envs, group, chunk, width):
@@ -176,6 +176,7 @@
             scratch_shapes=[
                 pltpu.VMEM((2, per_sector * extent, extent), jnp.bfloat16),
                 pltpu.VMEM((sectors, extent, terms * width), jnp.bfloat16),
+                pltpu.VMEM((group + 1, terms, extent, width), jnp.bfloat16),
             ],
         ),
         out_shape=pltpu.HBM(shape, jnp.bfloat16),
@@ -303,6 +304,10 @@
 
     buffer = spread(depth_index.reshape(1), right_home, term_links, sector_rows, wavefunction, slots)
     arrived = lax.all_to_all(buffer, REMAP, 0, 0, tiled=True)
+    parts = [right_env[..., at : at + LANES] for at in range(0, width, LANES)]
+    above, below = shift(parts[0], "zh", -1), shift(parts[0], "zh", 1)
+    arrived, above, below = lax.optimization_barrier((arrived, above, below))
+    across = shift(above[:1], "zh", -1), shift(below[1:], "zh", 1)
     labels = arrived[:, 2 * SHARE, : 1 + terms].astype(jnp.int32)
     match = labels.T[:, None, :] == jnp.arange(count, dtype=jnp.int32)[None, :, None]
     source = jnp.sum(jnp.where(match, jnp.arange(slots, dtype=jnp.int32), 0), axis=2)
@@ -310,12 +315,11 @@
     peers = lax.rem(source[1:] + moved_by, slots)
     ordered = order(source[0], term_links, sector_cols, arrived)
 
-    parts = [right_env[..., at : at + LANES] for at in range(0, width, LANES)]
-    above, below = shift(parts[0], "zh", -1), shift(parts[0], "zh", 1)
-    across = shift(above[:1], "zh", -1), shift(below[1:], "zh", 1)
-
     slices = lax.all_gather(ordered[None], DEPTH)
     around = lax.all_gather(ordered, "zh")
+    around, second = lax.optimization_barrier((around, parts[1]))
+    next_above, next_below = shift(second, "zh", -1), shift(second, "zh", 1)
+    next_across = shift(next_above[:1], "zh", -1), shift(next_below[1:], "zh", 1)
     others = lax.dynamic_slice_in_dim(jnp.concatenate([around, around]), layer + 1, layers - 1)
     far_targets = others[:, count, 0, : terms * count].astype(jnp.int32)
     far_targets = lax.rem(far_targets + moved_by, slots)
@@ -324,16 +328,13 @@
     targets = lax.rem((term_links // count).reshape(1, terms * count) + moved_by, slots)
     envs = [[(right_env, term) for term in range(terms)]]
     products = right_products(place, targets, slices, envs, group, 0, width)
-    products, above, below = lax.optimization_barrier((products, above, below))
+    after = products, next_above, next_below
+    products, next_above, next_below = lax.optimization_barrier(after)
     own = exchange(products)
 
-    across, second = lax.optimization_barrier((across, parts[1]))
-    next_above, next_below = shift(second, "zh", -1), shift(second, "zh", 1)
-    next_across = shift(next_above[:1], "zh", -1), shift(next_below[1:], "zh", 1)
-
     products = far_products(place, far_targets, far_slices, above, below, across, group)
-    after = products, far_slices, next_above, next_below
-    products, far_slices, next_above, next_below = lax.optimization_barrier(after)
+    after = products, far_slices, next_across
+    products, far_slices, next_across = lax.optimization_barrier(after)
     far = exchange(products)
     partial = left_products(place, peers, own, far, left_env, 0, False)
     partial = partial.reshape((-1, 2) + partial.shape[1:])

time: 287 us -> 290 us (1.010)
  blocking collectives: 42.8 us -> 16.7 us
  starting transfers between devices: 54.1 us -> 71 us
  waiting for transfers between devices: 125 us -> 138 us
  Pallas kernels: 39.6 us -> 35.3 us
  local copies, waits for them, and re-layouts: 6.42 us -> 9.49 us
    all_to_all x1 -> x0, blocking collectives: 27.6 us -> none  [local(): arrived = lax.all_to_all(buffer, REMAP, 0, 0, tiled=True)]
    all_to_all x3, waiting for transfers between devices: 31.7 us -> 58.8 us  [exchange(): lax.all_to_all(products, axes, 0, 0, axis_index_groups=groups, tiled=True)]
    ppermute x10, waiting for transfers between devices: 57.8 us -> 39.4 us  [shift(): lax.ppermute(array, axis, [(i, (i + step) % size) for i in range(size)])]
    all_to_all x0 -> x1, starting transfers between devices: none -> 13.7 us  [local(): arrived = lax.all_to_all(buffer, REMAP, 0, 0, tiled=True)]
    all_to_all x3, starting transfers between devices: 16.5 us -> 22 us  [exchange(): lax.all_to_all(products, axes, 0, 0, axis_index_groups=groups, tiled=True)]
    pallas_call x3, Pallas kernels: 25.2 us -> 20.8 us  [right_products(): pl.pallas_call(right_kernel, grid_spec=pltpu.PrefetchScalarGridSpec(num_s...]
    all_to_all x1, starting transfers between devices: 7.26 us -> 4.18 us  [local(): shares = lax.all_to_all(pair.astype(jnp.bfloat16), 'y', 0, 0, tiled=True)]
  transfers between devices with their start and end apart: 17 -> 18, of which waited for: 10 -> 8; matrix products, arithmetic and copies ran while one was open for 2% -> 3% of each run, Pallas kernels for 12% -> 11%
where the time goes in v10:
time: 290 us; the launch traced here: 289 us
  waiting for transfers between devices  138 us (48%)
  starting transfers between devices  71 us (24%)
  Pallas kernels  35.3 us (12%)
  blocking collectives  16.7 us (6%)
  between operations  13.4 us (5%)
  local copies, waits for them, and re-layouts  9.49 us (3%)
  other arithmetic  4.64 us (2%)
    all_to_all x3, waiting for transfers between devices, exchange(): lax.all_to_all(products, axes, 0, 0, axis_index_groups=groups, tiled=True)  58.8 us
    ppermute x10, waiting for transfers between devices, shift(): lax.ppermute(array, axis, [(i, (i + step) % size) for i in range(size)])  39.4 us
    ppermute x10, starting transfers between devices, shift(): lax.ppermute(array, axis, [(i, (i + step) % size) for i in range(size)])  31.1 us
    all_to_all x3, starting transfers between devices, exchange(): lax.all_to_all(products, axes, 0, 0, axis_index_groups=groups, tiled=True)  22 us
    pallas_call x3, Pallas kernels, right_products(): pl.pallas_call(right_kernel, grid_spec=pltpu.PrefetchScalarGridSpec(num_s...  20.8 us
    all_gather x1, waiting for transfers between devices, local(): slices = lax.all_gather(ordered[None], DEPTH)  18.7 us
    all_gather x1, blocking collectives, local(): around = lax.all_gather(ordered, 'zh')  16.7 us
    all_to_all x1, waiting for transfers between devices, local(): shares = lax.all_to_all(pair.astype(jnp.bfloat16), 'y', 0, 0, tiled=True)  14.3 us
  transfers between devices with their start and end apart: 18, of which 8 were waited for; matrix products, arithmetic and copies ran while one was open for 3% of the time, Pallas kernels for 11%

profile of v10, /device:TPU:1, one launch (start us, length us, event | category | flops | bytes accessed | tf_op | source)
XLA Modules:
  0.0 288.9 jit_solution(1862460188425556174)
XLA Ops:
  6.5 2.7 spread_blocks.1
  9.3 13.7 %all-to-all-start = ((bf16[32,48,128]{2,1,0:T(8,128)(2,1)}), bf16[32,48,128]{2,1,0:T(8,128)(2,1)S(1)}, u32[]{:S(2)}, u32[]{:S(2)}) async-start(bf16[32,48,128]{2,1,0:T(8,128)(2,1)} %spread_blocks.1), calls=%async_computation | async-start | bytes 786432 | tf_op jit(solution)/shard_map/all_to_all | solution.py:306
  24.2 5.3 %collective-permute-start = (bf16[2,4,256,128]{3,2,1,0:T(8,128)(2,1)S(1)}, bf16[2,4,256,128]{3,2,1,0:T(8,128)(2,1)S(1)}, u32[]{:S(2)}, u32[]{:S(2)}) collective-permute-start(bf16[2,4,256,128]{3,2,1,0:T(8,128)(2,1)S(1)} %get-tuple-element.34), channel_id=1, source_target_pairs={{0,384},{128,0},{256,128},{384,256},{1,385},{129,1},{257,129},{385... | collective-permute-start | bytes 1572872 | tf_op jit(solution)/shard_map/ppermute | solution.py:273
  31.4 24.8 %collective-permute-done.refs_0_.refs_1_ = bf16[2,4,256,128]{3,2,1,0:T(8,128)(2,1)S(1)} collective-permute-done((bf16[2,4,256,128]{3,2,1,0:T(8,128)(2,1)S(1)}, bf16[2,4,256,128]{3,2,1,0:T(8,128)(2,1)S(1)}, u32[]{:S(2)}, u32[]{:S(2)}) %collective-permute-start) | collective-permute-done | bytes 524320 | tf_op jit(solution)/shard_map/ppermute | solution.py:273
  58.8 16.7 %all-gather.1 = bf16[68,32,128]{2,1,0:T(8,128)(2,1)S(1)} all-gather(bf16[17,32,128]{2,1,0:T(8,128)(2,1)} %order_blocks.1), channel_id=3, replica_groups=mesh['zh'=4,'zl'=2,'x'=4,'y'=8,'core'=2] {'zh'}, dimensions={0}, use_global_device_ids=true | all-gather | bytes 696320 | tf_op jit(solution)/shard_map/all_gather | solution.py:319
  76.5 2.8 collective-permute-start.2
  79.3 3.4 %collective-permute-start.3 = (bf16[2,4,256,128]{3,2,1,0:T(8,128)(2,1)}, bf16[2,4,256,128]{3,2,1,0:T(8,128)(2,1)}, u32[]{:S(2)}, u32[]{:S(2)}) collective-permute-start(bf16[2,4,256,128]{3,2,1,0:T(8,128)(2,1)} %get-tuple-element.20), channel_id=1, source_target_pairs={{0,128},{128,256},{256,384},{384,0},{1,129},{129,257},{257,385},{3... | collective-permute-start | bytes 1572872 | tf_op jit(solution)/shard_map/ppermute | solution.py:273
  82.9 18.7 %all-gather.6.cloned.1.call-done = bf16[272,32,128]{2,1,0:T(8,128)(2,1)} async-done(((bf16[17,32,128]{2,1,0:T(8,128)(2,1)}), bf16[272,32,128]{2,1,0:T(8,128)(2,1)}) %all-gather.6.cloned.1.call-update) | async-done | bytes 2228240 | tf_op jit(solution)/shard_map/all_gather | solution.py:318
  101.6 5.0 %right_products.3 = bf16[8,1,2,256,256]{4,3,2,1,0:T(8,128)(2,1)} custom-call(s32[3]{0:T(128)S(1)} %pad_add_fusion.place_ref, s32[1,32]{1,0:T(1,128)S(1)} %compare_select_fusion.targets_ref, bf16[16,1,17,32,128]{4,3,2,1,0:T(8,128)(2,1)} %bitcast.23, bf16[2,4,256,256]{3,2,1,0:T(8,128)(2,1)S(1)} %copy-done, bf16[2,4,256,256]{3,2,1,0:T(8,128)(2,1)S(1)} %copy-done), custom_call_target="tpu_custom_call" | custom-call | tf_op jit(solution)/shard_map/right_products/pallas_call | solution.py:163
  106.7 7.8 %all-to-all-start.1 = ((bf16[8,1,2,256,256]{4,3,2,1,0:T(8,128)(2,1)}), bf16[8,1,2,256,256]{4,3,2,1,0:T(8,128)(2,1)S(1)}, u32[]{:S(2)}, u32[]{:S(2)}) async-start(bf16[8,1,2,256,256]{4,3,2,1,0:T(8,128)(2,1)} %right_products.3), calls=%async_computation.1 | async-start | bytes 4194304 | tf_op jit(solution)/shard_map/all_to_all | solution.py:289
  114.5 3.7 %collective-permute-start.4 = (bf16[1,4,256,128]{3,2,1,0:T(8,128)(2,1)S(1)}, bf16[1,4,256,128]{3,2,1,0:T(8,128)(2,1)S(1)}, u32[]{:S(2)}, u32[]{:S(2)}) collective-permute-start(bf16[1,4,256,128]{3,2,1,0:T(8,128)(2,1)S(1)} %slice.36), channel_id=1, source_target_pairs={{0,384},{128,0},{256,128},{384,256},{1,385},{129,1},{257,129},{385... | collective-permute-start | bytes 786440 | tf_op jit(solution)/shard_map/ppermute | solution.py:273
  122.4 4.9 %collective-permute-start.6 = (bf16[1,4,256,128]{3,2,1,0:T(8,128)(2,1)}, bf16[1,4,256,128]{3,2,1,0:T(8,128)(2,1)S(1)}, u32[]{:S(2)}, u32[]{:S(2)}) collective-permute-start(bf16[1,4,256,128]{3,2,1,0:T(8,128)(2,1)} %slice.41), channel_id=1, source_target_pairs={{0,384},{128,0},{256,128},{384,256},{1,385},{129,1},{257,129},{385... | collective-permute-start | bytes 786440 | tf_op jit(solution)/shard_map/ppermute | solution.py:273
  131.6 13.0 %collective-permute-done.4.refs_2_ = bf16[1,4,256,128]{3,2,1,0:T(8,128)(2,1)S(1)} collective-permute-done((bf16[1,4,256,128]{3,2,1,0:T(8,128)(2,1)S(1)}, bf16[1,4,256,128]{3,2,1,0:T(8,128)(2,1)S(1)}, u32[]{:S(2)}, u32[]{:S(2)}) %collective-permute-start.4) | collective-permute-done | bytes 262176 | tf_op jit(solution)/shard_map/ppermute | solution.py:273
  146.0 7.0 %all-gather.8.cloned.1.call-done = bf16[48,17,32,128]{3,2,1,0:T(8,128)(2,1)} async-done(((bf16[3,17,32,128]{3,2,1,0:T(8,128)(2,1)}), bf16[48,17,32,128]{3,2,1,0:T(8,128)(2,1)}) %all-gather.8.cloned.1.call-update) | async-done | bytes 6684688 | tf_op jit(solution)/shard_map/all_gather | solution.py:326
  154.9 7.7 %right_products.4 = bf16[8,3,2,256,128]{4,3,2,1,0:T(8,128)(2,1)} custom-call(s32[3]{0:T(128)S(1)} %pad_add_fusion.place_ref, s32[3,32]{1,0:T(4,128)S(1)} %negate_select_fusion.targets_ref, bf16[16,3,17,32,128]{4,3,2,1,0:T(8,128)(2,1)} %bitcast.20, bf16[2,4,256,128]{3,2,1,0:T(8,128)(2,1)S(1)} %collective-permute-done.refs_0_.refs_1_, ...), custom_call_target="tpu_custom_call" | custom-call | tf_op jit(solution)/shard_map/right_products/pallas_call | solution.py:163
  162.7 8.0 %all-to-all-start.2 = ((bf16[8,3,2,256,128]{4,3,2,1,0:T(8,128)(2,1)}), bf16[8,3,2,256,128]{4,3,2,1,0:T(8,128)(2,1)}, u32[]{:S(2)}, u32[]{:S(2)}) async-start(bf16[8,3,2,256,128]{4,3,2,1,0:T(8,128)(2,1)} %right_products.4), calls=%async_computation.2 | async-start | bytes 6291456 | tf_op jit(solution)/shard_map/all_to_all | solution.py:289
  170.7 8.0 %right_products.5 = bf16[8,3,2,256,128]{4,3,2,1,0:T(8,128)(2,1)} custom-call(s32[3]{0:T(128)S(1)} %pad_add_fusion.place_ref, s32[3,32]{1,0:T(4,128)S(1)} %negate_select_fusion.targets_ref, bf16[16,3,17,32,128]{4,3,2,1,0:T(8,128)(2,1)} %bitcast.21, bf16[2,4,256,128]{3,2,1,0:T(8,128)(2,1)} %collective-permute-done.2.refs_0_.refs_1_, ...), custom_call_target="tpu_custom_call" | custom-call | tf_op jit(solution)/shard_map/right_products/pallas_call | solution.py:163
  178.7 27.7 %all-to-all-done.2.far_ref = bf16[8,3,2,256,128]{4,3,2,1,0:T(8,128)(2,1)} async-done(((bf16[8,3,2,256,128]{4,3,2,1,0:T(8,128)(2,1)}), bf16[8,3,2,256,128]{4,3,2,1,0:T(8,128)(2,1)}, u32[]{:S(2)}, u32[]{:S(2)}) %all-to-all-start.2) | async-done | bytes 3145760 | tf_op jit(solution)/shard_map/all_to_all | solution.py:289
  206.4 6.2 %all-to-all-start.3 = ((bf16[8,3,2,256,128]{4,3,2,1,0:T(8,128)(2,1)}), bf16[8,3,2,256,128]{4,3,2,1,0:T(8,128)(2,1)}, u32[]{:S(2)}, u32[]{:S(2)}) async-start(bf16[8,3,2,256,128]{4,3,2,1,0:T(8,128)(2,1)} %right_products.5), calls=%async_computation.4 | async-start | bytes 6291456 | tf_op jit(solution)/shard_map/all_to_all | solution.py:289
  212.6 5.4 %left_products.2 = bf16[16,16,16,128]{3,2,1,0:T(8,128)(2,1)} custom-call(s32[3]{0:T(128)S(1)} %pad_add_fusion.place_ref, s32[2,16]{1,0:T(2,128)S(1)} %compare_select_fusion.2.from_ref, bf16[8,1,2,256,256]{4,3,2,1,0:T(8,128)(2,1)S(1)} %all-to-all-done.1.near_ref, bf16[8,3,2,256,128]{4,3,2,1,0:T(8,128)(2,1)} %all-to-all-done.2.far_ref, ...), custom_call_target="tpu_custom_call" | custom-call | tf_op jit(solution)/shard_map/left_products/pallas_call | solution.py:253
  218.0 31.1 %all-to-all-done.3.far_ref = bf16[8,3,2,256,128]{4,3,2,1,0:T(8,128)(2,1)} async-done(((bf16[8,3,2,256,128]{4,3,2,1,0:T(8,128)(2,1)}), bf16[8,3,2,256,128]{4,3,2,1,0:T(8,128)(2,1)}, u32[]{:S(2)}, u32[]{:S(2)}) %all-to-all-start.3) | async-done | bytes 3145760 | tf_op jit(solution)/shard_map/all_to_all | solution.py:289
  249.1 4.6 %left_products.3 = (bf16[8,16,16,128]{3,2,1,0:T(8,128)(2,1)S(1)}, bf16[8,16,16,128]{3,2,1,0:T(8,128)(2,1)S(1)}) custom-call(s32[3]{0:T(128)S(1)} %pad_add_fusion.place_ref, s32[2,16]{1,0:T(2,128)S(1)} %compare_select_fusion.2.from_ref, bf16[8,1,2,256,256]{4,3,2,1,0:T(8,128)(2,1)S(1)} %all-to-all-done.1.near_ref, ...), custom_call_target="tpu_custom_call" | custom-call | tf_op jit(solution)/shard_map/left_products/pallas_call | solution.py:253
  258.5 4.2 %all-to-all-start.4 = ((bf16[8,16,16,128]{3,2,1,0:T(8,128)(2,1)}), bf16[8,16,16,128]{3,2,1,0:T(8,128)(2,1)S(1)}, u32[]{:S(2)}, u32[]{:S(2)}) async-start(bf16[8,16,16,128]{3,2,1,0:T(8,128)(2,1)} %add_convert_fusion), calls=%async_computation.5 | async-start | bytes 1048576 | tf_op jit(solution)/shard_map/all_to_all | solution.py:352
  266.3 14.3 %all-to-all-done.4 = bf16[8,16,16,128]{3,2,1,0:T(8,128)(2,1)S(1)} async-done(((bf16[8,16,16,128]{3,2,1,0:T(8,128)(2,1)}), bf16[8,16,16,128]{3,2,1,0:T(8,128)(2,1)S(1)}, u32[]{:S(2)}, u32[]{:S(2)}) %all-to-all-start.4) | async-done | bytes 524320 | tf_op jit(solution)/shard_map/all_to_all | solution.py:352
  (67 shorter events, 28.7 us)
Async XLA Ops:
  6.5 16.5 %copy-start = (bf16[2,4,256,256]{3,2,1,0:T(8,128)(2,1)S(1)}, bf16[2,4,256,256]{3,2,1,0:T(8,128)(2,1)}, u32[]{:S(2)}) copy-start(bf16[2,4,256,256]{3,2,1,0:T(8,128)(2,1)} %refs_1_.1) | copy-start | bytes 3145732
  9.3 46.9 %all-to-all-start = ((bf16[32,48,128]{2,1,0:T(8,128)(2,1)}), bf16[32,48,128]{2,1,0:T(8,128)(2,1)S(1)}, u32[]{:S(2)}, u32[]{:S(2)}) async-start(bf16[32,48,128]{2,1,0:T(8,128)(2,1)} %spread_blocks.1), calls=%async_computation | async-start | bytes 786432 | tf_op jit(solution)/shard_map/all_to_all | solution.py:306
  23.0 59.7 %copy-start.7 = (s32[2,16]{1,0:T(2,128)S(1)}, s32[2,16]{1,0:T(2,128)}, u32[]{:S(2)}) copy-start(s32[2,16]{1,0:T(2,128)} %links_ref.3) | copy-start | bytes 388
  23.0 78.6 %all-gather.6.cloned.1.call-start = ((), (), s32[]{:S(2)}) async-start(), calls=%async_computation.7 | async-start | bytes 2367488 | tf_op jit(solution)/shard_map/all_gather | solution.py:318
  24.2 32.0 %collective-permute-start = (bf16[2,4,256,128]{3,2,1,0:T(8,128)(2,1)S(1)}, bf16[2,4,256,128]{3,2,1,0:T(8,128)(2,1)S(1)}, u32[]{:S(2)}, u32[]{:S(2)}) collective-permute-start(bf16[2,4,256,128]{3,2,1,0:T(8,128)(2,1)S(1)} %get-tuple-element.34), channel_id=1, source_target_pairs={{0,384},{128,0},{256,128},{384,256},{1,385},{129,1},{257,129},{385... | collective-permute-start | bytes 1572872 | tf_op jit(solution)/shard_map/ppermute | solution.py:273
  29.4 26.7 %collective-permute-start.1 = (bf16[2,4,256,128]{3,2,1,0:T(8,128)(2,1)S(1)}, bf16[2,4,256,128]{3,2,1,0:T(8,128)(2,1)S(1)}, u32[]{:S(2)}, u32[]{:S(2)}) collective-permute-start(bf16[2,4,256,128]{3,2,1,0:T(8,128)(2,1)S(1)} %get-tuple-element.34), channel_id=1, source_target_pairs={{0,128},{128,256},{256,384},{384,0},{1,129},{129,257},{257,385},{3... | collective-permute-start | bytes 1572872 | tf_op jit(solution)/shard_map/ppermute | solution.py:273
  58.8 94.2 %all-gather.8.cloned.1.call-start = ((), (), s32[]{:S(2)}) async-start(), calls=%async_computation.8 | async-start | bytes 7102464 | tf_op jit(solution)/shard_map/all_gather | solution.py:326
  76.5 30.1 %collective-permute-start.2 = (bf16[2,4,256,128]{3,2,1,0:T(8,128)(2,1)}, bf16[2,4,256,128]{3,2,1,0:T(8,128)(2,1)}, u32[]{:S(2)}, u32[]{:S(2)}) collective-permute-start(bf16[2,4,256,128]{3,2,1,0:T(8,128)(2,1)} %get-tuple-element.20), channel_id=1, source_target_pairs={{0,384},{128,0},{256,128},{384,256},{1,385},{129,1},{257,129},{385... | collective-permute-start | bytes 1572872 | tf_op jit(solution)/shard_map/ppermute | solution.py:273
  79.3 27.3 %collective-permute-start.3 = (bf16[2,4,256,128]{3,2,1,0:T(8,128)(2,1)}, bf16[2,4,256,128]{3,2,1,0:T(8,128)(2,1)}, u32[]{:S(2)}, u32[]{:S(2)}) collective-permute-start(bf16[2,4,256,128]{3,2,1,0:T(8,128)(2,1)} %get-tuple-element.20), channel_id=1, source_target_pairs={{0,128},{128,256},{256,384},{384,0},{1,129},{129,257},{257,385},{3... | collective-permute-start | bytes 1572872 | tf_op jit(solution)/shard_map/ppermute | solution.py:273
  106.7 56.0 %all-to-all-start.1 = ((bf16[8,1,2,256,256]{4,3,2,1,0:T(8,128)(2,1)}), bf16[8,1,2,256,256]{4,3,2,1,0:T(8,128)(2,1)S(1)}, u32[]{:S(2)}, u32[]{:S(2)}) async-start(bf16[8,1,2,256,256]{4,3,2,1,0:T(8,128)(2,1)} %right_products.3), calls=%async_computation.1 | async-start | bytes 4194304 | tf_op jit(solution)/shard_map/all_to_all | solution.py:289
  114.5 30.1 %collective-permute-start.4 = (bf16[1,4,256,128]{3,2,1,0:T(8,128)(2,1)S(1)}, bf16[1,4,256,128]{3,2,1,0:T(8,128)(2,1)S(1)}, u32[]{:S(2)}, u32[]{:S(2)}) collective-permute-start(bf16[1,4,256,128]{3,2,1,0:T(8,128)(2,1)S(1)} %slice.36), channel_id=1, source_target_pairs={{0,384},{128,0},{256,128},{384,256},{1,385},{129,1},{257,129},{385... | collective-permute-start | bytes 786440 | tf_op jit(solution)/shard_map/ppermute | solution.py:273
  118.2 27.1 %collective-permute-start.5 = (bf16[1,4,256,128]{3,2,1,0:T(8,128)(2,1)S(1)}, bf16[1,4,256,128]{3,2,1,0:T(8,128)(2,1)S(1)}, u32[]{:S(2)}, u32[]{:S(2)}) collective-permute-start(bf16[1,4,256,128]{3,2,1,0:T(8,128)(2,1)S(1)} %slice.37), channel_id=1, source_target_pairs={{0,128},{128,256},{256,384},{384,0},{1,129},{129,257},{257,385},{3... | collective-permute-start | bytes 786440 | tf_op jit(solution)/shard_map/ppermute | solution.py:273
  122.4 40.3 %collective-permute-start.6 = (bf16[1,4,256,128]{3,2,1,0:T(8,128)(2,1)}, bf16[1,4,256,128]{3,2,1,0:T(8,128)(2,1)S(1)}, u32[]{:S(2)}, u32[]{:S(2)}) collective-permute-start(bf16[1,4,256,128]{3,2,1,0:T(8,128)(2,1)} %slice.41), channel_id=1, source_target_pairs={{0,384},{128,0},{256,128},{384,256},{1,385},{129,1},{257,129},{385... | collective-permute-start | bytes 786440 | tf_op jit(solution)/shard_map/ppermute | solution.py:273
  128.9 33.7 %collective-permute-start.7 = (bf16[1,4,256,128]{3,2,1,0:T(8,128)(2,1)}, bf16[1,4,256,128]{3,2,1,0:T(8,128)(2,1)}, u32[]{:S(2)}, u32[]{:S(2)}) collective-permute-start(bf16[1,4,256,128]{3,2,1,0:T(8,128)(2,1)} %slice.42), channel_id=1, source_target_pairs={{0,128},{128,256},{256,384},{384,0},{1,129},{129,257},{257,385},{3... | collective-permute-start | bytes 786440 | tf_op jit(solution)/shard_map/ppermute | solution.py:273
  153.0 0.9 copy-start.3
  154.0 0.9 copy-start.5
  162.7 43.7 %all-to-all-start.2 = ((bf16[8,3,2,256,128]{4,3,2,1,0:T(8,128)(2,1)}), bf16[8,3,2,256,128]{4,3,2,1,0:T(8,128)(2,1)}, u32[]{:S(2)}, u32[]{:S(2)}) async-start(bf16[8,3,2,256,128]{4,3,2,1,0:T(8,128)(2,1)} %right_products.4), calls=%async_computation.2 | async-start | bytes 6291456 | tf_op jit(solution)/shard_map/all_to_all | solution.py:289
  178.7 33.9 %copy-start.1 = (bf16[2,4,256,256]{3,2,1,0:T(8,128)(2,1)S(1)}, bf16[2,4,256,256]{3,2,1,0:T(8,128)(2,1)}, u32[]{:S(2)}) copy-start(bf16[2,4,256,256]{3,2,1,0:T(8,128)(2,1)} %env_ref.3) | copy-start | bytes 3145732
  206.4 42.7 %all-to-all-start.3 = ((bf16[8,3,2,256,128]{4,3,2,1,0:T(8,128)(2,1)}), bf16[8,3,2,256,128]{4,3,2,1,0:T(8,128)(2,1)}, u32[]{:S(2)}, u32[]{:S(2)}) async-start(bf16[8,3,2,256,128]{4,3,2,1,0:T(8,128)(2,1)} %right_products.5), calls=%async_computation.4 | async-start | bytes 6291456 | tf_op jit(solution)/shard_map/all_to_all | solution.py:289
  212.6 50.4 %reduce-scatter.2.cloned.1.call-start = ((), (), s32[]{:S(2)}) async-start(), calls=%async_computation.6 | async-start | bytes 1179648 | tf_op jit(solution)/shard_map/reduce_scatter | solution.py:341
  253.7 8.9 %copy-start.8 = (s32[4]{0:T(128)S(1)}, s32[4]{0:T(128)}, u32[]{:S(2)}) copy-start(s32[4]{0:T(128)} %rows_ref.1) | copy-start | bytes 52
  253.8 3.8 %collective-permute-start.9 = (bf16[8,16,16,128]{3,2,1,0:T(8,128)(2,1)S(1)}, bf16[8,16,16,128]{3,2,1,0:T(8,128)(2,1)S(1)}, u32[]{:S(2)}, u32[]{:S(2)}) collective-permute-start(bf16[8,16,16,128]{3,2,1,0:T(8,128)(2,1)S(1)} %get-tuple-element.32), channel_id=1, source_target_pairs={{0,1},{1,0},{2,3},{3,2},{4,5},{5,4},{6,7},{7,6},{8,9},{9,8},{10,11... | collective-permute-start | bytes 1572872 | tf_op jit(solution)/shard_map/ppermute | solution.py:273
  258.5 22.1 %all-to-all-start.4 = ((bf16[8,16,16,128]{3,2,1,0:T(8,128)(2,1)}), bf16[8,16,16,128]{3,2,1,0:T(8,128)(2,1)S(1)}, u32[]{:S(2)}, u32[]{:S(2)}) async-start(bf16[8,16,16,128]{3,2,1,0:T(8,128)(2,1)} %add_convert_fusion), calls=%async_computation.5 | async-start | bytes 1048576 | tf_op jit(solution)/shard_map/all_to_all | solution.py:352
  263.8 16.9 %collective-permute-start.8 = (bf16[16,16,128]{2,1,0:T(8,128)(2,1)S(1)}, bf16[16,16,128]{2,1,0:T(8,128)(2,1)S(1)}, u32[]{:S(2)}, u32[]{:S(2)}) collective-permute-start(bf16[16,16,128]{2,1,0:T(8,128)(2,1)S(1)} %dynamic-slice_bitcast_fusion), channel_id=1, source_target_pairs={{0,1},{1,0},{2,3},{3,2},{4,5},{5,4},{6,7},{7,6},{8,9},{9,8},{10,11... | collective-permute-start | bytes 196616 | tf_op jit(solution)/shard_map/ppermute | solution.py:273
  (3 other events, 2.2 us)
Sparse Core Ops, SparseCore 0:
  58.9 42.6 all-gather.5
  103.7 49.2 all-gather.7
  218.1 33.8 reduce-scatter.1

commit v11 on v10

--- a/solution.py
+++ b/solution.py
@@ -185,15 +185,6 @@
     )(place, targets, in_hbm(slices), *[array for array, _ in flat])
 
 
-def far_products(place, targets, slices, above, below, across, group):
-    envs = [
-        [(above, 0), (above, 1)],
-        [(across[0], 0), (across[1], 0)],
-        [(below, 0), (below, 1)],
-    ]
-    return right_products(place, targets, slices, envs, group, 0, LANES)
-
-
 def left_partials(place_ref, from_ref, near_ref, far_ref, env_ref, placed_ref):
     terms, count = from_ref.shape
     group, near, _, extent, width = near_ref.shape
@@ -304,10 +295,10 @@
 
     buffer = spread(depth_index.reshape(1), right_home, term_links, sector_rows, wavefunction, slots)
     arrived = lax.all_to_all(buffer, REMAP, 0, 0, tiled=True)
-    parts = [right_env[..., at : at + LANES] for at in range(0, width, LANES)]
-    above, below = shift(parts[0], "zh", -1), shift(parts[0], "zh", 1)
+    first, second = right_env[..., :LANES], right_env[..., LANES:]
+    early, rest = first[:1], jnp.concatenate([first[1:], second])
+    above, below = shift(early, "zh", -1), shift(early, "zh", 1)
     arrived, above, below = lax.optimization_barrier((arrived, above, below))
-    across = shift(above[:1], "zh", -1), shift(below[1:], "zh", 1)
     labels = arrived[:, 2 * SHARE, : 1 + terms].astype(jnp.int32)
     match = labels.T[:, None, :] == jnp.arange(count, dtype=jnp.int32)[None, :, None]
     source = jnp.sum(jnp.where(match, jnp.arange(slots, dtype=jnp.int32), 0), axis=2)
@@ -317,9 +308,12 @@
 
     slices = lax.all_gather(ordered[None], DEPTH)
     around = lax.all_gather(ordered, "zh")
-    around, second = lax.optimization_barrier((around, parts[1]))
-    next_above, next_below = shift(second, "zh", -1), shift(second, "zh", 1)
-    next_across = shift(next_above[:1], "zh", -1), shift(next_below[1:], "zh", 1)
+    around, rest = lax.optimization_barrier((around, rest))
+    rest_above, rest_below = shift(rest, "zh", -1), shift(rest, "zh", 1)
+    across = (
+        shift(jnp.concatenate([above, rest_above[1:2]]), "zh", -1),
+        shift(jnp.concatenate([rest_below[:1], rest_below[2:]]), "zh", 1),
+    )
     others = lax.dynamic_slice_in_dim(jnp.concatenate([around, around]), layer + 1, layers - 1)
     far_targets = others[:, count, 0, : terms * count].astype(jnp.int32)
     far_targets = lax.rem(far_targets + moved_by, slots)
@@ -328,13 +322,17 @@
     targets = lax.rem((term_links // count).reshape(1, terms * count) + moved_by, slots)
     envs = [[(right_env, term) for term in range(terms)]]
     products = right_products(place, targets, slices, envs, group, 0, width)
-    after = products, next_above, next_below
-    products, next_above, next_below = lax.optimization_barrier(after)
+    after = products, rest_above, rest_below
+    products, rest_above, rest_below = lax.optimization_barrier(after)
     own = exchange(products)
 
-    products = far_products(place, far_targets, far_slices, above, below, across, group)
-    after = products, far_slices, next_across
-    products, far_slices, next_across = lax.optimization_barrier(after)
+    envs = [
+        [(above, 0), (rest_above, 0)],
+        [(across[0], 0), (across[1], 0)],
+        [(below, 0), (rest_below, 0)],
+    ]
+    products = right_products(place, far_targets, far_slices, envs, group, 0, LANES)
+    far_slices, products = lax.optimization_barrier((far_slices, products))
     far = exchange(products)
     partial = left_products(place, peers, own, far, left_env, 0, False)
     partial = partial.reshape((-1, 2) + partial.shape[1:])
@@ -343,9 +341,12 @@
     kept = lax.dynamic_index_in_dim(summed, core_index, 0, False)
     pieces = [kept.astype(jnp.float32) + received.astype(jnp.float32)]
 
-    products = far_products(
-        place, far_targets, far_slices, next_above, next_below, next_across, group
-    )
+    envs = [
+        [(rest_above, 1), (rest_above, 2)],
+        [(across[0], 1), (across[1], 1)],
+        [(rest_below, 1), (rest_below, 2)],
+    ]
+    products = right_products(place, far_targets, far_slices, envs, group, 0, LANES)
     far = exchange(products)
     keep, send = left_products(place, peers, own, far, left_env, 1, True)
     pair = keep.astype(jnp.float32) + shift(send, "core", 1).astype(jnp.float32)

time: 290 us -> 291 us (level)
  waiting for transfers between devices: 138 us -> 144 us
  starting transfers between devices: 71 us -> 65.2 us
    ppermute x10 -> x8, waiting for transfers between devices: 39.4 us -> 53 us  [shift(): lax.ppermute(array, axis, [(i, (i + step) % size) for i in range(size)])]
    all_gather x1, waiting for transfers between devices: 7.04 us -> 0.01 us  [local(): far_slices = lax.all_gather(others, DEPTH)]
    ppermute x10 -> x8, starting transfers between devices: 31.1 us -> 24.8 us  [shift(): lax.ppermute(array, axis, [(i, (i + step) % size) for i in range(size)])]
    unnamed x18 -> x32, local copies, waits for them, and re-layouts: 3.32 us -> 7.07 us
    all_to_all x1, starting transfers between devices: 4.18 us -> 7.58 us  [local(): shares = lax.all_to_all(pair.astype(jnp.bfloat16), 'y', 0, 0, tiled=True)]
    slice x5, local copies, waits for them, and re-layouts: 4.47 us -> 1.1 us  [the longest x1 0.97 us: local(): rest_above[1:2]]
    all_to_all x3, starting transfers between devices: 22 us -> 18.9 us  [exchange(): lax.all_to_all(products, axes, 0, 0, axis_index_groups=groups, tiled=True)]
  transfers between devices with their start and end apart: 18 -> 16, of which waited for: 8 -> 11; matrix products, arithmetic and copies ran while one was open for 3% -> 2% of each run, Pallas kernels for 11% -> 11%
where the time goes in v11:
time: 291 us; the launch traced here: 290 us
  waiting for transfers between devices  144 us (49%)
  starting transfers between devices  65.2 us (22%)
  Pallas kernels  35 us (12%)
  blocking collectives  16.5 us (6%)
  between operations  13.4 us (5%)
  local copies, waits for them, and re-layouts  9.92 us (3%)
  other arithmetic  5.68 us (2%)
    all_to_all x3, waiting for transfers between devices, exchange(): lax.all_to_all(products, axes, 0, 0, axis_index_groups=groups, tiled=True)  59.1 us
    ppermute x8, waiting for transfers between devices, shift(): lax.ppermute(array, axis, [(i, (i + step) % size) for i in range(size)])  53 us
    ppermute x8, starting transfers between devices, shift(): lax.ppermute(array, axis, [(i, (i + step) % size) for i in range(size)])  24.8 us
    pallas_call x3, Pallas kernels, right_products(): pl.pallas_call(right_kernel, grid_spec=pltpu.PrefetchScalarGridSpec(num_s...  20.5 us
    all_to_all x3, starting transfers between devices, exchange(): lax.all_to_all(products, axes, 0, 0, axis_index_groups=groups, tiled=True)  18.9 us
    all_gather x1, waiting for transfers between devices, local(): slices = lax.all_gather(ordered[None], DEPTH)  17.6 us
    all_gather x1, blocking collectives, local(): around = lax.all_gather(ordered, 'zh')  16.5 us
    all_to_all x1, waiting for transfers between devices, local(): shares = lax.all_to_all(pair.astype(jnp.bfloat16), 'y', 0, 0, tiled=True)  14.3 us
  transfers between devices with their start and end apart: 16, of which 11 were waited for; matrix products, arithmetic and copies ran while one was open for 2% of the time, Pallas kernels for 11%

profile of v11, /device:TPU:1, one launch (start us, length us, event | category | flops | bytes accessed | tf_op | source)
XLA Modules:
  0.0 289.8 jit_solution(17322290619504782350)
XLA Ops:
  6.5 2.7 spread_blocks.1
  9.3 13.8 %all-to-all-start = ((bf16[32,48,128]{2,1,0:T(8,128)(2,1)}), bf16[32,48,128]{2,1,0:T(8,128)(2,1)S(1)}, u32[]{:S(2)}, u32[]{:S(2)}) async-start(bf16[32,48,128]{2,1,0:T(8,128)(2,1)} %spread_blocks.1), calls=%async_computation | async-start | bytes 786432 | tf_op jit(solution)/shard_map/all_to_all | solution.py:297
  23.3 5.3 %collective-permute-start = (bf16[1,4,256,128]{3,2,1,0:T(8,128)(2,1)S(1)}, bf16[1,4,256,128]{3,2,1,0:T(8,128)(2,1)S(1)}, u32[]{:S(2)}, u32[]{:S(2)}) collective-permute-start(bf16[1,4,256,128]{3,2,1,0:T(8,128)(2,1)S(1)} %get-tuple-element.30), channel_id=1, source_target_pairs={{0,384},{128,0},{256,128},{384,256},{1,385},{129,1},{257,129},{385... | collective-permute-start | bytes 786440 | tf_op jit(solution)/shard_map/ppermute | solution.py:264
  30.5 14.6 %collective-permute-done.refs_0_ = bf16[1,4,256,128]{3,2,1,0:T(8,128)(2,1)S(1)} collective-permute-done((bf16[1,4,256,128]{3,2,1,0:T(8,128)(2,1)S(1)}, bf16[1,4,256,128]{3,2,1,0:T(8,128)(2,1)S(1)}, u32[]{:S(2)}, u32[]{:S(2)}) %collective-permute-start) | collective-permute-done | bytes 262176 | tf_op jit(solution)/shard_map/ppermute | solution.py:264
  49.0 16.5 %all-gather.1 = bf16[68,32,128]{2,1,0:T(8,128)(2,1)S(1)} all-gather(bf16[17,32,128]{2,1,0:T(8,128)(2,1)S(1)} %copy-done.13), channel_id=3, replica_groups=mesh['zh'=4,'zl'=2,'x'=4,'y'=8,'core'=2] {'zh'}, dimensions={0}, use_global_device_ids=true | all-gather | bytes 696320 | tf_op jit(solution)/shard_map/all_gather | solution.py:310
  68.9 3.7 %collective-permute-start.3 = (bf16[3,4,256,128]{3,2,1,0:T(8,128)(2,1)}, bf16[3,4,256,128]{3,2,1,0:T(8,128)(2,1)S(1)}, u32[]{:S(2)}, u32[]{:S(2)}) collective-permute-start(bf16[3,4,256,128]{3,2,1,0:T(8,128)(2,1)} %pad_maximum_fusion), channel_id=1, source_target_pairs={{0,128},{128,256},{256,384},{384,0},{1,129},{129,257},{257,385},{3... | collective-permute-start | bytes 2359304 | tf_op jit(solution)/shard_map/ppermute | solution.py:264
  72.9 17.6 %all-gather.6.cloned.1.call-done = bf16[272,32,128]{2,1,0:T(8,128)(2,1)} async-done(((bf16[17,32,128]{2,1,0:T(8,128)(2,1)}), bf16[272,32,128]{2,1,0:T(8,128)(2,1)}) %all-gather.6.cloned.1.call-update) | async-done | bytes 2228240 | tf_op jit(solution)/shard_map/all_gather | solution.py:309
  90.4 5.1 %right_products.3 = bf16[8,1,2,256,256]{4,3,2,1,0:T(8,128)(2,1)} custom-call(s32[3]{0:T(128)S(1)} %pad_add_fusion.place_ref, s32[1,32]{1,0:T(1,128)S(1)} %compare_select_fusion.targets_ref, bf16[16,1,17,32,128]{4,3,2,1,0:T(8,128)(2,1)} %bitcast.23, bf16[2,4,256,256]{3,2,1,0:T(8,128)(2,1)S(1)} %copy-done, bf16[2,4,256,256]{3,2,1,0:T(8,128)(2,1)S(1)} %copy-done), custom_call_target="tpu_custom_call" | custom-call | tf_op jit(solution)/shard_map/right_products/pallas_call | solution.py:163
  95.5 9.2 %collective-permute-done.2.refs_1_.refs_0_ = bf16[3,4,256,128]{3,2,1,0:T(8,128)(2,1)S(1)} collective-permute-done((bf16[3,4,256,128]{3,2,1,0:T(8,128)(2,1)}, bf16[3,4,256,128]{3,2,1,0:T(8,128)(2,1)S(1)}, u32[]{:S(2)}, u32[]{:S(2)}) %collective-permute-start.2) | collective-permute-done | bytes 786464 | tf_op jit(solution)/shard_map/ppermute | solution.py:264
  106.5 7.4 %all-to-all-start.1 = ((bf16[8,1,2,256,256]{4,3,2,1,0:T(8,128)(2,1)}), bf16[8,1,2,256,256]{4,3,2,1,0:T(8,128)(2,1)S(1)}, u32[]{:S(2)}, u32[]{:S(2)}) async-start(bf16[8,1,2,256,256]{4,3,2,1,0:T(8,128)(2,1)} %right_products.3), calls=%async_computation.1 | async-start | bytes 4194304 | tf_op jit(solution)/shard_map/all_to_all | solution.py:280
  114.9 3.7 %collective-permute-start.4 = (bf16[2,4,256,128]{3,2,1,0:T(8,128)(2,1)S(1)}, bf16[2,4,256,128]{3,2,1,0:T(8,128)(2,1)S(1)}, u32[]{:S(2)}, u32[]{:S(2)}) collective-permute-start(bf16[2,4,256,128]{3,2,1,0:T(8,128)(2,1)S(1)} %pad_maximum_fusion.1), channel_id=1, source_target_pairs={{0,384},{128,0},{256,128},{384,256},{1,385},{129,1},{257,129},{385... | collective-permute-start | bytes 1572872 | tf_op jit(solution)/shard_map/ppermute | solution.py:264
  121.9 23.3 %collective-permute-done.4.refs_2_ = bf16[2,4,256,128]{3,2,1,0:T(8,128)(2,1)S(1)} collective-permute-done((bf16[2,4,256,128]{3,2,1,0:T(8,128)(2,1)S(1)}, bf16[2,4,256,128]{3,2,1,0:T(8,128)(2,1)S(1)}, u32[]{:S(2)}, u32[]{:S(2)}) %collective-permute-start.4) | collective-permute-done | bytes 524320 | tf_op jit(solution)/shard_map/ppermute | solution.py:264
  152.5 7.7 %right_products.4 = bf16[8,3,2,256,128]{4,3,2,1,0:T(8,128)(2,1)} custom-call(s32[3]{0:T(128)S(1)} %pad_add_fusion.place_ref, s32[3,32]{1,0:T(4,128)S(1)} %negate_select_fusion.targets_ref, bf16[16,3,17,32,128]{4,3,2,1,0:T(8,128)(2,1)} %bitcast.20, bf16[1,4,256,128]{3,2,1,0:T(8,128)(2,1)S(1)} %copy-done.9, bf16[3,4,256,128]{3,2,1,0:T(8,128)(2,1)S(1)} %copy-done.2, ...), custom_call_target="tpu_custom_call" | custom-call | tf_op jit(solution)/shard_map/right_products/pallas_call | solution.py:163
  160.2 6.3 %all-to-all-start.2 = ((bf16[8,3,2,256,128]{4,3,2,1,0:T(8,128)(2,1)}), bf16[8,3,2,256,128]{4,3,2,1,0:T(8,128)(2,1)}, u32[]{:S(2)}, u32[]{:S(2)}) async-start(bf16[8,3,2,256,128]{4,3,2,1,0:T(8,128)(2,1)} %right_products.4), calls=%async_computation.2 | async-start | bytes 6291456 | tf_op jit(solution)/shard_map/all_to_all | solution.py:280
  168.8 7.7 %right_products.5 = bf16[8,3,2,256,128]{4,3,2,1,0:T(8,128)(2,1)} custom-call(s32[3]{0:T(128)S(1)} %pad_add_fusion.place_ref, s32[3,32]{1,0:T(4,128)S(1)} %negate_select_fusion.targets_ref, bf16[16,3,17,32,128]{4,3,2,1,0:T(8,128)(2,1)} %bitcast.21, bf16[3,4,256,128]{3,2,1,0:T(8,128)(2,1)S(1)} %copy-done.3, bf16[3,4,256,128]{3,2,1,0:T(8,128)(2,1)S(1)} %copy-done.3, ...), custom_call_target="tpu_custom_call" | custom-call | tf_op jit(solution)/shard_map/right_products/pallas_call | solution.py:163
  176.5 27.2 %all-to-all-done.2.far_ref = bf16[8,3,2,256,128]{4,3,2,1,0:T(8,128)(2,1)} async-done(((bf16[8,3,2,256,128]{4,3,2,1,0:T(8,128)(2,1)}), bf16[8,3,2,256,128]{4,3,2,1,0:T(8,128)(2,1)}, u32[]{:S(2)}, u32[]{:S(2)}) %all-to-all-start.2) | async-done | bytes 3145760 | tf_op jit(solution)/shard_map/all_to_all | solution.py:280
  203.7 5.2 %all-to-all-start.3 = ((bf16[8,3,2,256,128]{4,3,2,1,0:T(8,128)(2,1)}), bf16[8,3,2,256,128]{4,3,2,1,0:T(8,128)(2,1)}, u32[]{:S(2)}, u32[]{:S(2)}) async-start(bf16[8,3,2,256,128]{4,3,2,1,0:T(8,128)(2,1)} %right_products.5), calls=%async_computation.4 | async-start | bytes 6291456 | tf_op jit(solution)/shard_map/all_to_all | solution.py:280
  209.0 5.4 %left_products.2 = bf16[16,16,16,128]{3,2,1,0:T(8,128)(2,1)} custom-call(s32[3]{0:T(128)S(1)} %pad_add_fusion.place_ref, s32[2,16]{1,0:T(2,128)S(1)} %compare_select_fusion.2.from_ref, bf16[8,1,2,256,256]{4,3,2,1,0:T(8,128)(2,1)S(1)} %all-to-all-done.1.near_ref, bf16[8,3,2,256,128]{4,3,2,1,0:T(8,128)(2,1)} %all-to-all-done.2.far_ref, ...), custom_call_target="tpu_custom_call" | custom-call | tf_op jit(solution)/shard_map/left_products/pallas_call | solution.py:244
  214.4 31.9 %all-to-all-done.3.far_ref = bf16[8,3,2,256,128]{4,3,2,1,0:T(8,128)(2,1)} async-done(((bf16[8,3,2,256,128]{4,3,2,1,0:T(8,128)(2,1)}), bf16[8,3,2,256,128]{4,3,2,1,0:T(8,128)(2,1)}, u32[]{:S(2)}, u32[]{:S(2)}) %all-to-all-start.3) | async-done | bytes 3145760 | tf_op jit(solution)/shard_map/all_to_all | solution.py:280
  246.2 4.7 %left_products.3 = (bf16[8,16,16,128]{3,2,1,0:T(8,128)(2,1)S(1)}, bf16[8,16,16,128]{3,2,1,0:T(8,128)(2,1)S(1)}) custom-call(s32[3]{0:T(128)S(1)} %pad_add_fusion.place_ref, s32[2,16]{1,0:T(2,128)S(1)} %compare_select_fusion.2.from_ref, bf16[8,1,2,256,256]{4,3,2,1,0:T(8,128)(2,1)S(1)} %all-to-all-done.1.near_ref, ...), custom_call_target="tpu_custom_call" | custom-call | tf_op jit(solution)/shard_map/left_products/pallas_call | solution.py:244
  250.9 2.7 collective-permute-start.7
  256.0 7.6 %all-to-all-start.4 = ((bf16[8,16,16,128]{3,2,1,0:T(8,128)(2,1)}), bf16[8,16,16,128]{3,2,1,0:T(8,128)(2,1)S(1)}, u32[]{:S(2)}, u32[]{:S(2)}) async-start(bf16[8,16,16,128]{3,2,1,0:T(8,128)(2,1)} %add_convert_fusion), calls=%async_computation.5 | async-start | bytes 1048576 | tf_op jit(solution)/shard_map/all_to_all | solution.py:353
  264.7 2.5 collective-permute-start.6
  267.3 14.3 %all-to-all-done.4 = bf16[8,16,16,128]{3,2,1,0:T(8,128)(2,1)S(1)} async-done(((bf16[8,16,16,128]{3,2,1,0:T(8,128)(2,1)}), bf16[8,16,16,128]{3,2,1,0:T(8,128)(2,1)S(1)}, u32[]{:S(2)}, u32[]{:S(2)}) %all-to-all-start.4) | async-done | bytes 524320 | tf_op jit(solution)/shard_map/all_to_all | solution.py:353
  (80 shorter events, 30.4 us)
Async XLA Ops:
  6.5 16.7 %copy-start = (bf16[2,4,256,256]{3,2,1,0:T(8,128)(2,1)S(1)}, bf16[2,4,256,256]{3,2,1,0:T(8,128)(2,1)}, u32[]{:S(2)}) copy-start(bf16[2,4,256,256]{3,2,1,0:T(8,128)(2,1)} %refs_1_.1) | copy-start | bytes 3145732
  9.3 38.7 %slice-start = ((bf16[2,4,256,256]{3,2,1,0:T(8,128)(2,1)}), bf16[2,4,256,128]{3,2,1,0:T(8,128)(2,1)S(1)}, s32[]{:S(2)}) async-start(bf16[2,4,256,256]{3,2,1,0:T(8,128)(2,1)} %refs_1_.1), calls=%async_computation.9 | async-start | bytes 1048576 | tf_op jit(solution)/shard_map/slice | solution.py:298
  9.3 36.0 %all-to-all-start = ((bf16[32,48,128]{2,1,0:T(8,128)(2,1)}), bf16[32,48,128]{2,1,0:T(8,128)(2,1)S(1)}, u32[]{:S(2)}, u32[]{:S(2)}) async-start(bf16[32,48,128]{2,1,0:T(8,128)(2,1)} %spread_blocks.1), calls=%async_computation | async-start | bytes 786432 | tf_op jit(solution)/shard_map/all_to_all | solution.py:297
  23.1 67.3 %all-gather.6.cloned.1.call-start = ((), (), s32[]{:S(2)}) async-start(), calls=%async_computation.7 | async-start | bytes 2367488 | tf_op jit(solution)/shard_map/all_gather | solution.py:309
  23.3 21.8 %collective-permute-start = (bf16[1,4,256,128]{3,2,1,0:T(8,128)(2,1)S(1)}, bf16[1,4,256,128]{3,2,1,0:T(8,128)(2,1)S(1)}, u32[]{:S(2)}, u32[]{:S(2)}) collective-permute-start(bf16[1,4,256,128]{3,2,1,0:T(8,128)(2,1)S(1)} %get-tuple-element.30), channel_id=1, source_target_pairs={{0,384},{128,0},{256,128},{384,256},{1,385},{129,1},{257,129},{385... | collective-permute-start | bytes 786440 | tf_op jit(solution)/shard_map/ppermute | solution.py:264
  28.6 16.7 %collective-permute-start.1 = (bf16[1,4,256,128]{3,2,1,0:T(8,128)(2,1)S(1)}, bf16[1,4,256,128]{3,2,1,0:T(8,128)(2,1)S(1)}, u32[]{:S(2)}, u32[]{:S(2)}) collective-permute-start(bf16[1,4,256,128]{3,2,1,0:T(8,128)(2,1)S(1)} %get-tuple-element.30), channel_id=1, source_target_pairs={{0,128},{128,256},{256,384},{384,0},{1,129},{129,257},{257,385},{3... | collective-permute-start | bytes 786440 | tf_op jit(solution)/shard_map/ppermute | solution.py:264
  45.1 69.8 %copy-start.8 = (bf16[1,4,256,128]{3,2,1,0:T(8,128)(2,1)}, bf16[1,4,256,128]{3,2,1,0:T(8,128)(2,1)S(1)}, u32[]{:S(2)}) copy-start(bf16[1,4,256,128]{3,2,1,0:T(8,128)(2,1)S(1)} %collective-permute-done.refs_0_) | copy-start | bytes 786436
  45.3 21.1 %copy-start.10 = (bf16[1,4,256,128]{3,2,1,0:T(8,128)(2,1)}, bf16[1,4,256,128]{3,2,1,0:T(8,128)(2,1)S(1)}, u32[]{:S(2)}) copy-start(bf16[1,4,256,128]{3,2,1,0:T(8,128)(2,1)S(1)} %collective-permute-done.1.refs_4_) | copy-start | bytes 786436
  47.9 100.5 %all-gather.8.cloned.1.call-start = ((), (), s32[]{:S(2)}) async-start(), calls=%async_computation.8 | async-start | bytes 7102464 | tf_op jit(solution)/shard_map/all_gather | solution.py:320
  48.0 24.7 %copy-start.14 = (s32[2,16]{1,0:T(2,128)S(1)}, s32[2,16]{1,0:T(2,128)}, u32[]{:S(2)}) copy-start(s32[2,16]{1,0:T(2,128)} %links_ref.3) | copy-start | bytes 388
  66.4 38.2 %collective-permute-start.2 = (bf16[3,4,256,128]{3,2,1,0:T(8,128)(2,1)}, bf16[3,4,256,128]{3,2,1,0:T(8,128)(2,1)S(1)}, u32[]{:S(2)}, u32[]{:S(2)}) collective-permute-start(bf16[3,4,256,128]{3,2,1,0:T(8,128)(2,1)} %pad_maximum_fusion), channel_id=1, source_target_pairs={{0,384},{128,0},{256,128},{384,256},{1,385},{129,1},{257,129},{385... | collective-permute-start | bytes 2359304 | tf_op jit(solution)/shard_map/ppermute | solution.py:264
  68.9 37.6 %collective-permute-start.3 = (bf16[3,4,256,128]{3,2,1,0:T(8,128)(2,1)}, bf16[3,4,256,128]{3,2,1,0:T(8,128)(2,1)S(1)}, u32[]{:S(2)}, u32[]{:S(2)}) collective-permute-start(bf16[3,4,256,128]{3,2,1,0:T(8,128)(2,1)} %pad_maximum_fusion), channel_id=1, source_target_pairs={{0,128},{128,256},{256,384},{384,0},{1,129},{129,257},{257,385},{3... | collective-permute-start | bytes 2359304 | tf_op jit(solution)/shard_map/ppermute | solution.py:264
  104.7 1.9 copy-start.1
  106.5 53.7 %all-to-all-start.1 = ((bf16[8,1,2,256,256]{4,3,2,1,0:T(8,128)(2,1)}), bf16[8,1,2,256,256]{4,3,2,1,0:T(8,128)(2,1)S(1)}, u32[]{:S(2)}, u32[]{:S(2)}) async-start(bf16[8,1,2,256,256]{4,3,2,1,0:T(8,128)(2,1)} %right_products.3), calls=%async_computation.1 | async-start | bytes 4194304 | tf_op jit(solution)/shard_map/all_to_all | solution.py:280
  114.9 30.3 %collective-permute-start.4 = (bf16[2,4,256,128]{3,2,1,0:T(8,128)(2,1)S(1)}, bf16[2,4,256,128]{3,2,1,0:T(8,128)(2,1)S(1)}, u32[]{:S(2)}, u32[]{:S(2)}) collective-permute-start(bf16[2,4,256,128]{3,2,1,0:T(8,128)(2,1)S(1)} %pad_maximum_fusion.1), channel_id=1, source_target_pairs={{0,384},{128,0},{256,128},{384,256},{1,385},{129,1},{257,129},{385... | collective-permute-start | bytes 1572872 | tf_op jit(solution)/shard_map/ppermute | solution.py:264
  118.7 29.0 %collective-permute-start.5 = (bf16[2,4,256,128]{3,2,1,0:T(8,128)(2,1)S(1)}, bf16[2,4,256,128]{3,2,1,0:T(8,128)(2,1)S(1)}, u32[]{:S(2)}, u32[]{:S(2)}) collective-permute-start(bf16[2,4,256,128]{3,2,1,0:T(8,128)(2,1)S(1)} %pad_maximum_fusion.2), channel_id=1, source_target_pairs={{0,128},{128,256},{256,384},{384,0},{1,129},{129,257},{257,385},{3... | collective-permute-start | bytes 1572872 | tf_op jit(solution)/shard_map/ppermute | solution.py:264
  160.2 43.5 %all-to-all-start.2 = ((bf16[8,3,2,256,128]{4,3,2,1,0:T(8,128)(2,1)}), bf16[8,3,2,256,128]{4,3,2,1,0:T(8,128)(2,1)}, u32[]{:S(2)}, u32[]{:S(2)}) async-start(bf16[8,3,2,256,128]{4,3,2,1,0:T(8,128)(2,1)} %right_products.4), calls=%async_computation.2 | async-start | bytes 6291456 | tf_op jit(solution)/shard_map/all_to_all | solution.py:280
  176.5 32.5 %copy-start.4 = (bf16[2,4,256,256]{3,2,1,0:T(8,128)(2,1)S(1)}, bf16[2,4,256,256]{3,2,1,0:T(8,128)(2,1)}, u32[]{:S(2)}) copy-start(bf16[2,4,256,256]{3,2,1,0:T(8,128)(2,1)} %env_ref.3) | copy-start | bytes 3145732
  203.7 42.5 %all-to-all-start.3 = ((bf16[8,3,2,256,128]{4,3,2,1,0:T(8,128)(2,1)}), bf16[8,3,2,256,128]{4,3,2,1,0:T(8,128)(2,1)}, u32[]{:S(2)}, u32[]{:S(2)}) async-start(bf16[8,3,2,256,128]{4,3,2,1,0:T(8,128)(2,1)} %right_products.5), calls=%async_computation.4 | async-start | bytes 6291456 | tf_op jit(solution)/shard_map/all_to_all | solution.py:280
  209.0 54.9 %reduce-scatter.2.cloned.1.call-start = ((), (), s32[]{:S(2)}) async-start(), calls=%async_computation.6 | async-start | bytes 1179648 | tf_op jit(solution)/shard_map/reduce_scatter | solution.py:339
  250.9 12.7 %copy-start.15 = (s32[4]{0:T(128)S(1)}, s32[4]{0:T(128)}, u32[]{:S(2)}) copy-start(s32[4]{0:T(128)} %rows_ref.1) | copy-start | bytes 52
  250.9 4.2 %collective-permute-start.7 = (bf16[8,16,16,128]{3,2,1,0:T(8,128)(2,1)S(1)}, bf16[8,16,16,128]{3,2,1,0:T(8,128)(2,1)S(1)}, u32[]{:S(2)}, u32[]{:S(2)}) collective-permute-start(bf16[8,16,16,128]{3,2,1,0:T(8,128)(2,1)S(1)} %get-tuple-element.28), channel_id=1, source_target_pairs={{0,1},{1,0},{2,3},{3,2},{4,5},{5,4},{6,7},{7,6},{8,9},{9,8},{10,11... | collective-permute-start | bytes 1572872 | tf_op jit(solution)/shard_map/ppermute | solution.py:264
  256.0 25.5 %all-to-all-start.4 = ((bf16[8,16,16,128]{3,2,1,0:T(8,128)(2,1)}), bf16[8,16,16,128]{3,2,1,0:T(8,128)(2,1)S(1)}, u32[]{:S(2)}, u32[]{:S(2)}) async-start(bf16[8,16,16,128]{3,2,1,0:T(8,128)(2,1)} %add_convert_fusion), calls=%async_computation.5 | async-start | bytes 1048576 | tf_op jit(solution)/shard_map/all_to_all | solution.py:353
  264.7 16.9 %collective-permute-start.6 = (bf16[16,16,128]{2,1,0:T(8,128)(2,1)S(1)}, bf16[16,16,128]{2,1,0:T(8,128)(2,1)S(1)}, u32[]{:S(2)}, u32[]{:S(2)}) collective-permute-start(bf16[16,16,128]{2,1,0:T(8,128)(2,1)S(1)} %dynamic-slice_bitcast_fusion), channel_id=1, source_target_pairs={{0,1},{1,0},{2,3},{3,2},{4,5},{5,4},{6,7},{7,6},{8,9},{9,8},{10,11... | collective-permute-start | bytes 196616 | tf_op jit(solution)/shard_map/ppermute | solution.py:264
  (9 other events, 8.9 us)
Sparse Core Ops, SparseCore 0:
  48.0 42.3 all-gather.5
  92.5 49.2 all-gather.7
  214.5 36.0 reduce-scatter.1

commit v12 on v8

--- a/solution.py
+++ b/solution.py
@@ -117,8 +117,8 @@
     )(source, term_links, sector_cols, arrived)
 
 
-def right_kernel(place_ref, targets_ref, slices_ref, *refs):
-    envs, (out_ref, moved_ref, env_ref) = refs[:-3], refs[-3:]
+def right_kernel(aliased, place_ref, targets_ref, slices_ref, *refs):
+    envs, (out_ref, moved_ref, env_ref, slot_ref) = refs[: -4 - aliased], refs[-4:]
     group, _, terms, extent, width = out_ref.shape
     sectors = env_ref.shape[0]
     depth, count = slices_ref.shape[0], slices_ref.shape[2] - 1
@@ -146,51 +146,50 @@
             for term in range(terms):
                 owner = targets_ref[turn, term * count + sector * per_sector + place]
 
-                @pl.when(lax.div(owner, group) == place_ref[0])
-                def _(place=place, term=term, owner=owner):
-                    out_ref[lax.rem(owner, group), 0, term] = product[
-                        place * extent : (place + 1) * extent, term * width : (term + 1) * width
-                    ]
-
-
-def right_products(place, targets, slices, envs, group, chunk, width):
+                here = lax.div(owner, group) == place_ref[0]
+                slot_ref[jnp.where(here, lax.rem(owner, group), group), term] = product[
+                    place * extent : (place + 1) * extent, term * width : (term + 1) * width
+                ]
+    out_ref[:, 0] = slot_ref[:group]
+
+
+def right_products(place, targets, slices, envs, group, width, first=0, stride=1, into=None):
     depth, layers, blocks, tall, lanes = slices.shape
     terms = len(envs[0])
     sectors, extent = envs[0][0][0].shape[1:3]
     per_sector = (blocks - 1) // sectors
     flat = [pair for layer in envs for pair in layer]
-    shape = (group, layers, terms, extent, width)
+    extra = [] if into is None else [into]
     return pl.pallas_call(
-        right_kernel,
+        functools.partial(right_kernel, len(extra)),
         grid_spec=pltpu.PrefetchScalarGridSpec(
             num_scalar_prefetch=2,
-            grid=(layers,),
-            in_specs=[pl.BlockSpec((depth, 1, blocks, tall, lanes), lambda i, p, t: (0, i, 0, 0, 0))]
+            grid=(len(envs),),
+            in_specs=[
+                pl.BlockSpec(
+                    (depth, 1, blocks, tall, lanes),
+                    lambda i, p, t: (0, first + stride * i, 0, 0, 0),
+                )
+            ]
             + [
-                pl.BlockSpec(
-                    (1, sectors, extent, width), lambda i, p, t, term=term: (term, 0, 0, chunk)
-                )
+                pl.BlockSpec((1, sectors, extent, width), lambda i, p, t, term=term: (term, 0, 0, 0))
                 for _, term in flat
-            ],
-            out_specs=pl.BlockSpec((group, 1, terms, extent, width), lambda i, p, t: (0, i, 0, 0, 0)),
+            ]
+            + [pl.BlockSpec(memory_space=pl.ANY)] * len(extra),
+            out_specs=pl.BlockSpec(
+                (group, 1, terms, extent, width), lambda i, p, t: (0, first + stride * i, 0, 0, 0)
+            ),
             scratch_shapes=[
                 pltpu.VMEM((2, per_sector * extent, extent), jnp.bfloat16),
                 pltpu.VMEM((sectors, extent, terms * width), jnp.bfloat16),
+                pltpu.VMEM((group + 1, terms, extent, width), jnp.bfloat16),
             ],
         ),
-        out_shape=pltpu.HBM(shape, jnp.bfloat16),
+        out_shape=pltpu.HBM((group, layers, terms, extent, width), jnp.bfloat16),
+        input_output_aliases={3 + len(flat): 0} if extra else {},
         compiler_params=pltpu.CompilerParams(vmem_limit_bytes=VMEM_LIMIT),
         name="right_products",
-    )(place, targets, in_hbm(slices), *[array for array, _ in flat])
-
-
-def far_products(place, targets, slices, above, below, across, group):
-    envs = [
-        [(above, 0), (above, 1)],
-        [(across[0], 0), (across[1], 0)],
-        [(below, 0), (below, 1)],
-    ]
-    return right_products(place, targets, slices, envs, group, 0, LANES)
+    )(place, targets, in_hbm(slices), *[array for array, _ in flat], *extra)
 
 
 def left_partials(place_ref, from_ref, near_ref, far_ref, env_ref, placed_ref):
@@ -323,7 +322,7 @@
 
     targets = lax.rem((term_links // count).reshape(1, terms * count) + moved_by, slots)
     envs = [[(right_env, term) for term in range(terms)]]
-    products = right_products(place, targets, slices, envs, group, 0, width)
+    products = right_products(place, targets, slices, envs, group, width)
     products, above, below = lax.optimization_barrier((products, above, below))
     own = exchange(products)
 
@@ -331,7 +330,12 @@
     next_above, next_below = shift(second, "zh", -1), shift(second, "zh", 1)
     next_across = shift(next_above[:1], "zh", -1), shift(next_below[1:], "zh", 1)
 
-    products = far_products(place, far_targets, far_slices, above, below, across, group)
+    envs = [
+        [(above, 0), (above, 1)],
+        [(across[0], 0), (across[1], 0)],
+        [(below, 0), (below, 1)],
+    ]
+    products = right_products(place, far_targets, far_slices, envs, group, LANES)
     after = products, far_slices, next_above, next_below
     products, far_slices, next_above, next_below = lax.optimization_barrier(after)
     far = exchange(products)
@@ -342,8 +346,12 @@
     kept = lax.dynamic_index_in_dim(summed, core_index, 0, False)
     pieces = [kept.astype(jnp.float32) + received.astype(jnp.float32)]
 
-    products = far_products(
-        place, far_targets, far_slices, next_above, next_below, next_across, group
+    sides = jnp.stack([far_targets[0], far_targets[2]])
+    envs = [[(next_above, 0), (next_above, 1)], [(next_below, 0), (next_below, 1)]]
+    products = right_products(place, sides, far_slices, envs, group, LANES, 0, 2)
+    envs = [[(next_across[0], 0), (next_across[1], 0)]]
+    products = right_products(
+        place, far_targets[1:2], far_slices, envs, group, LANES, 1, 1, products
     )
     far = exchange(products)
     keep, send = left_products(place, peers, own, far, left_env, 1, True)

time: 287 us -> 277 us (0.965)
  waiting for transfers between devices: 125 us -> 120 us
  starting transfers between devices: 54.1 us -> 50.8 us
    ppermute x10, waiting for transfers between devices: 57.8 us -> 51.6 us  [shift(): lax.ppermute(array, axis, [(i, (i + step) % size) for i in range(size)])]
    all_to_all x1, starting transfers between devices: 7.26 us -> 3.91 us  [local(): shares = lax.all_to_all(pair.astype(jnp.bfloat16), 'y', 0, 0, tiled=True)]
    pallas_call x3 -> x4, Pallas kernels: 25.2 us -> 23 us  [right_products(): pl.pallas_call(functools.partial(right_kernel, len(extra)), grid_spec=plt...]
  transfers between devices with their start and end apart: 17 -> 17, of which waited for: 10 -> 11; matrix products, arithmetic and copies ran while one was open for 2% -> 2% of each run, Pallas kernels for 12% -> 12%
where the time goes in v12:
time: 277 us; the launch traced here: 276 us
  waiting for transfers between devices  120 us (43%)
  starting transfers between devices  50.8 us (18%)
  blocking collectives  42.8 us (15%)
  Pallas kernels  37.5 us (14%)
  between operations  13.4 us (5%)
  local copies, waits for them, and re-layouts  6.65 us (2%)
  other arithmetic  4.65 us (2%)
    ppermute x10, waiting for transfers between devices, shift(): lax.ppermute(array, axis, [(i, (i + step) % size) for i in range(size)])  51.6 us
    all_to_all x3, waiting for transfers between devices, exchange(): lax.all_to_all(products, axes, 0, 0, axis_index_groups=groups, tiled=True)  33.1 us
    ppermute x10, starting transfers between devices, shift(): lax.ppermute(array, axis, [(i, (i + step) % size) for i in range(size)])  30.1 us
    all_to_all x1, blocking collectives, local(): arrived = lax.all_to_all(buffer, REMAP, 0, 0, tiled=True)  27.6 us
    pallas_call x4, Pallas kernels, right_products(): pl.pallas_call(functools.partial(right_kernel, len(extra)), grid_spec=plt...  23 us
    all_to_all x3, starting transfers between devices, exchange(): lax.all_to_all(products, axes, 0, 0, axis_index_groups=groups, tiled=True)  16.8 us
    all_gather x1, waiting for transfers between devices, local(): slices = lax.all_gather(ordered[None], DEPTH)  16.6 us
    all_gather x1, blocking collectives, local(): around = lax.all_gather(ordered, 'zh')  15.1 us
  transfers between devices with their start and end apart: 17, of which 11 were waited for; matrix products, arithmetic and copies ran while one was open for 2% of the time, Pallas kernels for 12%

profile of v12, /device:TPU:1, one launch (start us, length us, event | category | flops | bytes accessed | tf_op | source)
XLA Modules:
  0.0 275.9 jit_solution(406922178800697050)
XLA Ops:
  9.3 27.6 %all_to_all.25.in_ref = bf16[32,48,128]{2,1,0:T(8,128)(2,1)S(1)} all-to-all(bf16[32,48,128]{2,1,0:T(8,128)(2,1)} %spread_blocks.1), channel_id=1, replica_groups=mesh['zh'=4,'zl'=2,'x'=4,'y'=8,'core'=2] {'zh','zl','x'}, dimensions={0} | all-to-all | bytes 786432 | tf_op jit(solution)/shard_map/all_to_all | solution.py:304
  39.5 15.1 %all-gather.1 = bf16[68,32,128]{2,1,0:T(8,128)(2,1)S(1)} all-gather(bf16[17,32,128]{2,1,0:T(8,128)(2,1)} %order_blocks.1), channel_id=3, replica_groups=mesh['zh'=4,'zl'=2,'x'=4,'y'=8,'core'=2] {'zh'}, dimensions={0}, use_global_device_ids=true | all-gather | bytes 696320 | tf_op jit(solution)/shard_map/all_gather | solution.py:317
  56.7 3.5 %collective-permute-start = (bf16[2,4,256,128]{3,2,1,0:T(8,128)(2,1)S(1)}, bf16[2,4,256,128]{3,2,1,0:T(8,128)(2,1)S(1)}, u32[]{:S(2)}, u32[]{:S(2)}) collective-permute-start(bf16[2,4,256,128]{3,2,1,0:T(8,128)(2,1)S(1)} %get-tuple-element.30), channel_id=1, source_target_pairs={{0,384},{128,0},{256,128},{384,256},{1,385},{129,1},{257,129},{385... | collective-permute-start | bytes 1572872 | tf_op jit(solution)/shard_map/ppermute | solution.py:271
  63.1 16.6 %all-gather.6.cloned.1.call-done = bf16[272,32,128]{2,1,0:T(8,128)(2,1)} async-done(((bf16[17,32,128]{2,1,0:T(8,128)(2,1)}), bf16[272,32,128]{2,1,0:T(8,128)(2,1)}) %all-gather.6.cloned.1.call-update) | async-done | bytes 2228240 | tf_op jit(solution)/shard_map/all_gather | solution.py:316
  79.7 5.0 %right_products.4 = bf16[8,1,2,256,256]{4,3,2,1,0:T(8,128)(2,1)} custom-call(s32[3]{0:T(128)S(1)} %pad_add_fusion.1.place_ref, s32[1,32]{1,0:T(1,128)S(1)} %compare_select_fusion.targets_ref, bf16[16,1,17,32,128]{4,3,2,1,0:T(8,128)(2,1)} %bitcast.24, bf16[2,4,256,256]{3,2,1,0:T(8,128)(2,1)S(1)} %copy-done, bf16[2,4,256,256]{3,2,1,0:T(8,128)(2,1)S(1)} %copy-done), custom_call_target="tpu_custom_call" | custom-call | tf_op jit(solution)/shard_map/right_products/pallas_call | solution.py:163
  86.0 6.3 %all-to-all-start.1 = ((bf16[8,1,2,256,256]{4,3,2,1,0:T(8,128)(2,1)}), bf16[8,1,2,256,256]{4,3,2,1,0:T(8,128)(2,1)S(1)}, u32[]{:S(2)}, u32[]{:S(2)}) async-start(bf16[8,1,2,256,256]{4,3,2,1,0:T(8,128)(2,1)} %right_products.4), calls=%async_computation.1 | async-start | bytes 4194304 | tf_op jit(solution)/shard_map/all_to_all | solution.py:287
  92.4 3.9 %collective-permute-start.2 = (bf16[1,4,256,128]{3,2,1,0:T(8,128)(2,1)S(1)}, bf16[1,4,256,128]{3,2,1,0:T(8,128)(2,1)S(1)}, u32[]{:S(2)}, u32[]{:S(2)}) collective-permute-start(bf16[1,4,256,128]{3,2,1,0:T(8,128)(2,1)S(1)} %slice.54), channel_id=1, source_target_pairs={{0,384},{128,0},{256,128},{384,256},{1,385},{129,1},{257,129},{385... | collective-permute-start | bytes 786440 | tf_op jit(solution)/shard_map/ppermute | solution.py:271
  98.6 20.2 %collective-permute-done.2.refs_2_ = bf16[1,4,256,128]{3,2,1,0:T(8,128)(2,1)S(1)} collective-permute-done((bf16[1,4,256,128]{3,2,1,0:T(8,128)(2,1)S(1)}, bf16[1,4,256,128]{3,2,1,0:T(8,128)(2,1)S(1)}, u32[]{:S(2)}, u32[]{:S(2)}) %collective-permute-start.2) | collective-permute-done | bytes 262176 | tf_op jit(solution)/shard_map/ppermute | solution.py:271
  119.6 3.1 %collective-permute-start.4 = (bf16[2,4,256,128]{3,2,1,0:T(8,128)(2,1)}, bf16[2,4,256,128]{3,2,1,0:T(8,128)(2,1)S(1)}, u32[]{:S(2)}, u32[]{:S(2)}) collective-permute-start(bf16[2,4,256,128]{3,2,1,0:T(8,128)(2,1)} %get-tuple-element.22), channel_id=1, source_target_pairs={{0,384},{128,0},{256,128},{384,256},{1,385},{129,1},{257,129},{385... | collective-permute-start | bytes 1572872 | tf_op jit(solution)/shard_map/ppermute | solution.py:271
  122.7 3.1 %collective-permute-start.5 = (bf16[2,4,256,128]{3,2,1,0:T(8,128)(2,1)}, bf16[2,4,256,128]{3,2,1,0:T(8,128)(2,1)S(1)}, u32[]{:S(2)}, u32[]{:S(2)}) collective-permute-start(bf16[2,4,256,128]{3,2,1,0:T(8,128)(2,1)} %get-tuple-element.22), channel_id=1, source_target_pairs={{0,128},{128,256},{256,384},{384,0},{1,129},{129,257},{257,385},{3... | collective-permute-start | bytes 1572872 | tf_op jit(solution)/shard_map/ppermute | solution.py:271
  126.5 4.5 %all-gather.8.cloned.1.call-done = bf16[48,17,32,128]{3,2,1,0:T(8,128)(2,1)} async-done(((bf16[3,17,32,128]{3,2,1,0:T(8,128)(2,1)}), bf16[48,17,32,128]{3,2,1,0:T(8,128)(2,1)}) %all-gather.8.cloned.1.call-update) | async-done | bytes 6684688 | tf_op jit(solution)/shard_map/all_gather | solution.py:321
  134.1 7.8 %right_products.5 = bf16[8,3,2,256,128]{4,3,2,1,0:T(8,128)(2,1)} custom-call(s32[3]{0:T(128)S(1)} %pad_add_fusion.1.place_ref, s32[3,32]{1,0:T(4,128)S(1)} %negate_select_fusion.targets_ref, bf16[16,3,17,32,128]{4,3,2,1,0:T(8,128)(2,1)} %bitcast.20, bf16[2,4,256,128]{3,2,1,0:T(8,128)(2,1)S(1)} %copy-done.3, bf16[2,4,256,128]{3,2,1,0:T(8,128)(2,1)S(1)} %copy-done.3, ...), custom_call_target="tpu_custom_call" | custom-call | tf_op jit(solution)/shard_map/right_products/pallas_call | solution.py:163
  144.6 6.3 %collective-permute-done.5.refs_2_.refs_3_ = bf16[2,4,256,128]{3,2,1,0:T(8,128)(2,1)S(1)} collective-permute-done((bf16[2,4,256,128]{3,2,1,0:T(8,128)(2,1)}, bf16[2,4,256,128]{3,2,1,0:T(8,128)(2,1)S(1)}, u32[]{:S(2)}, u32[]{:S(2)}) %collective-permute-start.5) | collective-permute-done | bytes 524320 | tf_op jit(solution)/shard_map/ppermute | solution.py:271
  150.9 5.4 %all-to-all-start.2 = ((bf16[8,3,2,256,128]{4,3,2,1,0:T(8,128)(2,1)}), bf16[8,3,2,256,128]{4,3,2,1,0:T(8,128)(2,1)}, u32[]{:S(2)}, u32[]{:S(2)}) async-start(bf16[8,3,2,256,128]{4,3,2,1,0:T(8,128)(2,1)} %right_products.5), calls=%async_computation.2 | async-start | bytes 6291456 | tf_op jit(solution)/shard_map/all_to_all | solution.py:287
  159.0 3.5 %collective-permute-start.8 = (bf16[1,4,256,128]{3,2,1,0:T(8,128)(2,1)S(1)}, bf16[1,4,256,128]{3,2,1,0:T(8,128)(2,1)S(1)}, u32[]{:S(2)}, u32[]{:S(2)}) collective-permute-start(bf16[1,4,256,128]{3,2,1,0:T(8,128)(2,1)S(1)} %slice.57), channel_id=1, source_target_pairs={{0,128},{128,256},{256,384},{384,0},{1,129},{129,257},{257,385},{3... | collective-permute-start | bytes 786440 | tf_op jit(solution)/shard_map/ppermute | solution.py:271
  162.6 5.7 %right_products.6.refs_2_ = bf16[8,3,2,256,128]{4,3,2,1,0:T(8,128)(2,1)} custom-call(s32[3]{0:T(128)S(1)} %pad_add_fusion.1.place_ref, s32[2,32]{1,0:T(2,128)S(1)} %pad_add_fusion.targets_ref, bf16[16,3,17,32,128]{4,3,2,1,0:T(8,128)(2,1)} %bitcast.21, bf16[2,4,256,128]{3,2,1,0:T(8,128)(2,1)S(1)} %collective-permute-done.4.refs_0_.refs_1_, ...), custom_call_target="tpu_custom_call" | custom-call | tf_op jit(solution)/shard_map/right_products/pallas_call | solution.py:163
  168.3 19.5 %collective-permute-done.7.refs_0_ = bf16[1,4,256,128]{3,2,1,0:T(8,128)(2,1)S(1)} collective-permute-done((bf16[1,4,256,128]{3,2,1,0:T(8,128)(2,1)S(1)}, bf16[1,4,256,128]{3,2,1,0:T(8,128)(2,1)S(1)}, u32[]{:S(2)}, u32[]{:S(2)}) %collective-permute-start.7) | collective-permute-done | bytes 262176 | tf_op jit(solution)/shard_map/ppermute | solution.py:271
  187.8 4.5 %right_products.7 = bf16[8,3,2,256,128]{4,3,2,1,0:T(8,128)(2,1)} custom-call(s32[3]{0:T(128)S(1)} %pad_add_fusion.1.place_ref, s32[1,32]{1,0:T(1,128)S(1)} %get-tuple-element.33.targets_ref, bf16[16,3,17,32,128]{4,3,2,1,0:T(8,128)(2,1)} %bitcast.22, bf16[1,4,256,128]{3,2,1,0:T(8,128)(2,1)S(1)} %collective-permute-done.7.refs_0_, ...), custom_call_target="tpu_custom_call", output_to_operand_aliasing={{}: (5, {})} | custom-call | tf_op jit(solution)/shard_map/right_products/pallas_call | solution.py:163
  193.7 5.1 %all-to-all-start.3 = ((bf16[8,3,2,256,128]{4,3,2,1,0:T(8,128)(2,1)}), bf16[8,3,2,256,128]{4,3,2,1,0:T(8,128)(2,1)}, u32[]{:S(2)}, u32[]{:S(2)}) async-start(bf16[8,3,2,256,128]{4,3,2,1,0:T(8,128)(2,1)} %right_products.7), calls=%async_computation.4 | async-start | bytes 6291456 | tf_op jit(solution)/shard_map/all_to_all | solution.py:287
  198.8 5.4 %left_products.2 = bf16[16,16,16,128]{3,2,1,0:T(8,128)(2,1)} custom-call(s32[3]{0:T(128)S(1)} %pad_add_fusion.1.place_ref, s32[2,16]{1,0:T(2,128)S(1)} %compare_select_fusion.2.from_ref, bf16[8,1,2,256,256]{4,3,2,1,0:T(8,128)(2,1)S(1)} %all-to-all-done.1.near_ref, bf16[8,3,2,256,128]{4,3,2,1,0:T(8,128)(2,1)} %all-to-all-done.2.far_ref, ...), custom_call_target="tpu_custom_call" | custom-call | tf_op jit(solution)/shard_map/left_products/pallas_call | solution.py:251
  204.2 31.7 %all-to-all-done.3.far_ref = bf16[8,3,2,256,128]{4,3,2,1,0:T(8,128)(2,1)} async-done(((bf16[8,3,2,256,128]{4,3,2,1,0:T(8,128)(2,1)}), bf16[8,3,2,256,128]{4,3,2,1,0:T(8,128)(2,1)}, u32[]{:S(2)}, u32[]{:S(2)}) %all-to-all-start.3) | async-done | bytes 3145760 | tf_op jit(solution)/shard_map/all_to_all | solution.py:287
  235.8 4.6 %left_products.3 = (bf16[8,16,16,128]{3,2,1,0:T(8,128)(2,1)S(1)}, bf16[8,16,16,128]{3,2,1,0:T(8,128)(2,1)S(1)}) custom-call(s32[3]{0:T(128)S(1)} %pad_add_fusion.1.place_ref, s32[2,16]{1,0:T(2,128)S(1)} %compare_select_fusion.2.from_ref, bf16[8,1,2,256,256]{4,3,2,1,0:T(8,128)(2,1)S(1)} %all-to-all-done.1.near_ref, ...), custom_call_target="tpu_custom_call" | custom-call | tf_op jit(solution)/shard_map/left_products/pallas_call | solution.py:251
  245.8 3.9 %all-to-all-start.4 = ((bf16[8,16,16,128]{3,2,1,0:T(8,128)(2,1)}), bf16[8,16,16,128]{3,2,1,0:T(8,128)(2,1)S(1)}, u32[]{:S(2)}, u32[]{:S(2)}) async-start(bf16[8,16,16,128]{3,2,1,0:T(8,128)(2,1)} %add_convert_fusion), calls=%async_computation.5 | async-start | bytes 1048576 | tf_op jit(solution)/shard_map/all_to_all | solution.py:359
  253.4 14.3 %all-to-all-done.4 = bf16[8,16,16,128]{3,2,1,0:T(8,128)(2,1)S(1)} async-done(((bf16[8,16,16,128]{3,2,1,0:T(8,128)(2,1)}), bf16[8,16,16,128]{3,2,1,0:T(8,128)(2,1)S(1)}, u32[]{:S(2)}, u32[]{:S(2)}) %all-to-all-start.4) | async-done | bytes 524320 | tf_op jit(solution)/shard_map/all_to_all | solution.py:359
  (73 shorter events, 35.9 us)
Async XLA Ops:
  6.5 49.1 %copy-start = (bf16[2,4,256,256]{3,2,1,0:T(8,128)(2,1)S(1)}, bf16[2,4,256,256]{3,2,1,0:T(8,128)(2,1)}, u32[]{:S(2)}) copy-start(bf16[2,4,256,256]{3,2,1,0:T(8,128)(2,1)} %refs_1_.1) | copy-start | bytes 3145732
  6.5 73.2 %all-gather.6.cloned.1.call-start = ((), (), s32[]{:S(2)}) async-start(), calls=%async_computation.7 | async-start | bytes 2367488 | tf_op jit(solution)/shard_map/all_gather | solution.py:316
  9.3 53.6 %copy-start.9 = (s32[2,16]{1,0:T(2,128)S(1)}, s32[2,16]{1,0:T(2,128)}, u32[]{:S(2)}) copy-start(s32[2,16]{1,0:T(2,128)} %links_ref.3) | copy-start | bytes 388
  39.5 91.5 %all-gather.8.cloned.1.call-start = ((), (), s32[]{:S(2)}) async-start(), calls=%async_computation.8 | async-start | bytes 7102464 | tf_op jit(solution)/shard_map/all_gather | solution.py:321
  56.7 28.1 %collective-permute-start = (bf16[2,4,256,128]{3,2,1,0:T(8,128)(2,1)S(1)}, bf16[2,4,256,128]{3,2,1,0:T(8,128)(2,1)S(1)}, u32[]{:S(2)}, u32[]{:S(2)}) collective-permute-start(bf16[2,4,256,128]{3,2,1,0:T(8,128)(2,1)S(1)} %get-tuple-element.30), channel_id=1, source_target_pairs={{0,384},{128,0},{256,128},{384,256},{1,385},{129,1},{257,129},{385... | collective-permute-start | bytes 1572872 | tf_op jit(solution)/shard_map/ppermute | solution.py:271
  60.2 25.9 %collective-permute-start.1 = (bf16[2,4,256,128]{3,2,1,0:T(8,128)(2,1)S(1)}, bf16[2,4,256,128]{3,2,1,0:T(8,128)(2,1)S(1)}, u32[]{:S(2)}, u32[]{:S(2)}) collective-permute-start(bf16[2,4,256,128]{3,2,1,0:T(8,128)(2,1)S(1)} %get-tuple-element.30), channel_id=1, source_target_pairs={{0,128},{128,256},{256,384},{384,0},{1,129},{129,257},{257,385},{3... | collective-permute-start | bytes 1572872 | tf_op jit(solution)/shard_map/ppermute | solution.py:271
  84.8 34.1 %copy-start.2 = (bf16[2,4,256,128]{3,2,1,0:T(8,128)(2,1)}, bf16[2,4,256,128]{3,2,1,0:T(8,128)(2,1)S(1)}, u32[]{:S(2)}) copy-start(bf16[2,4,256,128]{3,2,1,0:T(8,128)(2,1)S(1)} %collective-permute-done.refs_0_.refs_1_) | copy-start | bytes 1572868
  86.0 33.6 %copy-start.4 = (bf16[2,4,256,128]{3,2,1,0:T(8,128)(2,1)}, bf16[2,4,256,128]{3,2,1,0:T(8,128)(2,1)S(1)}, u32[]{:S(2)}) copy-start(bf16[2,4,256,128]{3,2,1,0:T(8,128)(2,1)S(1)} %collective-permute-done.1.refs_4_.refs_5_) | copy-start | bytes 1572868
  86.0 64.9 %all-to-all-start.1 = ((bf16[8,1,2,256,256]{4,3,2,1,0:T(8,128)(2,1)}), bf16[8,1,2,256,256]{4,3,2,1,0:T(8,128)(2,1)S(1)}, u32[]{:S(2)}, u32[]{:S(2)}) async-start(bf16[8,1,2,256,256]{4,3,2,1,0:T(8,128)(2,1)} %right_products.4), calls=%async_computation.1 | async-start | bytes 4194304 | tf_op jit(solution)/shard_map/all_to_all | solution.py:287
  92.4 26.4 %collective-permute-start.2 = (bf16[1,4,256,128]{3,2,1,0:T(8,128)(2,1)S(1)}, bf16[1,4,256,128]{3,2,1,0:T(8,128)(2,1)S(1)}, u32[]{:S(2)}, u32[]{:S(2)}) collective-permute-start(bf16[1,4,256,128]{3,2,1,0:T(8,128)(2,1)S(1)} %slice.54), channel_id=1, source_target_pairs={{0,384},{128,0},{256,128},{384,256},{1,385},{129,1},{257,129},{385... | collective-permute-start | bytes 786440 | tf_op jit(solution)/shard_map/ppermute | solution.py:271
  96.4 22.5 %collective-permute-start.3 = (bf16[1,4,256,128]{3,2,1,0:T(8,128)(2,1)S(1)}, bf16[1,4,256,128]{3,2,1,0:T(8,128)(2,1)S(1)}, u32[]{:S(2)}, u32[]{:S(2)}) collective-permute-start(bf16[1,4,256,128]{3,2,1,0:T(8,128)(2,1)S(1)} %slice.55), channel_id=1, source_target_pairs={{0,128},{128,256},{256,384},{384,0},{1,129},{129,257},{257,385},{3... | collective-permute-start | bytes 786440 | tf_op jit(solution)/shard_map/ppermute | solution.py:271
  119.6 25.0 %collective-permute-start.4 = (bf16[2,4,256,128]{3,2,1,0:T(8,128)(2,1)}, bf16[2,4,256,128]{3,2,1,0:T(8,128)(2,1)S(1)}, u32[]{:S(2)}, u32[]{:S(2)}) collective-permute-start(bf16[2,4,256,128]{3,2,1,0:T(8,128)(2,1)} %get-tuple-element.22), channel_id=1, source_target_pairs={{0,384},{128,0},{256,128},{384,256},{1,385},{129,1},{257,129},{385... | collective-permute-start | bytes 1572872 | tf_op jit(solution)/shard_map/ppermute | solution.py:271
  122.7 28.2 %collective-permute-start.5 = (bf16[2,4,256,128]{3,2,1,0:T(8,128)(2,1)}, bf16[2,4,256,128]{3,2,1,0:T(8,128)(2,1)S(1)}, u32[]{:S(2)}, u32[]{:S(2)}) collective-permute-start(bf16[2,4,256,128]{3,2,1,0:T(8,128)(2,1)} %get-tuple-element.22), channel_id=1, source_target_pairs={{0,128},{128,256},{256,384},{384,0},{1,129},{129,257},{257,385},{3... | collective-permute-start | bytes 1572872 | tf_op jit(solution)/shard_map/ppermute | solution.py:271
  131.0 1.0 copy-start.3
  150.9 42.7 %all-to-all-start.2 = ((bf16[8,3,2,256,128]{4,3,2,1,0:T(8,128)(2,1)}), bf16[8,3,2,256,128]{4,3,2,1,0:T(8,128)(2,1)}, u32[]{:S(2)}, u32[]{:S(2)}) async-start(bf16[8,3,2,256,128]{4,3,2,1,0:T(8,128)(2,1)} %right_products.5), calls=%async_computation.2 | async-start | bytes 6291456 | tf_op jit(solution)/shard_map/all_to_all | solution.py:287
  156.3 31.5 %collective-permute-start.7 = (bf16[1,4,256,128]{3,2,1,0:T(8,128)(2,1)S(1)}, bf16[1,4,256,128]{3,2,1,0:T(8,128)(2,1)S(1)}, u32[]{:S(2)}, u32[]{:S(2)}) collective-permute-start(bf16[1,4,256,128]{3,2,1,0:T(8,128)(2,1)S(1)} %slice.56), channel_id=1, source_target_pairs={{0,384},{128,0},{256,128},{384,256},{1,385},{129,1},{257,129},{385... | collective-permute-start | bytes 786440 | tf_op jit(solution)/shard_map/ppermute | solution.py:271
  159.0 28.8 %collective-permute-start.8 = (bf16[1,4,256,128]{3,2,1,0:T(8,128)(2,1)S(1)}, bf16[1,4,256,128]{3,2,1,0:T(8,128)(2,1)S(1)}, u32[]{:S(2)}, u32[]{:S(2)}) collective-permute-start(bf16[1,4,256,128]{3,2,1,0:T(8,128)(2,1)S(1)} %slice.57), channel_id=1, source_target_pairs={{0,128},{128,256},{256,384},{384,0},{1,129},{129,257},{257,385},{3... | collective-permute-start | bytes 786440 | tf_op jit(solution)/shard_map/ppermute | solution.py:271
  192.2 6.5 %copy-start.1 = (bf16[2,4,256,256]{3,2,1,0:T(8,128)(2,1)S(1)}, bf16[2,4,256,256]{3,2,1,0:T(8,128)(2,1)}, u32[]{:S(2)}) copy-start(bf16[2,4,256,256]{3,2,1,0:T(8,128)(2,1)} %env_ref.3) | copy-start | bytes 3145732
  193.7 42.2 %all-to-all-start.3 = ((bf16[8,3,2,256,128]{4,3,2,1,0:T(8,128)(2,1)}), bf16[8,3,2,256,128]{4,3,2,1,0:T(8,128)(2,1)}, u32[]{:S(2)}, u32[]{:S(2)}) async-start(bf16[8,3,2,256,128]{4,3,2,1,0:T(8,128)(2,1)} %right_products.7), calls=%async_computation.4 | async-start | bytes 6291456 | tf_op jit(solution)/shard_map/all_to_all | solution.py:287
  198.7 51.2 %reduce-scatter.2.cloned.1.call-start = ((), (), s32[]{:S(2)}) async-start(), calls=%async_computation.6 | async-start | bytes 1179648 | tf_op jit(solution)/shard_map/reduce_scatter | solution.py:344
  204.1 45.6 %copy-start.10 = (s32[4]{0:T(128)S(1)}, s32[4]{0:T(128)}, u32[]{:S(2)}) copy-start(s32[4]{0:T(128)} %rows_ref.1) | copy-start | bytes 52
  240.5 4.4 %collective-permute-start.9 = (bf16[8,16,16,128]{3,2,1,0:T(8,128)(2,1)S(1)}, bf16[8,16,16,128]{3,2,1,0:T(8,128)(2,1)S(1)}, u32[]{:S(2)}, u32[]{:S(2)}) collective-permute-start(bf16[8,16,16,128]{3,2,1,0:T(8,128)(2,1)S(1)} %get-tuple-element.28), channel_id=1, source_target_pairs={{0,1},{1,0},{2,3},{3,2},{4,5},{5,4},{6,7},{7,6},{8,9},{9,8},{10,11... | collective-permute-start | bytes 1572872 | tf_op jit(solution)/shard_map/ppermute | solution.py:271
  245.8 21.9 %all-to-all-start.4 = ((bf16[8,16,16,128]{3,2,1,0:T(8,128)(2,1)}), bf16[8,16,16,128]{3,2,1,0:T(8,128)(2,1)S(1)}, u32[]{:S(2)}, u32[]{:S(2)}) async-start(bf16[8,16,16,128]{3,2,1,0:T(8,128)(2,1)} %add_convert_fusion), calls=%async_computation.5 | async-start | bytes 1048576 | tf_op jit(solution)/shard_map/all_to_all | solution.py:359
  250.8 16.9 %collective-permute-start.6 = (bf16[16,16,128]{2,1,0:T(8,128)(2,1)S(1)}, bf16[16,16,128]{2,1,0:T(8,128)(2,1)S(1)}, u32[]{:S(2)}, u32[]{:S(2)}) collective-permute-start(bf16[16,16,128]{2,1,0:T(8,128)(2,1)S(1)} %dynamic-slice_bitcast_fusion), channel_id=1, source_target_pairs={{0,1},{1,0},{2,3},{3,2},{4,5},{5,4},{6,7},{7,6},{8,9},{9,8},{10,11... | collective-permute-start | bytes 196616 | tf_op jit(solution)/shard_map/ppermute | solution.py:271
  (4 other events, 3.5 us)
Sparse Core Ops, SparseCore 0:
  39.6 40.1 all-gather.5
  81.9 49.1 all-gather.7
  204.3 37.1 reduce-scatter.1

commit v13 on v12

--- a/solution.py
+++ b/solution.py
@@ -323,10 +323,10 @@
     targets = lax.rem((term_links // count).reshape(1, terms * count) + moved_by, slots)
     envs = [[(right_env, term) for term in range(terms)]]
     products = right_products(place, targets, slices, envs, group, width)
-    products, above, below = lax.optimization_barrier((products, above, below))
+    after = products, above, below, parts[1]
+    products, above, below, second = lax.optimization_barrier(after)
     own = exchange(products)
 
-    across, second = lax.optimization_barrier((across, parts[1]))
     next_above, next_below = shift(second, "zh", -1), shift(second, "zh", 1)
     next_across = shift(next_above[:1], "zh", -1), shift(next_below[1:], "zh", 1)
 

time: 277 us -> 280 us (1.011)
  starting transfers between devices: 50.8 us -> 60.2 us
  waiting for transfers between devices: 120 us -> 111 us
    ppermute x10, waiting for transfers between devices: 51.6 us -> 42.2 us  [shift(): lax.ppermute(array, axis, [(i, (i + step) % size) for i in range(size)])]
    all_to_all x3, starting transfers between devices: 16.8 us -> 22.3 us  [exchange(): lax.all_to_all(products, axes, 0, 0, axis_index_groups=groups, tiled=True)]
    all_to_all x3, waiting for transfers between devices: 33.1 us -> 37.7 us  [exchange(): lax.all_to_all(products, axes, 0, 0, axis_index_groups=groups, tiled=True)]
    all_gather x1, waiting for transfers between devices: 4.49 us -> 0.01 us  [local(): far_slices = lax.all_gather(others, DEPTH)]
    ppermute x10, starting transfers between devices: 30.1 us -> 34.3 us  [shift(): lax.ppermute(array, axis, [(i, (i + step) % size) for i in range(size)])]
  transfers between devices with their start and end apart: 17 -> 17, of which waited for: 11 -> 9; matrix products, arithmetic and copies ran while one was open for 2% -> 2% of each run, Pallas kernels for 12% -> 12%
where the time goes in v13:
time: 280 us; the launch traced here: 279 us
  waiting for transfers between devices  111 us (40%)
  starting transfers between devices  60.2 us (22%)
  blocking collectives  42.8 us (15%)
  Pallas kernels  37.5 us (13%)
  between operations  13.4 us (5%)
  local copies, waits for them, and re-layouts  9.26 us (3%)
  other arithmetic  4.64 us (2%)
    ppermute x10, waiting for transfers between devices, shift(): lax.ppermute(array, axis, [(i, (i + step) % size) for i in range(size)])  42.2 us
    all_to_all x3, waiting for transfers between devices, exchange(): lax.all_to_all(products, axes, 0, 0, axis_index_groups=groups, tiled=True)  37.7 us
    ppermute x10, starting transfers between devices, shift(): lax.ppermute(array, axis, [(i, (i + step) % size) for i in range(size)])  34.3 us
    all_to_all x1, blocking collectives, local(): arrived = lax.all_to_all(buffer, REMAP, 0, 0, tiled=True)  27.6 us
    pallas_call x4, Pallas kernels, right_products(): pl.pallas_call(functools.partial(right_kernel, len(extra)), grid_spec=plt...  23 us
    all_to_all x3, starting transfers between devices, exchange(): lax.all_to_all(products, axes, 0, 0, axis_index_groups=groups, tiled=True)  22.3 us
    all_gather x1, waiting for transfers between devices, local(): slices = lax.all_gather(ordered[None], DEPTH)  16.7 us
    all_gather x1, blocking collectives, local(): around = lax.all_gather(ordered, 'zh')  15.1 us
  transfers between devices with their start and end apart: 17, of which 9 were waited for; matrix products, arithmetic and copies ran while one was open for 2% of the time, Pallas kernels for 12%

profile of v13, /device:TPU:1, one launch (start us, length us, event | category | flops | bytes accessed | tf_op | source)
XLA Modules:
  0.0 279.0 jit_solution(9465981293068638862)
XLA Ops:
  6.5 2.7 spread_blocks.1
  9.3 27.6 %all_to_all.25.in_ref = bf16[32,48,128]{2,1,0:T(8,128)(2,1)S(1)} all-to-all(bf16[32,48,128]{2,1,0:T(8,128)(2,1)} %spread_blocks.1), channel_id=1, replica_groups=mesh['zh'=4,'zl'=2,'x'=4,'y'=8,'core'=2] {'zh','zl','x'}, dimensions={0} | all-to-all | bytes 786432 | tf_op jit(solution)/shard_map/all_to_all | solution.py:304
  39.5 15.1 %all-gather.1 = bf16[68,32,128]{2,1,0:T(8,128)(2,1)S(1)} all-gather(bf16[17,32,128]{2,1,0:T(8,128)(2,1)} %order_blocks.1), channel_id=3, replica_groups=mesh['zh'=4,'zl'=2,'x'=4,'y'=8,'core'=2] {'zh'}, dimensions={0}, use_global_device_ids=true | all-gather | bytes 696320 | tf_op jit(solution)/shard_map/all_gather | solution.py:317
  56.6 3.5 %collective-permute-start = (bf16[2,4,256,128]{3,2,1,0:T(8,128)(2,1)S(1)}, bf16[2,4,256,128]{3,2,1,0:T(8,128)(2,1)S(1)}, u32[]{:S(2)}, u32[]{:S(2)}) collective-permute-start(bf16[2,4,256,128]{3,2,1,0:T(8,128)(2,1)S(1)} %get-tuple-element.26), channel_id=1, source_target_pairs={{0,384},{128,0},{256,128},{384,256},{1,385},{129,1},{257,129},{385... | collective-permute-start | bytes 1572872 | tf_op jit(solution)/shard_map/ppermute | solution.py:271
  63.0 16.7 %all-gather.6.cloned.1.call-done = bf16[272,32,128]{2,1,0:T(8,128)(2,1)} async-done(((bf16[17,32,128]{2,1,0:T(8,128)(2,1)}), bf16[272,32,128]{2,1,0:T(8,128)(2,1)}) %all-gather.6.cloned.1.call-update) | async-done | bytes 2228240 | tf_op jit(solution)/shard_map/all_gather | solution.py:316
  79.7 5.0 %right_products.4 = bf16[8,1,2,256,256]{4,3,2,1,0:T(8,128)(2,1)} custom-call(s32[3]{0:T(128)S(1)} %pad_add_fusion.1.place_ref, s32[1,32]{1,0:T(1,128)S(1)} %compare_select_fusion.targets_ref, bf16[16,1,17,32,128]{4,3,2,1,0:T(8,128)(2,1)} %bitcast.24, bf16[2,4,256,256]{3,2,1,0:T(8,128)(2,1)S(1)} %copy-done, bf16[2,4,256,256]{3,2,1,0:T(8,128)(2,1)S(1)} %copy-done), custom_call_target="tpu_custom_call" | custom-call | tf_op jit(solution)/shard_map/right_products/pallas_call | solution.py:163
  86.7 6.6 %all-to-all-start.1 = ((bf16[8,1,2,256,256]{4,3,2,1,0:T(8,128)(2,1)}), bf16[8,1,2,256,256]{4,3,2,1,0:T(8,128)(2,1)S(1)}, u32[]{:S(2)}, u32[]{:S(2)}) async-start(bf16[8,1,2,256,256]{4,3,2,1,0:T(8,128)(2,1)} %right_products.4), calls=%async_computation.1 | async-start | bytes 4194304 | tf_op jit(solution)/shard_map/all_to_all | solution.py:287
  93.3 3.7 %collective-permute-start.4 = (bf16[2,4,256,128]{3,2,1,0:T(8,128)(2,1)}, bf16[2,4,256,128]{3,2,1,0:T(8,128)(2,1)S(1)}, u32[]{:S(2)}, u32[]{:S(2)}) collective-permute-start(bf16[2,4,256,128]{3,2,1,0:T(8,128)(2,1)} %get-tuple-element.18), channel_id=1, source_target_pairs={{0,384},{128,0},{256,128},{384,256},{1,385},{129,1},{257,129},{385... | collective-permute-start | bytes 1572872 | tf_op jit(solution)/shard_map/ppermute | solution.py:271
  100.5 5.0 %collective-permute-start.2 = (bf16[1,4,256,128]{3,2,1,0:T(8,128)(2,1)S(1)}, bf16[1,4,256,128]{3,2,1,0:T(8,128)(2,1)S(1)}, u32[]{:S(2)}, u32[]{:S(2)}) collective-permute-start(bf16[1,4,256,128]{3,2,1,0:T(8,128)(2,1)S(1)} %slice.54), channel_id=1, source_target_pairs={{0,384},{128,0},{256,128},{384,256},{1,385},{129,1},{257,129},{385... | collective-permute-start | bytes 786440 | tf_op jit(solution)/shard_map/ppermute | solution.py:271
  109.1 26.3 %collective-permute-done.2.refs_2_ = bf16[1,4,256,128]{3,2,1,0:T(8,128)(2,1)S(1)} collective-permute-done((bf16[1,4,256,128]{3,2,1,0:T(8,128)(2,1)S(1)}, bf16[1,4,256,128]{3,2,1,0:T(8,128)(2,1)S(1)}, u32[]{:S(2)}, u32[]{:S(2)}) %collective-permute-start.2) | collective-permute-done | bytes 262176 | tf_op jit(solution)/shard_map/ppermute | solution.py:271
  141.6 7.8 %right_products.5 = bf16[8,3,2,256,128]{4,3,2,1,0:T(8,128)(2,1)} custom-call(s32[3]{0:T(128)S(1)} %pad_add_fusion.1.place_ref, s32[3,32]{1,0:T(4,128)S(1)} %negate_select_fusion.targets_ref, bf16[16,3,17,32,128]{4,3,2,1,0:T(8,128)(2,1)} %bitcast.20, bf16[2,4,256,128]{3,2,1,0:T(8,128)(2,1)S(1)} %copy-done.3, bf16[2,4,256,128]{3,2,1,0:T(8,128)(2,1)S(1)} %copy-done.3, ...), custom_call_target="tpu_custom_call" | custom-call | tf_op jit(solution)/shard_map/right_products/pallas_call | solution.py:163
  149.4 6.3 %all-to-all-start.2 = ((bf16[8,3,2,256,128]{4,3,2,1,0:T(8,128)(2,1)}), bf16[8,3,2,256,128]{4,3,2,1,0:T(8,128)(2,1)}, u32[]{:S(2)}, u32[]{:S(2)}) async-start(bf16[8,3,2,256,128]{4,3,2,1,0:T(8,128)(2,1)} %right_products.5), calls=%async_computation.2 | async-start | bytes 6291456 | tf_op jit(solution)/shard_map/all_to_all | solution.py:287
  155.7 8.1 %collective-permute-start.7 = (bf16[1,4,256,128]{3,2,1,0:T(8,128)(2,1)S(1)}, bf16[1,4,256,128]{3,2,1,0:T(8,128)(2,1)S(1)}, u32[]{:S(2)}, u32[]{:S(2)}) collective-permute-start(bf16[1,4,256,128]{3,2,1,0:T(8,128)(2,1)S(1)} %slice.56), channel_id=1, source_target_pairs={{0,384},{128,0},{256,128},{384,256},{1,385},{129,1},{257,129},{385... | collective-permute-start | bytes 786440 | tf_op jit(solution)/shard_map/ppermute | solution.py:271
  165.9 5.7 %right_products.6.refs_2_ = bf16[8,3,2,256,128]{4,3,2,1,0:T(8,128)(2,1)} custom-call(s32[3]{0:T(128)S(1)} %pad_add_fusion.1.place_ref, s32[2,32]{1,0:T(2,128)S(1)} %pad_add_fusion.targets_ref, bf16[16,3,17,32,128]{4,3,2,1,0:T(8,128)(2,1)} %bitcast.21, bf16[2,4,256,128]{3,2,1,0:T(8,128)(2,1)S(1)} %collective-permute-done.4.refs_0_.refs_1_, ...), custom_call_target="tpu_custom_call" | custom-call | tf_op jit(solution)/shard_map/right_products/pallas_call | solution.py:163
  171.6 10.8 %collective-permute-done.7.refs_0_ = bf16[1,4,256,128]{3,2,1,0:T(8,128)(2,1)S(1)} collective-permute-done((bf16[1,4,256,128]{3,2,1,0:T(8,128)(2,1)S(1)}, bf16[1,4,256,128]{3,2,1,0:T(8,128)(2,1)S(1)}, u32[]{:S(2)}, u32[]{:S(2)}) %collective-permute-start.7) | collective-permute-done | bytes 262176 | tf_op jit(solution)/shard_map/ppermute | solution.py:271
  182.4 4.4 %right_products.7 = bf16[8,3,2,256,128]{4,3,2,1,0:T(8,128)(2,1)} custom-call(s32[3]{0:T(128)S(1)} %pad_add_fusion.1.place_ref, s32[1,32]{1,0:T(1,128)S(1)} %get-tuple-element.29.targets_ref, bf16[16,3,17,32,128]{4,3,2,1,0:T(8,128)(2,1)} %bitcast.22, bf16[1,4,256,128]{3,2,1,0:T(8,128)(2,1)S(1)} %collective-permute-done.7.refs_0_, ...), custom_call_target="tpu_custom_call", output_to_operand_aliasing={{}: (5, {})} | custom-call | tf_op jit(solution)/shard_map/right_products/pallas_call | solution.py:163
  186.9 6.0 %all-to-all-done.2.far_ref = bf16[8,3,2,256,128]{4,3,2,1,0:T(8,128)(2,1)} async-done(((bf16[8,3,2,256,128]{4,3,2,1,0:T(8,128)(2,1)}), bf16[8,3,2,256,128]{4,3,2,1,0:T(8,128)(2,1)}, u32[]{:S(2)}, u32[]{:S(2)}) %all-to-all-start.2) | async-done | bytes 3145760 | tf_op jit(solution)/shard_map/all_to_all | solution.py:287
  192.8 9.4 %all-to-all-start.3 = ((bf16[8,3,2,256,128]{4,3,2,1,0:T(8,128)(2,1)}), bf16[8,3,2,256,128]{4,3,2,1,0:T(8,128)(2,1)}, u32[]{:S(2)}, u32[]{:S(2)}) async-start(bf16[8,3,2,256,128]{4,3,2,1,0:T(8,128)(2,1)} %right_products.7), calls=%async_computation.4 | async-start | bytes 6291456 | tf_op jit(solution)/shard_map/all_to_all | solution.py:287
  202.2 5.4 %left_products.2 = bf16[16,16,16,128]{3,2,1,0:T(8,128)(2,1)} custom-call(s32[3]{0:T(128)S(1)} %pad_add_fusion.1.place_ref, s32[2,16]{1,0:T(2,128)S(1)} %compare_select_fusion.2.from_ref, bf16[8,1,2,256,256]{4,3,2,1,0:T(8,128)(2,1)S(1)} %all-to-all-done.1.near_ref, bf16[8,3,2,256,128]{4,3,2,1,0:T(8,128)(2,1)} %all-to-all-done.2.far_ref, ...), custom_call_target="tpu_custom_call" | custom-call | tf_op jit(solution)/shard_map/left_products/pallas_call | solution.py:251
  207.6 31.8 %all-to-all-done.3.far_ref = bf16[8,3,2,256,128]{4,3,2,1,0:T(8,128)(2,1)} async-done(((bf16[8,3,2,256,128]{4,3,2,1,0:T(8,128)(2,1)}), bf16[8,3,2,256,128]{4,3,2,1,0:T(8,128)(2,1)}, u32[]{:S(2)}, u32[]{:S(2)}) %all-to-all-start.3) | async-done | bytes 3145760 | tf_op jit(solution)/shard_map/all_to_all | solution.py:287
  239.4 4.7 %left_products.3 = (bf16[8,16,16,128]{3,2,1,0:T(8,128)(2,1)S(1)}, bf16[8,16,16,128]{3,2,1,0:T(8,128)(2,1)S(1)}) custom-call(s32[3]{0:T(128)S(1)} %pad_add_fusion.1.place_ref, s32[2,16]{1,0:T(2,128)S(1)} %compare_select_fusion.2.from_ref, bf16[8,1,2,256,256]{4,3,2,1,0:T(8,128)(2,1)S(1)} %all-to-all-done.1.near_ref, ...), custom_call_target="tpu_custom_call" | custom-call | tf_op jit(solution)/shard_map/left_products/pallas_call | solution.py:251
  244.1 2.8 collective-permute-start.9
  249.3 3.5 %all-to-all-start.4 = ((bf16[8,16,16,128]{3,2,1,0:T(8,128)(2,1)}), bf16[8,16,16,128]{3,2,1,0:T(8,128)(2,1)S(1)}, u32[]{:S(2)}, u32[]{:S(2)}) async-start(bf16[8,16,16,128]{3,2,1,0:T(8,128)(2,1)} %add_convert_fusion), calls=%async_computation.5 | async-start | bytes 1048576 | tf_op jit(solution)/shard_map/all_to_all | solution.py:359
  256.2 14.6 %all-to-all-done.4 = bf16[8,16,16,128]{3,2,1,0:T(8,128)(2,1)S(1)} async-done(((bf16[8,16,16,128]{3,2,1,0:T(8,128)(2,1)}), bf16[8,16,16,128]{3,2,1,0:T(8,128)(2,1)S(1)}, u32[]{:S(2)}, u32[]{:S(2)}) %all-to-all-start.4) | async-done | bytes 524320 | tf_op jit(solution)/shard_map/all_to_all | solution.py:359
  (73 shorter events, 32.1 us)
Async XLA Ops:
  6.5 49.1 %copy-start = (bf16[2,4,256,256]{3,2,1,0:T(8,128)(2,1)S(1)}, bf16[2,4,256,256]{3,2,1,0:T(8,128)(2,1)}, u32[]{:S(2)}) copy-start(bf16[2,4,256,256]{3,2,1,0:T(8,128)(2,1)} %refs_1_.1) | copy-start | bytes 3145732
  6.5 73.2 %all-gather.6.cloned.1.call-start = ((), (), s32[]{:S(2)}) async-start(), calls=%async_computation.7 | async-start | bytes 2367488 | tf_op jit(solution)/shard_map/all_gather | solution.py:316
  9.3 53.5 %copy-start.9 = (s32[2,16]{1,0:T(2,128)S(1)}, s32[2,16]{1,0:T(2,128)}, u32[]{:S(2)}) copy-start(s32[2,16]{1,0:T(2,128)} %links_ref.3) | copy-start | bytes 388
  39.5 99.1 %all-gather.8.cloned.1.call-start = ((), (), s32[]{:S(2)}) async-start(), calls=%async_computation.8 | async-start | bytes 7102464 | tf_op jit(solution)/shard_map/all_gather | solution.py:321
  56.6 28.2 %collective-permute-start = (bf16[2,4,256,128]{3,2,1,0:T(8,128)(2,1)S(1)}, bf16[2,4,256,128]{3,2,1,0:T(8,128)(2,1)S(1)}, u32[]{:S(2)}, u32[]{:S(2)}) collective-permute-start(bf16[2,4,256,128]{3,2,1,0:T(8,128)(2,1)S(1)} %get-tuple-element.26), channel_id=1, source_target_pairs={{0,384},{128,0},{256,128},{384,256},{1,385},{129,1},{257,129},{385... | collective-permute-start | bytes 1572872 | tf_op jit(solution)/shard_map/ppermute | solution.py:271
  60.1 25.9 %collective-permute-start.1 = (bf16[2,4,256,128]{3,2,1,0:T(8,128)(2,1)S(1)}, bf16[2,4,256,128]{3,2,1,0:T(8,128)(2,1)S(1)}, u32[]{:S(2)}, u32[]{:S(2)}) collective-permute-start(bf16[2,4,256,128]{3,2,1,0:T(8,128)(2,1)S(1)} %get-tuple-element.26), channel_id=1, source_target_pairs={{0,128},{128,256},{256,384},{384,0},{1,129},{129,257},{257,385},{3... | collective-permute-start | bytes 1572872 | tf_op jit(solution)/shard_map/ppermute | solution.py:271
  84.8 1.2 copy-start.2
  86.7 62.6 %all-to-all-start.1 = ((bf16[8,1,2,256,256]{4,3,2,1,0:T(8,128)(2,1)}), bf16[8,1,2,256,256]{4,3,2,1,0:T(8,128)(2,1)S(1)}, u32[]{:S(2)}, u32[]{:S(2)}) async-start(bf16[8,1,2,256,256]{4,3,2,1,0:T(8,128)(2,1)} %right_products.4), calls=%async_computation.1 | async-start | bytes 4194304 | tf_op jit(solution)/shard_map/all_to_all | solution.py:287
  93.3 56.0 %collective-permute-start.4 = (bf16[2,4,256,128]{3,2,1,0:T(8,128)(2,1)}, bf16[2,4,256,128]{3,2,1,0:T(8,128)(2,1)S(1)}, u32[]{:S(2)}, u32[]{:S(2)}) collective-permute-start(bf16[2,4,256,128]{3,2,1,0:T(8,128)(2,1)} %get-tuple-element.18), channel_id=1, source_target_pairs={{0,384},{128,0},{256,128},{384,256},{1,385},{129,1},{257,129},{385... | collective-permute-start | bytes 1572872 | tf_op jit(solution)/shard_map/ppermute | solution.py:271
  97.1 52.3 %collective-permute-start.5 = (bf16[2,4,256,128]{3,2,1,0:T(8,128)(2,1)}, bf16[2,4,256,128]{3,2,1,0:T(8,128)(2,1)S(1)}, u32[]{:S(2)}, u32[]{:S(2)}) collective-permute-start(bf16[2,4,256,128]{3,2,1,0:T(8,128)(2,1)} %get-tuple-element.18), channel_id=1, source_target_pairs={{0,128},{128,256},{256,384},{384,0},{1,129},{129,257},{257,385},{3... | collective-permute-start | bytes 1572872 | tf_op jit(solution)/shard_map/ppermute | solution.py:271
  100.5 34.9 %collective-permute-start.2 = (bf16[1,4,256,128]{3,2,1,0:T(8,128)(2,1)S(1)}, bf16[1,4,256,128]{3,2,1,0:T(8,128)(2,1)S(1)}, u32[]{:S(2)}, u32[]{:S(2)}) collective-permute-start(bf16[1,4,256,128]{3,2,1,0:T(8,128)(2,1)S(1)} %slice.54), channel_id=1, source_target_pairs={{0,384},{128,0},{256,128},{384,256},{1,385},{129,1},{257,129},{385... | collective-permute-start | bytes 786440 | tf_op jit(solution)/shard_map/ppermute | solution.py:271
  106.4 31.4 %collective-permute-start.3 = (bf16[1,4,256,128]{3,2,1,0:T(8,128)(2,1)S(1)}, bf16[1,4,256,128]{3,2,1,0:T(8,128)(2,1)S(1)}, u32[]{:S(2)}, u32[]{:S(2)}) collective-permute-start(bf16[1,4,256,128]{3,2,1,0:T(8,128)(2,1)S(1)} %slice.55), channel_id=1, source_target_pairs={{0,128},{128,256},{256,384},{384,0},{1,129},{129,257},{257,385},{3... | collective-permute-start | bytes 786440 | tf_op jit(solution)/shard_map/ppermute | solution.py:271
  138.6 1.0 copy-start.3
  139.6 1.0 copy-start.5
  149.4 43.4 %all-to-all-start.2 = ((bf16[8,3,2,256,128]{4,3,2,1,0:T(8,128)(2,1)}), bf16[8,3,2,256,128]{4,3,2,1,0:T(8,128)(2,1)}, u32[]{:S(2)}, u32[]{:S(2)}) async-start(bf16[8,3,2,256,128]{4,3,2,1,0:T(8,128)(2,1)} %right_products.5), calls=%async_computation.2 | async-start | bytes 6291456 | tf_op jit(solution)/shard_map/all_to_all | solution.py:287
  155.7 26.7 %collective-permute-start.7 = (bf16[1,4,256,128]{3,2,1,0:T(8,128)(2,1)S(1)}, bf16[1,4,256,128]{3,2,1,0:T(8,128)(2,1)S(1)}, u32[]{:S(2)}, u32[]{:S(2)}) collective-permute-start(bf16[1,4,256,128]{3,2,1,0:T(8,128)(2,1)S(1)} %slice.56), channel_id=1, source_target_pairs={{0,384},{128,0},{256,128},{384,256},{1,385},{129,1},{257,129},{385... | collective-permute-start | bytes 786440 | tf_op jit(solution)/shard_map/ppermute | solution.py:271
  163.9 18.5 %collective-permute-start.8 = (bf16[1,4,256,128]{3,2,1,0:T(8,128)(2,1)S(1)}, bf16[1,4,256,128]{3,2,1,0:T(8,128)(2,1)S(1)}, u32[]{:S(2)}, u32[]{:S(2)}) collective-permute-start(bf16[1,4,256,128]{3,2,1,0:T(8,128)(2,1)S(1)} %slice.57), channel_id=1, source_target_pairs={{0,128},{128,256},{256,384},{384,0},{1,129},{129,257},{257,385},{3... | collective-permute-start | bytes 786440 | tf_op jit(solution)/shard_map/ppermute | solution.py:271
  186.9 15.4 %copy-start.1 = (bf16[2,4,256,256]{3,2,1,0:T(8,128)(2,1)S(1)}, bf16[2,4,256,256]{3,2,1,0:T(8,128)(2,1)}, u32[]{:S(2)}) copy-start(bf16[2,4,256,256]{3,2,1,0:T(8,128)(2,1)} %env_ref.3) | copy-start | bytes 3145732
  192.8 46.6 %all-to-all-start.3 = ((bf16[8,3,2,256,128]{4,3,2,1,0:T(8,128)(2,1)}), bf16[8,3,2,256,128]{4,3,2,1,0:T(8,128)(2,1)}, u32[]{:S(2)}, u32[]{:S(2)}) async-start(bf16[8,3,2,256,128]{4,3,2,1,0:T(8,128)(2,1)} %right_products.7), calls=%async_computation.4 | async-start | bytes 6291456 | tf_op jit(solution)/shard_map/all_to_all | solution.py:287
  202.2 50.8 %reduce-scatter.2.cloned.1.call-start = ((), (), s32[]{:S(2)}) async-start(), calls=%async_computation.6 | async-start | bytes 1179648 | tf_op jit(solution)/shard_map/reduce_scatter | solution.py:344
  207.6 45.2 %copy-start.10 = (s32[4]{0:T(128)S(1)}, s32[4]{0:T(128)}, u32[]{:S(2)}) copy-start(s32[4]{0:T(128)} %rows_ref.1) | copy-start | bytes 52
  244.1 4.3 %collective-permute-start.9 = (bf16[8,16,16,128]{3,2,1,0:T(8,128)(2,1)S(1)}, bf16[8,16,16,128]{3,2,1,0:T(8,128)(2,1)S(1)}, u32[]{:S(2)}, u32[]{:S(2)}) collective-permute-start(bf16[8,16,16,128]{3,2,1,0:T(8,128)(2,1)S(1)} %get-tuple-element.24), channel_id=1, source_target_pairs={{0,1},{1,0},{2,3},{3,2},{4,5},{5,4},{6,7},{7,6},{8,9},{9,8},{10,11... | collective-permute-start | bytes 1572872 | tf_op jit(solution)/shard_map/ppermute | solution.py:271
  249.3 21.4 %all-to-all-start.4 = ((bf16[8,16,16,128]{3,2,1,0:T(8,128)(2,1)}), bf16[8,16,16,128]{3,2,1,0:T(8,128)(2,1)S(1)}, u32[]{:S(2)}, u32[]{:S(2)}) async-start(bf16[8,16,16,128]{3,2,1,0:T(8,128)(2,1)} %add_convert_fusion), calls=%async_computation.5 | async-start | bytes 1048576 | tf_op jit(solution)/shard_map/all_to_all | solution.py:359
  253.9 16.9 %collective-permute-start.6 = (bf16[16,16,128]{2,1,0:T(8,128)(2,1)S(1)}, bf16[16,16,128]{2,1,0:T(8,128)(2,1)S(1)}, u32[]{:S(2)}, u32[]{:S(2)}) collective-permute-start(bf16[16,16,128]{2,1,0:T(8,128)(2,1)S(1)} %dynamic-slice_bitcast_fusion), channel_id=1, source_target_pairs={{0,1},{1,0},{2,3},{3,2},{4,5},{5,4},{6,7},{7,6},{8,9},{9,8},{10,11... | collective-permute-start | bytes 196616 | tf_op jit(solution)/shard_map/ppermute | solution.py:271
  (4 other events, 3.3 us)
Sparse Core Ops, SparseCore 0:
  39.6 40.1 all-gather.5
  81.9 49.1 all-gather.7
  207.8 36.0 reduce-scatter.1

commit v14 on v12

--- a/solution.py
+++ b/solution.py
@@ -327,8 +327,9 @@
     own = exchange(products)
 
     across, second = lax.optimization_barrier((across, parts[1]))
-    next_above, next_below = shift(second, "zh", -1), shift(second, "zh", 1)
-    next_across = shift(next_above[:1], "zh", -1), shift(next_below[1:], "zh", 1)
+    next_above, next_below = shift(second[:1], "zh", -1), shift(second[:1], "zh", 1)
+    late_above, late_below = shift(second[1:], "zh", -1), shift(second[1:], "zh", 1)
+    next_across = shift(next_above, "zh", -1), shift(late_below, "zh", 1)
 
     envs = [
         [(above, 0), (above, 1)],
@@ -347,7 +348,7 @@
     pieces = [kept.astype(jnp.float32) + received.astype(jnp.float32)]
 
     sides = jnp.stack([far_targets[0], far_targets[2]])
-    envs = [[(next_above, 0), (next_above, 1)], [(next_below, 0), (next_below, 1)]]
+    envs = [[(next_above, 0), (late_above, 0)], [(next_below, 0), (late_below, 0)]]
     products = right_products(place, sides, far_slices, envs, group, LANES, 0, 2)
     envs = [[(next_across[0], 0), (next_across[1], 0)]]
     products = right_products(

time: 277 us -> 286 us (1.032)
  starting transfers between devices: 50.8 us -> 64.3 us
  waiting for transfers between devices: 120 us -> 114 us
    ppermute x10 -> x12, starting transfers between devices: 30.1 us -> 36 us  [shift(): lax.ppermute(array, axis, [(i, (i + step) % size) for i in range(size)])]
    all_to_all x3, starting transfers between devices: 16.8 us -> 21.7 us  [exchange(): lax.all_to_all(products, axes, 0, 0, axis_index_groups=groups, tiled=True)]
    ppermute x10 -> x12, waiting for transfers between devices: 51.6 us -> 49.2 us  [shift(): lax.ppermute(array, axis, [(i, (i + step) % size) for i in range(size)])]
  transfers between devices with their start and end apart: 17 -> 19, of which waited for: 11 -> 10; matrix products, arithmetic and copies ran while one was open for 2% -> 2% of each run, Pallas kernels for 12% -> 12%
where the time goes in v14:
time: 286 us; the launch traced here: 285 us
  waiting for transfers between devices  114 us (40%)
  starting transfers between devices  64.3 us (22%)
  blocking collectives  42.8 us (15%)
  Pallas kernels  37.5 us (13%)
  between operations  13.4 us (5%)
  local copies, waits for them, and re-layouts  7.99 us (3%)
  other arithmetic  4.61 us (2%)
    ppermute x12, waiting for transfers between devices, shift(): lax.ppermute(array, axis, [(i, (i + step) % size) for i in range(size)])  49.2 us
    ppermute x12, starting transfers between devices, shift(): lax.ppermute(array, axis, [(i, (i + step) % size) for i in range(size)])  36 us
    all_to_all x3, waiting for transfers between devices, exchange(): lax.all_to_all(products, axes, 0, 0, axis_index_groups=groups, tiled=True)  31.8 us
    all_to_all x1, blocking collectives, local(): arrived = lax.all_to_all(buffer, REMAP, 0, 0, tiled=True)  27.6 us
    pallas_call x4, Pallas kernels, right_products(): pl.pallas_call(functools.partial(right_kernel, len(extra)), grid_spec=plt...  23 us
    all_to_all x3, starting transfers between devices, exchange(): lax.all_to_all(products, axes, 0, 0, axis_index_groups=groups, tiled=True)  21.7 us
    all_gather x1, waiting for transfers between devices, local(): slices = lax.all_gather(ordered[None], DEPTH)  16.7 us
    all_gather x1, blocking collectives, local(): around = lax.all_gather(ordered, 'zh')  15.1 us
  transfers between devices with their start and end apart: 19, of which 10 were waited for; matrix products, arithmetic and copies ran while one was open for 2% of the time, Pallas kernels for 12%

profile of v14, /device:TPU:1, one launch (start us, length us, event | category | flops | bytes accessed | tf_op | source)
XLA Modules:
  0.0 284.6 jit_solution(10262585893998335761)
XLA Ops:
  9.3 27.6 %all_to_all.25.in_ref = bf16[32,48,128]{2,1,0:T(8,128)(2,1)S(1)} all-to-all(bf16[32,48,128]{2,1,0:T(8,128)(2,1)} %spread_blocks.1), channel_id=1, replica_groups=mesh['zh'=4,'zl'=2,'x'=4,'y'=8,'core'=2] {'zh','zl','x'}, dimensions={0} | all-to-all | bytes 786432 | tf_op jit(solution)/shard_map/all_to_all | solution.py:304
  39.5 15.1 %all-gather.1 = bf16[68,32,128]{2,1,0:T(8,128)(2,1)S(1)} all-gather(bf16[17,32,128]{2,1,0:T(8,128)(2,1)} %order_blocks.1), channel_id=3, replica_groups=mesh['zh'=4,'zl'=2,'x'=4,'y'=8,'core'=2] {'zh'}, dimensions={0}, use_global_device_ids=true | all-gather | bytes 696320 | tf_op jit(solution)/shard_map/all_gather | solution.py:317
  56.7 3.5 %collective-permute-start = (bf16[2,4,256,128]{3,2,1,0:T(8,128)(2,1)S(1)}, bf16[2,4,256,128]{3,2,1,0:T(8,128)(2,1)S(1)}, u32[]{:S(2)}, u32[]{:S(2)}) collective-permute-start(bf16[2,4,256,128]{3,2,1,0:T(8,128)(2,1)S(1)} %get-tuple-element.30), channel_id=1, source_target_pairs={{0,384},{128,0},{256,128},{384,256},{1,385},{129,1},{257,129},{385... | collective-permute-start | bytes 1572872 | tf_op jit(solution)/shard_map/ppermute | solution.py:271
  63.1 16.7 %all-gather.6.cloned.1.call-done = bf16[272,32,128]{2,1,0:T(8,128)(2,1)} async-done(((bf16[17,32,128]{2,1,0:T(8,128)(2,1)}), bf16[272,32,128]{2,1,0:T(8,128)(2,1)}) %all-gather.6.cloned.1.call-update) | async-done | bytes 2228240 | tf_op jit(solution)/shard_map/all_gather | solution.py:316
  79.7 5.1 %right_products.4 = bf16[8,1,2,256,256]{4,3,2,1,0:T(8,128)(2,1)} custom-call(s32[3]{0:T(128)S(1)} %pad_add_fusion.1.place_ref, s32[1,32]{1,0:T(1,128)S(1)} %compare_select_fusion.targets_ref, bf16[16,1,17,32,128]{4,3,2,1,0:T(8,128)(2,1)} %bitcast.24, bf16[2,4,256,256]{3,2,1,0:T(8,128)(2,1)S(1)} %copy-done, bf16[2,4,256,256]{3,2,1,0:T(8,128)(2,1)S(1)} %copy-done), custom_call_target="tpu_custom_call" | custom-call | tf_op jit(solution)/shard_map/right_products/pallas_call | solution.py:163
  86.0 6.3 %all-to-all-start.1 = ((bf16[8,1,2,256,256]{4,3,2,1,0:T(8,128)(2,1)}), bf16[8,1,2,256,256]{4,3,2,1,0:T(8,128)(2,1)S(1)}, u32[]{:S(2)}, u32[]{:S(2)}) async-start(bf16[8,1,2,256,256]{4,3,2,1,0:T(8,128)(2,1)} %right_products.4), calls=%async_computation.1 | async-start | bytes 4194304 | tf_op jit(solution)/shard_map/all_to_all | solution.py:287
  92.4 3.8 %collective-permute-start.2 = (bf16[1,4,256,128]{3,2,1,0:T(8,128)(2,1)S(1)}, bf16[1,4,256,128]{3,2,1,0:T(8,128)(2,1)S(1)}, u32[]{:S(2)}, u32[]{:S(2)}) collective-permute-start(bf16[1,4,256,128]{3,2,1,0:T(8,128)(2,1)S(1)} %slice.56), channel_id=1, source_target_pairs={{0,384},{128,0},{256,128},{384,256},{1,385},{129,1},{257,129},{385... | collective-permute-start | bytes 786440 | tf_op jit(solution)/shard_map/ppermute | solution.py:271
  98.6 20.2 %collective-permute-done.2.refs_2_ = bf16[1,4,256,128]{3,2,1,0:T(8,128)(2,1)S(1)} collective-permute-done((bf16[1,4,256,128]{3,2,1,0:T(8,128)(2,1)S(1)}, bf16[1,4,256,128]{3,2,1,0:T(8,128)(2,1)S(1)}, u32[]{:S(2)}, u32[]{:S(2)}) %collective-permute-start.2) | collective-permute-done | bytes 262176 | tf_op jit(solution)/shard_map/ppermute | solution.py:271
  122.1 3.0 %collective-permute-start.4 = (bf16[1,4,256,128]{3,2,1,0:T(8,128)(2,1)}, bf16[1,4,256,128]{3,2,1,0:T(8,128)(2,1)S(1)}, u32[]{:S(2)}, u32[]{:S(2)}) collective-permute-start(bf16[1,4,256,128]{3,2,1,0:T(8,128)(2,1)} %get-tuple-element.32), channel_id=1, source_target_pairs={{0,384},{128,0},{256,128},{384,256},{1,385},{129,1},{257,129},{385... | collective-permute-start | bytes 786440 | tf_op jit(solution)/shard_map/ppermute | solution.py:271
  125.1 3.2 %collective-permute-start.5 = (bf16[1,4,256,128]{3,2,1,0:T(8,128)(2,1)}, bf16[1,4,256,128]{3,2,1,0:T(8,128)(2,1)}, u32[]{:S(2)}, u32[]{:S(2)}) collective-permute-start(bf16[1,4,256,128]{3,2,1,0:T(8,128)(2,1)} %get-tuple-element.32), channel_id=1, source_target_pairs={{0,128},{128,256},{256,384},{384,0},{1,129},{129,257},{257,385},{3... | collective-permute-start | bytes 786440 | tf_op jit(solution)/shard_map/ppermute | solution.py:271
  132.9 7.8 %right_products.5 = bf16[8,3,2,256,128]{4,3,2,1,0:T(8,128)(2,1)} custom-call(s32[3]{0:T(128)S(1)} %pad_add_fusion.1.place_ref, s32[3,32]{1,0:T(4,128)S(1)} %negate_select_fusion.targets_ref, bf16[16,3,17,32,128]{4,3,2,1,0:T(8,128)(2,1)} %bitcast.20, bf16[2,4,256,128]{3,2,1,0:T(8,128)(2,1)S(1)} %collective-permute-done.refs_0_.refs_1_, ...), custom_call_target="tpu_custom_call" | custom-call | tf_op jit(solution)/shard_map/right_products/pallas_call | solution.py:163
  142.5 6.4 %all-to-all-start.2 = ((bf16[8,3,2,256,128]{4,3,2,1,0:T(8,128)(2,1)}), bf16[8,3,2,256,128]{4,3,2,1,0:T(8,128)(2,1)}, u32[]{:S(2)}, u32[]{:S(2)}) async-start(bf16[8,3,2,256,128]{4,3,2,1,0:T(8,128)(2,1)} %right_products.5), calls=%async_computation.2 | async-start | bytes 6291456 | tf_op jit(solution)/shard_map/all_to_all | solution.py:287
  150.8 5.5 %collective-permute-start.10 = (bf16[1,4,256,128]{3,2,1,0:T(8,128)(2,1)S(1)}, bf16[1,4,256,128]{3,2,1,0:T(8,128)(2,1)S(1)}, u32[]{:S(2)}, u32[]{:S(2)}) collective-permute-start(bf16[1,4,256,128]{3,2,1,0:T(8,128)(2,1)S(1)} %copy-done.7), channel_id=1, source_target_pairs={{0,384},{128,0},{256,128},{384,256},{1,385},{129,1},{257,129},{385... | collective-permute-start | bytes 786440 | tf_op jit(solution)/shard_map/ppermute | solution.py:271
  156.3 2.8 collective-permute-start.7
  159.1 5.2 %collective-permute-done.8.refs_3_ = bf16[1,4,256,128]{3,2,1,0:T(8,128)(2,1)S(1)} collective-permute-done((bf16[1,4,256,128]{3,2,1,0:T(8,128)(2,1)S(1)}, bf16[1,4,256,128]{3,2,1,0:T(8,128)(2,1)S(1)}, u32[]{:S(2)}, u32[]{:S(2)}) %collective-permute-start.8) | collective-permute-done | bytes 262176 | tf_op jit(solution)/shard_map/ppermute | solution.py:271
  166.2 19.3 %collective-permute-done.10.refs_1_ = bf16[1,4,256,128]{3,2,1,0:T(8,128)(2,1)S(1)} collective-permute-done((bf16[1,4,256,128]{3,2,1,0:T(8,128)(2,1)S(1)}, bf16[1,4,256,128]{3,2,1,0:T(8,128)(2,1)S(1)}, u32[]{:S(2)}, u32[]{:S(2)}) %collective-permute-start.10) | collective-permute-done | bytes 262176 | tf_op jit(solution)/shard_map/ppermute | solution.py:271
  185.5 5.7 %right_products.6.refs_2_ = bf16[8,3,2,256,128]{4,3,2,1,0:T(8,128)(2,1)} custom-call(s32[3]{0:T(128)S(1)} %pad_add_fusion.1.place_ref, s32[2,32]{1,0:T(2,128)S(1)} %pad_add_fusion.targets_ref, bf16[16,3,17,32,128]{4,3,2,1,0:T(8,128)(2,1)} %bitcast.21, bf16[1,4,256,128]{3,2,1,0:T(8,128)(2,1)S(1)} %collective-permute-done.4.refs_0_, ...), custom_call_target="tpu_custom_call" | custom-call | tf_op jit(solution)/shard_map/right_products/pallas_call | solution.py:163
  191.3 4.4 %right_products.7 = bf16[8,3,2,256,128]{4,3,2,1,0:T(8,128)(2,1)} custom-call(s32[3]{0:T(128)S(1)} %pad_add_fusion.1.place_ref, s32[1,32]{1,0:T(1,128)S(1)} %get-tuple-element.35.targets_ref, bf16[16,3,17,32,128]{4,3,2,1,0:T(8,128)(2,1)} %bitcast.22, bf16[1,4,256,128]{3,2,1,0:T(8,128)(2,1)S(1)} %collective-permute-done.7.refs_0_, ...), custom_call_target="tpu_custom_call", output_to_operand_aliasing={{}: (5, {})} | custom-call | tf_op jit(solution)/shard_map/right_products/pallas_call | solution.py:163
  195.7 8.9 %all-to-all-start.3 = ((bf16[8,3,2,256,128]{4,3,2,1,0:T(8,128)(2,1)}), bf16[8,3,2,256,128]{4,3,2,1,0:T(8,128)(2,1)}, u32[]{:S(2)}, u32[]{:S(2)}) async-start(bf16[8,3,2,256,128]{4,3,2,1,0:T(8,128)(2,1)} %right_products.7), calls=%async_computation.4 | async-start | bytes 6291456 | tf_op jit(solution)/shard_map/all_to_all | solution.py:287
  204.6 5.4 %left_products.2 = bf16[16,16,16,128]{3,2,1,0:T(8,128)(2,1)} custom-call(s32[3]{0:T(128)S(1)} %pad_add_fusion.1.place_ref, s32[2,16]{1,0:T(2,128)S(1)} %compare_select_fusion.2.from_ref, bf16[8,1,2,256,256]{4,3,2,1,0:T(8,128)(2,1)S(1)} %all-to-all-done.1.near_ref, bf16[8,3,2,256,128]{4,3,2,1,0:T(8,128)(2,1)} %all-to-all-done.2.far_ref, ...), custom_call_target="tpu_custom_call" | custom-call | tf_op jit(solution)/shard_map/left_products/pallas_call | solution.py:251
  210.0 31.8 %all-to-all-done.3.far_ref = bf16[8,3,2,256,128]{4,3,2,1,0:T(8,128)(2,1)} async-done(((bf16[8,3,2,256,128]{4,3,2,1,0:T(8,128)(2,1)}), bf16[8,3,2,256,128]{4,3,2,1,0:T(8,128)(2,1)}, u32[]{:S(2)}, u32[]{:S(2)}) %all-to-all-start.3) | async-done | bytes 3145760 | tf_op jit(solution)/shard_map/all_to_all | solution.py:287
  241.8 4.7 %left_products.3 = (bf16[8,16,16,128]{3,2,1,0:T(8,128)(2,1)S(1)}, bf16[8,16,16,128]{3,2,1,0:T(8,128)(2,1)S(1)}) custom-call(s32[3]{0:T(128)S(1)} %pad_add_fusion.1.place_ref, s32[2,16]{1,0:T(2,128)S(1)} %compare_select_fusion.2.from_ref, bf16[8,1,2,256,256]{4,3,2,1,0:T(8,128)(2,1)S(1)} %all-to-all-done.1.near_ref, ...), custom_call_target="tpu_custom_call" | custom-call | tf_op jit(solution)/shard_map/left_products/pallas_call | solution.py:251
  251.7 6.7 %all-to-all-start.4 = ((bf16[8,16,16,128]{3,2,1,0:T(8,128)(2,1)}), bf16[8,16,16,128]{3,2,1,0:T(8,128)(2,1)S(1)}, u32[]{:S(2)}, u32[]{:S(2)}) async-start(bf16[8,16,16,128]{3,2,1,0:T(8,128)(2,1)} %add_convert_fusion), calls=%async_computation.5 | async-start | bytes 1048576 | tf_op jit(solution)/shard_map/all_to_all | solution.py:360
  262.0 14.3 %all-to-all-done.4 = bf16[8,16,16,128]{3,2,1,0:T(8,128)(2,1)S(1)} async-done(((bf16[8,16,16,128]{3,2,1,0:T(8,128)(2,1)}), bf16[8,16,16,128]{3,2,1,0:T(8,128)(2,1)S(1)}, u32[]{:S(2)}, u32[]{:S(2)}) %all-to-all-start.4) | async-done | bytes 524320 | tf_op jit(solution)/shard_map/all_to_all | solution.py:360
  (74 shorter events, 38.0 us)
Async XLA Ops:
  6.5 49.0 %copy-start = (bf16[2,4,256,256]{3,2,1,0:T(8,128)(2,1)S(1)}, bf16[2,4,256,256]{3,2,1,0:T(8,128)(2,1)}, u32[]{:S(2)}) copy-start(bf16[2,4,256,256]{3,2,1,0:T(8,128)(2,1)} %refs_1_.1) | copy-start | bytes 3145732
  6.5 73.2 %all-gather.6.cloned.1.call-start = ((), (), s32[]{:S(2)}) async-start(), calls=%async_computation.7 | async-start | bytes 2367488 | tf_op jit(solution)/shard_map/all_gather | solution.py:316
  9.3 53.6 %copy-start.8 = (s32[2,16]{1,0:T(2,128)S(1)}, s32[2,16]{1,0:T(2,128)}, u32[]{:S(2)}) copy-start(s32[2,16]{1,0:T(2,128)} %links_ref.3) | copy-start | bytes 388
  39.5 91.5 %all-gather.8.cloned.1.call-start = ((), (), s32[]{:S(2)}) async-start(), calls=%async_computation.8 | async-start | bytes 7102464 | tf_op jit(solution)/shard_map/all_gather | solution.py:321
  56.7 28.1 %collective-permute-start = (bf16[2,4,256,128]{3,2,1,0:T(8,128)(2,1)S(1)}, bf16[2,4,256,128]{3,2,1,0:T(8,128)(2,1)S(1)}, u32[]{:S(2)}, u32[]{:S(2)}) collective-permute-start(bf16[2,4,256,128]{3,2,1,0:T(8,128)(2,1)S(1)} %get-tuple-element.30), channel_id=1, source_target_pairs={{0,384},{128,0},{256,128},{384,256},{1,385},{129,1},{257,129},{385... | collective-permute-start | bytes 1572872 | tf_op jit(solution)/shard_map/ppermute | solution.py:271
  60.1 25.9 %collective-permute-start.1 = (bf16[2,4,256,128]{3,2,1,0:T(8,128)(2,1)S(1)}, bf16[2,4,256,128]{3,2,1,0:T(8,128)(2,1)S(1)}, u32[]{:S(2)}, u32[]{:S(2)}) collective-permute-start(bf16[2,4,256,128]{3,2,1,0:T(8,128)(2,1)S(1)} %get-tuple-element.30), channel_id=1, source_target_pairs={{0,128},{128,256},{256,384},{384,0},{1,129},{129,257},{257,385},{3... | collective-permute-start | bytes 1572872 | tf_op jit(solution)/shard_map/ppermute | solution.py:271
  86.0 56.5 %all-to-all-start.1 = ((bf16[8,1,2,256,256]{4,3,2,1,0:T(8,128)(2,1)}), bf16[8,1,2,256,256]{4,3,2,1,0:T(8,128)(2,1)S(1)}, u32[]{:S(2)}, u32[]{:S(2)}) async-start(bf16[8,1,2,256,256]{4,3,2,1,0:T(8,128)(2,1)} %right_products.4), calls=%async_computation.1 | async-start | bytes 4194304 | tf_op jit(solution)/shard_map/all_to_all | solution.py:287
  92.4 26.4 %collective-permute-start.2 = (bf16[1,4,256,128]{3,2,1,0:T(8,128)(2,1)S(1)}, bf16[1,4,256,128]{3,2,1,0:T(8,128)(2,1)S(1)}, u32[]{:S(2)}, u32[]{:S(2)}) collective-permute-start(bf16[1,4,256,128]{3,2,1,0:T(8,128)(2,1)S(1)} %slice.56), channel_id=1, source_target_pairs={{0,384},{128,0},{256,128},{384,256},{1,385},{129,1},{257,129},{385... | collective-permute-start | bytes 786440 | tf_op jit(solution)/shard_map/ppermute | solution.py:271
  96.2 23.3 %collective-permute-start.3 = (bf16[1,4,256,128]{3,2,1,0:T(8,128)(2,1)S(1)}, bf16[1,4,256,128]{3,2,1,0:T(8,128)(2,1)S(1)}, u32[]{:S(2)}, u32[]{:S(2)}) collective-permute-start(bf16[1,4,256,128]{3,2,1,0:T(8,128)(2,1)S(1)} %slice.57), channel_id=1, source_target_pairs={{0,128},{128,256},{256,384},{384,0},{1,129},{129,257},{257,385},{3... | collective-permute-start | bytes 786440 | tf_op jit(solution)/shard_map/ppermute | solution.py:271
  122.1 18.6 %collective-permute-start.4 = (bf16[1,4,256,128]{3,2,1,0:T(8,128)(2,1)}, bf16[1,4,256,128]{3,2,1,0:T(8,128)(2,1)S(1)}, u32[]{:S(2)}, u32[]{:S(2)}) collective-permute-start(bf16[1,4,256,128]{3,2,1,0:T(8,128)(2,1)} %get-tuple-element.32), channel_id=1, source_target_pairs={{0,384},{128,0},{256,128},{384,256},{1,385},{129,1},{257,129},{385... | collective-permute-start | bytes 786440 | tf_op jit(solution)/shard_map/ppermute | solution.py:271
  125.1 17.4 %collective-permute-start.5 = (bf16[1,4,256,128]{3,2,1,0:T(8,128)(2,1)}, bf16[1,4,256,128]{3,2,1,0:T(8,128)(2,1)}, u32[]{:S(2)}, u32[]{:S(2)}) collective-permute-start(bf16[1,4,256,128]{3,2,1,0:T(8,128)(2,1)} %get-tuple-element.32), channel_id=1, source_target_pairs={{0,128},{128,256},{256,384},{384,0},{1,129},{129,257},{257,385},{3... | collective-permute-start | bytes 786440 | tf_op jit(solution)/shard_map/ppermute | solution.py:271
  140.7 8.2 %copy-start.7 = (bf16[1,4,256,128]{3,2,1,0:T(8,128)(2,1)S(1)}, bf16[1,4,256,128]{3,2,1,0:T(8,128)(2,1)}, u32[]{:S(2)}) copy-start(bf16[1,4,256,128]{3,2,1,0:T(8,128)(2,1)} %get-tuple-element.31) | copy-start | bytes 786436
  142.5 53.2 %all-to-all-start.2 = ((bf16[8,3,2,256,128]{4,3,2,1,0:T(8,128)(2,1)}), bf16[8,3,2,256,128]{4,3,2,1,0:T(8,128)(2,1)}, u32[]{:S(2)}, u32[]{:S(2)}) async-start(bf16[8,3,2,256,128]{4,3,2,1,0:T(8,128)(2,1)} %right_products.5), calls=%async_computation.2 | async-start | bytes 6291456 | tf_op jit(solution)/shard_map/all_to_all | solution.py:287
  148.9 15.4 %collective-permute-start.8 = (bf16[1,4,256,128]{3,2,1,0:T(8,128)(2,1)S(1)}, bf16[1,4,256,128]{3,2,1,0:T(8,128)(2,1)S(1)}, u32[]{:S(2)}, u32[]{:S(2)}) collective-permute-start(bf16[1,4,256,128]{3,2,1,0:T(8,128)(2,1)S(1)} %copy-done.7), channel_id=1, source_target_pairs={{0,128},{128,256},{256,384},{384,0},{1,129},{129,257},{257,385},{3... | collective-permute-start | bytes 786440 | tf_op jit(solution)/shard_map/ppermute | solution.py:271
  150.8 34.7 %collective-permute-start.10 = (bf16[1,4,256,128]{3,2,1,0:T(8,128)(2,1)S(1)}, bf16[1,4,256,128]{3,2,1,0:T(8,128)(2,1)S(1)}, u32[]{:S(2)}, u32[]{:S(2)}) collective-permute-start(bf16[1,4,256,128]{3,2,1,0:T(8,128)(2,1)S(1)} %copy-done.7), channel_id=1, source_target_pairs={{0,384},{128,0},{256,128},{384,256},{1,385},{129,1},{257,129},{385... | collective-permute-start | bytes 786440 | tf_op jit(solution)/shard_map/ppermute | solution.py:271
  156.3 35.0 %collective-permute-start.7 = (bf16[1,4,256,128]{3,2,1,0:T(8,128)(2,1)S(1)}, bf16[1,4,256,128]{3,2,1,0:T(8,128)(2,1)S(1)}, u32[]{:S(2)}, u32[]{:S(2)}) collective-permute-start(bf16[1,4,256,128]{3,2,1,0:T(8,128)(2,1)S(1)} %collective-permute-done.4.refs_0_), channel_id=1, source_target_pairs={{0,384},{128,0},{256,128},{384,256},{1,385},{129,1},{257,129},{385... | collective-permute-start | bytes 786440 | tf_op jit(solution)/shard_map/ppermute | solution.py:271
  164.3 27.0 %collective-permute-start.9 = (bf16[1,4,256,128]{3,2,1,0:T(8,128)(2,1)S(1)}, bf16[1,4,256,128]{3,2,1,0:T(8,128)(2,1)S(1)}, u32[]{:S(2)}, u32[]{:S(2)}) collective-permute-start(bf16[1,4,256,128]{3,2,1,0:T(8,128)(2,1)S(1)} %collective-permute-done.8.refs_3_), channel_id=1, source_target_pairs={{0,128},{128,256},{256,384},{384,0},{1,129},{129,257},{257,385},{3... | collective-permute-start | bytes 786440 | tf_op jit(solution)/shard_map/ppermute | solution.py:271
  195.7 9.0 %copy-start.1 = (bf16[2,4,256,256]{3,2,1,0:T(8,128)(2,1)S(1)}, bf16[2,4,256,256]{3,2,1,0:T(8,128)(2,1)}, u32[]{:S(2)}) copy-start(bf16[2,4,256,256]{3,2,1,0:T(8,128)(2,1)} %env_ref.3) | copy-start | bytes 3145732
  195.7 46.2 %all-to-all-start.3 = ((bf16[8,3,2,256,128]{4,3,2,1,0:T(8,128)(2,1)}), bf16[8,3,2,256,128]{4,3,2,1,0:T(8,128)(2,1)}, u32[]{:S(2)}, u32[]{:S(2)}) async-start(bf16[8,3,2,256,128]{4,3,2,1,0:T(8,128)(2,1)} %right_products.7), calls=%async_computation.4 | async-start | bytes 6291456 | tf_op jit(solution)/shard_map/all_to_all | solution.py:287
  204.6 54.0 %reduce-scatter.2.cloned.1.call-start = ((), (), s32[]{:S(2)}) async-start(), calls=%async_computation.6 | async-start | bytes 1179648 | tf_op jit(solution)/shard_map/reduce_scatter | solution.py:345
  210.0 48.3 %copy-start.9 = (s32[4]{0:T(128)S(1)}, s32[4]{0:T(128)}, u32[]{:S(2)}) copy-start(s32[4]{0:T(128)} %rows_ref.1) | copy-start | bytes 52
  246.5 4.3 %collective-permute-start.11 = (bf16[8,16,16,128]{3,2,1,0:T(8,128)(2,1)S(1)}, bf16[8,16,16,128]{3,2,1,0:T(8,128)(2,1)S(1)}, u32[]{:S(2)}, u32[]{:S(2)}) collective-permute-start(bf16[8,16,16,128]{3,2,1,0:T(8,128)(2,1)S(1)} %get-tuple-element.28), channel_id=1, source_target_pairs={{0,1},{1,0},{2,3},{3,2},{4,5},{5,4},{6,7},{7,6},{8,9},{9,8},{10,11... | collective-permute-start | bytes 1572872 | tf_op jit(solution)/shard_map/ppermute | solution.py:271
  251.7 24.6 %all-to-all-start.4 = ((bf16[8,16,16,128]{3,2,1,0:T(8,128)(2,1)}), bf16[8,16,16,128]{3,2,1,0:T(8,128)(2,1)S(1)}, u32[]{:S(2)}, u32[]{:S(2)}) async-start(bf16[8,16,16,128]{3,2,1,0:T(8,128)(2,1)} %add_convert_fusion), calls=%async_computation.5 | async-start | bytes 1048576 | tf_op jit(solution)/shard_map/all_to_all | solution.py:360
  259.4 16.9 %collective-permute-start.6 = (bf16[16,16,128]{2,1,0:T(8,128)(2,1)S(1)}, bf16[16,16,128]{2,1,0:T(8,128)(2,1)S(1)}, u32[]{:S(2)}, u32[]{:S(2)}) collective-permute-start(bf16[16,16,128]{2,1,0:T(8,128)(2,1)S(1)} %dynamic-slice_bitcast_fusion), channel_id=1, source_target_pairs={{0,1},{1,0},{2,3},{3,2},{4,5},{5,4},{6,7},{7,6},{8,9},{9,8},{10,11... | collective-permute-start | bytes 196616 | tf_op jit(solution)/shard_map/ppermute | solution.py:271
  (5 other events, 4.1 us)
Sparse Core Ops, SparseCore 0:
  39.6 40.1 all-gather.5
  81.9 49.1 all-gather.7
  210.1 39.2 reduce-scatter.1
